TPU v7x, 32 devices: a whole 2x2x4 slice. The times are simulated.
32 devices in a mesh: worker: 4 (over y, x), fsdp: 8 (over z, core).
Axes of the slice: x: 2, y: 2, z: 4, core: 2. Of those that a mesh axis runs over, the one named last changes fastest.
Arguments:
- params: float32 [4, 4096, 128], P('worker', 'fsdp'), may hold values from -6 to 6
- first_moment: float32 [4, 4096, 128], P('worker', 'fsdp'), may hold values from -4 to 4
- second_moment: float32 [4, 4096, 128], P('worker', 'fsdp'), may hold values from 0.05 to 2
- global_fragment: float32 [1024, 128], P('fsdp'), may hold values from -6 to 6
- outer_momentum: float32 [1024, 128], P('fsdp'), may hold values from -6 to 6
- features: bfloat16 [4, 1024, 4096], P('worker', 'fsdp'), may hold values from -6 to 6
- cotangent: bfloat16 [4, 1024, 128], P('worker', 'fsdp'), may hold values from -192 to 192
- token_counts: int32 [4], replicated, may hold values from 128 to 1024
- fragment_index: int32 [1], replicated, may hold values from 0 to 3
Outputs:
- new_params: float32 [4, 4096, 128], P('worker', 'fsdp')
- new_first: float32 [4, 4096, 128], P('worker', 'fsdp')
- new_second: float32 [4, 4096, 128], P('worker', 'fsdp')
- new_global: float32 [1024, 128], P('fsdp')
- new_momentum: float32 [1024, 128], P('fsdp')
All inputs are finite; a program needn't handle non-finite values.
Results may differ from a plain program's by a relative error of at most 0.0003.
Values sent between devices are 32-bit elements; how exact they have to be, the bound alone decides.
No kernel may reach another device: no remote copies, remote signals or barrier semaphores. Data moves between devices by JAX's collectives and lax.ppermute only.
A program may use at most 64 MiB of HBM per device.

v0:
```python
import jax
import jax.numpy as jnp
from jax import lax
from jax.sharding import PartitionSpec as P

FRAGS = 4


BETA_ONE = 0.9
BETA_TWO = 0.95
CORRECT_ONE = 0.6513216
CORRECT_TWO = 0.401263
ADAM_EPS = 1e-08
LEARN_RATE = 0.02
DECAY_RATE = 0.1
NESTEROV = 0.9
OUTER_RATE = 0.7
MIXING = 0.5


def contract_rows(left_rows, right_rows):
    return lax.dot_general(
        left_rows, right_rows, (((0,), (0,)), ((), ())), preferred_element_type=jnp.float32
    )


def body(
    params,
    first_moment,
    second_moment,
    global_fragment,
    outer_momentum,
    features,
    cotangent,
    token_counts,
    fragment_index,
):
    worker = lax.axis_index("worker")
    live_count = lax.dynamic_index_in_dim(token_counts, worker, 0, keepdims=False)
    tok_local = features.shape[1]
    positions = lax.axis_index("fsdp") * tok_local + lax.iota(jnp.int32, tok_local)
    valid_rows = (positions < live_count)[:, None]
    masked = jnp.where(valid_rows, cotangent[0], jnp.zeros_like(cotangent[0]))
    feats = features[0]
    local_rows = params.shape[1]
    term = contract_rows(feats, masked)
    summed = lax.psum_scatter(term, "fsdp", scatter_dimension=0, tiled=True)
    gradient = summed / live_count.astype(jnp.float32)
    fragment = fragment_index[0]
    width = params.shape[2]
    before = params[0]
    before_three = before.reshape(local_rows // FRAGS, FRAGS, width)
    old_piece = lax.dynamic_index_in_dim(before_three, fragment, 1, keepdims=False)
    token_total = jnp.sum(token_counts).astype(jnp.float32)
    drift_term = live_count.astype(jnp.float32) * (global_fragment - old_piece)
    pseudo_grad = lax.psum(drift_term, "worker") / token_total
    momentum = NESTEROV * outer_momentum + pseudo_grad
    fresh_global = global_fragment - OUTER_RATE * (pseudo_grad + NESTEROV * momentum)
    first_new = BETA_ONE * first_moment[0] + (1.0 - BETA_ONE) * gradient
    second_new = BETA_TWO * second_moment[0] + (1.0 - BETA_TWO) * gradient * gradient
    update = first_new / CORRECT_ONE / (jnp.sqrt(second_new / CORRECT_TWO) + ADAM_EPS)
    inner_params = before - LEARN_RATE * (update + DECAY_RATE * before)
    inner_three = inner_params.reshape(local_rows // FRAGS, FRAGS, width)
    inner_piece = lax.dynamic_index_in_dim(inner_three, fragment, 1, keepdims=False)
    mixed_piece = MIXING * fresh_global + (1.0 - MIXING) * inner_piece
    result = lax.dynamic_update_index_in_dim(inner_three, mixed_piece, fragment, 1).reshape(
        local_rows, width
    )
    return (result[None], first_new[None], second_new[None], fresh_global, momentum)


def solution(mesh):
    placed = (
        P("worker", "fsdp", None),
        P("worker", "fsdp", None),
        P("worker", "fsdp", None),
        P("fsdp", None),
        P("fsdp", None),
        P("worker", "fsdp", None),
        P("worker", "fsdp", None),
        P(),
        P(),
    )
    return jax.shard_map(
        body,
        mesh=mesh,
        in_specs=placed,
        out_specs=(
            P("worker", "fsdp", None),
            P("worker", "fsdp", None),
            P("worker", "fsdp", None),
            P("fsdp", None),
            P("fsdp", None),
        ),
        check_vma=False,
    )
```

profile of v0, /device:TPU:0, one launch (start us, length us, event | category | flops | bytes accessed | tf_op | source)
XLA Modules:
  0.0 72.6 jit_solution(16273754278569493980)
XLA Ops:
  8.0 0.0 copy-start
  8.0 0.0 reduce-scatter.2.cloned.1.call-start
  8.1 1.3 %dynamic_slice.11 = s32[1]{0:T(128)} dynamic-slice(s32[4]{0:T(128)} %param.16, s32[]{:T(128)S(6)} %select_n.18), dynamic_slice_sizes={1} | dynamic-slice | bytes 12 | tf_op jit(solution)/shard_map/jit(dynamic_index_in_dim)/dynamic_slice | solution.py:39
  9.4 0.7 add_compare_fusion
  10.0 0.0 copy-done
  10.0 0.0 copy-start.1
  10.1 0.0 copy-start.5
  10.1 2.7 %convolution_bitcast_fusion = f32[4096,128]{0,1:T(8,128)} fusion(bf16[1,128,4096]{2,1,0:T(8,128)(2,1)S(1)} %copy-done, bf16[1,128,128]{2,1,0:T(8,128)(2,1)} %param.15, pred[128]{0:T(512)(128)(4,1)S(1)} %add_compare_fusion), kind=kOutput, calls=%fused_computation | convolution fusion | flops 134234112 | bytes 3178624 | tf_op jit(solution)/shard_map/dot_general | solution.py:22
  12.8 0.0 reduce-scatter.2.cloned.1.call-update
  12.8 0.0 all-reduce.2.cloned.1.call-start
  14.2 0.0 copy-done.1
  14.2 0.1 constant_dynamic-slice_fusion.1
  14.3 0.0 copy-done.5
  14.3 0.6 subtract_multiply_fusion
  14.9 0.0 all-reduce.2.cloned.1.call-update
  15.0 0.1 copy.23
  15.1 0.0 copy-done.7
  15.1 0.6 reduce_sum.9
  15.7 0.0 copy-done.3
  15.7 0.1 copy.24
  15.9 0.0 copy-done.4
  15.9 0.1 copy.25
  16.7 34.8 %reduce-scatter.2.cloned.1.call-done = f32[512,128]{0,1:T(8,128)} async-done(((f32[4096,128]{0,1:T(8,128)}), f32[512,128]{0,1:T(8,128)}) %reduce-scatter.2.cloned.1.call-update) | async-done | bytes 262160 | tf_op jit(solution)/shard_map/reduce_scatter | solution.py:47
  51.5 1.2 %fusion.10 = (f32[1,512,128]{1,2,0:T(8,128)S(1)}, f32[512,128]{0,1:T(8,128)S(1)}, f32[1,512,128]{1,2,0:T(8,128)S(1)}) fusion(f32[512,128]{0,1:T(8,128)} %reduce-scatter.2.cloned.1.call-done, f32[]{:T(128)S(6)} %convert_element_type.7, f32[1,512,128]{1,2,0:T(8,128)S(1)} %copy.25, f32[1,512,128]{1,2,0:T(8,128)S(1)} %copy.24, f32[1,512,128]{1,2,0:T(8,128)S(1)} %copy.23), kind=kLoop, calls=%fused_computation.24 | loop fusion | flops 1048576 | bytes 1835012 | tf_op jit(solution)/shard_map/broadcast_in_dim | solution.py:69
  52.7 0.1 copy.26
  52.8 0.1 constant_dynamic-slice_fusion
  52.9 7.6 %all-reduce.2.cloned.1.call-done = f32[128,128]{1,0:T(8,128)} async-done(((f32[128,128]{1,0:T(8,128)}), f32[128,128]{1,0:T(8,128)}) %all-reduce.2.cloned.1.call-update) | async-done | bytes 65552 | tf_op jit(solution)/shard_map/psum | solution.py:56
  60.5 1.5 %add_multiply_fusion = (f32[128,128]{1,0:T(8,128)S(1)}, f32[128,128]{1,0:T(8,128)}, f32[128,128]{1,0:T(8,128)}) fusion(f32[128,128]{1,0:T(8,128)S(1)} %bitcast.51, f32[128,128]{1,0:T(8,128)S(1)} %copy-done.5, f32[128,128]{1,0:T(8,128)} %all-reduce.2.cloned.1.call-done, f32[]{:T(128)S(6)} %convert_element_type.8, f32[128,128]{1,0:T(8,128)S(1)} %copy-done.6), kind=kLoop, calls=%fused_computation.10 | loop fusion | flops 147456 | bytes 458756 | tf_op jit(solution)/shard_map/add | solution.py:65
  62.0 1.5 %dynamic_update_slice.4 = f32[128,4,128]{2,1,0:T(4,128)S(1)} dynamic-update-slice(f32[128,4,128]{2,1,0:T(4,128)S(1)} %bitcast.48, f32[128,1,128]{2,1,0:T(1,128)S(1)} %bitcast.52, s32[]{:T(128)} %constant.14.clone.1, s32[]{:T(128)S(6)} %select_n.21, s32[]{:T(128)} %constant.14.clone.1) | dynamic-update-slice | bytes 131076 | tf_op jit(solution)/shard_map/jit(dynamic_update_index_in_dim)/dynamic_update_slice | solution.py:66
  63.5 0.0 copy-start.2
  63.5 0.8 %copy.28 = f32[1,512,128]{2,1,0:T(8,128)} copy(f32[1,512,128]{1,2,0:T(8,128)S(1)} %get-tuple-element.20) | data formatting | bytes 524288
  64.3 0.8 %copy.29 = f32[1,512,128]{2,1,0:T(8,128)} copy(f32[1,512,128]{1,2,0:T(8,128)S(1)} %get-tuple-element.18) | data formatting | bytes 524288
  (6 shorter events, 0.0 us)
Async XLA Ops:
  8.0 2.0 %copy-start = (bf16[1,128,4096]{2,1,0:T(8,128)(2,1)S(1)}, bf16[1,128,4096]{2,1,0:T(8,128)(2,1)}, u32[]{:S(2)}) copy-start(bf16[1,128,4096]{2,1,0:T(8,128)(2,1)} %param.14) | copy-start | bytes 3145732
  8.0 43.5 %reduce-scatter.2.cloned.1.call-start = ((), (), s32[]{:S(2)}) async-start(), calls=%async_computation.1 | async-start | bytes 2359296 | tf_op jit(solution)/shard_map/reduce_scatter | solution.py:47
  10.0 4.1 %copy-start.1 = (f32[1,512,128]{2,1,0:T(8,128)S(1)}, f32[1,512,128]{2,1,0:T(8,128)}, u32[]{:S(2)}) copy-start(f32[1,512,128]{2,1,0:T(8,128)} %param.9) | copy-start | bytes 786436
  10.1 4.2 %copy-start.5 = (f32[128,128]{1,0:T(8,128)S(1)}, f32[128,128]{1,0:T(8,128)}, u32[]{:S(2)}) copy-start(f32[128,128]{1,0:T(8,128)} %param.12) | copy-start | bytes 196612
  12.8 2.3 %copy-start.7 = (s32[4]{0:T(128)S(1)}, s32[4]{0:T(128)}, u32[]{:S(2)}) copy-start(s32[4]{0:T(128)} %param.16) | copy-start | bytes 52
  12.8 3.0 %copy-start.3 = (f32[1,512,128]{2,1,0:T(8,128)S(1)}, f32[1,512,128]{2,1,0:T(8,128)}, u32[]{:S(2)}) copy-start(f32[1,512,128]{2,1,0:T(8,128)} %param.10) | copy-start | bytes 786436
  12.8 3.1 %copy-start.4 = (f32[1,512,128]{2,1,0:T(8,128)S(1)}, f32[1,512,128]{2,1,0:T(8,128)}, u32[]{:S(2)}) copy-start(f32[1,512,128]{2,1,0:T(8,128)} %param.11) | copy-start | bytes 786436
  12.8 47.7 %all-reduce.2.cloned.1.call-start = ((), (), s32[]{:S(2)}) async-start(), calls=%async_computation.2 | async-start | bytes 131072 | tf_op jit(solution)/shard_map/psum | solution.py:56
  14.9 45.6 %copy-start.6 = (f32[128,128]{1,0:T(8,128)S(1)}, f32[128,128]{1,0:T(8,128)}, u32[]{:S(2)}) copy-start(f32[128,128]{1,0:T(8,128)} %param.13) | copy-start | bytes 196612
  63.5 1.7 %copy-start.2 = (f32[128,4,128]{2,1,0:T(4,128)}, f32[128,4,128]{2,1,0:T(4,128)S(1)}, u32[]{:S(2)}) copy-start(f32[128,4,128]{2,1,0:T(4,128)S(1)} %dynamic_update_slice.4) | copy-start | bytes 786436
Sparse Core Ops, SparseCore 0:
  12.9 38.5 reduce-scatter.1
Sparse Core Ops, SparseCore 1:
  16.7 43.7 all-reduce.1
where the time goes:
time: 72.9 us; the launch traced here: 72.6 us
  waiting for transfers between devices  42.5 us (58%)
  between operations  17.6 us (24%)
  local copies, waits for them, and re-layouts  5.13 us (7%)
  other arithmetic  4.62 us (6%)
  matrix products  2.68 us (4%)
    reduce_scatter x1, waiting for transfers between devices, body(): summed = lax.psum_scatter(term, 'fsdp', scatter_dimension=0, tiled=True)  34.8 us
    psum x1, waiting for transfers between devices, body(): pseudo_grad = lax.psum(drift_term, 'worker') / token_total  7.64 us
    dot_general x1, matrix products, contract_rows(): lax.dot_general(left_rows, right_rows, (((0,), (0,)), ((), ())), preferre...  2.68 us
    unnamed x21, local copies, waits for them, and re-layouts  2.1 us
    add x1, other arithmetic, body(): mixed_piece = MIXING * fresh_global + (1.0 - MIXING) * inner_piece  1.51 us
    dynamic_update_slice x1, local copies, waits for them, and re-layouts, body(): lax.dynamic_update_index_in_dim(inner_three, mixed_piece, fragment, 1)  1.46 us
  transfers between devices with their start and end apart: 2, of which 2 were waited for; matrix products, arithmetic and copies ran while one was open for 4% of the time, Pallas kernels for 0%

commit v1 on v0

v1 whole, which is shorter than its diff:
```python
import functools

import jax
import jax.numpy as jnp
from jax import lax
from jax.experimental import pallas as pl
from jax.experimental.pallas import tpu as pltpu
from jax.sharding import PartitionSpec as P

FRAGS = 4
LANES = 128

BETA_ONE = 0.9
BETA_TWO = 0.95
CORRECT_ONE = 0.6513216
CORRECT_TWO = 0.401263
ADAM_EPS = 1e-08
LEARN_RATE = 0.02
DECAY_RATE = 0.1
NESTEROV = 0.9
OUTER_RATE = 0.7
MIXING = 0.5

VMEM = pl.BlockSpec(memory_space=pltpu.VMEM)
SMEM = pl.BlockSpec(memory_space=pltpu.SMEM)
HBM = pl.BlockSpec(memory_space=pl.ANY)
ROOM = 8 << 20


def masked_rows(counts, cot_ref):
    tokens = cot_ref.shape[1]
    live = counts[lax.axis_index("worker")] - lax.axis_index("fsdp") * tokens
    cot = cot_ref[0].astype(jnp.float32)
    rows = lax.broadcasted_iota(jnp.int32, cot.shape, 0)
    return jnp.where(rows < live, cot, 0.0).astype(jnp.bfloat16)


def products(order, counts, cot_ref, features, held, sems, put):
    rows = held.shape[2]
    me = lax.axis_index("fsdp")
    copies = []
    for slot, q in enumerate(order):
        columns = pl.ds(pl.multiple_of((me ^ q) * rows, LANES), rows)
        copies.append(pltpu.make_async_copy(features.at[0, :, columns], held.at[slot], sems.at[slot]))
        copies[-1].start()
    masked = masked_rows(counts, cot_ref)
    for slot, q in enumerate(order):
        copies[slot].wait()
        put(q, lax.dot_general(masked, held[slot], (((0,), (0,)), ((), ())), preferred_element_type=jnp.float32))


def first_kernel(order, counts, cot_ref, features, away, kept, held, sems):
    def put(q, value):
        (away if q & 1 else kept)[0] = value

    products(order, counts, cot_ref, features, held, sems, put)


def rest_kernel(order, counts, fragment, cot_ref, params, global_fragment, features, away, kept, drift, held, sems):
    def put(q, value):
        (away if q & 1 else kept)[q // 2] = value

    products(order, counts, cot_ref, features, held, sems, put)
    pieces = global_fragment.shape[0]
    old = params[0, pl.ds(fragment[0], pieces, stride=FRAGS), :]
    drift[...] = counts[lax.axis_index("worker")].astype(jnp.float32) * (global_fragment[...] - old)


def adam(before, first, second, gradient):
    first_new = BETA_ONE * first + (1.0 - BETA_ONE) * gradient
    second_new = BETA_TWO * second + (1.0 - BETA_TWO) * gradient * gradient
    update = first_new / CORRECT_ONE / (jnp.sqrt(second_new / CORRECT_TWO) + ADAM_EPS)
    return before - LEARN_RATE * (update + DECAY_RATE * before), first_new, second_new


def outer(pseudo_grad, global_fragment, outer_momentum):
    momentum = NESTEROV * outer_momentum + pseudo_grad
    return global_fragment - OUTER_RATE * (pseudo_grad + NESTEROV * momentum), momentum


def last_kernel(
    workers, terms, counts, fragment, params, first, second, global_fragment, outer_momentum, drift_sum, *refs
):
    parts, (new_params, new_first, new_second, new_global, new_momentum) = refs[:terms], refs[terms:]
    live = counts[lax.axis_index("worker")].astype(jnp.float32)
    total = counts[0]
    for other in range(1, workers):
        total = total + counts[other]
    fresh, momentum = outer(drift_sum[...] / total.astype(jnp.float32), global_fragment[...], outer_momentum[...])
    new_global[...] = fresh
    new_momentum[...] = momentum
    rows = params.shape[1]
    for at in range(0, rows, LANES):
        here = pl.ds(at, LANES)
        summed = parts[0][0, :, here]
        for part in parts[1:]:
            summed = summed + part[0, :, here]
        gradient = summed.T / live
        new_params[0, here, :], new_first[0, here, :], new_second[0, here, :] = adam(
            params[0, here, :], first[0, here, :], second[0, here, :], gradient
        )
    mine = pl.ds(fragment[0], rows // FRAGS, stride=FRAGS)
    new_params[0, mine, :] = MIXING * fresh + (1.0 - MIXING) * new_params[0, mine, :]


def hop(value, axis, devices, bit):
    return lax.ppermute(value, axis, [(d, d ^ bit) for d in range(devices)])


def doubling_sum(value, axis, devices):
    bit = devices // 2
    while bit:
        value = value + hop(value, axis, devices, bit)
        bit //= 2
    return value


def fast_body(mesh):
    workers, devices = mesh.shape["worker"], mesh.shape["fsdp"]

    def body(
        params, first, second, global_fragment, outer_momentum, features, cotangent, token_counts, fragment_index
    ):
        rows, width = params.shape[1:]
        pieces, tokens = global_fragment.shape[0], features.shape[1]
        far = devices - 2
        orders = ([far + 1, far], [q + s for q in range(far - 2, -1, -2) for s in (1, 0)])
        block = functools.partial(jax.ShapeDtypeStruct, dtype=jnp.float32)

        def scratch(count):
            return [pltpu.VMEM((count, tokens, rows), jnp.bfloat16), pltpu.SemaphoreType.DMA((count,))]

        def cost(count):
            return pl.CostEstimate(
                flops=2 * count * tokens * rows * width,
                bytes_accessed=count * rows * (2 * tokens + 4 * width),
                transcendentals=0,
            )

        room = pltpu.CompilerParams(vmem_limit_bytes=ROOM)
        away_far, kept_far = pl.pallas_call(
            functools.partial(first_kernel, orders[0]),
            out_shape=[block((1, width, rows))] * 2,
            in_specs=[SMEM, VMEM, HBM],
            out_specs=[VMEM] * 2,
            scratch_shapes=scratch(2),
            compiler_params=room,
            cost_estimate=cost(2),
        )(token_counts, cotangent, features)
        come_far = hop(away_far, "fsdp", devices, 1)
        near = devices // 2 - 1
        away, kept, drift = pl.pallas_call(
            functools.partial(rest_kernel, orders[1]),
            out_shape=[block((near, width, rows))] * 2 + [block((pieces, width))],
            in_specs=[SMEM, SMEM, VMEM, VMEM, VMEM, HBM],
            out_specs=[VMEM] * 3,
            scratch_shapes=scratch(2 * near),
            compiler_params=room,
            cost_estimate=cost(2 * near),
        )(token_counts, fragment_index, cotangent, params, global_fragment, features)
        come = hop(away, "fsdp", devices, 1)
        step_far = hop(kept_far + come_far, "fsdp", devices, 2)
        step_near = hop(kept[1:2] + come[1:2], "fsdp", devices, 2)
        last = hop(kept[2:3] + come[2:3] + step_far, "fsdp", devices, 4)
        drift_sum = doubling_sum(drift, "worker", workers)
        parts = (kept[0:1], come[0:1], step_near, last)
        state = block(params.shape)
        piece = block(global_fragment.shape)
        return pl.pallas_call(
            functools.partial(last_kernel, workers, len(parts)),
            out_shape=[state] * 3 + [piece] * 2,
            in_specs=[SMEM] * 2 + [VMEM] * (6 + len(parts)),
            out_specs=[VMEM] * 5,
            compiler_params=room,
            cost_estimate=pl.CostEstimate(
                flops=30 * rows * width, bytes_accessed=40 * rows * width, transcendentals=2 * rows * width
            ),
        )(
            token_counts,
            fragment_index,
            params,
            first,
            second,
            global_fragment,
            outer_momentum,
            drift_sum,
            *parts,
        )

    return body


def plain_body(mesh):
    workers, devices = mesh.shape["worker"], mesh.shape["fsdp"]

    def body(
        params, first, second, global_fragment, outer_momentum, features, cotangent, token_counts, fragment_index
    ):
        rows, width = params.shape[1:]
        tokens = features.shape[1]
        me = lax.axis_index("fsdp")
        count = lax.dynamic_index_in_dim(token_counts, lax.axis_index("worker"), 0, keepdims=False)
        live = count.astype(jnp.float32)
        valid = (me * tokens + lax.iota(jnp.int32, tokens) < count)[:, None]
        masked = jnp.where(valid, cotangent[0], jnp.zeros_like(cotangent[0]))
        term = lax.dot_general(features[0], masked, (((0,), (0,)), ((), ())), preferred_element_type=jnp.float32)
        blocks = jnp.take(term.reshape(devices, rows, width), me ^ jnp.arange(devices, dtype=jnp.int32), axis=0)
        bit = 1
        while bit < devices:
            blocks = blocks.reshape(-1, 2, rows, width)
            blocks = blocks[:, 0] + hop(blocks[:, 1], "fsdp", devices, bit)
            bit *= 2
        gradient = blocks[0] / live
        grouped = (rows // FRAGS, FRAGS, width)
        old = lax.dynamic_index_in_dim(params[0].reshape(grouped), fragment_index[0], 1, keepdims=False)
        drift_sum = doubling_sum(live * (global_fragment - old), "worker", workers)
        total = jnp.sum(token_counts).astype(jnp.float32)
        fresh, momentum = outer(drift_sum / total, global_fragment, outer_momentum)
        inner, first_new, second_new = adam(params[0], first[0], second[0], gradient)
        inner = inner.reshape(grouped)
        piece = lax.dynamic_index_in_dim(inner, fragment_index[0], 1, keepdims=False)
        mixed = MIXING * fresh + (1.0 - MIXING) * piece
        merged = lax.dynamic_update_index_in_dim(inner, mixed, fragment_index[0], 1).reshape(rows, width)
        return merged[None], first_new[None], second_new[None], fresh, momentum

    return body


def solution(mesh):
    devices = mesh.shape["fsdp"]

    def pick(*arrays):
        rows = arrays[0].shape[1]
        body = fast_body(mesh) if devices == 8 and rows % LANES == 0 else plain_body(mesh)
        return body(*arrays)

    state = P("worker", "fsdp", None)
    piece = P("fsdp", None)
    return jax.shard_map(
        pick,
        mesh=mesh,
        in_specs=(state, state, state, piece, piece, state, state, P(), P()),
        out_specs=(state, state, state, piece, piece),
        check_vma=False,
    )
```

time: 72.9 us -> 36.9 us (0.51)
  waiting for transfers between devices: 42.5 us -> 15.7 us
  between operations: 17.6 us -> 1.4 us
  starting transfers between devices: 0.08 us -> 10.9 us
  Pallas kernels: 0 us -> 4.58 us
  other arithmetic: 4.62 us -> 0.26 us
  matrix products: 2.68 us -> 0 us
  local copies, waits for them, and re-layouts: 5.13 us -> 3.8 us
    reduce_scatter x1 -> x0, waiting for transfers between devices: 34.8 us -> none  [body(): summed = lax.psum_scatter(term, 'fsdp', scatter_dimension=0, tiled=True)]
    ppermute x0 -> x7, waiting for transfers between devices: none -> 15.7 us  [hop(): return lax.ppermute(value, axis, [(d, d ^ bit) for d in range(devices)])]
    ppermute x0 -> x7, starting transfers between devices: none -> 10.9 us  [hop(): return lax.ppermute(value, axis, [(d, d ^ bit) for d in range(devices)])]
    psum x1 -> x0, waiting for transfers between devices: 7.64 us -> none  [body(): pseudo_grad = lax.psum(drift_term, 'worker') / token_total]
    pallas_call x0 -> x3, Pallas kernels: none -> 4.58 us  [the longest x1 1.83 us: body(): pl.pallas_call(functools.partial(rest_kernel, orders[1]), out_shape=[bloc...]
    dot_general x1 -> x0, matrix products: 2.68 us -> none  [contract_rows(): lax.dot_general(left_rows, right_rows, (((0,), (0,)), ((), ())), preferre...]
    unnamed x21 -> x22, local copies, waits for them, and re-layouts: 2.1 us -> 3.8 us
    dynamic_update_slice x1 -> x0, local copies, waits for them, and re-layouts: 1.46 us -> none  [body(): lax.dynamic_update_index_in_dim(inner_three, mixed_piece, fragment, 1)]
  transfers between devices with their start and end apart: 2 -> 7, of which waited for: 2 -> 6; matrix products, arithmetic and copies ran while one was open for 4% -> 0% of each run, Pallas kernels for 0% -> 3%
where the time goes in v1:
time: 36.9 us; the launch traced here: 36.6 us
  waiting for transfers between devices  15.7 us (43%)
  starting transfers between devices  10.9 us (30%)
  Pallas kernels  4.58 us (12%)
  local copies, waits for them, and re-layouts  3.8 us (10%)
  between operations  1.4 us (4%)
    ppermute x7, waiting for transfers between devices, hop(): return lax.ppermute(value, axis, [(d, d ^ bit) for d in range(devices)])  15.7 us
    ppermute x7, starting transfers between devices, hop(): return lax.ppermute(value, axis, [(d, d ^ bit) for d in range(devices)])  10.9 us
    unnamed x22, local copies, waits for them, and re-layouts  3.8 us
    pallas_call x1, Pallas kernels, body(): pl.pallas_call(functools.partial(rest_kernel, orders[1]), out_shape=[bloc...  1.83 us
    pallas_call x1, Pallas kernels, body(): pl.pallas_call(functools.partial(last_kernel, workers, len(parts)), out_s...  1.75 us
    pallas_call x1, Pallas kernels, body(): pl.pallas_call(functools.partial(first_kernel, orders[0]), out_shape=[blo...  1 us
  transfers between devices with their start and end apart: 7, of which 6 were waited for; matrix products, arithmetic and copies ran while one was open for 0% of the time, Pallas kernels for 3%

profile of v1, /device:TPU:0, one launch (start us, length us, event | category | flops | bytes accessed | tf_op | source)
XLA Modules:
  0.0 36.6 jit_solution(3589683707745098840)
XLA Ops:
  0.6 0.0 copy-start.10
  1.3 0.0 copy-done.10
  1.3 0.0 copy-start
  1.3 1.2 %copy-done = bf16[1,128,4096]{2,1,0:T(8,128)(2,1)S(1)} copy-done((bf16[1,128,4096]{2,1,0:T(8,128)(2,1)S(1)}, bf16[1,128,4096]{2,1,0:T(8,128)(2,1)}, u32[]{:S(2)}) %copy-start) | copy-done | bytes 1048600
  2.5 0.9 %copy-done.2 = f32[1,512,128]{2,1,0:T(8,128)S(1)} copy-done((f32[1,512,128]{2,1,0:T(8,128)S(1)}, f32[1,512,128]{2,1,0:T(8,128)}, u32[]{:S(2)}) %copy-start.2) | copy-done | bytes 262168
  3.5 0.8 %copy-done.6 = f32[128,128]{1,0:T(8,128)S(1)} copy-done((f32[128,128]{1,0:T(8,128)S(1)}, f32[128,128]{1,0:T(8,128)}, u32[]{:S(2)}) %copy-start.6) | copy-done | bytes 65560
  4.3 0.8 %copy-done.8 = bf16[1,128,128]{2,1,0:T(8,128)(2,1)S(1)} copy-done((bf16[1,128,128]{2,1,0:T(8,128)(2,1)S(1)}, bf16[1,128,128]{2,1,0:T(8,128)(2,1)}, u32[]{:S(2)}) %copy-start.8) | copy-done | bytes 32792
  5.1 1.8 %shard_map.128 = (f32[3,128,512]{2,1,0:T(8,128)S(1)}, f32[3,128,512]{2,1,0:T(8,128)S(1)}, f32[128,128]{1,0:T(8,128)S(1)}) custom-call(s32[4]{0:T(128)S(1)} %copy-done.10, s32[1]{0:T(128)S(6)} %copy.14.fragment, bf16[1,128,128]{2,1,0:T(8,128)(2,1)S(1)} %copy-done.8, f32[1,512,128]{2,1,0:T(8,128)S(1)} %copy-done.2, f32[128,128]{1,0:T(8,128)S(1)} %copy-done.6, ...), custom_call_target="tpu_custom_call" | custom-call | flops 100663296 | bytes 2359296 | tf_op jit(solution)/shard_map/pallas_call | solution.py:152
  6.9 0.5 %collective-permute-start.2 = (f32[3,128,512]{2,1,0:T(8,128)S(1)}, f32[3,128,512]{2,1,0:T(8,128)S(1)}, u32[]{:S(2)}, u32[]{:S(2)}) collective-permute-start(f32[3,128,512]{2,1,0:T(8,128)S(1)} %get-tuple-element.12), channel_id=1, source_target_pairs={{0,1},{1,0},{2,3},{3,2},{4,5},{5,4},{6,7},{7,6},{8,9},{9,8},{10,11... | collective-permute-start | bytes 2359304 | tf_op jit(solution)/shard_map/ppermute | solution.py:107
  7.4 0.0 copy-done.1
  7.4 1.0 %shard_map.129 = (f32[1,128,512]{2,1,0:T(8,128)S(1)}, f32[1,128,512]{2,1,0:T(8,128)S(1)}) custom-call(s32[4]{0:T(128)S(1)} %copy-done.10, bf16[1,128,128]{2,1,0:T(8,128)(2,1)S(1)} %copy-done.8, bf16[1,128,4096]{2,1,0:T(8,128)(2,1)S(1)} %copy-done.1), custom_call_target="tpu_custom_call" | custom-call | flops 33554432 | bytes 786432 | tf_op jit(solution)/shard_map/pallas_call | solution.py:141
  8.5 0.1 collective-permute-start.4
  8.6 1.5 %collective-permute-done.4 = f32[1,128,512]{2,1,0:T(8,128)S(1)} collective-permute-done((f32[1,128,512]{2,1,0:T(8,128)S(1)}, f32[1,128,512]{2,1,0:T(8,128)S(1)}, u32[]{:S(2)}, u32[]{:S(2)}) %collective-permute-start.4) | collective-permute-done | bytes 262176 | tf_op jit(solution)/shard_map/ppermute | solution.py:107
  10.1 2.8 %collective-permute-start.5 = (f32[1,128,512]{2,1,0:T(8,128)S(1)}, f32[1,128,512]{2,1,0:T(8,128)S(1)}, u32[]{:S(2)}, u32[]{:S(2)}) collective-permute-start(f32[1,128,512]{2,1,0:T(8,128)S(1)} %add.22), channel_id=1, source_target_pairs={{0,2},{1,3},{2,0},{3,1},{4,6},{5,7},{6,4},{7,5},{8,10},{9,11},{10,... | collective-permute-start | bytes 786440 | tf_op jit(solution)/shard_map/ppermute | solution.py:107
  12.9 6.8 %collective-permute-done.5 = f32[1,128,512]{2,1,0:T(8,128)S(1)} collective-permute-done((f32[1,128,512]{2,1,0:T(8,128)S(1)}, f32[1,128,512]{2,1,0:T(8,128)S(1)}, u32[]{:S(2)}, u32[]{:S(2)}) %collective-permute-start.5) | collective-permute-done | bytes 262176 | tf_op jit(solution)/shard_map/ppermute | solution.py:107
  19.7 0.0 collective-permute-done.2
  19.7 0.2 fusion
  19.9 0.0 copy-start.3
  19.9 2.8 %collective-permute-start.6 = (f32[1,128,512]{2,1,0:T(8,128)S(1)}, f32[1,128,512]{2,1,0:T(8,128)S(1)}, u32[]{:S(2)}, u32[]{:S(2)}) collective-permute-start(f32[1,128,512]{2,1,0:T(8,128)S(1)} %get-tuple-element.15), channel_id=1, source_target_pairs={{0,4},{1,5},{2,6},{3,7},{4,0},{5,1},{6,2},{7,3},{8,12},{9,13},{10,... | collective-permute-start | bytes 786440 | tf_op jit(solution)/shard_map/ppermute | solution.py:107
  22.8 1.6 %collective-permute-start.3 = (f32[1,128,512]{2,1,0:T(8,128)S(1)}, f32[1,128,512]{2,1,0:T(8,128)S(1)}, u32[]{:S(2)}, u32[]{:S(2)}) collective-permute-start(f32[1,128,512]{2,1,0:T(8,128)S(1)} %get-tuple-element.16), channel_id=1, source_target_pairs={{0,2},{1,3},{2,0},{3,1},{4,6},{5,7},{6,4},{7,5},{8,10},{9,11},{10,... | collective-permute-start | bytes 786440 | tf_op jit(solution)/shard_map/ppermute | solution.py:107
  24.3 1.5 %collective-permute-start = (f32[128,128]{1,0:T(8,128)S(1)}, f32[128,128]{1,0:T(8,128)S(1)}, u32[]{:S(2)}, u32[]{:S(2)}) collective-permute-start(f32[128,128]{1,0:T(8,128)S(1)} %get-tuple-element.10), channel_id=1, source_target_pairs={{0,16},{8,24},{16,0},{24,8},{1,17},{9,25},{17,1},{25,9},{2,18},{10... | collective-permute-start | bytes 196616 | tf_op jit(solution)/shard_map/ppermute | solution.py:107
  25.8 2.7 %collective-permute-done = f32[128,128]{1,0:T(8,128)S(1)} collective-permute-done((f32[128,128]{1,0:T(8,128)S(1)}, f32[128,128]{1,0:T(8,128)S(1)}, u32[]{:S(2)}, u32[]{:S(2)}) %collective-permute-start) | collective-permute-done | bytes 65568 | tf_op jit(solution)/shard_map/ppermute | solution.py:107
  28.6 0.0 copy-start.7
  28.6 0.0 copy-start.9
  28.6 1.6 %collective-permute-start.1 = (f32[128,128]{1,0:T(8,128)S(1)}, f32[128,128]{1,0:T(8,128)S(1)}, u32[]{:S(2)}, u32[]{:S(2)}) collective-permute-start(f32[128,128]{1,0:T(8,128)S(1)} %add.18), channel_id=1, source_target_pairs={{0,8},{8,0},{16,24},{24,16},{1,9},{9,1},{17,25},{25,17},{2,10},{10... | collective-permute-start | bytes 196616 | tf_op jit(solution)/shard_map/ppermute | solution.py:107
  30.2 2.8 %collective-permute-done.1 = f32[128,128]{1,0:T(8,128)S(1)} collective-permute-done((f32[128,128]{1,0:T(8,128)S(1)}, f32[128,128]{1,0:T(8,128)S(1)}, u32[]{:S(2)}, u32[]{:S(2)}) %collective-permute-start.1) | collective-permute-done | bytes 65568 | tf_op jit(solution)/shard_map/ppermute | solution.py:107
  33.0 1.7 %collective-permute-done.6.refs_3_ = f32[1,128,512]{2,1,0:T(8,128)S(1)} collective-permute-done((f32[1,128,512]{2,1,0:T(8,128)S(1)}, f32[1,128,512]{2,1,0:T(8,128)S(1)}, u32[]{:S(2)}, u32[]{:S(2)}) %collective-permute-start.6) | collective-permute-done | bytes 262176 | tf_op jit(solution)/shard_map/ppermute | solution.py:107
  34.6 0.2 collective-permute-done.3.refs_2_
  34.8 0.0 copy-done.4
  34.8 0.0 copy-done.7
  34.8 0.0 copy-done.9
  34.9 1.8 %shard_map.130 = (f32[1,512,128]{2,1,0:T(8,128)}, f32[1,512,128]{2,1,0:T(8,128)}, f32[1,512,128]{2,1,0:T(8,128)}, f32[128,128]{1,0:T(8,128)}, f32[128,128]{1,0:T(8,128)}) custom-call(s32[4]{0:T(128)S(1)} %copy-done.10, s32[1]{0:T(128)S(6)} %copy.14.fragment, f32[1,512,128]{2,1,0:T(8,128)S(1)} %copy-done.3, f32[1,512,128]{2,1,0:T(8,128)S(1)} %copy-done.4, ...), custom_call_target="tpu_custom_call" | custom-call | flops 1966080 | bytes 2621440 | tf_op jit(solution)/shard_map/pallas_call | solution.py:169
  (11 shorter events, 0.1 us)
Async XLA Ops:
  0.6 0.7 %copy-start.10 = (s32[4]{0:T(128)S(1)}, s32[4]{0:T(128)}, u32[]{:S(2)}) copy-start(s32[4]{0:T(128)} %counts.5) | copy-start | bytes 52
  1.3 1.2 %copy-start = (bf16[1,128,4096]{2,1,0:T(8,128)(2,1)S(1)}, bf16[1,128,4096]{2,1,0:T(8,128)(2,1)}, u32[]{:S(2)}) copy-start(bf16[1,128,4096]{2,1,0:T(8,128)(2,1)} %features.3) | copy-start | bytes 3145732
  2.5 0.9 %copy-start.2 = (f32[1,512,128]{2,1,0:T(8,128)S(1)}, f32[1,512,128]{2,1,0:T(8,128)}, u32[]{:S(2)}) copy-start(f32[1,512,128]{2,1,0:T(8,128)} %params.3) | copy-start | bytes 786436
  3.5 0.8 %copy-start.6 = (f32[128,128]{1,0:T(8,128)S(1)}, f32[128,128]{1,0:T(8,128)}, u32[]{:S(2)}) copy-start(f32[128,128]{1,0:T(8,128)} %global_fragment.3) | copy-start | bytes 196612
  4.3 0.8 %copy-start.8 = (bf16[1,128,128]{2,1,0:T(8,128)(2,1)S(1)}, bf16[1,128,128]{2,1,0:T(8,128)(2,1)}, u32[]{:S(2)}) copy-start(bf16[1,128,128]{2,1,0:T(8,128)(2,1)} %cot_ref.3) | copy-start | bytes 98308
  5.1 2.4 %copy-start.1 = (bf16[1,128,4096]{2,1,0:T(8,128)(2,1)S(1)}, bf16[1,128,4096]{2,1,0:T(8,128)(2,1)}, u32[]{:S(2)}) copy-start(bf16[1,128,4096]{2,1,0:T(8,128)(2,1)} %features.3) | copy-start | bytes 3145732
  6.9 12.8 %collective-permute-start.2 = (f32[3,128,512]{2,1,0:T(8,128)S(1)}, f32[3,128,512]{2,1,0:T(8,128)S(1)}, u32[]{:S(2)}, u32[]{:S(2)}) collective-permute-start(f32[3,128,512]{2,1,0:T(8,128)S(1)} %get-tuple-element.12), channel_id=1, source_target_pairs={{0,1},{1,0},{2,3},{3,2},{4,5},{5,4},{6,7},{7,6},{8,9},{9,8},{10,11... | collective-permute-start | bytes 2359304 | tf_op jit(solution)/shard_map/ppermute | solution.py:107
  8.5 1.6 %collective-permute-start.4 = (f32[1,128,512]{2,1,0:T(8,128)S(1)}, f32[1,128,512]{2,1,0:T(8,128)S(1)}, u32[]{:S(2)}, u32[]{:S(2)}) collective-permute-start(f32[1,128,512]{2,1,0:T(8,128)S(1)} %get-tuple-element.14), channel_id=1, source_target_pairs={{0,1},{1,0},{2,3},{3,2},{4,5},{5,4},{6,7},{7,6},{8,9},{9,8},{10,11... | collective-permute-start | bytes 786440 | tf_op jit(solution)/shard_map/ppermute | solution.py:107
  10.1 9.6 %collective-permute-start.5 = (f32[1,128,512]{2,1,0:T(8,128)S(1)}, f32[1,128,512]{2,1,0:T(8,128)S(1)}, u32[]{:S(2)}, u32[]{:S(2)}) collective-permute-start(f32[1,128,512]{2,1,0:T(8,128)S(1)} %add.22), channel_id=1, source_target_pairs={{0,2},{1,3},{2,0},{3,1},{4,6},{5,7},{6,4},{7,5},{8,10},{9,11},{10,... | collective-permute-start | bytes 786440 | tf_op jit(solution)/shard_map/ppermute | solution.py:107
  19.7 15.1 %copy-start.4 = (f32[1,512,128]{2,1,0:T(8,128)S(1)}, f32[1,512,128]{2,1,0:T(8,128)}, u32[]{:S(2)}) copy-start(f32[1,512,128]{2,1,0:T(8,128)} %first.1) | copy-start | bytes 786436
  19.7 15.1 %copy-start.5 = (f32[1,512,128]{2,1,0:T(8,128)S(1)}, f32[1,512,128]{2,1,0:T(8,128)}, u32[]{:S(2)}) copy-start(f32[1,512,128]{2,1,0:T(8,128)} %second.1) | copy-start | bytes 786436
  19.9 14.9 %copy-start.3 = (f32[1,512,128]{2,1,0:T(8,128)S(1)}, f32[1,512,128]{2,1,0:T(8,128)}, u32[]{:S(2)}) copy-start(f32[1,512,128]{2,1,0:T(8,128)} %params.3) | copy-start | bytes 786436
  19.9 14.7 %collective-permute-start.6 = (f32[1,128,512]{2,1,0:T(8,128)S(1)}, f32[1,128,512]{2,1,0:T(8,128)S(1)}, u32[]{:S(2)}, u32[]{:S(2)}) collective-permute-start(f32[1,128,512]{2,1,0:T(8,128)S(1)} %get-tuple-element.15), channel_id=1, source_target_pairs={{0,4},{1,5},{2,6},{3,7},{4,0},{5,1},{6,2},{7,3},{8,12},{9,13},{10,... | collective-permute-start | bytes 786440 | tf_op jit(solution)/shard_map/ppermute | solution.py:107
  22.8 12.1 %collective-permute-start.3 = (f32[1,128,512]{2,1,0:T(8,128)S(1)}, f32[1,128,512]{2,1,0:T(8,128)S(1)}, u32[]{:S(2)}, u32[]{:S(2)}) collective-permute-start(f32[1,128,512]{2,1,0:T(8,128)S(1)} %get-tuple-element.16), channel_id=1, source_target_pairs={{0,2},{1,3},{2,0},{3,1},{4,6},{5,7},{6,4},{7,5},{8,10},{9,11},{10,... | collective-permute-start | bytes 786440 | tf_op jit(solution)/shard_map/ppermute | solution.py:107
  24.3 4.3 %collective-permute-start = (f32[128,128]{1,0:T(8,128)S(1)}, f32[128,128]{1,0:T(8,128)S(1)}, u32[]{:S(2)}, u32[]{:S(2)}) collective-permute-start(f32[128,128]{1,0:T(8,128)S(1)} %get-tuple-element.10), channel_id=1, source_target_pairs={{0,16},{8,24},{16,0},{24,8},{1,17},{9,25},{17,1},{25,9},{2,18},{10... | collective-permute-start | bytes 196616 | tf_op jit(solution)/shard_map/ppermute | solution.py:107
  28.6 6.2 %copy-start.7 = (f32[128,128]{1,0:T(8,128)S(1)}, f32[128,128]{1,0:T(8,128)}, u32[]{:S(2)}) copy-start(f32[128,128]{1,0:T(8,128)} %global_fragment.3) | copy-start | bytes 196612
  28.6 6.2 %copy-start.9 = (f32[128,128]{1,0:T(8,128)S(1)}, f32[128,128]{1,0:T(8,128)}, u32[]{:S(2)}) copy-start(f32[128,128]{1,0:T(8,128)} %outer_momentum.1) | copy-start | bytes 196612
  28.6 4.3 %collective-permute-start.1 = (f32[128,128]{1,0:T(8,128)S(1)}, f32[128,128]{1,0:T(8,128)S(1)}, u32[]{:S(2)}, u32[]{:S(2)}) collective-permute-start(f32[128,128]{1,0:T(8,128)S(1)} %add.18), channel_id=1, source_target_pairs={{0,8},{8,0},{16,24},{24,16},{1,9},{9,1},{17,25},{25,17},{2,10},{10... | collective-permute-start | bytes 196616 | tf_op jit(solution)/shard_map/ppermute | solution.py:107

commit v2 on v1

--- a/solution.py
+++ b/solution.py
@@ -23,47 +23,60 @@
 
 VMEM = pl.BlockSpec(memory_space=pltpu.VMEM)
 SMEM = pl.BlockSpec(memory_space=pltpu.SMEM)
-HBM = pl.BlockSpec(memory_space=pl.ANY)
+HBM = pl.BlockSpec(memory_space=pltpu.HBM)
+ANY = pl.BlockSpec(memory_space=pl.ANY)
 ROOM = 8 << 20
 
 
-def masked_rows(counts, cot_ref):
-    tokens = cot_ref.shape[1]
-    live = counts[lax.axis_index("worker")] - lax.axis_index("fsdp") * tokens
-    cot = cot_ref[0].astype(jnp.float32)
-    rows = lax.broadcasted_iota(jnp.int32, cot.shape, 0)
-    return jnp.where(rows < live, cot, 0.0).astype(jnp.bfloat16)
-
-
-def products(order, counts, cot_ref, features, held, sems, put):
-    rows = held.shape[2]
-    me = lax.axis_index("fsdp")
-    copies = []
+def masked_rows(live, cotangent):
+    rows = lax.broadcasted_iota(jnp.int32, cotangent.shape, 0)
+    return jnp.where(rows < live, cotangent.astype(jnp.float32), 0.0).astype(jnp.bfloat16)
+
+
+def columns_of(relative, rows):
+    return pl.ds(pl.multiple_of((lax.axis_index("fsdp") ^ relative) * rows, LANES), rows)
+
+
+def product_halves(masked, features):
+    value = lax.dot_general(masked, features, (((0,), (0,)), ((), ())), preferred_element_type=jnp.float32)
+    half = value.shape[1] // 2
+    return value[:, :half], value[:, half:]
+
+
+def first_kernel(order, counts, cotangent, features, away, kept, counts_held, cot_held, held, sems):
+    small = [
+        pltpu.make_async_copy(counts, counts_held, sems.at[0]),
+        pltpu.make_async_copy(cotangent, cot_held, sems.at[1]),
+    ]
+    blocks = [
+        pltpu.make_async_copy(features.at[0, :, columns_of(q, held.shape[2])], held.at[slot], sems.at[2 + slot])
+        for slot, q in enumerate(order)
+    ]
+    for copy in small + blocks:
+        copy.start()
+    for copy in small:
+        copy.wait()
+    tokens = cot_held.shape[1]
+    live = counts_held[lax.axis_index("worker")] - lax.axis_index("fsdp") * tokens
+    masked = masked_rows(live, cot_held[0])
     for slot, q in enumerate(order):
-        columns = pl.ds(pl.multiple_of((me ^ q) * rows, LANES), rows)
-        copies.append(pltpu.make_async_copy(features.at[0, :, columns], held.at[slot], sems.at[slot]))
-        copies[-1].start()
-    masked = masked_rows(counts, cot_ref)
-    for slot, q in enumerate(order):
-        copies[slot].wait()
-        put(q, lax.dot_general(masked, held[slot], (((0,), (0,)), ((), ())), preferred_element_type=jnp.float32))
-
-
-def first_kernel(order, counts, cot_ref, features, away, kept, held, sems):
-    def put(q, value):
-        (away if q & 1 else kept)[0] = value
-
-    products(order, counts, cot_ref, features, held, sems, put)
-
-
-def rest_kernel(order, counts, fragment, cot_ref, params, global_fragment, features, away, kept, drift, held, sems):
-    def put(q, value):
-        (away if q & 1 else kept)[q // 2] = value
-
-    products(order, counts, cot_ref, features, held, sems, put)
-    pieces = global_fragment.shape[0]
-    old = params[0, pl.ds(fragment[0], pieces, stride=FRAGS), :]
-    drift[...] = counts[lax.axis_index("worker")].astype(jnp.float32) * (global_fragment[...] - old)
+        blocks[slot].wait()
+        into = away if q & 1 else kept
+        into[0], into[1] = product_halves(masked, held[slot])
+
+
+def rest_kernel(
+    order, counts, fragment, cotangent, params, global_fragment, features, after, away, kept, drift
+):
+    del after
+    tokens = cotangent.shape[1]
+    count = counts[lax.axis_index("worker")]
+    masked = masked_rows(count - lax.axis_index("fsdp") * tokens, cotangent[0])
+    for q in order:
+        into, at = (away if q & 1 else kept), 2 * (q // 2)
+        into[at], into[at + 1] = product_halves(masked, features[0, :, columns_of(q, params.shape[1])])
+    old = params[0, pl.ds(fragment[0], global_fragment.shape[0], stride=FRAGS), :]
+    drift[...] = count.astype(jnp.float32) * (global_fragment[...] - old)
 
 
 def adam(before, first, second, gradient):
@@ -79,28 +92,58 @@
 
 
 def last_kernel(
-    workers, terms, counts, fragment, params, first, second, global_fragment, outer_momentum, drift_sum, *refs
+    workers,
+    counts,
+    fragment,
+    params,
+    first,
+    second,
+    global_fragment,
+    outer_momentum,
+    drift_sum,
+    kept,
+    come,
+    near,
+    *refs,
 ):
-    parts, (new_params, new_first, new_second, new_global, new_momentum) = refs[:terms], refs[terms:]
+    far, (new_params, new_first, new_second, new_global, new_momentum, *held), sems = refs[:2], refs[2:-1], refs[-1]
+    held_params, held_first, held_second, held_global, held_momentum = held
     live = counts[lax.axis_index("worker")].astype(jnp.float32)
     total = counts[0]
     for other in range(1, workers):
         total = total + counts[other]
     fresh, momentum = outer(drift_sum[...] / total.astype(jnp.float32), global_fragment[...], outer_momentum[...])
-    new_global[...] = fresh
-    new_momentum[...] = momentum
-    rows = params.shape[1]
-    for at in range(0, rows, LANES):
+    held_global[...] = fresh
+    held_momentum[...] = momentum
+    copies = [
+        pltpu.make_async_copy(held_global, new_global, sems.at[0]),
+        pltpu.make_async_copy(held_momentum, new_momentum, sems.at[1]),
+    ]
+    for copy in copies:
+        copy.start()
+    half = kept.shape[2]
+    group = LANES // FRAGS
+    for number, at in enumerate(range(0, params.shape[1], LANES)):
+        which, lanes = at // half, pl.ds(at % half, LANES)
         here = pl.ds(at, LANES)
-        summed = parts[0][0, :, here]
-        for part in parts[1:]:
-            summed = summed + part[0, :, here]
+        summed = kept[which, :, lanes] + come[which, :, lanes] + near[which, :, lanes] + far[which][0, :, lanes]
         gradient = summed.T / live
-        new_params[0, here, :], new_first[0, here, :], new_second[0, here, :] = adam(
+        inner, held_first[here, :], held_second[here, :] = adam(
             params[0, here, :], first[0, here, :], second[0, here, :], gradient
         )
-    mine = pl.ds(fragment[0], rows // FRAGS, stride=FRAGS)
-    new_params[0, mine, :] = MIXING * fresh + (1.0 - MIXING) * new_params[0, mine, :]
+        held_params[here, :] = inner
+        mine = pl.ds(at + fragment[0], group, stride=FRAGS)
+        piece = held_global[pl.ds(number * group, group), :]
+        held_params[mine, :] = MIXING * piece + (1.0 - MIXING) * held_params[mine, :]
+        for slot, (source, target) in enumerate(
+            ((held_first, new_first), (held_second, new_second), (held_params, new_params))
+        ):
+            copies.append(
+                pltpu.make_async_copy(source.at[here], target.at[0, here], sems.at[2 + 3 * number + slot])
+            )
+            copies[-1].start()
+    for copy in copies:
+        copy.wait()
 
 
 def hop(value, axis, devices, bit):
@@ -123,12 +166,8 @@
     ):
         rows, width = params.shape[1:]
         pieces, tokens = global_fragment.shape[0], features.shape[1]
-        far = devices - 2
-        orders = ([far + 1, far], [q + s for q in range(far - 2, -1, -2) for s in (1, 0)])
         block = functools.partial(jax.ShapeDtypeStruct, dtype=jnp.float32)
-
-        def scratch(count):
-            return [pltpu.VMEM((count, tokens, rows), jnp.bfloat16), pltpu.SemaphoreType.DMA((count,))]
+        halves = lambda count: block((2 * count, width, rows // 2))
 
         def cost(count):
             return pl.CostEstimate(
@@ -139,38 +178,44 @@
 
         room = pltpu.CompilerParams(vmem_limit_bytes=ROOM)
         away_far, kept_far = pl.pallas_call(
-            functools.partial(first_kernel, orders[0]),
-            out_shape=[block((1, width, rows))] * 2,
-            in_specs=[SMEM, VMEM, HBM],
+            functools.partial(first_kernel, (7, 6)),
+            out_shape=[halves(1)] * 2,
+            in_specs=[HBM] * 3,
             out_specs=[VMEM] * 2,
-            scratch_shapes=scratch(2),
+            scratch_shapes=[
+                pltpu.SMEM(token_counts.shape, token_counts.dtype),
+                pltpu.VMEM(cotangent.shape, cotangent.dtype),
+                pltpu.VMEM((2, tokens, rows), features.dtype),
+                pltpu.SemaphoreType.DMA((4,)),
+            ],
             compiler_params=room,
             cost_estimate=cost(2),
         )(token_counts, cotangent, features)
         come_far = hop(away_far, "fsdp", devices, 1)
-        near = devices // 2 - 1
         away, kept, drift = pl.pallas_call(
-            functools.partial(rest_kernel, orders[1]),
-            out_shape=[block((near, width, rows))] * 2 + [block((pieces, width))],
-            in_specs=[SMEM, SMEM, VMEM, VMEM, VMEM, HBM],
+            functools.partial(rest_kernel, (5, 4, 3, 2, 1, 0)),
+            out_shape=[halves(3)] * 2 + [block((pieces, width))],
+            in_specs=[SMEM, SMEM, VMEM, VMEM, VMEM, VMEM, ANY],
             out_specs=[VMEM] * 3,
-            scratch_shapes=scratch(2 * near),
             compiler_params=room,
-            cost_estimate=cost(2 * near),
-        )(token_counts, fragment_index, cotangent, params, global_fragment, features)
+            cost_estimate=cost(6),
+        )(token_counts, fragment_index, cotangent, params, global_fragment, features, kept_far)
         come = hop(away, "fsdp", devices, 1)
-        step_far = hop(kept_far + come_far, "fsdp", devices, 2)
-        step_near = hop(kept[1:2] + come[1:2], "fsdp", devices, 2)
-        last = hop(kept[2:3] + come[2:3] + step_far, "fsdp", devices, 4)
+        far = [hop(kept_far[h : h + 1] + come_far[h : h + 1], "fsdp", devices, 2) for h in (0, 1)]
+        near, pass_on = lax.optimization_barrier((kept[2:4] + come[2:4], kept[4:6] + come[4:6]))
+        near = hop(near, "fsdp", devices, 2)
+        far = [hop(pass_on[h : h + 1] + far[h], "fsdp", devices, 4) for h in (0, 1)]
         drift_sum = doubling_sum(drift, "worker", workers)
-        parts = (kept[0:1], come[0:1], step_near, last)
         state = block(params.shape)
         piece = block(global_fragment.shape)
         return pl.pallas_call(
-            functools.partial(last_kernel, workers, len(parts)),
+            functools.partial(last_kernel, workers),
             out_shape=[state] * 3 + [piece] * 2,
-            in_specs=[SMEM] * 2 + [VMEM] * (6 + len(parts)),
-            out_specs=[VMEM] * 5,
+            in_specs=[SMEM] * 2 + [VMEM] * 11,
+            out_specs=[HBM] * 5,
+            scratch_shapes=[pltpu.VMEM((rows, width), jnp.float32)] * 3
+            + [pltpu.VMEM((pieces, width), jnp.float32)] * 2
+            + [pltpu.SemaphoreType.DMA((2 + 3 * rows // LANES,))],
             compiler_params=room,
             cost_estimate=pl.CostEstimate(
                 flops=30 * rows * width, bytes_accessed=40 * rows * width, transcendentals=2 * rows * width
@@ -184,7 +229,10 @@
             global_fragment,
             outer_momentum,
             drift_sum,
-            *parts,
+            kept,
+            come,
+            near,
+            *far,
         )
 
     return body

time: 36.9 us -> 34.8 us (0.943)
  starting transfers between devices: 10.9 us -> 12.9 us
  local copies, waits for them, and re-layouts: 3.8 us -> 2 us
  waiting for transfers between devices: 15.7 us -> 14.4 us
  Pallas kernels: 4.58 us -> 3.7 us
    ppermute x7 -> x9, starting transfers between devices: 10.9 us -> 12.9 us  [hop(): return lax.ppermute(value, axis, [(d, d ^ bit) for d in range(devices)])]
    unnamed x22 -> x16, local copies, waits for them, and re-layouts: 3.8 us -> 2 us
    ppermute x7 -> x9, waiting for transfers between devices: 15.7 us -> 14.4 us  [hop(): return lax.ppermute(value, axis, [(d, d ^ bit) for d in range(devices)])]
    pallas_call x3, Pallas kernels: 4.58 us -> 3.7 us  [the longest x1 1.78 us: body(): pl.pallas_call(functools.partial(last_kernel, workers), out_shape=[state]...]
  transfers between devices with their start and end apart: 7 -> 9, of which waited for: 6 -> 5; matrix products, arithmetic and copies ran while one was open for 0% -> 0% of each run, Pallas kernels for 3% -> 0%
where the time goes in v2:
time: 34.8 us; the launch traced here: 34.6 us
  waiting for transfers between devices  14.4 us (41%)
  starting transfers between devices  12.9 us (37%)
  Pallas kernels  3.7 us (11%)
  local copies, waits for them, and re-layouts  2 us (6%)
  between operations  1.4 us (4%)
    ppermute x9, waiting for transfers between devices, hop(): return lax.ppermute(value, axis, [(d, d ^ bit) for d in range(devices)])  14.4 us
    ppermute x9, starting transfers between devices, hop(): return lax.ppermute(value, axis, [(d, d ^ bit) for d in range(devices)])  12.9 us
    unnamed x16, local copies, waits for them, and re-layouts  2 us
    pallas_call x1, Pallas kernels, body(): pl.pallas_call(functools.partial(last_kernel, workers), out_shape=[state]...  1.78 us
    pallas_call x1, Pallas kernels, body(): pl.pallas_call(functools.partial(first_kernel, (7, 6)), out_shape=[halves...  0.97 us
    pallas_call x1, Pallas kernels, body(): pl.pallas_call(functools.partial(rest_kernel, (5, 4, 3, 2, 1, 0)), out_sh...  0.95 us
  transfers between devices with their start and end apart: 9, of which 5 were waited for; matrix products, arithmetic and copies ran while one was open for 0% of the time, Pallas kernels for 0%

profile of v2, /device:TPU:0, one launch (start us, length us, event | category | flops | bytes accessed | tf_op | source)
XLA Modules:
  0.0 34.6 jit_solution(17243464339115692169)
XLA Ops:
  0.6 0.0 copy-start.7
  1.3 0.0 copy-done.7
  1.3 0.0 copy-start
  1.3 1.2 %copy-done = bf16[1,128,4096]{2,1,0:T(8,128)(2,1)S(1)} copy-done((bf16[1,128,4096]{2,1,0:T(8,128)(2,1)S(1)}, bf16[1,128,4096]{2,1,0:T(8,128)(2,1)}, u32[]{:S(2)}) %copy-start) | copy-done | bytes 1048600
  2.5 0.8 %copy-done.5 = bf16[1,128,128]{2,1,0:T(8,128)(2,1)S(1)} copy-done((bf16[1,128,128]{2,1,0:T(8,128)(2,1)S(1)}, bf16[1,128,128]{2,1,0:T(8,128)(2,1)}, u32[]{:S(2)}) %copy-start.5) | copy-done | bytes 32792
  3.3 1.0 %shard_map.128 = (f32[2,128,256]{2,1,0:T(8,128)S(1)}, f32[2,128,256]{2,1,0:T(8,128)S(1)}) custom-call(s32[4]{0:T(128)S(1)} %copy-done.7, bf16[1,128,128]{2,1,0:T(8,128)(2,1)S(1)} %copy-done.5, bf16[1,128,4096]{2,1,0:T(8,128)(2,1)S(1)} %copy-done), custom_call_target="tpu_custom_call" | custom-call | flops 33554432 | bytes 786432 | tf_op jit(solution)/shard_map/pallas_call | solution.py:180
  4.3 0.0 copy-done.1
  4.3 0.0 copy-done.2
  4.3 0.9 %shard_map.129 = (f32[6,128,256]{2,1,0:T(8,128)S(1)}, f32[6,128,256]{2,1,0:T(8,128)S(1)}, f32[128,128]{1,0:T(8,128)S(1)}) custom-call(s32[4]{0:T(128)S(1)} %copy-done.7, s32[1]{0:T(128)S(6)} %copy.14.fragment, bf16[1,128,128]{2,1,0:T(8,128)(2,1)S(1)} %copy-done.5, f32[1,512,128]{2,1,0:T(8,128)S(1)} %copy-done.1, f32[128,128]{1,0:T(8,128)S(1)} %copy-done.2, ...), custom_call_target="tpu_custom_call" | custom-call | flops 100663296 | bytes 2359296 | tf_op jit(solution)/shard_map/pallas_call | solution.py:195
  5.3 0.5 %collective-permute-start.2 = (f32[6,128,256]{2,1,0:T(8,128)S(1)}, f32[6,128,256]{2,1,0:T(8,128)S(1)}, u32[]{:S(2)}, u32[]{:S(2)}) collective-permute-start(f32[6,128,256]{2,1,0:T(8,128)S(1)} %get-tuple-element.15), channel_id=1, source_target_pairs={{0,1},{1,0},{2,3},{3,2},{4,5},{5,4},{6,7},{7,6},{8,9},{9,8},{10,11... | collective-permute-start | bytes 2359304 | tf_op jit(solution)/shard_map/ppermute | solution.py:150
  5.8 0.1 collective-permute-start.4
  5.8 2.9 %collective-permute-start = (f32[128,128]{1,0:T(8,128)S(1)}, f32[128,128]{1,0:T(8,128)S(1)}, u32[]{:S(2)}, u32[]{:S(2)}) collective-permute-start(f32[128,128]{1,0:T(8,128)S(1)} %get-tuple-element.13), channel_id=1, source_target_pairs={{0,16},{8,24},{16,0},{24,8},{1,17},{9,25},{17,1},{25,9},{2,18},{10... | collective-permute-start | bytes 196616 | tf_op jit(solution)/shard_map/ppermute | solution.py:150
  8.8 0.0 collective-permute-done.4
  8.8 2.3 %collective-permute-start.7 = (f32[1,128,256]{2,1,0:T(8,128)S(1)}, f32[1,128,256]{2,1,0:T(8,128)S(1)}, u32[]{:S(2)}, u32[]{:S(2)}) collective-permute-start(f32[1,128,256]{2,1,0:T(8,128)S(1)} %get-tuple-element.21), channel_id=1, source_target_pairs={{0,2},{1,3},{2,0},{3,1},{4,6},{5,7},{6,4},{7,5},{8,10},{9,11},{10,... | collective-permute-start | bytes 393224 | tf_op jit(solution)/shard_map/ppermute | solution.py:150
  11.1 0.1 collective-permute-start.5
  11.2 0.0 collective-permute-done.2.come
  11.2 0.1 slice_add_fusion
  11.3 2.0 %collective-permute-start.3 = (f32[2,128,256]{2,1,0:T(8,128)S(1)}, f32[2,128,256]{2,1,0:T(8,128)S(1)}, u32[]{:S(2)}, u32[]{:S(2)}) collective-permute-start(f32[2,128,256]{2,1,0:T(8,128)S(1)} %get-tuple-element.16), channel_id=1, source_target_pairs={{0,2},{1,3},{2,0},{3,1},{4,6},{5,7},{6,4},{7,5},{8,10},{9,11},{10,... | collective-permute-start | bytes 786440 | tf_op jit(solution)/shard_map/ppermute | solution.py:150
  13.3 2.1 %collective-permute-done.7 = f32[1,128,256]{2,1,0:T(8,128)S(1)} collective-permute-done((f32[1,128,256]{2,1,0:T(8,128)S(1)}, f32[1,128,256]{2,1,0:T(8,128)S(1)}, u32[]{:S(2)}, u32[]{:S(2)}) %collective-permute-start.7) | collective-permute-done | bytes 131104 | tf_op jit(solution)/shard_map/ppermute | solution.py:150
  15.4 2.8 %collective-permute-done.5 = f32[1,128,256]{2,1,0:T(8,128)S(1)} collective-permute-done((f32[1,128,256]{2,1,0:T(8,128)S(1)}, f32[1,128,256]{2,1,0:T(8,128)S(1)}, u32[]{:S(2)}, u32[]{:S(2)}) %collective-permute-start.5) | collective-permute-done | bytes 131104 | tf_op jit(solution)/shard_map/ppermute | solution.py:150
  18.2 0.0 copy-start.3
  18.2 3.1 %collective-permute-start.8 = (f32[1,128,256]{2,1,0:T(8,128)S(1)}, f32[1,128,256]{2,1,0:T(8,128)S(1)}, u32[]{:S(2)}, u32[]{:S(2)}) collective-permute-start(f32[1,128,256]{2,1,0:T(8,128)S(1)} %get-tuple-element.23), channel_id=1, source_target_pairs={{0,4},{1,5},{2,6},{3,7},{4,0},{5,1},{6,2},{7,3},{8,12},{9,13},{10,... | collective-permute-start | bytes 393224 | tf_op jit(solution)/shard_map/ppermute | solution.py:150
  21.4 0.1 collective-permute-start.6
  21.5 0.0 collective-permute-done
  21.5 0.0 copy-start.6
  21.5 1.8 %collective-permute-start.1 = (f32[128,128]{1,0:T(8,128)S(1)}, f32[128,128]{1,0:T(8,128)S(1)}, u32[]{:S(2)}, u32[]{:S(2)}) collective-permute-start(f32[128,128]{1,0:T(8,128)S(1)} %add.24), channel_id=1, source_target_pairs={{0,8},{8,0},{16,24},{24,16},{1,9},{9,1},{17,25},{25,17},{2,10},{10... | collective-permute-start | bytes 196616 | tf_op jit(solution)/shard_map/ppermute | solution.py:150
  23.3 2.5 %collective-permute-done.1 = f32[128,128]{1,0:T(8,128)S(1)} collective-permute-done((f32[128,128]{1,0:T(8,128)S(1)}, f32[128,128]{1,0:T(8,128)S(1)}, u32[]{:S(2)}, u32[]{:S(2)}) %collective-permute-start.1) | collective-permute-done | bytes 65568 | tf_op jit(solution)/shard_map/ppermute | solution.py:150
  25.8 0.6 %collective-permute-done.8.refs_1_ = f32[1,128,256]{2,1,0:T(8,128)S(1)} collective-permute-done((f32[1,128,256]{2,1,0:T(8,128)S(1)}, f32[1,128,256]{2,1,0:T(8,128)S(1)}, u32[]{:S(2)}, u32[]{:S(2)}) %collective-permute-start.8) | collective-permute-done | bytes 131104 | tf_op jit(solution)/shard_map/ppermute | solution.py:150
  26.4 6.4 %collective-permute-done.6.refs_0_ = f32[1,128,256]{2,1,0:T(8,128)S(1)} collective-permute-done((f32[1,128,256]{2,1,0:T(8,128)S(1)}, f32[1,128,256]{2,1,0:T(8,128)S(1)}, u32[]{:S(2)}, u32[]{:S(2)}) %collective-permute-start.6) | collective-permute-done | bytes 131104 | tf_op jit(solution)/shard_map/ppermute | solution.py:150
  32.8 0.0 collective-permute-done.3.near
  32.8 0.0 copy-done.3
  32.8 1.8 %shard_map.130 = (f32[1,512,128]{2,1,0:T(8,128)}, f32[1,512,128]{2,1,0:T(8,128)}, f32[1,512,128]{2,1,0:T(8,128)}, f32[128,128]{1,0:T(8,128)}, f32[128,128]{1,0:T(8,128)}) custom-call(s32[4]{0:T(128)S(1)} %copy-done.7, s32[1]{0:T(128)S(6)} %copy.14.fragment, f32[1,512,128]{2,1,0:T(8,128)S(1)} %copy-done.1, f32[1,512,128]{2,1,0:T(8,128)S(1)} %copy-done.3, ...), custom_call_target="tpu_custom_call" | custom-call | flops 1966080 | bytes 2621440 | tf_op jit(solution)/shard_map/pallas_call | solution.py:211
  (10 shorter events, 0.1 us)
Async XLA Ops:
  0.6 0.7 %copy-start.7 = (s32[4]{0:T(128)S(1)}, s32[4]{0:T(128)}, u32[]{:S(2)}) copy-start(s32[4]{0:T(128)} %counts.5) | copy-start | bytes 52
  1.3 1.2 %copy-start = (bf16[1,128,4096]{2,1,0:T(8,128)(2,1)S(1)}, bf16[1,128,4096]{2,1,0:T(8,128)(2,1)}, u32[]{:S(2)}) copy-start(bf16[1,128,4096]{2,1,0:T(8,128)(2,1)} %features.3) | copy-start | bytes 3145732
  2.5 0.8 %copy-start.5 = (bf16[1,128,128]{2,1,0:T(8,128)(2,1)S(1)}, bf16[1,128,128]{2,1,0:T(8,128)(2,1)}, u32[]{:S(2)}) copy-start(bf16[1,128,128]{2,1,0:T(8,128)(2,1)} %cotangent.3) | copy-start | bytes 98308
  3.3 1.0 %copy-start.1 = (f32[1,512,128]{2,1,0:T(8,128)S(1)}, f32[1,512,128]{2,1,0:T(8,128)}, u32[]{:S(2)}) copy-start(f32[1,512,128]{2,1,0:T(8,128)} %params.3) | copy-start | bytes 786436
  3.3 1.0 %copy-start.2 = (f32[128,128]{1,0:T(8,128)S(1)}, f32[128,128]{1,0:T(8,128)}, u32[]{:S(2)}) copy-start(f32[128,128]{1,0:T(8,128)} %global_fragment.3) | copy-start | bytes 196612
  5.3 5.9 %collective-permute-start.2 = (f32[6,128,256]{2,1,0:T(8,128)S(1)}, f32[6,128,256]{2,1,0:T(8,128)S(1)}, u32[]{:S(2)}, u32[]{:S(2)}) collective-permute-start(f32[6,128,256]{2,1,0:T(8,128)S(1)} %get-tuple-element.15), channel_id=1, source_target_pairs={{0,1},{1,0},{2,3},{3,2},{4,5},{5,4},{6,7},{7,6},{8,9},{9,8},{10,11... | collective-permute-start | bytes 2359304 | tf_op jit(solution)/shard_map/ppermute | solution.py:150
  5.8 3.0 %collective-permute-start.4 = (f32[2,128,256]{2,1,0:T(8,128)S(1)}, f32[2,128,256]{2,1,0:T(8,128)S(1)}, u32[]{:S(2)}, u32[]{:S(2)}) collective-permute-start(f32[2,128,256]{2,1,0:T(8,128)S(1)} %get-tuple-element.18), channel_id=1, source_target_pairs={{0,1},{1,0},{2,3},{3,2},{4,5},{5,4},{6,7},{7,6},{8,9},{9,8},{10,11... | collective-permute-start | bytes 786440 | tf_op jit(solution)/shard_map/ppermute | solution.py:150
  5.8 15.6 %collective-permute-start = (f32[128,128]{1,0:T(8,128)S(1)}, f32[128,128]{1,0:T(8,128)S(1)}, u32[]{:S(2)}, u32[]{:S(2)}) collective-permute-start(f32[128,128]{1,0:T(8,128)S(1)} %get-tuple-element.13), channel_id=1, source_target_pairs={{0,16},{8,24},{16,0},{24,8},{1,17},{9,25},{17,1},{25,9},{2,18},{10... | collective-permute-start | bytes 196616 | tf_op jit(solution)/shard_map/ppermute | solution.py:150
  8.8 6.5 %collective-permute-start.7 = (f32[1,128,256]{2,1,0:T(8,128)S(1)}, f32[1,128,256]{2,1,0:T(8,128)S(1)}, u32[]{:S(2)}, u32[]{:S(2)}) collective-permute-start(f32[1,128,256]{2,1,0:T(8,128)S(1)} %get-tuple-element.21), channel_id=1, source_target_pairs={{0,2},{1,3},{2,0},{3,1},{4,6},{5,7},{6,4},{7,5},{8,10},{9,11},{10,... | collective-permute-start | bytes 393224 | tf_op jit(solution)/shard_map/ppermute | solution.py:150
  11.1 7.1 %collective-permute-start.5 = (f32[1,128,256]{2,1,0:T(8,128)S(1)}, f32[1,128,256]{2,1,0:T(8,128)S(1)}, u32[]{:S(2)}, u32[]{:S(2)}) collective-permute-start(f32[1,128,256]{2,1,0:T(8,128)S(1)} %get-tuple-element.22), channel_id=1, source_target_pairs={{0,2},{1,3},{2,0},{3,1},{4,6},{5,7},{6,4},{7,5},{8,10},{9,11},{10,... | collective-permute-start | bytes 393224 | tf_op jit(solution)/shard_map/ppermute | solution.py:150
  11.3 21.5 %collective-permute-start.3 = (f32[2,128,256]{2,1,0:T(8,128)S(1)}, f32[2,128,256]{2,1,0:T(8,128)S(1)}, u32[]{:S(2)}, u32[]{:S(2)}) collective-permute-start(f32[2,128,256]{2,1,0:T(8,128)S(1)} %get-tuple-element.16), channel_id=1, source_target_pairs={{0,2},{1,3},{2,0},{3,1},{4,6},{5,7},{6,4},{7,5},{8,10},{9,11},{10,... | collective-permute-start | bytes 786440 | tf_op jit(solution)/shard_map/ppermute | solution.py:150
  18.2 14.6 %copy-start.4 = (f32[1,512,128]{2,1,0:T(8,128)S(1)}, f32[1,512,128]{2,1,0:T(8,128)}, u32[]{:S(2)}) copy-start(f32[1,512,128]{2,1,0:T(8,128)} %second.1) | copy-start | bytes 786436
  18.2 14.6 %copy-start.3 = (f32[1,512,128]{2,1,0:T(8,128)S(1)}, f32[1,512,128]{2,1,0:T(8,128)}, u32[]{:S(2)}) copy-start(f32[1,512,128]{2,1,0:T(8,128)} %first.1) | copy-start | bytes 786436
  18.2 8.2 %collective-permute-start.8 = (f32[1,128,256]{2,1,0:T(8,128)S(1)}, f32[1,128,256]{2,1,0:T(8,128)S(1)}, u32[]{:S(2)}, u32[]{:S(2)}) collective-permute-start(f32[1,128,256]{2,1,0:T(8,128)S(1)} %get-tuple-element.23), channel_id=1, source_target_pairs={{0,4},{1,5},{2,6},{3,7},{4,0},{5,1},{6,2},{7,3},{8,12},{9,13},{10,... | collective-permute-start | bytes 393224 | tf_op jit(solution)/shard_map/ppermute | solution.py:150
  21.4 11.4 %collective-permute-start.6 = (f32[1,128,256]{2,1,0:T(8,128)S(1)}, f32[1,128,256]{2,1,0:T(8,128)S(1)}, u32[]{:S(2)}, u32[]{:S(2)}) collective-permute-start(f32[1,128,256]{2,1,0:T(8,128)S(1)} %get-tuple-element.24), channel_id=1, source_target_pairs={{0,4},{1,5},{2,6},{3,7},{4,0},{5,1},{6,2},{7,3},{8,12},{9,13},{10,... | collective-permute-start | bytes 393224 | tf_op jit(solution)/shard_map/ppermute | solution.py:150
  21.5 11.3 %copy-start.6 = (f32[128,128]{1,0:T(8,128)S(1)}, f32[128,128]{1,0:T(8,128)}, u32[]{:S(2)}) copy-start(f32[128,128]{1,0:T(8,128)} %outer_momentum.1) | copy-start | bytes 196612
  21.5 4.3 %collective-permute-start.1 = (f32[128,128]{1,0:T(8,128)S(1)}, f32[128,128]{1,0:T(8,128)S(1)}, u32[]{:S(2)}, u32[]{:S(2)}) collective-permute-start(f32[128,128]{1,0:T(8,128)S(1)} %add.24), channel_id=1, source_target_pairs={{0,8},{8,0},{16,24},{24,16},{1,9},{9,1},{17,25},{25,17},{2,10},{10... | collective-permute-start | bytes 196616 | tf_op jit(solution)/shard_map/ppermute | solution.py:150

commit v3 on v2

v3 whole, which is shorter than its diff:
```python
import functools

import jax
import jax.numpy as jnp
from jax import lax
from jax.experimental import pallas as pl
from jax.experimental.pallas import tpu as pltpu
from jax.sharding import PartitionSpec as P

FRAGS = 4
LANES = 128

BETA_ONE = 0.9
BETA_TWO = 0.95
CORRECT_ONE = 0.6513216
CORRECT_TWO = 0.401263
ADAM_EPS = 1e-08
LEARN_RATE = 0.02
DECAY_RATE = 0.1
NESTEROV = 0.9
OUTER_RATE = 0.7
MIXING = 0.5

VMEM = pl.BlockSpec(memory_space=pltpu.VMEM)
SMEM = pl.BlockSpec(memory_space=pltpu.SMEM)
HBM = pl.BlockSpec(memory_space=pltpu.HBM)
ANY = pl.BlockSpec(memory_space=pl.ANY)
ROOM = 8 << 20


def masked_rows(live, cotangent):
    rows = lax.broadcasted_iota(jnp.int32, cotangent.shape, 0)
    return jnp.where(rows < live, cotangent.astype(jnp.float32), 0.0).astype(jnp.bfloat16)


def columns_of(relative, rows):
    return pl.ds(pl.multiple_of((lax.axis_index("fsdp") ^ relative) * rows, LANES), rows)


def product_halves(masked, features):
    value = lax.dot_general(masked, features, (((0,), (0,)), ((), ())), preferred_element_type=jnp.float32)
    half = value.shape[1] // 2
    return value[:, :half], value[:, half:]


def product_kernel(
    order,
    counts,
    cotangent,
    features,
    away_far,
    kept_far,
    away,
    kept,
    masked,
    counts_held,
    cot_held,
    held,
    sems,
):
    targets = [(away_far, 0), (kept_far, 0)]
    targets += [((away if q & 1 else kept), 2 * (q // 2)) for q in order[2:]]
    small = [
        pltpu.make_async_copy(counts, counts_held, sems.at[0]),
        pltpu.make_async_copy(cotangent, cot_held, sems.at[1]),
    ]
    blocks = [
        pltpu.make_async_copy(features.at[0, :, columns_of(q, held.shape[2])], held.at[slot], sems.at[2 + slot])
        for slot, q in enumerate(order)
    ]
    for copy in small + blocks:
        copy.start()
    for copy in small:
        copy.wait()
    tokens = cot_held.shape[1]
    live = counts_held[lax.axis_index("worker")] - lax.axis_index("fsdp") * tokens
    masked[...] = masked_rows(live, cot_held[0])
    for slot, q in enumerate(order):
        blocks[slot].wait()
        into, at = targets[slot]
        into[at], into[at + 1] = product_halves(masked[...], held[slot])


def drift_kernel(counts, fragment, params, global_fragment, after, drift, inverse, *held_and_sems):
    del after
    held, sems = held_and_sems[:-1], held_and_sems[-1]
    copies = [
        pltpu.make_async_copy(source, target, sems.at[slot])
        for slot, (source, target) in enumerate(zip((counts, fragment, params, global_fragment), held))
    ]
    for copy in copies:
        copy.start()
    for copy in copies:
        copy.wait()
    counts_held, fragment_held, params_held, global_held = held
    count = counts_held[lax.axis_index("worker")].astype(jnp.float32)
    old = params_held[0, pl.ds(fragment_held[0], drift.shape[0], stride=FRAGS), :]
    drift[...] = count * (global_held[...] - old)
    inverse[...] = jnp.ones_like(inverse) / count


def add_kernel(picks, *refs):
    total = None
    for ref, pick in zip(refs, picks):
        if pick is not None:
            total = ref[pick] if total is None else total + ref[pick]
    refs[-1][...] = total


def outer_kernel(
    workers,
    counts,
    fragment,
    global_fragment,
    outer_momentum,
    drift_sum,
    new_global,
    new_momentum,
    scale,
    mix,
    *held_and_sems,
):
    held, sems = held_and_sems[:-1], held_and_sems[-1]
    copies = [
        pltpu.make_async_copy(source, target, sems.at[slot])
        for slot, (source, target) in enumerate(zip((counts, fragment, global_fragment, outer_momentum), held))
    ]
    for copy in copies:
        copy.start()
    scale[...] = jnp.ones_like(scale)
    mix[...] = jnp.zeros_like(mix)
    for copy in copies:
        copy.wait()
    counts_held, fragment_held, global_held, momentum_held = held
    total = counts_held[0]
    for other in range(1, workers):
        total = total + counts_held[other]
    fresh, momentum = outer(drift_sum[...] / total.astype(jnp.float32), global_held[...], momentum_held[...])
    new_global[...] = fresh
    new_momentum[...] = momentum
    mine = pl.ds(fragment_held[0], fresh.shape[0], stride=FRAGS)
    mix[mine, :] = MIXING * fresh
    scale[mine, :] = jnp.full_like(fresh, 1.0 - MIXING)


def adam(before, first, second, gradient):
    first_new = BETA_ONE * first + (1.0 - BETA_ONE) * gradient
    second_new = BETA_TWO * second + (1.0 - BETA_TWO) * gradient * gradient
    update = first_new * (1.0 / CORRECT_ONE) / (jnp.sqrt(second_new * (1.0 / CORRECT_TWO)) + ADAM_EPS)
    return before - LEARN_RATE * (update + DECAY_RATE * before), first_new, second_new


def outer(pseudo_grad, global_fragment, outer_momentum):
    momentum = NESTEROV * outer_momentum + pseudo_grad
    return global_fragment - OUTER_RATE * (pseudo_grad + NESTEROV * momentum), momentum


def half_step(half, states, sums, inverse, held):
    params, first, second = states
    kept, come, far, near = sums
    held_first, held_second = held
    rows = kept.shape[2]
    for lane in range(0, rows, LANES):
        lanes, there = pl.ds(lane, LANES), pl.ds(half * rows + lane, LANES)
        summed = kept[half, :, lanes] + come[half, :, lanes] + near[0, :, lanes] + far[0, :, lanes]
        inner, held_first[lanes, :], held_second[lanes, :] = adam(
            params[0, there, :], first[0, there, :], second[0, there, :], summed.T * inverse[0:1, :]
        )
        yield lanes, there, inner


def left_kernel(
    params, first, second, kept, come, far, near, inverse, inner, new_first, new_second, held_first, held_second, sems
):
    copies = []
    for lanes, there, value in half_step(
        0, (params, first, second), (kept, come, far, near), inverse, (held_first, held_second)
    ):
        inner[lanes, :] = value
        for source, target in ((held_first, new_first), (held_second, new_second)):
            copies.append(pltpu.make_async_copy(source.at[lanes], target.at[0, there], sems.at[len(copies)]))
            copies[-1].start()
    for copy in copies:
        copy.wait()


def right_kernel(
    params,
    first,
    second,
    kept,
    come,
    far,
    near,
    inverse,
    scale,
    mix,
    inner,
    left_first,
    left_second,
    new_params,
    new_first,
    new_second,
    held_left,
    held_right,
    held_first,
    held_second,
    sems,
):
    del left_first, left_second
    left = pl.ds(0, inner.shape[0])
    held_left[...] = scale[left, :] * inner[...] + mix[left, :]
    copies = [pltpu.make_async_copy(held_left, new_params.at[0, left], sems.at[0])]
    copies[-1].start()
    for lanes, there, value in half_step(
        1, (params, first, second), (kept, come, far, near), inverse, (held_first, held_second)
    ):
        held_right[lanes, :] = scale[there, :] * value + mix[there, :]
        for source, target in ((held_first, new_first), (held_second, new_second), (held_right, new_params)):
            copies.append(pltpu.make_async_copy(source.at[lanes], target.at[0, there], sems.at[len(copies)]))
            copies[-1].start()
    for copy in copies:
        copy.wait()


def hop(value, axis, devices, bit):
    return lax.ppermute(value, axis, [(d, d ^ bit) for d in range(devices)])


def doubling_sum(value, axis, devices):
    bit = devices // 2
    while bit:
        value = value + hop(value, axis, devices, bit)
        bit //= 2
    return value


def fast_body(mesh):
    workers, devices = mesh.shape["worker"], mesh.shape["fsdp"]

    def body(
        params, first, second, global_fragment, outer_momentum, features, cotangent, token_counts, fragment_index
    ):
        rows, width = params.shape[1:]
        pieces, tokens = global_fragment.shape[0], features.shape[1]
        block = functools.partial(jax.ShapeDtypeStruct, dtype=jnp.float32)
        halves = lambda count: block((2 * count, width, rows // 2))

        def cost(count):
            return pl.CostEstimate(
                flops=2 * count * tokens * rows * width,
                bytes_accessed=count * rows * (2 * tokens + 4 * width),
                transcendentals=0,
            )

        room = pltpu.CompilerParams(vmem_limit_bytes=ROOM)
        free = pl.CostEstimate(flops=0, bytes_accessed=0, transcendentals=0)
        far_fragment = fragment_index
        far_counts, far_features, far_cotangent, far_params, far_global, far_momentum = (
            pltpu.with_memory_space_constraint(array, pltpu.HBM)
            for array in (
                token_counts,
                features,
                cotangent,
                params,
                global_fragment,
                outer_momentum,
            )
        )
        held_counts = pltpu.SMEM(token_counts.shape, token_counts.dtype)
        held_fragment = pltpu.SMEM(fragment_index.shape, fragment_index.dtype)
        held_piece = pltpu.VMEM(global_fragment.shape, global_fragment.dtype)

        order = tuple(q + s for q in range(devices - 2, -1, -2) for s in (1, 0))
        away_far, kept_far, away, kept = pl.pallas_call(
            functools.partial(product_kernel, order),
            out_shape=[halves(1)] * 2 + [halves(devices // 2 - 1)] * 2,
            in_specs=[HBM] * 3,
            out_specs=[VMEM] * 4,
            scratch_shapes=[
                pltpu.VMEM((tokens, width), jnp.bfloat16),
                held_counts,
                pltpu.VMEM(cotangent.shape, cotangent.dtype),
                pltpu.VMEM((devices, tokens, rows), features.dtype),
                pltpu.SemaphoreType.DMA((2 + devices,)),
            ],
            compiler_params=room,
            cost_estimate=cost(devices),
        )(far_counts, far_cotangent, far_features)

        def add(*terms):
            picks = [pick for _, pick in terms]
            return pl.pallas_call(
                functools.partial(add_kernel, picks),
                out_shape=block((1, width, rows // 2)),
                in_specs=[ANY if pick is None else VMEM for pick in picks],
                out_specs=VMEM,
                compiler_params=room,
                cost_estimate=free,
            )(*(array for array, _ in terms))

        def part(number):
            return slice(number, number + 1)

        come_far = hop(away_far, "fsdp", devices, 1)
        sent = add((kept_far, part(0)), (come_far, part(0)), (far_fragment, None))
        far_left = hop(sent, "fsdp", devices, 2)
        away, _ = lax.optimization_barrier((away, sent))
        come = hop(away, "fsdp", devices, 1)
        drift, inverse = pl.pallas_call(
            drift_kernel,
            out_shape=[block((pieces, width)), block((8, width))],
            in_specs=[HBM] * 4 + [ANY],
            out_specs=[VMEM] * 2,
            scratch_shapes=[
                held_counts,
                held_fragment,
                pltpu.VMEM(params.shape, params.dtype),
                held_piece,
                pltpu.SemaphoreType.DMA((4,)),
            ],
            compiler_params=room,
            cost_estimate=free,
        )(far_counts, far_fragment, far_params, far_global, sent)
        sent = add((kept_far, part(1)), (come_far, part(1)), (drift, None))
        far_right = hop(sent, "fsdp", devices, 2)
        passed = add((kept, part(4)), (come, part(4)), (far_left, part(0)))
        far_left = hop(passed, "fsdp", devices, 4)
        near_left = add((kept, part(2)), (come, part(2)), (passed, None))
        far_right = add((kept, part(5)), (come, part(5)), (far_right, part(0)), (near_left, None))
        near_right = add((kept, part(3)), (come, part(3)), (far_right, None))
        drift, _ = lax.optimization_barrier((drift, sent))
        bit = workers // 2
        while bit:
            drift = drift + hop(drift, "worker", workers, bit)
            drift, _ = lax.optimization_barrier((drift, near_right))
            bit //= 2
        near_left = hop(near_left, "fsdp", devices, 2)
        far_right = hop(far_right, "fsdp", devices, 4)
        near_right = hop(near_right, "fsdp", devices, 2)
        state = block(params.shape)
        piece = block(global_fragment.shape)
        whole = block((rows, width))
        new_global, new_momentum, scale, mix = pl.pallas_call(
            functools.partial(outer_kernel, workers),
            out_shape=[piece, piece, whole, whole],
            in_specs=[HBM] * 4 + [VMEM],
            out_specs=[VMEM] * 4,
            scratch_shapes=[held_counts, held_fragment, held_piece, held_piece, pltpu.SemaphoreType.DMA((4,))],
            compiler_params=room,
            cost_estimate=free,
        )(far_counts, far_fragment, far_global, far_momentum, drift)
        half = rows // 2
        groups = half // LANES
        held_half = pltpu.VMEM((half, width), jnp.float32)
        inner, new_first, new_second = pl.pallas_call(
            left_kernel,
            out_shape=[block((half, width)), state, state],
            in_specs=[VMEM] * 8,
            out_specs=[VMEM, HBM, HBM],
            scratch_shapes=[held_half] * 2 + [pltpu.SemaphoreType.DMA((2 * groups,))],
            compiler_params=room,
            cost_estimate=pl.CostEstimate(
                flops=30 * half * width, bytes_accessed=40 * half * width, transcendentals=2 * half * width
            ),
        )(params, first, second, kept, come, far_left, near_left, inverse)
        new_params, new_first, new_second = pl.pallas_call(
            right_kernel,
            out_shape=[state] * 3,
            in_specs=[VMEM] * 11 + [HBM] * 2,
            out_specs=[HBM] * 3,
            input_output_aliases={11: 1, 12: 2},
            scratch_shapes=[held_half] * 4 + [pltpu.SemaphoreType.DMA((1 + 3 * groups,))],
            compiler_params=room,
            cost_estimate=free,
        )(params, first, second, kept, come, far_right, near_right, inverse, scale, mix, inner, new_first, new_second)
        return new_params, new_first, new_second, new_global, new_momentum

    return body


def plain_body(mesh):
    workers, devices = mesh.shape["worker"], mesh.shape["fsdp"]

    def body(
        params, first, second, global_fragment, outer_momentum, features, cotangent, token_counts, fragment_index
    ):
        rows, width = params.shape[1:]
        tokens = features.shape[1]
        me = lax.axis_index("fsdp")
        count = lax.dynamic_index_in_dim(token_counts, lax.axis_index("worker"), 0, keepdims=False)
        live = count.astype(jnp.float32)
        valid = (me * tokens + lax.iota(jnp.int32, tokens) < count)[:, None]
        masked = jnp.where(valid, cotangent[0], jnp.zeros_like(cotangent[0]))
        term = lax.dot_general(features[0], masked, (((0,), (0,)), ((), ())), preferred_element_type=jnp.float32)
        blocks = jnp.take(term.reshape(devices, rows, width), me ^ jnp.arange(devices, dtype=jnp.int32), axis=0)
        bit = 1
        while bit < devices:
            blocks = blocks.reshape(-1, 2, rows, width)
            blocks = blocks[:, 0] + hop(blocks[:, 1], "fsdp", devices, bit)
            bit *= 2
        gradient = blocks[0] / live
        grouped = (rows // FRAGS, FRAGS, width)
        old = lax.dynamic_index_in_dim(params[0].reshape(grouped), fragment_index[0], 1, keepdims=False)
        drift_sum = doubling_sum(live * (global_fragment - old), "worker", workers)
        total = jnp.sum(token_counts).astype(jnp.float32)
        fresh, momentum = outer(drift_sum / total, global_fragment, outer_momentum)
        inner, first_new, second_new = adam(params[0], first[0], second[0], gradient)
        inner = inner.reshape(grouped)
        piece = lax.dynamic_index_in_dim(inner, fragment_index[0], 1, keepdims=False)
        mixed = MIXING * fresh + (1.0 - MIXING) * piece
        merged = lax.dynamic_update_index_in_dim(inner, mixed, fragment_index[0], 1).reshape(rows, width)
        return merged[None], first_new[None], second_new[None], fresh, momentum

    return body


def solution(mesh):
    devices = mesh.shape["fsdp"]

    def pick(*arrays):
        rows = arrays[0].shape[1]
        body = fast_body(mesh) if devices == 8 and rows % LANES == 0 else plain_body(mesh)
        return body(*arrays)

    state = P("worker", "fsdp", None)
    piece = P("fsdp", None)
    return jax.shard_map(
        pick,
        mesh=mesh,
        in_specs=(state, state, state, piece, piece, state, state, P(), P()),
        out_specs=(state, state, state, piece, piece),
        check_vma=False,
    )
```

time: 34.8 us -> 30 us (0.86)
  waiting for transfers between devices: 14.4 us -> 6.26 us
  Pallas kernels: 3.7 us -> 7.36 us
  local copies, waits for them, and re-layouts: 2 us -> 0.02 us
  starting transfers between devices: 12.9 us -> 14.7 us
    ppermute x9 -> x10, waiting for transfers between devices: 14.4 us -> 6.26 us  [hop(): return lax.ppermute(value, axis, [(d, d ^ bit) for d in range(devices)])]
    pallas_call x3 -> x11, Pallas kernels: 3.7 us -> 7.36 us  [the longest x1 2.7 us: body(): pl.pallas_call(functools.partial(product_kernel, order), out_shape=[halve...]
    unnamed x16 -> x6, local copies, waits for them, and re-layouts: 2 us -> 0.02 us
    ppermute x9 -> x10, starting transfers between devices: 12.9 us -> 14.7 us  [hop(): return lax.ppermute(value, axis, [(d, d ^ bit) for d in range(devices)])]
  transfers between devices with their start and end apart: 9 -> 10, of which waited for: 5 -> 4; matrix products, arithmetic and copies ran while one was open for 0% -> 0% of each run, Pallas kernels for 0% -> 12%
where the time goes in v3:
time: 30 us; the launch traced here: 29.8 us
  starting transfers between devices  14.7 us (49%)
  Pallas kernels  7.36 us (25%)
  waiting for transfers between devices  6.26 us (21%)
  between operations  1.44 us (5%)
    ppermute x10, starting transfers between devices, hop(): return lax.ppermute(value, axis, [(d, d ^ bit) for d in range(devices)])  14.7 us
    ppermute x10, waiting for transfers between devices, hop(): return lax.ppermute(value, axis, [(d, d ^ bit) for d in range(devices)])  6.26 us
    pallas_call x1, Pallas kernels, body(): pl.pallas_call(functools.partial(product_kernel, order), out_shape=[halve...  2.7 us
    pallas_call x1, Pallas kernels, body(): pl.pallas_call(functools.partial(outer_kernel, workers), out_shape=[piece...  1.59 us
    pallas_call x1, Pallas kernels, body(): pl.pallas_call(right_kernel, out_shape=[state] * 3, in_specs=[VMEM] * 11...  1.05 us
    pallas_call x1, Pallas kernels, body(): pl.pallas_call(drift_kernel, out_shape=[block((pieces, width)), block((8,...  1.01 us
    pallas_call x1, Pallas kernels, body(): pl.pallas_call(left_kernel, out_shape=[block((half, width)), state, state...  0.9 us
  transfers between devices with their start and end apart: 10, of which 4 were waited for; matrix products, arithmetic and copies ran while one was open for 0% of the time, Pallas kernels for 12%

profile of v3, /device:TPU:0, one launch (start us, length us, event | category | flops | bytes accessed | tf_op | source)
XLA Modules:
  0.0 29.8 jit_solution(2360617229188752512)
XLA Ops:
  0.6 2.7 %shard_map.128 = (f32[2,128,256]{2,1,0:T(8,128)S(1)}, f32[2,128,256]{2,1,0:T(8,128)S(1)}, f32[6,128,256]{2,1,0:T(8,128)S(1)}, f32[6,128,256]{2,1,0:T(8,128)S(1)}) custom-call(s32[4]{0:T(128)} %counts.5, bf16[1,128,128]{2,1,0:T(8,128)(2,1)} %cotangent.1, bf16[1,128,4096]{2,1,0:T(8,128)(2,1)} %features.1), custom_call_target="tpu_custom_call" | custom-call | flops 134217728 | bytes 3145728 | tf_op jit(solution)/shard_map/pallas_call | solution.py:275
  3.3 0.5 %collective-permute-start = (f32[2,128,256]{2,1,0:T(8,128)S(1)}, f32[2,128,256]{2,1,0:T(8,128)S(1)}, u32[]{:S(2)}, u32[]{:S(2)}) collective-permute-start(f32[2,128,256]{2,1,0:T(8,128)S(1)} %get-tuple-element.28), channel_id=1, source_target_pairs={{0,1},{1,0},{2,3},{3,2},{4,5},{5,4},{6,7},{7,6},{8,9},{9,8},{10,11... | collective-permute-start | bytes 786440 | tf_op jit(solution)/shard_map/ppermute | solution.py:227
  4.5 0.5 %collective-permute-done.refs_1_ = f32[2,128,256]{2,1,0:T(8,128)S(1)} collective-permute-done((f32[2,128,256]{2,1,0:T(8,128)S(1)}, f32[2,128,256]{2,1,0:T(8,128)S(1)}, u32[]{:S(2)}, u32[]{:S(2)}) %collective-permute-start) | collective-permute-done | bytes 262176 | tf_op jit(solution)/shard_map/ppermute | solution.py:227
  5.0 0.4 %collective-permute-start.1 = (f32[6,128,256]{2,1,0:T(8,128)S(1)}, f32[6,128,256]{2,1,0:T(8,128)S(1)}, u32[]{:S(2)}, u32[]{:S(2)}) collective-permute-start(f32[6,128,256]{2,1,0:T(8,128)S(1)} %get-tuple-element.29), channel_id=1, source_target_pairs={{0,1},{1,0},{2,3},{3,2},{4,5},{5,4},{6,7},{7,6},{8,9},{9,8},{10,11... | collective-permute-start | bytes 2359304 | tf_op jit(solution)/shard_map/ppermute | solution.py:227
  5.5 2.7 %collective-permute-start.3 = (f32[1,128,256]{2,1,0:T(8,128)S(1)}, f32[1,128,256]{2,1,0:T(8,128)S(1)}, u32[]{:S(2)}, u32[]{:S(2)}) collective-permute-start(f32[1,128,256]{2,1,0:T(8,128)S(1)} %shard_map.129.after), channel_id=1, source_target_pairs={{0,2},{1,3},{2,0},{3,1},{4,6},{5,7},{6,4},{7,5},{8,10},{9,11},{10,... | collective-permute-start | bytes 393224 | tf_op jit(solution)/shard_map/ppermute | solution.py:227
  8.2 1.0 %shard_map.130 = (f32[128,128]{1,0:T(8,128)S(1)}, f32[8,128]{1,0:T(8,128)S(1)}) custom-call(s32[4]{0:T(128)} %counts.5, s32[1]{0:T(128)S(6)} %copy.18.refs_2_.fragment, f32[1,512,128]{2,1,0:T(8,128)} %params.5, f32[128,128]{1,0:T(8,128)} %global_fragment.3, f32[1,128,256]{2,1,0:T(8,128)S(1)} %shard_map.129.after), custom_call_target="tpu_custom_call" | custom-call | tf_op jit(solution)/shard_map/pallas_call | solution.py:310
  9.2 0.1 collective-permute-start.2
  9.3 2.0 %collective-permute-start.6 = (f32[128,128]{1,0:T(8,128)S(1)}, f32[128,128]{1,0:T(8,128)S(1)}, u32[]{:S(2)}, u32[]{:S(2)}) collective-permute-start(f32[128,128]{1,0:T(8,128)S(1)} %get-tuple-element.32.refs_2_), channel_id=1, source_target_pairs={{0,16},{8,24},{16,0},{24,8},{1,17},{9,25},{17,1},{25,9},{2,18},{10... | collective-permute-start | bytes 196616 | tf_op jit(solution)/shard_map/ppermute | solution.py:227
  11.3 1.1 %collective-permute-done.3.refs_2_ = f32[1,128,256]{2,1,0:T(8,128)S(1)} collective-permute-done((f32[1,128,256]{2,1,0:T(8,128)S(1)}, f32[1,128,256]{2,1,0:T(8,128)S(1)}, u32[]{:S(2)}, u32[]{:S(2)}) %collective-permute-start.3) | collective-permute-done | bytes 131104 | tf_op jit(solution)/shard_map/ppermute | solution.py:227
  12.4 0.0 collective-permute-done.1.refs_1_.come
  12.4 2.2 %collective-permute-start.9 = (f32[1,128,256]{2,1,0:T(8,128)S(1)}, f32[1,128,256]{2,1,0:T(8,128)S(1)}, u32[]{:S(2)}, u32[]{:S(2)}) collective-permute-start(f32[1,128,256]{2,1,0:T(8,128)S(1)} %shard_map.133.refs_3_), channel_id=1, source_target_pairs={{0,2},{1,3},{2,0},{3,1},{4,6},{5,7},{6,4},{7,5},{8,10},{9,11},{10,... | collective-permute-start | bytes 393224 | tf_op jit(solution)/shard_map/ppermute | solution.py:227
  14.6 2.6 %collective-permute-start.8 = (f32[1,128,256]{2,1,0:T(8,128)S(1)}, f32[1,128,256]{2,1,0:T(8,128)S(1)}, u32[]{:S(2)}, u32[]{:S(2)}) collective-permute-start(f32[1,128,256]{2,1,0:T(8,128)S(1)} %shard_map.132.refs_2_), channel_id=1, source_target_pairs={{0,4},{1,5},{2,6},{3,7},{4,0},{5,1},{6,2},{7,3},{8,12},{9,13},{10,... | collective-permute-start | bytes 393224 | tf_op jit(solution)/shard_map/ppermute | solution.py:227
  17.2 0.0 collective-permute-done.2.refs_2_
  17.3 0.0 copy-start.2
  17.3 0.0 copy-start
  17.3 0.0 copy-start.1
  17.3 0.3 %collective-permute-start.5 = (f32[1,128,256]{2,1,0:T(8,128)S(1)}, f32[1,128,256]{2,1,0:T(8,128)S(1)}, u32[]{:S(2)}, u32[]{:S(2)}) collective-permute-start(f32[1,128,256]{2,1,0:T(8,128)S(1)} %shard_map.135), channel_id=1, source_target_pairs={{0,2},{1,3},{2,0},{3,1},{4,6},{5,7},{6,4},{7,5},{8,10},{9,11},{10,... | collective-permute-start | bytes 393224 | tf_op jit(solution)/shard_map/ppermute | solution.py:227
  17.6 2.4 %collective-permute-start.4 = (f32[1,128,256]{2,1,0:T(8,128)S(1)}, f32[1,128,256]{2,1,0:T(8,128)S(1)}, u32[]{:S(2)}, u32[]{:S(2)}) collective-permute-start(f32[1,128,256]{2,1,0:T(8,128)S(1)} %shard_map.134.refs_2_), channel_id=1, source_target_pairs={{0,4},{1,5},{2,6},{3,7},{4,0},{5,1},{6,2},{7,3},{8,12},{9,13},{10,... | collective-permute-start | bytes 393224 | tf_op jit(solution)/shard_map/ppermute | solution.py:227
  20.0 0.0 collective-permute-done.6
  20.0 1.6 %collective-permute-start.7 = (f32[128,128]{1,0:T(8,128)S(1)}, f32[128,128]{1,0:T(8,128)S(1)}, u32[]{:S(2)}, u32[]{:S(2)}) collective-permute-start(f32[128,128]{1,0:T(8,128)S(1)} %add.6), channel_id=1, source_target_pairs={{0,8},{8,0},{16,24},{24,16},{1,9},{9,1},{17,25},{25,17},{2,10},{10... | collective-permute-start | bytes 196616 | tf_op jit(solution)/shard_map/ppermute | solution.py:227
  21.6 2.8 %collective-permute-done.7 = f32[128,128]{1,0:T(8,128)S(1)} collective-permute-done((f32[128,128]{1,0:T(8,128)S(1)}, f32[128,128]{1,0:T(8,128)S(1)}, u32[]{:S(2)}, u32[]{:S(2)}) %collective-permute-start.7) | collective-permute-done | bytes 65568 | tf_op jit(solution)/shard_map/ppermute | solution.py:227
  24.3 1.6 %shard_map.136 = (f32[128,128]{1,0:T(8,128)}, f32[128,128]{1,0:T(8,128)}, f32[512,128]{1,0:T(8,128)S(1)}, f32[512,128]{1,0:T(8,128)S(1)}) custom-call(s32[4]{0:T(128)} %counts.5, s32[1]{0:T(128)S(6)} %copy.18.refs_2_.fragment, f32[128,128]{1,0:T(8,128)} %global_fragment.3, f32[128,128]{1,0:T(8,128)} %outer_momentum.1, f32[128,128]{1,0:T(8,128)S(1)} %add.7.drift_sum), custom_call_target="tpu_custom_call" | custom-call | tf_op jit(solution)/shard_map/pallas_call | solution.py:344
  25.9 0.0 collective-permute-done.9.near
  26.0 0.0 collective-permute-done.8.far
  26.0 0.0 copy-done.2
  26.0 0.0 copy-done
  26.0 0.0 copy-done.1
  26.0 0.9 %shard_map.137 = (f32[256,128]{1,0:T(8,128)S(1)}, f32[1,512,128]{2,1,0:T(8,128)}, f32[1,512,128]{2,1,0:T(8,128)}) custom-call(f32[1,512,128]{2,1,0:T(8,128)S(1)} %copy-done, f32[1,512,128]{2,1,0:T(8,128)S(1)} %copy-done.1, f32[1,512,128]{2,1,0:T(8,128)S(1)} %copy-done.2, f32[6,128,256]{2,1,0:T(8,128)S(1)} %get-tuple-element.25.refs_0_.kept, ...), custom_call_target="tpu_custom_call" | custom-call | flops 983040 | bytes 1310720 | tf_op jit(solution)/shard_map/pallas_call | solution.py:356
  26.9 0.0 collective-permute-done.5.near
  26.9 1.8 %collective-permute-done.4.far = f32[1,128,256]{2,1,0:T(8,128)S(1)} collective-permute-done((f32[1,128,256]{2,1,0:T(8,128)S(1)}, f32[1,128,256]{2,1,0:T(8,128)S(1)}, u32[]{:S(2)}, u32[]{:S(2)}) %collective-permute-start.4) | collective-permute-done | bytes 131104 | tf_op jit(solution)/shard_map/ppermute | solution.py:227
  28.8 1.0 %shard_map.138 = (f32[1,512,128]{2,1,0:T(8,128)}, f32[1,512,128]{2,1,0:T(8,128)}, f32[1,512,128]{2,1,0:T(8,128)}) custom-call(f32[1,512,128]{2,1,0:T(8,128)S(1)} %copy-done, f32[1,512,128]{2,1,0:T(8,128)S(1)} %copy-done.1, f32[1,512,128]{2,1,0:T(8,128)S(1)} %copy-done.2, ...), custom_call_target="tpu_custom_call", output_to_operand_aliasing={{1}: (11, {}), {2}: (12, {})} | custom-call | tf_op jit(solution)/shard_map/pallas_call | solution.py:367
  (8 shorter events, 0.1 us)
Async XLA Ops:
  3.3 1.7 %collective-permute-start = (f32[2,128,256]{2,1,0:T(8,128)S(1)}, f32[2,128,256]{2,1,0:T(8,128)S(1)}, u32[]{:S(2)}, u32[]{:S(2)}) collective-permute-start(f32[2,128,256]{2,1,0:T(8,128)S(1)} %get-tuple-element.28), channel_id=1, source_target_pairs={{0,1},{1,0},{2,3},{3,2},{4,5},{5,4},{6,7},{7,6},{8,9},{9,8},{10,11... | collective-permute-start | bytes 786440 | tf_op jit(solution)/shard_map/ppermute | solution.py:227
  5.0 7.4 %collective-permute-start.1 = (f32[6,128,256]{2,1,0:T(8,128)S(1)}, f32[6,128,256]{2,1,0:T(8,128)S(1)}, u32[]{:S(2)}, u32[]{:S(2)}) collective-permute-start(f32[6,128,256]{2,1,0:T(8,128)S(1)} %get-tuple-element.29), channel_id=1, source_target_pairs={{0,1},{1,0},{2,3},{3,2},{4,5},{5,4},{6,7},{7,6},{8,9},{9,8},{10,11... | collective-permute-start | bytes 2359304 | tf_op jit(solution)/shard_map/ppermute | solution.py:227
  5.5 6.9 %collective-permute-start.3 = (f32[1,128,256]{2,1,0:T(8,128)S(1)}, f32[1,128,256]{2,1,0:T(8,128)S(1)}, u32[]{:S(2)}, u32[]{:S(2)}) collective-permute-start(f32[1,128,256]{2,1,0:T(8,128)S(1)} %shard_map.129.after), channel_id=1, source_target_pairs={{0,2},{1,3},{2,0},{3,1},{4,6},{5,7},{6,4},{7,5},{8,10},{9,11},{10,... | collective-permute-start | bytes 393224 | tf_op jit(solution)/shard_map/ppermute | solution.py:227
  9.2 8.0 %collective-permute-start.2 = (f32[1,128,256]{2,1,0:T(8,128)S(1)}, f32[1,128,256]{2,1,0:T(8,128)S(1)}, u32[]{:S(2)}, u32[]{:S(2)}) collective-permute-start(f32[1,128,256]{2,1,0:T(8,128)S(1)} %shard_map.131), channel_id=1, source_target_pairs={{0,2},{1,3},{2,0},{3,1},{4,6},{5,7},{6,4},{7,5},{8,10},{9,11},{10,... | collective-permute-start | bytes 393224 | tf_op jit(solution)/shard_map/ppermute | solution.py:227
  9.3 10.7 %collective-permute-start.6 = (f32[128,128]{1,0:T(8,128)S(1)}, f32[128,128]{1,0:T(8,128)S(1)}, u32[]{:S(2)}, u32[]{:S(2)}) collective-permute-start(f32[128,128]{1,0:T(8,128)S(1)} %get-tuple-element.32.refs_2_), channel_id=1, source_target_pairs={{0,16},{8,24},{16,0},{24,8},{1,17},{9,25},{17,1},{25,9},{2,18},{10... | collective-permute-start | bytes 196616 | tf_op jit(solution)/shard_map/ppermute | solution.py:227
  12.4 13.5 %collective-permute-start.9 = (f32[1,128,256]{2,1,0:T(8,128)S(1)}, f32[1,128,256]{2,1,0:T(8,128)S(1)}, u32[]{:S(2)}, u32[]{:S(2)}) collective-permute-start(f32[1,128,256]{2,1,0:T(8,128)S(1)} %shard_map.133.refs_3_), channel_id=1, source_target_pairs={{0,2},{1,3},{2,0},{3,1},{4,6},{5,7},{6,4},{7,5},{8,10},{9,11},{10,... | collective-permute-start | bytes 393224 | tf_op jit(solution)/shard_map/ppermute | solution.py:227
  14.6 11.3 %collective-permute-start.8 = (f32[1,128,256]{2,1,0:T(8,128)S(1)}, f32[1,128,256]{2,1,0:T(8,128)S(1)}, u32[]{:S(2)}, u32[]{:S(2)}) collective-permute-start(f32[1,128,256]{2,1,0:T(8,128)S(1)} %shard_map.132.refs_2_), channel_id=1, source_target_pairs={{0,4},{1,5},{2,6},{3,7},{4,0},{5,1},{6,2},{7,3},{8,12},{9,13},{10,... | collective-permute-start | bytes 393224 | tf_op jit(solution)/shard_map/ppermute | solution.py:227
  17.3 8.7 %copy-start.2 = (f32[1,512,128]{2,1,0:T(8,128)S(1)}, f32[1,512,128]{2,1,0:T(8,128)}, u32[]{:S(2)}) copy-start(f32[1,512,128]{2,1,0:T(8,128)} %second.3) | copy-start | bytes 786436
  17.3 8.7 %copy-start = (f32[1,512,128]{2,1,0:T(8,128)S(1)}, f32[1,512,128]{2,1,0:T(8,128)}, u32[]{:S(2)}) copy-start(f32[1,512,128]{2,1,0:T(8,128)} %params.5) | copy-start | bytes 786436
  17.3 8.7 %copy-start.1 = (f32[1,512,128]{2,1,0:T(8,128)S(1)}, f32[1,512,128]{2,1,0:T(8,128)}, u32[]{:S(2)}) copy-start(f32[1,512,128]{2,1,0:T(8,128)} %first.3) | copy-start | bytes 786436
  17.3 9.6 %collective-permute-start.5 = (f32[1,128,256]{2,1,0:T(8,128)S(1)}, f32[1,128,256]{2,1,0:T(8,128)S(1)}, u32[]{:S(2)}, u32[]{:S(2)}) collective-permute-start(f32[1,128,256]{2,1,0:T(8,128)S(1)} %shard_map.135), channel_id=1, source_target_pairs={{0,2},{1,3},{2,0},{3,1},{4,6},{5,7},{6,4},{7,5},{8,10},{9,11},{10,... | collective-permute-start | bytes 393224 | tf_op jit(solution)/shard_map/ppermute | solution.py:227
  17.6 11.1 %collective-permute-start.4 = (f32[1,128,256]{2,1,0:T(8,128)S(1)}, f32[1,128,256]{2,1,0:T(8,128)S(1)}, u32[]{:S(2)}, u32[]{:S(2)}) collective-permute-start(f32[1,128,256]{2,1,0:T(8,128)S(1)} %shard_map.134.refs_2_), channel_id=1, source_target_pairs={{0,4},{1,5},{2,6},{3,7},{4,0},{5,1},{6,2},{7,3},{8,12},{9,13},{10,... | collective-permute-start | bytes 393224 | tf_op jit(solution)/shard_map/ppermute | solution.py:227
  20.0 4.3 %collective-permute-start.7 = (f32[128,128]{1,0:T(8,128)S(1)}, f32[128,128]{1,0:T(8,128)S(1)}, u32[]{:S(2)}, u32[]{:S(2)}) collective-permute-start(f32[128,128]{1,0:T(8,128)S(1)} %add.6), channel_id=1, source_target_pairs={{0,8},{8,0},{16,24},{24,16},{1,9},{9,1},{17,25},{25,17},{2,10},{10... | collective-permute-start | bytes 196616 | tf_op jit(solution)/shard_map/ppermute | solution.py:227

commit v4 on v3

--- a/solution.py
+++ b/solution.py
@@ -43,42 +43,40 @@
     return value[:, :half], value[:, half:]
 
 
-def product_kernel(
-    order,
-    counts,
-    cotangent,
-    features,
-    away_far,
-    kept_far,
-    away,
-    kept,
-    masked,
-    counts_held,
-    cot_held,
-    held,
-    sems,
-):
-    targets = [(away_far, 0), (kept_far, 0)]
-    targets += [((away if q & 1 else kept), 2 * (q // 2)) for q in order[2:]]
-    small = [
-        pltpu.make_async_copy(counts, counts_held, sems.at[0]),
-        pltpu.make_async_copy(cotangent, cot_held, sems.at[1]),
+def fetch(sources, targets, sems, start=0):
+    copies = [
+        pltpu.make_async_copy(source, target, sems.at[start + slot])
+        for slot, (source, target) in enumerate(zip(sources, targets))
     ]
-    blocks = [
-        pltpu.make_async_copy(features.at[0, :, columns_of(q, held.shape[2])], held.at[slot], sems.at[2 + slot])
-        for slot, q in enumerate(order)
-    ]
-    for copy in small + blocks:
+    for copy in copies:
         copy.start()
+    return copies
+
+
+def fetch_blocks(order, features, held, sems, start):
+    rows = held.shape[2]
+    sources = [features.at[0, :, columns_of(q, rows)] for q in order]
+    return fetch(sources, [held.at[slot] for slot in range(len(order))], sems, start)
+
+
+def first_kernel(order, counts, cotangent, features, away, kept, masked, counts_held, cot_held, held, sems):
+    small = fetch((counts, cotangent), (counts_held, cot_held), sems)
+    blocks = fetch_blocks(order, features, held, sems, len(small))
     for copy in small:
         copy.wait()
     tokens = cot_held.shape[1]
     live = counts_held[lax.axis_index("worker")] - lax.axis_index("fsdp") * tokens
     masked[...] = masked_rows(live, cot_held[0])
-    for slot, q in enumerate(order):
-        blocks[slot].wait()
-        into, at = targets[slot]
-        into[at], into[at + 1] = product_halves(masked[...], held[slot])
+    for block, slot, into in zip(blocks, range(len(order)), (away, kept)):
+        block.wait()
+        into[0], into[1] = product_halves(masked[...], held[slot])
+
+
+def rest_kernel(order, masked, features, away_pass, kept_pass, away, kept):
+    targets = ((away_pass, 0), (kept_pass, 0), (away, 2), (kept, 2), (away, 0), (kept, 0))
+    for q, (into, at) in zip(order, targets):
+        columns = columns_of(q, 2 * kept.shape[2])
+        into[at], into[at + 1] = product_halves(masked[...], features[0, :, columns])
 
 
 def drift_kernel(counts, fragment, params, global_fragment, after, drift, inverse, *held_and_sems):
@@ -271,24 +269,32 @@
         held_fragment = pltpu.SMEM(fragment_index.shape, fragment_index.dtype)
         held_piece = pltpu.VMEM(global_fragment.shape, global_fragment.dtype)
 
-        order = tuple(q + s for q in range(devices - 2, -1, -2) for s in (1, 0))
-        away_far, kept_far, away, kept = pl.pallas_call(
-            functools.partial(product_kernel, order),
-            out_shape=[halves(1)] * 2 + [halves(devices // 2 - 1)] * 2,
+        away_far, kept_far, masked = pl.pallas_call(
+            functools.partial(first_kernel, (7, 6)),
+            out_shape=[halves(1)] * 2 + [jax.ShapeDtypeStruct((tokens, width), jnp.bfloat16)],
             in_specs=[HBM] * 3,
-            out_specs=[VMEM] * 4,
+            out_specs=[VMEM] * 3,
             scratch_shapes=[
-                pltpu.VMEM((tokens, width), jnp.bfloat16),
                 held_counts,
                 pltpu.VMEM(cotangent.shape, cotangent.dtype),
-                pltpu.VMEM((devices, tokens, rows), features.dtype),
-                pltpu.SemaphoreType.DMA((2 + devices,)),
+                pltpu.VMEM((2, tokens, rows), features.dtype),
+                pltpu.SemaphoreType.DMA((4,)),
             ],
             compiler_params=room,
-            cost_estimate=cost(devices),
+            cost_estimate=cost(2),
+            name="far_products",
         )(far_counts, far_cotangent, far_features)
-
-        def add(*terms):
+        away_pass, kept_pass, away, kept = pl.pallas_call(
+            functools.partial(rest_kernel, (5, 4, 3, 2, 1, 0)),
+            out_shape=[halves(1)] * 2 + [halves(2)] * 2,
+            in_specs=[VMEM] * 2,
+            out_specs=[VMEM] * 4,
+            compiler_params=room,
+            cost_estimate=free,
+            name="rest_products",
+        )(masked, features)
+
+        def add(*terms, name):
             picks = [pick for _, pick in terms]
             return pl.pallas_call(
                 functools.partial(add_kernel, picks),
@@ -297,18 +303,21 @@
                 out_specs=VMEM,
                 compiler_params=room,
                 cost_estimate=free,
+                name=name,
             )(*(array for array, _ in terms))
 
         def part(number):
             return slice(number, number + 1)
 
         come_far = hop(away_far, "fsdp", devices, 1)
-        sent = add((kept_far, part(0)), (come_far, part(0)), (far_fragment, None))
+        sent = add((kept_far, part(0)), (come_far, part(0)), (far_fragment, None), name="add_a1")
         far_left = hop(sent, "fsdp", devices, 2)
-        away, _ = lax.optimization_barrier((away, sent))
+        away_pass, away, _ = lax.optimization_barrier((away_pass, away, sent))
+        come_pass = hop(away_pass, "fsdp", devices, 1)
         come = hop(away, "fsdp", devices, 1)
         drift, inverse = pl.pallas_call(
             drift_kernel,
+            name="drift",
             out_shape=[block((pieces, width)), block((8, width))],
             in_specs=[HBM] * 4 + [ANY],
             out_specs=[VMEM] * 2,
@@ -322,13 +331,13 @@
             compiler_params=room,
             cost_estimate=free,
         )(far_counts, far_fragment, far_params, far_global, sent)
-        sent = add((kept_far, part(1)), (come_far, part(1)), (drift, None))
+        sent = add((kept_far, part(1)), (come_far, part(1)), (drift, None), name="add_a2")
         far_right = hop(sent, "fsdp", devices, 2)
-        passed = add((kept, part(4)), (come, part(4)), (far_left, part(0)))
+        passed = add((kept_pass, part(0)), (come_pass, part(0)), (far_left, part(0)), name="add_c1")
         far_left = hop(passed, "fsdp", devices, 4)
-        near_left = add((kept, part(2)), (come, part(2)), (passed, None))
-        far_right = add((kept, part(5)), (come, part(5)), (far_right, part(0)), (near_left, None))
-        near_right = add((kept, part(3)), (come, part(3)), (far_right, None))
+        near_left = add((kept, part(2)), (come, part(2)), (passed, None), name="add_n1")
+        far_right = add((kept_pass, part(1)), (come_pass, part(1)), (far_right, part(0)), (passed, None), name="add_c2")
+        near_right = add((kept, part(3)), (come, part(3)), (far_right, None), name="add_n2")
         drift, _ = lax.optimization_barrier((drift, sent))
         bit = workers // 2
         while bit:
@@ -343,6 +352,7 @@
         whole = block((rows, width))
         new_global, new_momentum, scale, mix = pl.pallas_call(
             functools.partial(outer_kernel, workers),
+            name="outer_step",
             out_shape=[piece, piece, whole, whole],
             in_specs=[HBM] * 4 + [VMEM],
             out_specs=[VMEM] * 4,
@@ -355,6 +365,7 @@
         held_half = pltpu.VMEM((half, width), jnp.float32)
         inner, new_first, new_second = pl.pallas_call(
             left_kernel,
+            name="left_step",
             out_shape=[block((half, width)), state, state],
             in_specs=[VMEM] * 8,
             out_specs=[VMEM, HBM, HBM],
@@ -366,6 +377,7 @@
         )(params, first, second, kept, come, far_left, near_left, inverse)
         new_params, new_first, new_second = pl.pallas_call(
             right_kernel,
+            name="right_step",
             out_shape=[state] * 3,
             in_specs=[VMEM] * 11 + [HBM] * 2,
             out_specs=[HBM] * 3,

time: 30 us -> 27.3 us (0.910)
  waiting for transfers between devices: 6.26 us -> 3.78 us
  Pallas kernels: 7.36 us -> 6.53 us
  starting transfers between devices: 14.7 us -> 15.3 us
    ppermute x10 -> x11, waiting for transfers between devices: 6.26 us -> 3.78 us  [hop(): return lax.ppermute(value, axis, [(d, d ^ bit) for d in range(devices)])]
    pallas_call x5 -> x6, Pallas kernels: 7.25 us -> 6.42 us  [the longest x1 1.59 us: body(): pl.pallas_call(functools.partial(outer_kernel, workers), name='outer_step...]
    ppermute x10 -> x11, starting transfers between devices: 14.7 us -> 15.3 us  [hop(): return lax.ppermute(value, axis, [(d, d ^ bit) for d in range(devices)])]
  transfers between devices with their start and end apart: 10 -> 11, of which waited for: 4 -> 3; matrix products, arithmetic and copies ran while one was open for 0% -> 0% of each run, Pallas kernels for 12% -> 15%
where the time goes in v4:
time: 27.3 us; the launch traced here: 27.1 us
  starting transfers between devices  15.3 us (56%)
  Pallas kernels  6.53 us (24%)
  waiting for transfers between devices  3.78 us (14%)
  between operations  1.45 us (5%)
    ppermute x11, starting transfers between devices, hop(): return lax.ppermute(value, axis, [(d, d ^ bit) for d in range(devices)])  15.3 us
    ppermute x11, waiting for transfers between devices, hop(): return lax.ppermute(value, axis, [(d, d ^ bit) for d in range(devices)])  3.78 us
    pallas_call x1, Pallas kernels, body(): pl.pallas_call(functools.partial(outer_kernel, workers), name='outer_step...  1.59 us
    pallas_call x1, Pallas kernels, body(): pl.pallas_call(functools.partial(first_kernel, (7, 6)), out_shape=[halves...  1.47 us
    pallas_call x1, Pallas kernels, body(): pl.pallas_call(right_kernel, name='right_step', out_shape=[state] * 3, in...  1.05 us
    pallas_call x1, Pallas kernels, body(): pl.pallas_call(drift_kernel, name='drift', out_shape=[block((pieces, widt...  1.01 us
    pallas_call x1, Pallas kernels, body(): pl.pallas_call(left_kernel, name='left_step', out_shape=[block((half, wid...  0.9 us
  transfers between devices with their start and end apart: 11, of which 3 were waited for; matrix products, arithmetic and copies ran while one was open for 0% of the time, Pallas kernels for 15%

profile of v4, /device:TPU:0, one launch (start us, length us, event | category | flops | bytes accessed | tf_op | source)
XLA Modules:
  0.0 27.1 jit_solution(4418054421869421310)
XLA Ops:
  0.6 0.0 copy-start
  0.6 1.5 %far_products.1 = (f32[2,128,256]{2,1,0:T(8,128)S(1)}, f32[2,128,256]{2,1,0:T(8,128)S(1)}, bf16[128,128]{1,0:T(8,128)(2,1)S(1)}) custom-call(s32[4]{0:T(128)} %counts.5, bf16[1,128,128]{2,1,0:T(8,128)(2,1)} %cotangent.1, bf16[1,128,4096]{2,1,0:T(8,128)(2,1)} %features.3), custom_call_target="tpu_custom_call" | custom-call | flops 33554432 | bytes 786432 | tf_op jit(solution)/shard_map/far_products/pallas_call | solution.py:272
  2.1 0.5 %collective-permute-start = (f32[2,128,256]{2,1,0:T(8,128)S(1)}, f32[2,128,256]{2,1,0:T(8,128)S(1)}, u32[]{:S(2)}, u32[]{:S(2)}) collective-permute-start(f32[2,128,256]{2,1,0:T(8,128)S(1)} %get-tuple-element.34), channel_id=1, source_target_pairs={{0,1},{1,0},{2,3},{3,2},{4,5},{5,4},{6,7},{7,6},{8,9},{9,8},{10,11... | collective-permute-start | bytes 786440 | tf_op jit(solution)/shard_map/ppermute | solution.py:225
  3.3 0.0 copy-done
  3.3 0.4 %rest_products.1 = (f32[2,128,256]{2,1,0:T(8,128)S(1)}, f32[2,128,256]{2,1,0:T(8,128)S(1)}, f32[4,128,256]{2,1,0:T(8,128)S(1)}, f32[4,128,256]{2,1,0:T(8,128)S(1)}) custom-call(bf16[128,128]{1,0:T(8,128)(2,1)S(1)} %get-tuple-element.29.masked, bf16[1,128,4096]{2,1,0:T(8,128)(2,1)S(1)} %copy-done), custom_call_target="tpu_custom_call" | custom-call | tf_op jit(solution)/shard_map/rest_products/pallas_call | solution.py:287
  3.7 0.1 collective-permute-done.refs_1_
  3.8 0.4 %collective-permute-start.1 = (f32[4,128,256]{2,1,0:T(8,128)S(1)}, f32[4,128,256]{2,1,0:T(8,128)S(1)}, u32[]{:S(2)}, u32[]{:S(2)}) collective-permute-start(f32[4,128,256]{2,1,0:T(8,128)S(1)} %get-tuple-element.35), channel_id=1, source_target_pairs={{0,1},{1,0},{2,3},{3,2},{4,5},{5,4},{6,7},{7,6},{8,9},{9,8},{10,11... | collective-permute-start | bytes 1572872 | tf_op jit(solution)/shard_map/ppermute | solution.py:225
  4.3 0.1 collective-permute-start.2
  4.4 2.9 %collective-permute-start.4 = (f32[1,128,256]{2,1,0:T(8,128)S(1)}, f32[1,128,256]{2,1,0:T(8,128)S(1)}, u32[]{:S(2)}, u32[]{:S(2)}) collective-permute-start(f32[1,128,256]{2,1,0:T(8,128)S(1)} %add_a1.1.after), channel_id=1, source_target_pairs={{0,2},{1,3},{2,0},{3,1},{4,6},{5,7},{6,4},{7,5},{8,10},{9,11},{10,... | collective-permute-start | bytes 393224 | tf_op jit(solution)/shard_map/ppermute | solution.py:225
  7.3 1.0 %drift.1 = (f32[128,128]{1,0:T(8,128)S(1)}, f32[8,128]{1,0:T(8,128)S(1)}) custom-call(s32[4]{0:T(128)} %counts.5, s32[1]{0:T(128)S(6)} %copy.18.refs_2_.fragment, f32[1,512,128]{2,1,0:T(8,128)} %params.5, f32[128,128]{1,0:T(8,128)} %global_fragment.3, f32[1,128,256]{2,1,0:T(8,128)S(1)} %add_a1.1.after), custom_call_target="tpu_custom_call" | custom-call | tf_op jit(solution)/shard_map/drift/pallas_call | solution.py:318
  8.4 0.1 collective-permute-start.3
  8.5 2.0 %collective-permute-start.7 = (f32[128,128]{1,0:T(8,128)S(1)}, f32[128,128]{1,0:T(8,128)S(1)}, u32[]{:S(2)}, u32[]{:S(2)}) collective-permute-start(f32[128,128]{1,0:T(8,128)S(1)} %get-tuple-element.40.refs_2_), channel_id=1, source_target_pairs={{0,16},{8,24},{16,0},{24,8},{1,17},{9,25},{17,1},{25,9},{2,18},{10... | collective-permute-start | bytes 196616 | tf_op jit(solution)/shard_map/ppermute | solution.py:225
  10.4 0.9 %collective-permute-done.4.refs_2_ = f32[1,128,256]{2,1,0:T(8,128)S(1)} collective-permute-done((f32[1,128,256]{2,1,0:T(8,128)S(1)}, f32[1,128,256]{2,1,0:T(8,128)S(1)}, u32[]{:S(2)}, u32[]{:S(2)}) %collective-permute-start.4) | collective-permute-done | bytes 131104 | tf_op jit(solution)/shard_map/ppermute | solution.py:225
  11.3 0.0 collective-permute-done.2.refs_1_
  11.3 3.0 %collective-permute-start.9 = (f32[1,128,256]{2,1,0:T(8,128)S(1)}, f32[1,128,256]{2,1,0:T(8,128)S(1)}, u32[]{:S(2)}, u32[]{:S(2)}) collective-permute-start(f32[1,128,256]{2,1,0:T(8,128)S(1)} %add_c1.1.refs_3_.refs_2_), channel_id=1, source_target_pairs={{0,4},{1,5},{2,6},{3,7},{4,0},{5,1},{6,2},{7,3},{8,12},{9,13},{10,... | collective-permute-start | bytes 393224 | tf_op jit(solution)/shard_map/ppermute | solution.py:225
  14.3 0.0 collective-permute-done.1.refs_1_.come
  14.4 2.1 %collective-permute-start.10 = (f32[1,128,256]{2,1,0:T(8,128)S(1)}, f32[1,128,256]{2,1,0:T(8,128)S(1)}, u32[]{:S(2)}, u32[]{:S(2)}) collective-permute-start(f32[1,128,256]{2,1,0:T(8,128)S(1)} %add_n1.1), channel_id=1, source_target_pairs={{0,2},{1,3},{2,0},{3,1},{4,6},{5,7},{6,4},{7,5},{8,10},{9,11},{10,... | collective-permute-start | bytes 393224 | tf_op jit(solution)/shard_map/ppermute | solution.py:225
  16.5 0.0 collective-permute-done.3.refs_2_
  16.5 1.0 %collective-permute-start.5 = (f32[1,128,256]{2,1,0:T(8,128)S(1)}, f32[1,128,256]{2,1,0:T(8,128)S(1)}, u32[]{:S(2)}, u32[]{:S(2)}) collective-permute-start(f32[1,128,256]{2,1,0:T(8,128)S(1)} %add_c2.1.refs_2_), channel_id=1, source_target_pairs={{0,4},{1,5},{2,6},{3,7},{4,0},{5,1},{6,2},{7,3},{8,12},{9,13},{10,... | collective-permute-start | bytes 393224 | tf_op jit(solution)/shard_map/ppermute | solution.py:225
  17.5 0.0 copy-start.1
  17.5 0.0 copy-start.2
  17.5 1.6 %collective-permute-start.6 = (f32[1,128,256]{2,1,0:T(8,128)S(1)}, f32[1,128,256]{2,1,0:T(8,128)S(1)}, u32[]{:S(2)}, u32[]{:S(2)}) collective-permute-start(f32[1,128,256]{2,1,0:T(8,128)S(1)} %add_n2.1), channel_id=1, source_target_pairs={{0,2},{1,3},{2,0},{3,1},{4,6},{5,7},{6,4},{7,5},{8,10},{9,11},{10,... | collective-permute-start | bytes 393224 | tf_op jit(solution)/shard_map/ppermute | solution.py:225
  19.1 0.0 collective-permute-done.7
  19.1 1.6 %collective-permute-start.8 = (f32[128,128]{1,0:T(8,128)S(1)}, f32[128,128]{1,0:T(8,128)S(1)}, u32[]{:S(2)}, u32[]{:S(2)}) collective-permute-start(f32[128,128]{1,0:T(8,128)S(1)} %add.6), channel_id=1, source_target_pairs={{0,8},{8,0},{16,24},{24,16},{1,9},{9,1},{17,25},{25,17},{2,10},{10... | collective-permute-start | bytes 196616 | tf_op jit(solution)/shard_map/ppermute | solution.py:225
  20.7 2.8 %collective-permute-done.8 = f32[128,128]{1,0:T(8,128)S(1)} collective-permute-done((f32[128,128]{1,0:T(8,128)S(1)}, f32[128,128]{1,0:T(8,128)S(1)}, u32[]{:S(2)}, u32[]{:S(2)}) %collective-permute-start.8) | collective-permute-done | bytes 65568 | tf_op jit(solution)/shard_map/ppermute | solution.py:225
  23.5 1.6 %outer_step.1 = (f32[128,128]{1,0:T(8,128)}, f32[128,128]{1,0:T(8,128)}, f32[512,128]{1,0:T(8,128)S(1)}, f32[512,128]{1,0:T(8,128)S(1)}) custom-call(s32[4]{0:T(128)} %counts.5, s32[1]{0:T(128)S(6)} %copy.18.refs_2_.fragment, f32[128,128]{1,0:T(8,128)} %global_fragment.3, f32[128,128]{1,0:T(8,128)} %outer_momentum.1, f32[128,128]{1,0:T(8,128)S(1)} %add.7.drift_sum), custom_call_target="tpu_custom_call" | custom-call | tf_op jit(solution)/shard_map/outer_step/pallas_call | solution.py:353
  25.1 0.0 collective-permute-done.9.far
  25.1 0.0 collective-permute-done.10.near
  25.1 0.9 %left_step.1 = (f32[256,128]{1,0:T(8,128)S(1)}, f32[1,512,128]{2,1,0:T(8,128)}, f32[1,512,128]{2,1,0:T(8,128)}) custom-call(f32[1,512,128]{2,1,0:T(8,128)S(1)} %copy-done.1, f32[1,512,128]{2,1,0:T(8,128)S(1)} %copy-done.2, f32[1,512,128]{2,1,0:T(8,128)S(1)} %copy-done.3, f32[4,128,256]{2,1,0:T(8,128)S(1)} %get-tuple-element.30.refs_0_.kept, ...), custom_call_target="tpu_custom_call" | custom-call | flops 983040 | bytes 1310720 | tf_op jit(solution)/shard_map/left_step/pallas_call | solution.py:366
  26.0 0.0 collective-permute-done.5.far
  26.0 0.0 collective-permute-done.6.near
  26.1 1.1 %right_step.1 = (f32[1,512,128]{2,1,0:T(8,128)}, f32[1,512,128]{2,1,0:T(8,128)}, f32[1,512,128]{2,1,0:T(8,128)}) custom-call(f32[1,512,128]{2,1,0:T(8,128)S(1)} %copy-done.1, f32[1,512,128]{2,1,0:T(8,128)S(1)} %copy-done.2, f32[1,512,128]{2,1,0:T(8,128)S(1)} %copy-done.3, ...), custom_call_target="tpu_custom_call", output_to_operand_aliasing={{1}: (11, {}), {2}: (12, {})} | custom-call | tf_op jit(solution)/shard_map/right_step/pallas_call | solution.py:378
  (12 shorter events, 0.1 us)
Async XLA Ops:
  0.6 2.7 %copy-start = (bf16[1,128,4096]{2,1,0:T(8,128)(2,1)S(1)}, bf16[1,128,4096]{2,1,0:T(8,128)(2,1)}, u32[]{:S(2)}) copy-start(bf16[1,128,4096]{2,1,0:T(8,128)(2,1)} %features.3) | copy-start | bytes 3145732
  2.1 1.7 %collective-permute-start = (f32[2,128,256]{2,1,0:T(8,128)S(1)}, f32[2,128,256]{2,1,0:T(8,128)S(1)}, u32[]{:S(2)}, u32[]{:S(2)}) collective-permute-start(f32[2,128,256]{2,1,0:T(8,128)S(1)} %get-tuple-element.34), channel_id=1, source_target_pairs={{0,1},{1,0},{2,3},{3,2},{4,5},{5,4},{6,7},{7,6},{8,9},{9,8},{10,11... | collective-permute-start | bytes 786440 | tf_op jit(solution)/shard_map/ppermute | solution.py:225
  3.8 10.5 %collective-permute-start.1 = (f32[4,128,256]{2,1,0:T(8,128)S(1)}, f32[4,128,256]{2,1,0:T(8,128)S(1)}, u32[]{:S(2)}, u32[]{:S(2)}) collective-permute-start(f32[4,128,256]{2,1,0:T(8,128)S(1)} %get-tuple-element.35), channel_id=1, source_target_pairs={{0,1},{1,0},{2,3},{3,2},{4,5},{5,4},{6,7},{7,6},{8,9},{9,8},{10,11... | collective-permute-start | bytes 1572872 | tf_op jit(solution)/shard_map/ppermute | solution.py:225
  4.3 7.1 %collective-permute-start.2 = (f32[2,128,256]{2,1,0:T(8,128)S(1)}, f32[2,128,256]{2,1,0:T(8,128)S(1)}, u32[]{:S(2)}, u32[]{:S(2)}) collective-permute-start(f32[2,128,256]{2,1,0:T(8,128)S(1)} %get-tuple-element.37), channel_id=1, source_target_pairs={{0,1},{1,0},{2,3},{3,2},{4,5},{5,4},{6,7},{7,6},{8,9},{9,8},{10,11... | collective-permute-start | bytes 786440 | tf_op jit(solution)/shard_map/ppermute | solution.py:225
  4.4 6.9 %collective-permute-start.4 = (f32[1,128,256]{2,1,0:T(8,128)S(1)}, f32[1,128,256]{2,1,0:T(8,128)S(1)}, u32[]{:S(2)}, u32[]{:S(2)}) collective-permute-start(f32[1,128,256]{2,1,0:T(8,128)S(1)} %add_a1.1.after), channel_id=1, source_target_pairs={{0,2},{1,3},{2,0},{3,1},{4,6},{5,7},{6,4},{7,5},{8,10},{9,11},{10,... | collective-permute-start | bytes 393224 | tf_op jit(solution)/shard_map/ppermute | solution.py:225
  8.4 8.1 %collective-permute-start.3 = (f32[1,128,256]{2,1,0:T(8,128)S(1)}, f32[1,128,256]{2,1,0:T(8,128)S(1)}, u32[]{:S(2)}, u32[]{:S(2)}) collective-permute-start(f32[1,128,256]{2,1,0:T(8,128)S(1)} %add_a2.1), channel_id=1, source_target_pairs={{0,2},{1,3},{2,0},{3,1},{4,6},{5,7},{6,4},{7,5},{8,10},{9,11},{10,... | collective-permute-start | bytes 393224 | tf_op jit(solution)/shard_map/ppermute | solution.py:225
  8.5 10.7 %collective-permute-start.7 = (f32[128,128]{1,0:T(8,128)S(1)}, f32[128,128]{1,0:T(8,128)S(1)}, u32[]{:S(2)}, u32[]{:S(2)}) collective-permute-start(f32[128,128]{1,0:T(8,128)S(1)} %get-tuple-element.40.refs_2_), channel_id=1, source_target_pairs={{0,16},{8,24},{16,0},{24,8},{1,17},{9,25},{17,1},{25,9},{2,18},{10... | collective-permute-start | bytes 196616 | tf_op jit(solution)/shard_map/ppermute | solution.py:225
  11.3 13.7 %collective-permute-start.9 = (f32[1,128,256]{2,1,0:T(8,128)S(1)}, f32[1,128,256]{2,1,0:T(8,128)S(1)}, u32[]{:S(2)}, u32[]{:S(2)}) collective-permute-start(f32[1,128,256]{2,1,0:T(8,128)S(1)} %add_c1.1.refs_3_.refs_2_), channel_id=1, source_target_pairs={{0,4},{1,5},{2,6},{3,7},{4,0},{5,1},{6,2},{7,3},{8,12},{9,13},{10,... | collective-permute-start | bytes 393224 | tf_op jit(solution)/shard_map/ppermute | solution.py:225
  14.4 10.7 %collective-permute-start.10 = (f32[1,128,256]{2,1,0:T(8,128)S(1)}, f32[1,128,256]{2,1,0:T(8,128)S(1)}, u32[]{:S(2)}, u32[]{:S(2)}) collective-permute-start(f32[1,128,256]{2,1,0:T(8,128)S(1)} %add_n1.1), channel_id=1, source_target_pairs={{0,2},{1,3},{2,0},{3,1},{4,6},{5,7},{6,4},{7,5},{8,10},{9,11},{10,... | collective-permute-start | bytes 393224 | tf_op jit(solution)/shard_map/ppermute | solution.py:225
  16.5 9.6 %collective-permute-start.5 = (f32[1,128,256]{2,1,0:T(8,128)S(1)}, f32[1,128,256]{2,1,0:T(8,128)S(1)}, u32[]{:S(2)}, u32[]{:S(2)}) collective-permute-start(f32[1,128,256]{2,1,0:T(8,128)S(1)} %add_c2.1.refs_2_), channel_id=1, source_target_pairs={{0,4},{1,5},{2,6},{3,7},{4,0},{5,1},{6,2},{7,3},{8,12},{9,13},{10,... | collective-permute-start | bytes 393224 | tf_op jit(solution)/shard_map/ppermute | solution.py:225
  17.5 7.6 %copy-start.3 = (f32[1,512,128]{2,1,0:T(8,128)S(1)}, f32[1,512,128]{2,1,0:T(8,128)}, u32[]{:S(2)}) copy-start(f32[1,512,128]{2,1,0:T(8,128)} %second.3) | copy-start | bytes 786436
  17.5 7.6 %copy-start.1 = (f32[1,512,128]{2,1,0:T(8,128)S(1)}, f32[1,512,128]{2,1,0:T(8,128)}, u32[]{:S(2)}) copy-start(f32[1,512,128]{2,1,0:T(8,128)} %params.5) | copy-start | bytes 786436
  17.5 7.6 %copy-start.2 = (f32[1,512,128]{2,1,0:T(8,128)S(1)}, f32[1,512,128]{2,1,0:T(8,128)}, u32[]{:S(2)}) copy-start(f32[1,512,128]{2,1,0:T(8,128)} %first.3) | copy-start | bytes 786436
  17.5 8.5 %collective-permute-start.6 = (f32[1,128,256]{2,1,0:T(8,128)S(1)}, f32[1,128,256]{2,1,0:T(8,128)S(1)}, u32[]{:S(2)}, u32[]{:S(2)}) collective-permute-start(f32[1,128,256]{2,1,0:T(8,128)S(1)} %add_n2.1), channel_id=1, source_target_pairs={{0,2},{1,3},{2,0},{3,1},{4,6},{5,7},{6,4},{7,5},{8,10},{9,11},{10,... | collective-permute-start | bytes 393224 | tf_op jit(solution)/shard_map/ppermute | solution.py:225
  19.1 4.3 %collective-permute-start.8 = (f32[128,128]{1,0:T(8,128)S(1)}, f32[128,128]{1,0:T(8,128)S(1)}, u32[]{:S(2)}, u32[]{:S(2)}) collective-permute-start(f32[128,128]{1,0:T(8,128)S(1)} %add.6), channel_id=1, source_target_pairs={{0,8},{8,0},{16,24},{24,16},{1,9},{9,1},{17,25},{25,17},{2,10},{10... | collective-permute-start | bytes 196616 | tf_op jit(solution)/shard_map/ppermute | solution.py:225

commit v5 on v4

v5 whole, which is shorter than its diff:
```python
import functools

import jax
import jax.numpy as jnp
from jax import lax
from jax.experimental import pallas as pl
from jax.experimental.pallas import tpu as pltpu
from jax.sharding import PartitionSpec as P

FRAGS = 4
LANES = 128

BETA_ONE = 0.9
BETA_TWO = 0.95
CORRECT_ONE = 0.6513216
CORRECT_TWO = 0.401263
ADAM_EPS = 1e-08
LEARN_RATE = 0.02
DECAY_RATE = 0.1
NESTEROV = 0.9
OUTER_RATE = 0.7
MIXING = 0.5

VMEM = pl.BlockSpec(memory_space=pltpu.VMEM)
SMEM = pl.BlockSpec(memory_space=pltpu.SMEM)
HBM = pl.BlockSpec(memory_space=pltpu.HBM)
ANY = pl.BlockSpec(memory_space=pl.ANY)
ROOM = 8 << 20


def masked_rows(live, cotangent):
    rows = lax.broadcasted_iota(jnp.int32, cotangent.shape, 0)
    return jnp.where(rows < live, cotangent.astype(jnp.float32), 0.0).astype(jnp.bfloat16)


def columns_of(relative, rows, start, size):
    return pl.ds(pl.multiple_of((lax.axis_index("fsdp") ^ relative) * rows + start, LANES), size)


def product(masked, features):
    return lax.dot_general(masked, features, (((0,), (0,)), ((), ())), preferred_element_type=jnp.float32)


def fetch(sources, targets, sems, start=0):
    copies = [
        pltpu.make_async_copy(source, target, sems.at[start + slot])
        for slot, (source, target) in enumerate(zip(sources, targets))
    ]
    for copy in copies:
        copy.start()
    return copies


def first_kernel(order, counts, cotangent, features, away, kept, masked, counts_held, cot_held, held, sems):
    half = held.shape[2]
    small = fetch((counts, cotangent), (counts_held, cot_held), sems)
    columns = [columns_of(q, 2 * half, 0, half) for q in order]
    blocks = fetch([features.at[0, :, c] for c in columns], [held.at[n] for n in range(len(order))], sems, len(small))
    for copy in small:
        copy.wait()
    tokens = cot_held.shape[1]
    live = counts_held[lax.axis_index("worker")] - lax.axis_index("fsdp") * tokens
    masked[...] = masked_rows(live, cot_held[0])
    for slot, into in enumerate((away, kept)):
        blocks[slot].wait()
        into[0] = product(masked[...], held[slot])


def rest_kernel(masked, features, away_mid, kept_mid, away, kept):
    half = kept.shape[2]
    places = [(6, 1, 0), (4, 0, 1), (4, 1, 2), (2, 0, 3), (2, 1, 4), (0, 0, 0), (0, 1, 1)]
    for q, side, at in places:
        for core, into in ((1, away_mid if q else away), (0, kept_mid if q else kept)):
            into[at] = product(masked[...], features[0, :, columns_of(q + core, 2 * half, side * half, half)])


def drift_kernel(
    workers, counts, fragment, params, global_fragment, after, drift, scale, inverse, share, *held_and_sems
):
    del after
    held, sems = held_and_sems[:-1], held_and_sems[-1]
    copies = fetch((counts, fragment, params, global_fragment), held, sems)
    scale[...] = jnp.ones_like(scale)
    for copy in copies:
        copy.wait()
    counts_held, fragment_held, params_held, global_held = held
    mine = pl.ds(fragment_held[0], drift.shape[0], stride=FRAGS)
    count = counts_held[lax.axis_index("worker")].astype(jnp.float32)
    drift[...] = count * (global_held[...] - params_held[0, mine, :])
    scale[mine, :] = jnp.full_like(drift, 1.0 - MIXING)
    total = counts_held[0]
    for other in range(1, workers):
        total = total + counts_held[other]
    inverse[...] = jnp.ones_like(inverse) / count
    share[...] = jnp.ones_like(share) / total.astype(jnp.float32)


def add_kernel(picks, *refs):
    total = None
    for ref, pick in zip(refs, picks):
        if pick is not None:
            total = ref[pick] if total is None else total + ref[pick]
    refs[-1][...] = total


def adam(before, first, second, gradient):
    first_new = BETA_ONE * first + (1.0 - BETA_ONE) * gradient
    second_new = BETA_TWO * second + (1.0 - BETA_TWO) * gradient * gradient
    update = first_new * (1.0 / CORRECT_ONE) / (jnp.sqrt(second_new * (1.0 / CORRECT_TWO)) + ADAM_EPS)
    return before - LEARN_RATE * (update + DECAY_RATE * before), first_new, second_new


def outer(pseudo_grad, global_fragment, outer_momentum):
    momentum = NESTEROV * outer_momentum + pseudo_grad
    return global_fragment - OUTER_RATE * (pseudo_grad + NESTEROV * momentum), momentum


def half_step(half, states, sums, inverse, held):
    params, first, second = states
    kept, come, far, near = sums
    held_first, held_second = held
    rows = kept.shape[2]
    for lane in range(0, rows, LANES):
        lanes, there = pl.ds(lane, LANES), pl.ds(half * rows + lane, LANES)
        summed = kept[half, :, lanes] + come[half, :, lanes] + near[half, :, lanes] + far[0, :, lanes]
        inner, held_first[lanes, :], held_second[lanes, :] = adam(
            params[0, there, :], first[0, there, :], second[0, there, :], summed.T * inverse[0:1, :]
        )
        yield lanes, there, inner


def send(copies, sems, source, target):
    copies.append(pltpu.make_async_copy(source, target, sems.at[len(copies)]))
    copies[-1].start()


def left_kernel(
    params,
    first,
    second,
    kept,
    come,
    far,
    near,
    inverse,
    scale,
    share,
    global_fragment,
    outer_momentum,
    drift,
    other_drift,
    mix,
    new_params,
    new_first,
    new_second,
    new_global,
    new_momentum,
    held_params,
    held_first,
    held_second,
    held_global,
    held_momentum,
    spread,
    sems,
):
    copies = []
    fresh, momentum = outer((drift[...] + other_drift[...]) * share[0:1, :], global_fragment[...], outer_momentum[...])
    held_global[...] = fresh
    held_momentum[...] = momentum
    send(copies, sems, held_global, new_global)
    send(copies, sems, held_momentum, new_momentum)
    for at in range(FRAGS):
        spread[pl.ds(at, fresh.shape[0], stride=FRAGS), :] = fresh
    for lanes, there, value in half_step(
        0, (params, first, second), (kept, come, far, near), inverse, (held_first, held_second)
    ):
        held_params[lanes, :] = scale[there, :] * value + (1.0 - scale[there, :]) * spread[there, :]
        for source, target in ((held_first, new_first), (held_second, new_second), (held_params, new_params)):
            send(copies, sems, source.at[lanes], target.at[0, there])
    right = pl.ds(mix.shape[0], mix.shape[0])
    mix[...] = (1.0 - scale[right, :]) * spread[right, :]
    for copy in copies:
        copy.wait()


def right_kernel(
    params,
    first,
    second,
    kept,
    come,
    far,
    near,
    inverse,
    scale,
    mix,
    left_params,
    left_first,
    left_second,
    new_params,
    new_first,
    new_second,
    held_params,
    held_first,
    held_second,
    sems,
):
    del left_params, left_first, left_second
    copies = []
    for lanes, there, value in half_step(
        1, (params, first, second), (kept, come, far, near), inverse, (held_first, held_second)
    ):
        held_params[lanes, :] = scale[there, :] * value + mix[lanes, :]
        for source, target in ((held_first, new_first), (held_second, new_second), (held_params, new_params)):
            send(copies, sems, source.at[lanes], target.at[0, there])
    for copy in copies:
        copy.wait()


def hop(value, axis, devices, bit):
    return lax.ppermute(value, axis, [(d, d ^ bit) for d in range(devices)])


def doubling_sum(value, axis, devices):
    bit = devices // 2
    while bit:
        value = value + hop(value, axis, devices, bit)
        bit //= 2
    return value


def fast_body(mesh):
    workers, devices = mesh.shape["worker"], mesh.shape["fsdp"]

    def body(
        params, first, second, global_fragment, outer_momentum, features, cotangent, token_counts, fragment_index
    ):
        rows, width = params.shape[1:]
        pieces, tokens = global_fragment.shape[0], features.shape[1]
        block = functools.partial(jax.ShapeDtypeStruct, dtype=jnp.float32)

        def cost(count):
            return pl.CostEstimate(
                flops=2 * count * tokens * rows * width,
                bytes_accessed=count * rows * (2 * tokens + 4 * width),
                transcendentals=0,
            )

        room = pltpu.CompilerParams(vmem_limit_bytes=ROOM)
        free = pl.CostEstimate(flops=0, bytes_accessed=0, transcendentals=0)
        far_fragment = fragment_index
        far_counts, far_features, far_cotangent, far_params, far_global, far_momentum = (
            pltpu.with_memory_space_constraint(array, pltpu.HBM)
            for array in (
                token_counts,
                features,
                cotangent,
                params,
                global_fragment,
                outer_momentum,
            )
        )
        held_counts = pltpu.SMEM(token_counts.shape, token_counts.dtype)
        held_fragment = pltpu.SMEM(fragment_index.shape, fragment_index.dtype)
        held_piece = pltpu.VMEM(global_fragment.shape, global_fragment.dtype)

        half = rows // 2
        away_far, kept_far, masked = pl.pallas_call(
            functools.partial(first_kernel, (7, 6)),
            out_shape=[block((1, width, half))] * 2 + [jax.ShapeDtypeStruct((tokens, width), jnp.bfloat16)],
            in_specs=[HBM] * 3,
            out_specs=[VMEM] * 3,
            scratch_shapes=[
                held_counts,
                pltpu.VMEM(cotangent.shape, cotangent.dtype),
                pltpu.VMEM((2, tokens, half), features.dtype),
                pltpu.SemaphoreType.DMA((4,)),
            ],
            compiler_params=room,
            cost_estimate=cost(1),
            name="far_products",
        )(far_counts, far_cotangent, far_features)
        away_mid, kept_mid, away, kept = pl.pallas_call(
            rest_kernel,
            out_shape=[block((5, width, half))] * 2 + [block((2, width, half))] * 2,
            in_specs=[VMEM] * 2,
            out_specs=[VMEM] * 4,
            compiler_params=room,
            cost_estimate=free,
            name="rest_products",
        )(masked, features)

        def add(*terms, name, count=1):
            picks = [pick for _, pick in terms]
            return pl.pallas_call(
                functools.partial(add_kernel, picks),
                out_shape=block((count, width, half)),
                in_specs=[ANY if pick is None else VMEM for pick in picks],
                out_specs=VMEM,
                compiler_params=room,
                cost_estimate=free,
                name=name,
            )(*(array for array, _ in terms))

        def part(number, count=1):
            return slice(number, number + count)

        state, piece = block(params.shape), block(global_fragment.shape)
        come_far = hop(away_far, "fsdp", devices, 1)
        sent = add((kept_far, part(0)), (come_far, part(0)), (far_fragment, None), name="add_a1")
        far_left = hop(sent, "fsdp", devices, 2)
        away_mid, _ = lax.optimization_barrier((away_mid, sent))
        come_mid = hop(away_mid, "fsdp", devices, 1)
        drift, scale, inverse, share = pl.pallas_call(
            functools.partial(drift_kernel, workers),
            out_shape=[piece, block((rows, width)), block((8, width)), block((8, width))],
            in_specs=[HBM] * 4 + [ANY],
            out_specs=[VMEM] * 4,
            scratch_shapes=[
                held_counts,
                held_fragment,
                pltpu.VMEM(params.shape, params.dtype),
                held_piece,
                pltpu.SemaphoreType.DMA((4,)),
            ],
            compiler_params=room,
            cost_estimate=free,
            name="drift",
        )(far_counts, far_fragment, far_params, far_global, sent)
        sent = add((kept_mid, part(0)), (come_mid, part(0)), (drift, None), name="add_a2")
        far_right = hop(sent, "fsdp", devices, 2)
        near = add((kept_mid, part(3, 2)), (come_mid, part(3, 2)), (sent, None), name="add_n", count=2)
        near = hop(near, "fsdp", devices, 2)
        away, _ = lax.optimization_barrier((away, sent))
        come = hop(away, "fsdp", devices, 1)
        passed = add((kept_mid, part(1)), (come_mid, part(1)), (far_left, part(0)), name="add_c1")
        far_left = hop(passed, "fsdp", devices, 4)
        far_right = add((kept_mid, part(2)), (come_mid, part(2)), (far_right, part(0)), (passed, None), name="add_c2")
        drift, _ = lax.optimization_barrier((drift, sent))
        bit = workers // 2
        drifts = (drift, hop(drift, "worker", workers, bit))
        while bit > 1:
            bit //= 2
            drift = drifts[0] + drifts[1]
            drift, _ = lax.optimization_barrier((drift, far_right))
            drifts = (drift, hop(drift, "worker", workers, bit))
        far_right = hop(far_right, "fsdp", devices, 4)
        groups = half // LANES
        held_half = pltpu.VMEM((half, width), jnp.float32)
        mix, *results, new_global, new_momentum = pl.pallas_call(
            left_kernel,
            out_shape=[block((half, width)), state, state, state, piece, piece],
            in_specs=[VMEM] * 14,
            out_specs=[VMEM] + [HBM] * 5,
            scratch_shapes=[held_half] * 3
            + [held_piece] * 2
            + [pltpu.VMEM((rows, width), jnp.float32), pltpu.SemaphoreType.DMA((2 + 3 * groups,))],
            compiler_params=room,
            cost_estimate=pl.CostEstimate(
                flops=30 * half * width, bytes_accessed=40 * half * width, transcendentals=2 * half * width
            ),
            name="left_step",
        )(
            params,
            first,
            second,
            kept,
            come,
            far_left,
            near,
            inverse,
            scale,
            share,
            global_fragment,
            outer_momentum,
            *drifts,
        )
        new_params, new_first, new_second = pl.pallas_call(
            right_kernel,
            out_shape=[state] * 3,
            in_specs=[VMEM] * 10 + [HBM] * 3,
            out_specs=[HBM] * 3,
            input_output_aliases={10: 0, 11: 1, 12: 2},
            scratch_shapes=[held_half] * 3 + [pltpu.SemaphoreType.DMA((3 * groups,))],
            compiler_params=room,
            cost_estimate=free,
            name="right_step",
        )(params, first, second, kept, come, far_right, near, inverse, scale, mix, *results)
        return new_params, new_first, new_second, new_global, new_momentum

    return body


def plain_body(mesh):
    workers, devices = mesh.shape["worker"], mesh.shape["fsdp"]

    def body(
        params, first, second, global_fragment, outer_momentum, features, cotangent, token_counts, fragment_index
    ):
        rows, width = params.shape[1:]
        tokens = features.shape[1]
        me = lax.axis_index("fsdp")
        count = lax.dynamic_index_in_dim(token_counts, lax.axis_index("worker"), 0, keepdims=False)
        live = count.astype(jnp.float32)
        valid = (me * tokens + lax.iota(jnp.int32, tokens) < count)[:, None]
        masked = jnp.where(valid, cotangent[0], jnp.zeros_like(cotangent[0]))
        term = lax.dot_general(features[0], masked, (((0,), (0,)), ((), ())), preferred_element_type=jnp.float32)
        blocks = jnp.take(term.reshape(devices, rows, width), me ^ jnp.arange(devices, dtype=jnp.int32), axis=0)
        bit = 1
        while bit < devices:
            blocks = blocks.reshape(-1, 2, rows, width)
            blocks = blocks[:, 0] + hop(blocks[:, 1], "fsdp", devices, bit)
            bit *= 2
        gradient = blocks[0] / live
        grouped = (rows // FRAGS, FRAGS, width)
        old = lax.dynamic_index_in_dim(params[0].reshape(grouped), fragment_index[0], 1, keepdims=False)
        drift_sum = doubling_sum(live * (global_fragment - old), "worker", workers)
        total = jnp.sum(token_counts).astype(jnp.float32)
        fresh, momentum = outer(drift_sum / total, global_fragment, outer_momentum)
        inner, first_new, second_new = adam(params[0], first[0], second[0], gradient)
        inner = inner.reshape(grouped)
        piece = lax.dynamic_index_in_dim(inner, fragment_index[0], 1, keepdims=False)
        mixed = MIXING * fresh + (1.0 - MIXING) * piece
        merged = lax.dynamic_update_index_in_dim(inner, mixed, fragment_index[0], 1).reshape(rows, width)
        return merged[None], first_new[None], second_new[None], fresh, momentum

    return body


def solution(mesh):
    devices = mesh.shape["fsdp"]

    def pick(*arrays):
        rows = arrays[0].shape[1]
        body = fast_body(mesh) if devices == 8 and rows % LANES == 0 else plain_body(mesh)
        return body(*arrays)

    state = P("worker", "fsdp", None)
    piece = P("fsdp", None)
    return jax.shard_map(
        pick,
        mesh=mesh,
        in_specs=(state, state, state, piece, piece, state, state, P(), P()),
        out_specs=(state, state, state, piece, piece),
        check_vma=False,
    )
```

time: 27.3 us -> 31.6 us (1.16)
  waiting for transfers between devices: 3.78 us -> 11.6 us
  starting transfers between devices: 15.3 us -> 13.4 us
  Pallas kernels: 6.53 us -> 5 us
    ppermute x11 -> x10, waiting for transfers between devices: 3.78 us -> 11.6 us  [hop(): return lax.ppermute(value, axis, [(d, d ^ bit) for d in range(devices)])]
    ppermute x11 -> x10, starting transfers between devices: 15.3 us -> 13.4 us  [hop(): return lax.ppermute(value, axis, [(d, d ^ bit) for d in range(devices)])]
    pallas_call x12 -> x10, Pallas kernels: 6.53 us -> 5 us  [the longest x1 1.39 us: body(): pl.pallas_call(functools.partial(first_kernel, (7, 6)), out_shape=[block(...]
  transfers between devices with their start and end apart: 11 -> 10, of which waited for: 3 -> 3; matrix products, arithmetic and copies ran while one was open for 0% -> 0% of each run, Pallas kernels for 15% -> 8%
where the time goes in v5:
time: 31.6 us; the launch traced here: 31.4 us
  starting transfers between devices  13.4 us (42%)
  waiting for transfers between devices  11.6 us (37%)
  Pallas kernels  5 us (16%)
  between operations  1.44 us (5%)
    ppermute x10, starting transfers between devices, hop(): return lax.ppermute(value, axis, [(d, d ^ bit) for d in range(devices)])  13.4 us
    ppermute x10, waiting for transfers between devices, hop(): return lax.ppermute(value, axis, [(d, d ^ bit) for d in range(devices)])  11.6 us
    pallas_call x1, Pallas kernels, body(): pl.pallas_call(functools.partial(first_kernel, (7, 6)), out_shape=[block(...  1.39 us
    pallas_call x1, Pallas kernels, body(): pl.pallas_call(left_kernel, out_shape=[block((half, width)), state, state...  1.08 us
    pallas_call x1, Pallas kernels, body(): pl.pallas_call(functools.partial(drift_kernel, workers), out_shape=[piece...  1.03 us
    pallas_call x1, Pallas kernels, body(): pl.pallas_call(right_kernel, out_shape=[state] * 3, in_specs=[VMEM] * 10...  0.97 us
  transfers between devices with their start and end apart: 10, of which 3 were waited for; matrix products, arithmetic and copies ran while one was open for 0% of the time, Pallas kernels for 8%

profile of v5, /device:TPU:0, one launch (start us, length us, event | category | flops | bytes accessed | tf_op | source)
XLA Modules:
  0.0 31.4 jit_solution(8604120526588646932)
XLA Ops:
  0.6 0.0 copy-start
  0.6 1.4 %far_products.1 = (f32[1,128,256]{2,1,0:T(8,128)S(1)}, f32[1,128,256]{2,1,0:T(8,128)S(1)}, bf16[128,128]{1,0:T(8,128)(2,1)S(1)}) custom-call(s32[4]{0:T(128)} %counts.3, bf16[1,128,128]{2,1,0:T(8,128)(2,1)} %cotangent.1, bf16[1,128,4096]{2,1,0:T(8,128)(2,1)} %features.3), custom_call_target="tpu_custom_call" | custom-call | flops 16777216 | bytes 393216 | tf_op jit(solution)/shard_map/far_products/pallas_call | solution.py:268
  2.0 0.5 %collective-permute-start = (f32[1,128,256]{2,1,0:T(8,128)S(1)}, f32[1,128,256]{2,1,0:T(8,128)S(1)}, u32[]{:S(2)}, u32[]{:S(2)}) collective-permute-start(f32[1,128,256]{2,1,0:T(8,128)S(1)} %get-tuple-element.35), channel_id=1, source_target_pairs={{0,1},{1,0},{2,3},{3,2},{4,5},{5,4},{6,7},{7,6},{8,9},{9,8},{10,11... | collective-permute-start | bytes 393224 | tf_op jit(solution)/shard_map/ppermute | solution.py:221
  3.2 0.0 copy-done
  3.2 0.4 %rest_products.1 = (f32[5,128,256]{2,1,0:T(8,128)S(1)}, f32[5,128,256]{2,1,0:T(8,128)S(1)}, f32[2,128,256]{2,1,0:T(8,128)S(1)}, f32[2,128,256]{2,1,0:T(8,128)S(1)}) custom-call(bf16[128,128]{1,0:T(8,128)(2,1)S(1)} %get-tuple-element.29.masked, bf16[1,128,4096]{2,1,0:T(8,128)(2,1)S(1)} %copy-done), custom_call_target="tpu_custom_call" | custom-call | tf_op jit(solution)/shard_map/rest_products/pallas_call | solution.py:283
  3.6 0.0 collective-permute-done.refs_1_
  3.7 0.3 collective-permute-start.1
  4.0 2.8 %collective-permute-start.4 = (f32[1,128,256]{2,1,0:T(8,128)S(1)}, f32[1,128,256]{2,1,0:T(8,128)S(1)}, u32[]{:S(2)}, u32[]{:S(2)}) collective-permute-start(f32[1,128,256]{2,1,0:T(8,128)S(1)} %add_a1.1.after), channel_id=1, source_target_pairs={{0,2},{1,3},{2,0},{3,1},{4,6},{5,7},{6,4},{7,5},{8,10},{9,11},{10,... | collective-permute-start | bytes 393224 | tf_op jit(solution)/shard_map/ppermute | solution.py:221
  6.8 1.0 %drift.1 = (f32[128,128]{1,0:T(8,128)S(1)}, f32[512,128]{1,0:T(8,128)S(1)}, f32[8,128]{1,0:T(8,128)S(1)}, f32[8,128]{1,0:T(8,128)S(1)}) custom-call(s32[4]{0:T(128)} %counts.3, s32[1]{0:T(128)S(6)} %copy.20.refs_2_.fragment, f32[1,512,128]{2,1,0:T(8,128)} %params.5, f32[128,128]{1,0:T(8,128)} %global_fragment.3, f32[1,128,256]{2,1,0:T(8,128)S(1)} %add_a1.1.after), custom_call_target="tpu_custom_call" | custom-call | tf_op jit(solution)/shard_map/drift/pallas_call | solution.py:314
  7.9 0.0 collective-permute-done.1.refs_1_
  7.9 0.8 %collective-permute-start.6 = (f32[2,128,256]{2,1,0:T(8,128)S(1)}, f32[2,128,256]{2,1,0:T(8,128)S(1)}, u32[]{:S(2)}, u32[]{:S(2)}) collective-permute-start(f32[2,128,256]{2,1,0:T(8,128)S(1)} %add_n.1), channel_id=1, source_target_pairs={{0,2},{1,3},{2,0},{3,1},{4,6},{5,7},{6,4},{7,5},{8,10},{9,11},{10,... | collective-permute-start | bytes 786440 | tf_op jit(solution)/shard_map/ppermute | solution.py:221
  8.8 0.0 collective-permute-start.2
  8.8 1.2 %collective-permute-start.3 = (f32[1,128,256]{2,1,0:T(8,128)S(1)}, f32[1,128,256]{2,1,0:T(8,128)S(1)}, u32[]{:S(2)}, u32[]{:S(2)}) collective-permute-start(f32[1,128,256]{2,1,0:T(8,128)S(1)} %add_a2.1.refs_2_), channel_id=1, source_target_pairs={{0,2},{1,3},{2,0},{3,1},{4,6},{5,7},{6,4},{7,5},{8,10},{9,11},{10,... | collective-permute-start | bytes 393224 | tf_op jit(solution)/shard_map/ppermute | solution.py:221
  10.0 1.5 %collective-permute-start.8 = (f32[128,128]{1,0:T(8,128)S(1)}, f32[128,128]{1,0:T(8,128)S(1)}, u32[]{:S(2)}, u32[]{:S(2)}) collective-permute-start(f32[128,128]{1,0:T(8,128)S(1)} %get-tuple-element.42.refs_2_), channel_id=1, source_target_pairs={{0,16},{8,24},{16,0},{24,8},{1,17},{9,25},{17,1},{25,9},{2,18},{10... | collective-permute-start | bytes 196616 | tf_op jit(solution)/shard_map/ppermute | solution.py:221
  11.6 0.0 collective-permute-done.4.refs_2_
  11.6 2.7 %collective-permute-start.7 = (f32[1,128,256]{2,1,0:T(8,128)S(1)}, f32[1,128,256]{2,1,0:T(8,128)S(1)}, u32[]{:S(2)}, u32[]{:S(2)}) collective-permute-start(f32[1,128,256]{2,1,0:T(8,128)S(1)} %add_c1.1.refs_3_), channel_id=1, source_target_pairs={{0,4},{1,5},{2,6},{3,7},{4,0},{5,1},{6,2},{7,3},{8,12},{9,13},{10,... | collective-permute-start | bytes 393224 | tf_op jit(solution)/shard_map/ppermute | solution.py:221
  14.2 7.7 %collective-permute-done.3.refs_2_ = f32[1,128,256]{2,1,0:T(8,128)S(1)} collective-permute-done((f32[1,128,256]{2,1,0:T(8,128)S(1)}, f32[1,128,256]{2,1,0:T(8,128)S(1)}, u32[]{:S(2)}, u32[]{:S(2)}) %collective-permute-start.3) | collective-permute-done | bytes 131104 | tf_op jit(solution)/shard_map/ppermute | solution.py:221
  22.0 0.0 copy-start.4
  22.0 0.0 copy-start.5
  22.0 1.9 %collective-permute-start.5 = (f32[1,128,256]{2,1,0:T(8,128)S(1)}, f32[1,128,256]{2,1,0:T(8,128)S(1)}, u32[]{:S(2)}, u32[]{:S(2)}) collective-permute-start(f32[1,128,256]{2,1,0:T(8,128)S(1)} %add_c2.1), channel_id=1, source_target_pairs={{0,4},{1,5},{2,6},{3,7},{4,0},{5,1},{6,2},{7,3},{8,12},{9,13},{10,... | collective-permute-start | bytes 393224 | tf_op jit(solution)/shard_map/ppermute | solution.py:221
  23.9 0.0 collective-permute-done.8
  23.9 1.6 %collective-permute-start.9 = (f32[128,128]{1,0:T(8,128)S(1)}, f32[128,128]{1,0:T(8,128)S(1)}, u32[]{:S(2)}, u32[]{:S(2)}) collective-permute-start(f32[128,128]{1,0:T(8,128)S(1)} %add.3.drift), channel_id=1, source_target_pairs={{0,8},{8,0},{16,24},{24,16},{1,9},{9,1},{17,25},{25,17},{2,10},{10... | collective-permute-start | bytes 196616 | tf_op jit(solution)/shard_map/ppermute | solution.py:221
  25.5 0.0 collective-permute-done.7.far
  25.5 2.8 %collective-permute-done.9.other_drift = f32[128,128]{1,0:T(8,128)S(1)} collective-permute-done((f32[128,128]{1,0:T(8,128)S(1)}, f32[128,128]{1,0:T(8,128)S(1)}, u32[]{:S(2)}, u32[]{:S(2)}) %collective-permute-start.9) | collective-permute-done | bytes 65568 | tf_op jit(solution)/shard_map/ppermute | solution.py:221
  28.3 0.0 collective-permute-done.6.near
  28.3 0.0 collective-permute-done.2.come
  28.3 0.0 copy-done.1
  28.3 0.0 copy-done.2
  28.3 0.0 copy-done.3
  28.3 1.1 %left_step.1 = (f32[256,128]{1,0:T(8,128)S(1)}, f32[1,512,128]{2,1,0:T(8,128)}, f32[1,512,128]{2,1,0:T(8,128)}, f32[1,512,128]{2,1,0:T(8,128)}, f32[128,128]{1,0:T(8,128)}, /*index=5*/f32[128,128]{1,0:T(8,128)}) custom-call(f32[1,512,128]{2,1,0:T(8,128)S(1)} %copy-done.1, f32[1,512,128]{2,1,0:T(8,128)S(1)} %copy-done.2, f32[1,512,128]{2,1,0:T(8,128)S(1)} %copy-done.3, ...), custom_call_target="tpu_custom_call" | custom-call | flops 983040 | bytes 1310720 | tf_op jit(solution)/shard_map/left_step/pallas_call | solution.py:350
  29.4 1.1 %collective-permute-done.5.far = f32[1,128,256]{2,1,0:T(8,128)S(1)} collective-permute-done((f32[1,128,256]{2,1,0:T(8,128)S(1)}, f32[1,128,256]{2,1,0:T(8,128)S(1)}, u32[]{:S(2)}, u32[]{:S(2)}) %collective-permute-start.5) | collective-permute-done | bytes 131104 | tf_op jit(solution)/shard_map/ppermute | solution.py:221
  30.5 1.0 %right_step.1 = (f32[1,512,128]{2,1,0:T(8,128)}, f32[1,512,128]{2,1,0:T(8,128)}, f32[1,512,128]{2,1,0:T(8,128)}) custom-call(f32[1,512,128]{2,1,0:T(8,128)S(1)} %copy-done.1, f32[1,512,128]{2,1,0:T(8,128)S(1)} %copy-done.2, f32[1,512,128]{2,1,0:T(8,128)S(1)} %copy-done.3, ...), custom_call_target="tpu_custom_call", output_to_operand_aliasing={{0}: (10, {}), {1}: (11, {}), {2}: (12, {})} | custom-call | tf_op jit(solution)/shard_map/right_step/pallas_call | solution.py:378
  (11 shorter events, 0.1 us)
Async XLA Ops:
  0.6 2.6 %copy-start = (bf16[1,128,4096]{2,1,0:T(8,128)(2,1)S(1)}, bf16[1,128,4096]{2,1,0:T(8,128)(2,1)}, u32[]{:S(2)}) copy-start(bf16[1,128,4096]{2,1,0:T(8,128)(2,1)} %features.3) | copy-start | bytes 3145732
  2.0 1.6 %collective-permute-start = (f32[1,128,256]{2,1,0:T(8,128)S(1)}, f32[1,128,256]{2,1,0:T(8,128)S(1)}, u32[]{:S(2)}, u32[]{:S(2)}) collective-permute-start(f32[1,128,256]{2,1,0:T(8,128)S(1)} %get-tuple-element.35), channel_id=1, source_target_pairs={{0,1},{1,0},{2,3},{3,2},{4,5},{5,4},{6,7},{7,6},{8,9},{9,8},{10,11... | collective-permute-start | bytes 393224 | tf_op jit(solution)/shard_map/ppermute | solution.py:221
  3.7 4.2 %collective-permute-start.1 = (f32[5,128,256]{2,1,0:T(8,128)S(1)}, f32[5,128,256]{2,1,0:T(8,128)S(1)}, u32[]{:S(2)}, u32[]{:S(2)}) collective-permute-start(f32[5,128,256]{2,1,0:T(8,128)S(1)} %get-tuple-element.36), channel_id=1, source_target_pairs={{0,1},{1,0},{2,3},{3,2},{4,5},{5,4},{6,7},{7,6},{8,9},{9,8},{10,11... | collective-permute-start | bytes 1966088 | tf_op jit(solution)/shard_map/ppermute | solution.py:221
  4.0 7.6 %collective-permute-start.4 = (f32[1,128,256]{2,1,0:T(8,128)S(1)}, f32[1,128,256]{2,1,0:T(8,128)S(1)}, u32[]{:S(2)}, u32[]{:S(2)}) collective-permute-start(f32[1,128,256]{2,1,0:T(8,128)S(1)} %add_a1.1.after), channel_id=1, source_target_pairs={{0,2},{1,3},{2,0},{3,1},{4,6},{5,7},{6,4},{7,5},{8,10},{9,11},{10,... | collective-permute-start | bytes 393224 | tf_op jit(solution)/shard_map/ppermute | solution.py:221
  7.9 20.4 %collective-permute-start.6 = (f32[2,128,256]{2,1,0:T(8,128)S(1)}, f32[2,128,256]{2,1,0:T(8,128)S(1)}, u32[]{:S(2)}, u32[]{:S(2)}) collective-permute-start(f32[2,128,256]{2,1,0:T(8,128)S(1)} %add_n.1), channel_id=1, source_target_pairs={{0,2},{1,3},{2,0},{3,1},{4,6},{5,7},{6,4},{7,5},{8,10},{9,11},{10,... | collective-permute-start | bytes 786440 | tf_op jit(solution)/shard_map/ppermute | solution.py:221
  8.8 19.5 %collective-permute-start.2 = (f32[2,128,256]{2,1,0:T(8,128)S(1)}, f32[2,128,256]{2,1,0:T(8,128)S(1)}, u32[]{:S(2)}, u32[]{:S(2)}) collective-permute-start(f32[2,128,256]{2,1,0:T(8,128)S(1)} %get-tuple-element.38), channel_id=1, source_target_pairs={{0,1},{1,0},{2,3},{3,2},{4,5},{5,4},{6,7},{7,6},{8,9},{9,8},{10,11... | collective-permute-start | bytes 786440 | tf_op jit(solution)/shard_map/ppermute | solution.py:221
  8.8 13.2 %collective-permute-start.3 = (f32[1,128,256]{2,1,0:T(8,128)S(1)}, f32[1,128,256]{2,1,0:T(8,128)S(1)}, u32[]{:S(2)}, u32[]{:S(2)}) collective-permute-start(f32[1,128,256]{2,1,0:T(8,128)S(1)} %add_a2.1.refs_2_), channel_id=1, source_target_pairs={{0,2},{1,3},{2,0},{3,1},{4,6},{5,7},{6,4},{7,5},{8,10},{9,11},{10,... | collective-permute-start | bytes 393224 | tf_op jit(solution)/shard_map/ppermute | solution.py:221
  10.0 13.9 %collective-permute-start.8 = (f32[128,128]{1,0:T(8,128)S(1)}, f32[128,128]{1,0:T(8,128)S(1)}, u32[]{:S(2)}, u32[]{:S(2)}) collective-permute-start(f32[128,128]{1,0:T(8,128)S(1)} %get-tuple-element.42.refs_2_), channel_id=1, source_target_pairs={{0,16},{8,24},{16,0},{24,8},{1,17},{9,25},{17,1},{25,9},{2,18},{10... | collective-permute-start | bytes 196616 | tf_op jit(solution)/shard_map/ppermute | solution.py:221
  11.6 13.9 %collective-permute-start.7 = (f32[1,128,256]{2,1,0:T(8,128)S(1)}, f32[1,128,256]{2,1,0:T(8,128)S(1)}, u32[]{:S(2)}, u32[]{:S(2)}) collective-permute-start(f32[1,128,256]{2,1,0:T(8,128)S(1)} %add_c1.1.refs_3_), channel_id=1, source_target_pairs={{0,4},{1,5},{2,6},{3,7},{4,0},{5,1},{6,2},{7,3},{8,12},{9,13},{10,... | collective-permute-start | bytes 393224 | tf_op jit(solution)/shard_map/ppermute | solution.py:221
  22.0 6.3 %copy-start.1 = (f32[1,512,128]{2,1,0:T(8,128)S(1)}, f32[1,512,128]{2,1,0:T(8,128)}, u32[]{:S(2)}) copy-start(f32[1,512,128]{2,1,0:T(8,128)} %params.5) | copy-start | bytes 786436
  22.0 6.3 %copy-start.2 = (f32[1,512,128]{2,1,0:T(8,128)S(1)}, f32[1,512,128]{2,1,0:T(8,128)}, u32[]{:S(2)}) copy-start(f32[1,512,128]{2,1,0:T(8,128)} %first.3) | copy-start | bytes 786436
  22.0 6.3 %copy-start.3 = (f32[1,512,128]{2,1,0:T(8,128)S(1)}, f32[1,512,128]{2,1,0:T(8,128)}, u32[]{:S(2)}) copy-start(f32[1,512,128]{2,1,0:T(8,128)} %second.3) | copy-start | bytes 786436
  22.0 6.3 %copy-start.4 = (f32[128,128]{1,0:T(8,128)S(1)}, f32[128,128]{1,0:T(8,128)}, u32[]{:S(2)}) copy-start(f32[128,128]{1,0:T(8,128)} %global_fragment.3) | copy-start | bytes 196612
  22.0 6.3 %copy-start.5 = (f32[128,128]{1,0:T(8,128)S(1)}, f32[128,128]{1,0:T(8,128)}, u32[]{:S(2)}) copy-start(f32[128,128]{1,0:T(8,128)} %outer_momentum.1) | copy-start | bytes 196612
  22.0 8.5 %collective-permute-start.5 = (f32[1,128,256]{2,1,0:T(8,128)S(1)}, f32[1,128,256]{2,1,0:T(8,128)S(1)}, u32[]{:S(2)}, u32[]{:S(2)}) collective-permute-start(f32[1,128,256]{2,1,0:T(8,128)S(1)} %add_c2.1), channel_id=1, source_target_pairs={{0,4},{1,5},{2,6},{3,7},{4,0},{5,1},{6,2},{7,3},{8,12},{9,13},{10,... | collective-permute-start | bytes 393224 | tf_op jit(solution)/shard_map/ppermute | solution.py:221
  23.9 4.3 %collective-permute-start.9 = (f32[128,128]{1,0:T(8,128)S(1)}, f32[128,128]{1,0:T(8,128)S(1)}, u32[]{:S(2)}, u32[]{:S(2)}) collective-permute-start(f32[128,128]{1,0:T(8,128)S(1)} %add.3.drift), channel_id=1, source_target_pairs={{0,8},{8,0},{16,24},{24,16},{1,9},{9,1},{17,25},{25,17},{2,10},{10... | collective-permute-start | bytes 196616 | tf_op jit(solution)/shard_map/ppermute | solution.py:221

commit v6 on v5

--- a/solution.py
+++ b/solution.py
@@ -52,9 +52,9 @@
 
 
 def first_kernel(order, counts, cotangent, features, away, kept, masked, counts_held, cot_held, held, sems):
-    half = held.shape[2]
+    half = away.shape[2]
     small = fetch((counts, cotangent), (counts_held, cot_held), sems)
-    columns = [columns_of(q, 2 * half, 0, half) for q in order]
+    columns = [columns_of(q, 2 * half, 0, 2 * half) for q in order]
     blocks = fetch([features.at[0, :, c] for c in columns], [held.at[n] for n in range(len(order))], sems, len(small))
     for copy in small:
         copy.wait()
@@ -63,15 +63,17 @@
     masked[...] = masked_rows(live, cot_held[0])
     for slot, into in enumerate((away, kept)):
         blocks[slot].wait()
-        into[0] = product(masked[...], held[slot])
-
-
-def rest_kernel(masked, features, away_mid, kept_mid, away, kept):
-    half = kept.shape[2]
-    places = [(6, 1, 0), (4, 0, 1), (4, 1, 2), (2, 0, 3), (2, 1, 4), (0, 0, 0), (0, 1, 1)]
-    for q, side, at in places:
-        for core, into in ((1, away_mid if q else away), (0, kept_mid if q else kept)):
-            into[at] = product(masked[...], features[0, :, columns_of(q + core, 2 * half, side * half, half)])
+        for side in (0, 1):
+            into[side] = product(masked[...], held[slot, :, side * half : (side + 1) * half])
+
+
+def rest_kernel(masked, features, *targets):
+    half = targets[0].shape[2]
+    places = [(4, 0, 0, 0), (4, 1, 0, 1), (2, 0, 2, 2), (2, 1, 2, 3), (0, 0, 2, 0), (0, 1, 2, 1)]
+    for q, side, into, at in places:
+        for core in (1, 0):
+            columns = columns_of(q + core, 2 * half, side * half, half)
+            targets[into + 1 - core][at] = product(masked[...], features[0, :, columns])
 
 
 def drift_kernel(
@@ -122,7 +124,7 @@
     rows = kept.shape[2]
     for lane in range(0, rows, LANES):
         lanes, there = pl.ds(lane, LANES), pl.ds(half * rows + lane, LANES)
-        summed = kept[half, :, lanes] + come[half, :, lanes] + near[half, :, lanes] + far[0, :, lanes]
+        summed = kept[half, :, lanes] + come[half, :, lanes] + near[0, :, lanes] + far[0, :, lanes]
         inner, held_first[lanes, :], held_second[lanes, :] = adam(
             params[0, there, :], first[0, there, :], second[0, there, :], summed.T * inverse[0:1, :]
         )
@@ -267,22 +269,22 @@
         half = rows // 2
         away_far, kept_far, masked = pl.pallas_call(
             functools.partial(first_kernel, (7, 6)),
-            out_shape=[block((1, width, half))] * 2 + [jax.ShapeDtypeStruct((tokens, width), jnp.bfloat16)],
+            out_shape=[block((2, width, half))] * 2 + [jax.ShapeDtypeStruct((tokens, width), jnp.bfloat16)],
             in_specs=[HBM] * 3,
             out_specs=[VMEM] * 3,
             scratch_shapes=[
                 held_counts,
                 pltpu.VMEM(cotangent.shape, cotangent.dtype),
-                pltpu.VMEM((2, tokens, half), features.dtype),
+                pltpu.VMEM((2, tokens, rows), features.dtype),
                 pltpu.SemaphoreType.DMA((4,)),
             ],
             compiler_params=room,
-            cost_estimate=cost(1),
+            cost_estimate=cost(2),
             name="far_products",
         )(far_counts, far_cotangent, far_features)
-        away_mid, kept_mid, away, kept = pl.pallas_call(
+        away_pass, kept_pass, away, kept = pl.pallas_call(
             rest_kernel,
-            out_shape=[block((5, width, half))] * 2 + [block((2, width, half))] * 2,
+            out_shape=[block((2, width, half))] * 2 + [block((4, width, half))] * 2,
             in_specs=[VMEM] * 2,
             out_specs=[VMEM] * 4,
             compiler_params=room,
@@ -309,8 +311,9 @@
         come_far = hop(away_far, "fsdp", devices, 1)
         sent = add((kept_far, part(0)), (come_far, part(0)), (far_fragment, None), name="add_a1")
         far_left = hop(sent, "fsdp", devices, 2)
-        away_mid, _ = lax.optimization_barrier((away_mid, sent))
-        come_mid = hop(away_mid, "fsdp", devices, 1)
+        away_pass, away, _ = lax.optimization_barrier((away_pass, away, sent))
+        come_pass = hop(away_pass, "fsdp", devices, 1)
+        come = hop(away, "fsdp", devices, 1)
         drift, scale, inverse, share = pl.pallas_call(
             functools.partial(drift_kernel, workers),
             out_shape=[piece, block((rows, width)), block((8, width)), block((8, width))],
@@ -327,24 +330,24 @@
             cost_estimate=free,
             name="drift",
         )(far_counts, far_fragment, far_params, far_global, sent)
-        sent = add((kept_mid, part(0)), (come_mid, part(0)), (drift, None), name="add_a2")
+        sent = add((kept_far, part(1)), (come_far, part(1)), (drift, None), name="add_a2")
         far_right = hop(sent, "fsdp", devices, 2)
-        near = add((kept_mid, part(3, 2)), (come_mid, part(3, 2)), (sent, None), name="add_n", count=2)
-        near = hop(near, "fsdp", devices, 2)
-        away, _ = lax.optimization_barrier((away, sent))
-        come = hop(away, "fsdp", devices, 1)
-        passed = add((kept_mid, part(1)), (come_mid, part(1)), (far_left, part(0)), name="add_c1")
+        passed = add((kept_pass, part(0)), (come_pass, part(0)), (far_left, part(0)), name="add_c1")
         far_left = hop(passed, "fsdp", devices, 4)
-        far_right = add((kept_mid, part(2)), (come_mid, part(2)), (far_right, part(0)), (passed, None), name="add_c2")
+        near_left = add((kept, part(2)), (come, part(2)), (passed, None), name="add_n1")
+        far_right = add((kept_pass, part(1)), (come_pass, part(1)), (far_right, part(0)), (passed, None), name="add_c2")
+        near_right = add((kept, part(3)), (come, part(3)), (far_right, None), name="add_n2")
         drift, _ = lax.optimization_barrier((drift, sent))
         bit = workers // 2
         drifts = (drift, hop(drift, "worker", workers, bit))
         while bit > 1:
             bit //= 2
             drift = drifts[0] + drifts[1]
-            drift, _ = lax.optimization_barrier((drift, far_right))
+            drift, _ = lax.optimization_barrier((drift, near_right))
             drifts = (drift, hop(drift, "worker", workers, bit))
+        near_left = hop(near_left, "fsdp", devices, 2)
         far_right = hop(far_right, "fsdp", devices, 4)
+        near_right = hop(near_right, "fsdp", devices, 2)
         groups = half // LANES
         held_half = pltpu.VMEM((half, width), jnp.float32)
         mix, *results, new_global, new_momentum = pl.pallas_call(
@@ -367,7 +370,7 @@
             kept,
             come,
             far_left,
-            near,
+            near_left,
             inverse,
             scale,
             share,
@@ -385,7 +388,7 @@
             compiler_params=room,
             cost_estimate=free,
             name="right_step",
-        )(params, first, second, kept, come, far_right, near, inverse, scale, mix, *results)
+        )(params, first, second, kept, come, far_right, near_right, inverse, scale, mix, *results)
         return new_params, new_first, new_second, new_global, new_momentum
 
     return body

time: 31.6 us -> 26.9 us (0.85)
  waiting for transfers between devices: 11.6 us -> 4.86 us
  starting transfers between devices: 13.4 us -> 15.3 us
    ppermute x10 -> x11, waiting for transfers between devices: 11.6 us -> 4.86 us  [hop(): return lax.ppermute(value, axis, [(d, d ^ bit) for d in range(devices)])]
    ppermute x10 -> x11, starting transfers between devices: 13.4 us -> 15.3 us  [hop(): return lax.ppermute(value, axis, [(d, d ^ bit) for d in range(devices)])]
  transfers between devices with their start and end apart: 10 -> 11, of which waited for: 3 -> 6; matrix products, arithmetic and copies ran while one was open for 0% -> 0% of each run, Pallas kernels for 8% -> 10%
where the time goes in v6:
time: 26.9 us; the launch traced here: 26.7 us
  starting transfers between devices  15.3 us (57%)
  Pallas kernels  5.05 us (19%)
  waiting for transfers between devices  4.86 us (18%)
  between operations  1.42 us (5%)
    ppermute x11, starting transfers between devices, hop(): return lax.ppermute(value, axis, [(d, d ^ bit) for d in range(devices)])  15.3 us
    ppermute x11, waiting for transfers between devices, hop(): return lax.ppermute(value, axis, [(d, d ^ bit) for d in range(devices)])  4.86 us
    pallas_call x1, Pallas kernels, body(): pl.pallas_call(functools.partial(first_kernel, (7, 6)), out_shape=[block(...  1.47 us
    pallas_call x1, Pallas kernels, body(): pl.pallas_call(left_kernel, out_shape=[block((half, width)), state, state...  1.08 us
    pallas_call x1, Pallas kernels, body(): pl.pallas_call(functools.partial(drift_kernel, workers), out_shape=[piece...  1.03 us
    pallas_call x1, Pallas kernels, body(): pl.pallas_call(right_kernel, out_shape=[state] * 3, in_specs=[VMEM] * 10...  0.96 us
  transfers between devices with their start and end apart: 11, of which 6 were waited for; matrix products, arithmetic and copies ran while one was open for 0% of the time, Pallas kernels for 10%

profile of v6, /device:TPU:0, one launch (start us, length us, event | category | flops | bytes accessed | tf_op | source)
XLA Modules:
  0.0 26.7 jit_solution(655271989681098935)
XLA Ops:
  0.6 0.0 copy-start
  0.6 1.5 %far_products.1 = (f32[2,128,256]{2,1,0:T(8,128)S(1)}, f32[2,128,256]{2,1,0:T(8,128)S(1)}, bf16[128,128]{1,0:T(8,128)(2,1)S(1)}) custom-call(s32[4]{0:T(128)} %counts.3, bf16[1,128,128]{2,1,0:T(8,128)(2,1)} %cotangent.1, bf16[1,128,4096]{2,1,0:T(8,128)(2,1)} %features.3), custom_call_target="tpu_custom_call" | custom-call | flops 33554432 | bytes 786432 | tf_op jit(solution)/shard_map/far_products/pallas_call | solution.py:270
  2.1 0.5 %collective-permute-start = (f32[2,128,256]{2,1,0:T(8,128)S(1)}, f32[2,128,256]{2,1,0:T(8,128)S(1)}, u32[]{:S(2)}, u32[]{:S(2)}) collective-permute-start(f32[2,128,256]{2,1,0:T(8,128)S(1)} %get-tuple-element.34), channel_id=1, source_target_pairs={{0,1},{1,0},{2,3},{3,2},{4,5},{5,4},{6,7},{7,6},{8,9},{9,8},{10,11... | collective-permute-start | bytes 786440 | tf_op jit(solution)/shard_map/ppermute | solution.py:223
  3.3 0.0 copy-done
  3.3 0.4 %rest_products.1 = (f32[2,128,256]{2,1,0:T(8,128)S(1)}, f32[2,128,256]{2,1,0:T(8,128)S(1)}, f32[4,128,256]{2,1,0:T(8,128)S(1)}, f32[4,128,256]{2,1,0:T(8,128)S(1)}) custom-call(bf16[128,128]{1,0:T(8,128)(2,1)S(1)} %get-tuple-element.29.masked, bf16[1,128,4096]{2,1,0:T(8,128)(2,1)S(1)} %copy-done), custom_call_target="tpu_custom_call" | custom-call | tf_op jit(solution)/shard_map/rest_products/pallas_call | solution.py:285
  3.7 0.1 collective-permute-done.refs_1_
  3.8 0.4 %collective-permute-start.1 = (f32[4,128,256]{2,1,0:T(8,128)S(1)}, f32[4,128,256]{2,1,0:T(8,128)S(1)}, u32[]{:S(2)}, u32[]{:S(2)}) collective-permute-start(f32[4,128,256]{2,1,0:T(8,128)S(1)} %get-tuple-element.35), channel_id=1, source_target_pairs={{0,1},{1,0},{2,3},{3,2},{4,5},{5,4},{6,7},{7,6},{8,9},{9,8},{10,11... | collective-permute-start | bytes 1572872 | tf_op jit(solution)/shard_map/ppermute | solution.py:223
  4.3 0.1 collective-permute-start.2
  4.4 2.9 %collective-permute-start.4 = (f32[1,128,256]{2,1,0:T(8,128)S(1)}, f32[1,128,256]{2,1,0:T(8,128)S(1)}, u32[]{:S(2)}, u32[]{:S(2)}) collective-permute-start(f32[1,128,256]{2,1,0:T(8,128)S(1)} %add_a1.1.after), channel_id=1, source_target_pairs={{0,2},{1,3},{2,0},{3,1},{4,6},{5,7},{6,4},{7,5},{8,10},{9,11},{10,... | collective-permute-start | bytes 393224 | tf_op jit(solution)/shard_map/ppermute | solution.py:223
  7.3 1.0 %drift.1 = (f32[128,128]{1,0:T(8,128)S(1)}, f32[512,128]{1,0:T(8,128)S(1)}, f32[8,128]{1,0:T(8,128)S(1)}, f32[8,128]{1,0:T(8,128)S(1)}) custom-call(s32[4]{0:T(128)} %counts.3, s32[1]{0:T(128)S(6)} %copy.20.refs_2_.fragment, f32[1,512,128]{2,1,0:T(8,128)} %params.5, f32[128,128]{1,0:T(8,128)} %global_fragment.3, f32[1,128,256]{2,1,0:T(8,128)S(1)} %add_a1.1.after), custom_call_target="tpu_custom_call" | custom-call | tf_op jit(solution)/shard_map/drift/pallas_call | solution.py:317
  8.4 0.1 collective-permute-start.3
  8.5 2.0 %collective-permute-start.9 = (f32[128,128]{1,0:T(8,128)S(1)}, f32[128,128]{1,0:T(8,128)S(1)}, u32[]{:S(2)}, u32[]{:S(2)}) collective-permute-start(f32[128,128]{1,0:T(8,128)S(1)} %get-tuple-element.42.refs_2_), channel_id=1, source_target_pairs={{0,16},{8,24},{16,0},{24,8},{1,17},{9,25},{17,1},{25,9},{2,18},{10... | collective-permute-start | bytes 196616 | tf_op jit(solution)/shard_map/ppermute | solution.py:223
  10.4 0.9 %collective-permute-done.4.refs_2_ = f32[1,128,256]{2,1,0:T(8,128)S(1)} collective-permute-done((f32[1,128,256]{2,1,0:T(8,128)S(1)}, f32[1,128,256]{2,1,0:T(8,128)S(1)}, u32[]{:S(2)}, u32[]{:S(2)}) %collective-permute-start.4) | collective-permute-done | bytes 131104 | tf_op jit(solution)/shard_map/ppermute | solution.py:223
  11.3 0.0 collective-permute-done.2.refs_1_
  11.3 3.0 %collective-permute-start.7 = (f32[1,128,256]{2,1,0:T(8,128)S(1)}, f32[1,128,256]{2,1,0:T(8,128)S(1)}, u32[]{:S(2)}, u32[]{:S(2)}) collective-permute-start(f32[1,128,256]{2,1,0:T(8,128)S(1)} %add_c1.1.refs_3_.refs_2_), channel_id=1, source_target_pairs={{0,4},{1,5},{2,6},{3,7},{4,0},{5,1},{6,2},{7,3},{8,12},{9,13},{10,... | collective-permute-start | bytes 393224 | tf_op jit(solution)/shard_map/ppermute | solution.py:223
  14.3 0.0 collective-permute-done.1.refs_1_.come
  14.3 2.1 %collective-permute-start.8 = (f32[1,128,256]{2,1,0:T(8,128)S(1)}, f32[1,128,256]{2,1,0:T(8,128)S(1)}, u32[]{:S(2)}, u32[]{:S(2)}) collective-permute-start(f32[1,128,256]{2,1,0:T(8,128)S(1)} %add_n1.1), channel_id=1, source_target_pairs={{0,2},{1,3},{2,0},{3,1},{4,6},{5,7},{6,4},{7,5},{8,10},{9,11},{10,... | collective-permute-start | bytes 393224 | tf_op jit(solution)/shard_map/ppermute | solution.py:223
  16.5 0.0 collective-permute-done.3.refs_2_
  16.5 1.0 %collective-permute-start.5 = (f32[1,128,256]{2,1,0:T(8,128)S(1)}, f32[1,128,256]{2,1,0:T(8,128)S(1)}, u32[]{:S(2)}, u32[]{:S(2)}) collective-permute-start(f32[1,128,256]{2,1,0:T(8,128)S(1)} %add_c2.1.refs_2_), channel_id=1, source_target_pairs={{0,4},{1,5},{2,6},{3,7},{4,0},{5,1},{6,2},{7,3},{8,12},{9,13},{10,... | collective-permute-start | bytes 393224 | tf_op jit(solution)/shard_map/ppermute | solution.py:223
  17.5 0.0 copy-start.4
  17.6 0.0 copy-start.5
  17.6 1.5 %collective-permute-start.6 = (f32[1,128,256]{2,1,0:T(8,128)S(1)}, f32[1,128,256]{2,1,0:T(8,128)S(1)}, u32[]{:S(2)}, u32[]{:S(2)}) collective-permute-start(f32[1,128,256]{2,1,0:T(8,128)S(1)} %add_n2.1), channel_id=1, source_target_pairs={{0,2},{1,3},{2,0},{3,1},{4,6},{5,7},{6,4},{7,5},{8,10},{9,11},{10,... | collective-permute-start | bytes 393224 | tf_op jit(solution)/shard_map/ppermute | solution.py:223
  19.1 0.0 collective-permute-done.9
  19.1 1.6 %collective-permute-start.10 = (f32[128,128]{1,0:T(8,128)S(1)}, f32[128,128]{1,0:T(8,128)S(1)}, u32[]{:S(2)}, u32[]{:S(2)}) collective-permute-start(f32[128,128]{1,0:T(8,128)S(1)} %add.3.drift), channel_id=1, source_target_pairs={{0,8},{8,0},{16,24},{24,16},{1,9},{9,1},{17,25},{25,17},{2,10},{10... | collective-permute-start | bytes 196616 | tf_op jit(solution)/shard_map/ppermute | solution.py:223
  20.7 0.3 %collective-permute-done.7.far = f32[1,128,256]{2,1,0:T(8,128)S(1)} collective-permute-done((f32[1,128,256]{2,1,0:T(8,128)S(1)}, f32[1,128,256]{2,1,0:T(8,128)S(1)}, u32[]{:S(2)}, u32[]{:S(2)}) %collective-permute-start.7) | collective-permute-done | bytes 131104 | tf_op jit(solution)/shard_map/ppermute | solution.py:223
  21.1 2.4 %collective-permute-done.10.other_drift = f32[128,128]{1,0:T(8,128)S(1)} collective-permute-done((f32[128,128]{1,0:T(8,128)S(1)}, f32[128,128]{1,0:T(8,128)S(1)}, u32[]{:S(2)}, u32[]{:S(2)}) %collective-permute-start.10) | collective-permute-done | bytes 65568 | tf_op jit(solution)/shard_map/ppermute | solution.py:223
  23.5 0.0 collective-permute-done.8.near
  23.5 0.0 copy-done.1
  23.5 1.1 %left_step.1 = (f32[256,128]{1,0:T(8,128)S(1)}, f32[1,512,128]{2,1,0:T(8,128)}, f32[1,512,128]{2,1,0:T(8,128)}, f32[1,512,128]{2,1,0:T(8,128)}, f32[128,128]{1,0:T(8,128)}, /*index=5*/f32[128,128]{1,0:T(8,128)}) custom-call(f32[1,512,128]{2,1,0:T(8,128)S(1)} %copy-done.1, f32[1,512,128]{2,1,0:T(8,128)S(1)} %copy-done.2, f32[1,512,128]{2,1,0:T(8,128)S(1)} %copy-done.3, ...), custom_call_target="tpu_custom_call" | custom-call | flops 983040 | bytes 1310720 | tf_op jit(solution)/shard_map/left_step/pallas_call | solution.py:353
  24.6 0.4 %collective-permute-done.5.far = f32[1,128,256]{2,1,0:T(8,128)S(1)} collective-permute-done((f32[1,128,256]{2,1,0:T(8,128)S(1)}, f32[1,128,256]{2,1,0:T(8,128)S(1)}, u32[]{:S(2)}, u32[]{:S(2)}) %collective-permute-start.5) | collective-permute-done | bytes 131104 | tf_op jit(solution)/shard_map/ppermute | solution.py:223
  25.0 0.7 %collective-permute-done.6.near = f32[1,128,256]{2,1,0:T(8,128)S(1)} collective-permute-done((f32[1,128,256]{2,1,0:T(8,128)S(1)}, f32[1,128,256]{2,1,0:T(8,128)S(1)}, u32[]{:S(2)}, u32[]{:S(2)}) %collective-permute-start.6) | collective-permute-done | bytes 131104 | tf_op jit(solution)/shard_map/ppermute | solution.py:223
  25.7 1.0 %right_step.1 = (f32[1,512,128]{2,1,0:T(8,128)}, f32[1,512,128]{2,1,0:T(8,128)}, f32[1,512,128]{2,1,0:T(8,128)}) custom-call(f32[1,512,128]{2,1,0:T(8,128)S(1)} %copy-done.1, f32[1,512,128]{2,1,0:T(8,128)S(1)} %copy-done.2, f32[1,512,128]{2,1,0:T(8,128)S(1)} %copy-done.3, ...), custom_call_target="tpu_custom_call", output_to_operand_aliasing={{0}: (10, {}), {1}: (11, {}), {2}: (12, {})} | custom-call | tf_op jit(solution)/shard_map/right_step/pallas_call | solution.py:381
  (14 shorter events, 0.1 us)
Async XLA Ops:
  0.6 2.7 %copy-start = (bf16[1,128,4096]{2,1,0:T(8,128)(2,1)S(1)}, bf16[1,128,4096]{2,1,0:T(8,128)(2,1)}, u32[]{:S(2)}) copy-start(bf16[1,128,4096]{2,1,0:T(8,128)(2,1)} %features.3) | copy-start | bytes 3145732
  2.1 1.7 %collective-permute-start = (f32[2,128,256]{2,1,0:T(8,128)S(1)}, f32[2,128,256]{2,1,0:T(8,128)S(1)}, u32[]{:S(2)}, u32[]{:S(2)}) collective-permute-start(f32[2,128,256]{2,1,0:T(8,128)S(1)} %get-tuple-element.34), channel_id=1, source_target_pairs={{0,1},{1,0},{2,3},{3,2},{4,5},{5,4},{6,7},{7,6},{8,9},{9,8},{10,11... | collective-permute-start | bytes 786440 | tf_op jit(solution)/shard_map/ppermute | solution.py:223
  3.8 10.5 %collective-permute-start.1 = (f32[4,128,256]{2,1,0:T(8,128)S(1)}, f32[4,128,256]{2,1,0:T(8,128)S(1)}, u32[]{:S(2)}, u32[]{:S(2)}) collective-permute-start(f32[4,128,256]{2,1,0:T(8,128)S(1)} %get-tuple-element.35), channel_id=1, source_target_pairs={{0,1},{1,0},{2,3},{3,2},{4,5},{5,4},{6,7},{7,6},{8,9},{9,8},{10,11... | collective-permute-start | bytes 1572872 | tf_op jit(solution)/shard_map/ppermute | solution.py:223
  4.3 7.0 %collective-permute-start.2 = (f32[2,128,256]{2,1,0:T(8,128)S(1)}, f32[2,128,256]{2,1,0:T(8,128)S(1)}, u32[]{:S(2)}, u32[]{:S(2)}) collective-permute-start(f32[2,128,256]{2,1,0:T(8,128)S(1)} %get-tuple-element.37), channel_id=1, source_target_pairs={{0,1},{1,0},{2,3},{3,2},{4,5},{5,4},{6,7},{7,6},{8,9},{9,8},{10,11... | collective-permute-start | bytes 786440 | tf_op jit(solution)/shard_map/ppermute | solution.py:223
  4.4 6.9 %collective-permute-start.4 = (f32[1,128,256]{2,1,0:T(8,128)S(1)}, f32[1,128,256]{2,1,0:T(8,128)S(1)}, u32[]{:S(2)}, u32[]{:S(2)}) collective-permute-start(f32[1,128,256]{2,1,0:T(8,128)S(1)} %add_a1.1.after), channel_id=1, source_target_pairs={{0,2},{1,3},{2,0},{3,1},{4,6},{5,7},{6,4},{7,5},{8,10},{9,11},{10,... | collective-permute-start | bytes 393224 | tf_op jit(solution)/shard_map/ppermute | solution.py:223
  8.4 8.1 %collective-permute-start.3 = (f32[1,128,256]{2,1,0:T(8,128)S(1)}, f32[1,128,256]{2,1,0:T(8,128)S(1)}, u32[]{:S(2)}, u32[]{:S(2)}) collective-permute-start(f32[1,128,256]{2,1,0:T(8,128)S(1)} %add_a2.1), channel_id=1, source_target_pairs={{0,2},{1,3},{2,0},{3,1},{4,6},{5,7},{6,4},{7,5},{8,10},{9,11},{10,... | collective-permute-start | bytes 393224 | tf_op jit(solution)/shard_map/ppermute | solution.py:223
  8.5 10.6 %collective-permute-start.9 = (f32[128,128]{1,0:T(8,128)S(1)}, f32[128,128]{1,0:T(8,128)S(1)}, u32[]{:S(2)}, u32[]{:S(2)}) collective-permute-start(f32[128,128]{1,0:T(8,128)S(1)} %get-tuple-element.42.refs_2_), channel_id=1, source_target_pairs={{0,16},{8,24},{16,0},{24,8},{1,17},{9,25},{17,1},{25,9},{2,18},{10... | collective-permute-start | bytes 196616 | tf_op jit(solution)/shard_map/ppermute | solution.py:223
  11.3 9.7 %collective-permute-start.7 = (f32[1,128,256]{2,1,0:T(8,128)S(1)}, f32[1,128,256]{2,1,0:T(8,128)S(1)}, u32[]{:S(2)}, u32[]{:S(2)}) collective-permute-start(f32[1,128,256]{2,1,0:T(8,128)S(1)} %add_c1.1.refs_3_.refs_2_), channel_id=1, source_target_pairs={{0,4},{1,5},{2,6},{3,7},{4,0},{5,1},{6,2},{7,3},{8,12},{9,13},{10,... | collective-permute-start | bytes 393224 | tf_op jit(solution)/shard_map/ppermute | solution.py:223
  14.3 9.1 %collective-permute-start.8 = (f32[1,128,256]{2,1,0:T(8,128)S(1)}, f32[1,128,256]{2,1,0:T(8,128)S(1)}, u32[]{:S(2)}, u32[]{:S(2)}) collective-permute-start(f32[1,128,256]{2,1,0:T(8,128)S(1)} %add_n1.1), channel_id=1, source_target_pairs={{0,2},{1,3},{2,0},{3,1},{4,6},{5,7},{6,4},{7,5},{8,10},{9,11},{10,... | collective-permute-start | bytes 393224 | tf_op jit(solution)/shard_map/ppermute | solution.py:223
  16.5 8.5 %collective-permute-start.5 = (f32[1,128,256]{2,1,0:T(8,128)S(1)}, f32[1,128,256]{2,1,0:T(8,128)S(1)}, u32[]{:S(2)}, u32[]{:S(2)}) collective-permute-start(f32[1,128,256]{2,1,0:T(8,128)S(1)} %add_c2.1.refs_2_), channel_id=1, source_target_pairs={{0,4},{1,5},{2,6},{3,7},{4,0},{5,1},{6,2},{7,3},{8,12},{9,13},{10,... | collective-permute-start | bytes 393224 | tf_op jit(solution)/shard_map/ppermute | solution.py:223
  17.5 6.0 %copy-start.1 = (f32[1,512,128]{2,1,0:T(8,128)S(1)}, f32[1,512,128]{2,1,0:T(8,128)}, u32[]{:S(2)}) copy-start(f32[1,512,128]{2,1,0:T(8,128)} %params.5) | copy-start | bytes 786436
  17.5 6.0 %copy-start.2 = (f32[1,512,128]{2,1,0:T(8,128)S(1)}, f32[1,512,128]{2,1,0:T(8,128)}, u32[]{:S(2)}) copy-start(f32[1,512,128]{2,1,0:T(8,128)} %first.3) | copy-start | bytes 786436
  17.5 6.0 %copy-start.3 = (f32[1,512,128]{2,1,0:T(8,128)S(1)}, f32[1,512,128]{2,1,0:T(8,128)}, u32[]{:S(2)}) copy-start(f32[1,512,128]{2,1,0:T(8,128)} %second.3) | copy-start | bytes 786436
  17.5 5.9 %copy-start.4 = (f32[128,128]{1,0:T(8,128)S(1)}, f32[128,128]{1,0:T(8,128)}, u32[]{:S(2)}) copy-start(f32[128,128]{1,0:T(8,128)} %global_fragment.3) | copy-start | bytes 196612
  17.6 5.9 %copy-start.5 = (f32[128,128]{1,0:T(8,128)S(1)}, f32[128,128]{1,0:T(8,128)}, u32[]{:S(2)}) copy-start(f32[128,128]{1,0:T(8,128)} %outer_momentum.1) | copy-start | bytes 196612
  17.6 8.2 %collective-permute-start.6 = (f32[1,128,256]{2,1,0:T(8,128)S(1)}, f32[1,128,256]{2,1,0:T(8,128)S(1)}, u32[]{:S(2)}, u32[]{:S(2)}) collective-permute-start(f32[1,128,256]{2,1,0:T(8,128)S(1)} %add_n2.1), channel_id=1, source_target_pairs={{0,2},{1,3},{2,0},{3,1},{4,6},{5,7},{6,4},{7,5},{8,10},{9,11},{10,... | collective-permute-start | bytes 393224 | tf_op jit(solution)/shard_map/ppermute | solution.py:223
  19.1 4.3 %collective-permute-start.10 = (f32[128,128]{1,0:T(8,128)S(1)}, f32[128,128]{1,0:T(8,128)S(1)}, u32[]{:S(2)}, u32[]{:S(2)}) collective-permute-start(f32[128,128]{1,0:T(8,128)S(1)} %add.3.drift), channel_id=1, source_target_pairs={{0,8},{8,0},{16,24},{24,16},{1,9},{9,1},{17,25},{25,17},{2,10},{10... | collective-permute-start | bytes 196616 | tf_op jit(solution)/shard_map/ppermute | solution.py:223

commit v7 on v6

--- a/solution.py
+++ b/solution.py
@@ -69,7 +69,7 @@
 
 def rest_kernel(masked, features, *targets):
     half = targets[0].shape[2]
-    places = [(4, 0, 0, 0), (4, 1, 0, 1), (2, 0, 2, 2), (2, 1, 2, 3), (0, 0, 2, 0), (0, 1, 2, 1)]
+    places = [(4, 0, 0, 4), (4, 1, 0, 5), (2, 0, 0, 2), (2, 1, 0, 3), (0, 0, 0, 0), (0, 1, 0, 1)]
     for q, side, into, at in places:
         for core in (1, 0):
             columns = columns_of(q + core, 2 * half, side * half, half)
@@ -282,11 +282,11 @@
             cost_estimate=cost(2),
             name="far_products",
         )(far_counts, far_cotangent, far_features)
-        away_pass, kept_pass, away, kept = pl.pallas_call(
+        away, kept = pl.pallas_call(
             rest_kernel,
-            out_shape=[block((2, width, half))] * 2 + [block((4, width, half))] * 2,
+            out_shape=[block((6, width, half))] * 2,
             in_specs=[VMEM] * 2,
-            out_specs=[VMEM] * 4,
+            out_specs=[VMEM] * 2,
             compiler_params=room,
             cost_estimate=free,
             name="rest_products",
@@ -309,10 +309,9 @@
 
         state, piece = block(params.shape), block(global_fragment.shape)
         come_far = hop(away_far, "fsdp", devices, 1)
-        sent = add((kept_far, part(0)), (come_far, part(0)), (far_fragment, None), name="add_a1")
+        sent = add((kept_far, part(0)), (come_far, part(0)), name="add_a1")
         far_left = hop(sent, "fsdp", devices, 2)
-        away_pass, away, _ = lax.optimization_barrier((away_pass, away, sent))
-        come_pass = hop(away_pass, "fsdp", devices, 1)
+        away, _ = lax.optimization_barrier((away, sent))
         come = hop(away, "fsdp", devices, 1)
         drift, scale, inverse, share = pl.pallas_call(
             functools.partial(drift_kernel, workers),
@@ -332,11 +331,11 @@
         )(far_counts, far_fragment, far_params, far_global, sent)
         sent = add((kept_far, part(1)), (come_far, part(1)), (drift, None), name="add_a2")
         far_right = hop(sent, "fsdp", devices, 2)
-        passed = add((kept_pass, part(0)), (come_pass, part(0)), (far_left, part(0)), name="add_c1")
+        passed = add((kept, part(4)), (come, part(4)), (far_left, part(0)), name="add_c1")
         far_left = hop(passed, "fsdp", devices, 4)
-        near_left = add((kept, part(2)), (come, part(2)), (passed, None), name="add_n1")
-        far_right = add((kept_pass, part(1)), (come_pass, part(1)), (far_right, part(0)), (passed, None), name="add_c2")
-        near_right = add((kept, part(3)), (come, part(3)), (far_right, None), name="add_n2")
+        near_left = add((kept, part(2)), (come, part(2)), (sent, None), name="add_n1")
+        far_right = add((kept, part(5)), (come, part(5)), (far_right, part(0)), (passed, None), name="add_c2")
+        near_right = add((kept, part(3)), (come, part(3)), (passed, None), name="add_n2")
         drift, _ = lax.optimization_barrier((drift, sent))
         bit = workers // 2
         drifts = (drift, hop(drift, "worker", workers, bit))

time: 26.9 us -> 26.6 us (0.989)
  starting transfers between devices: 15.3 us -> 14.2 us
  waiting for transfers between devices: 4.86 us -> 5.71 us
    ppermute x11 -> x10, starting transfers between devices: 15.3 us -> 14.2 us  [hop(): return lax.ppermute(value, axis, [(d, d ^ bit) for d in range(devices)])]
    ppermute x11 -> x10, waiting for transfers between devices: 4.86 us -> 5.71 us  [hop(): return lax.ppermute(value, axis, [(d, d ^ bit) for d in range(devices)])]
  transfers between devices with their start and end apart: 11 -> 10, of which waited for: 6 -> 3; matrix products, arithmetic and copies ran while one was open for 0% -> 0% of each run, Pallas kernels for 10% -> 10%
where the time goes in v7:
time: 26.6 us; the launch traced here: 26.4 us
  starting transfers between devices  14.2 us (53%)
  waiting for transfers between devices  5.71 us (21%)
  Pallas kernels  5.07 us (19%)
  between operations  1.42 us (5%)
    ppermute x10, starting transfers between devices, hop(): return lax.ppermute(value, axis, [(d, d ^ bit) for d in range(devices)])  14.2 us
    ppermute x10, waiting for transfers between devices, hop(): return lax.ppermute(value, axis, [(d, d ^ bit) for d in range(devices)])  5.71 us
    pallas_call x1, Pallas kernels, body(): pl.pallas_call(functools.partial(first_kernel, (7, 6)), out_shape=[block(...  1.47 us
    pallas_call x1, Pallas kernels, body(): pl.pallas_call(left_kernel, out_shape=[block((half, width)), state, state...  1.08 us
    pallas_call x1, Pallas kernels, body(): pl.pallas_call(functools.partial(drift_kernel, workers), out_shape=[piece...  1.03 us
    pallas_call x1, Pallas kernels, body(): pl.pallas_call(right_kernel, out_shape=[state] * 3, in_specs=[VMEM] * 10...  0.96 us
  transfers between devices with their start and end apart: 10, of which 3 were waited for; matrix products, arithmetic and copies ran while one was open for 0% of the time, Pallas kernels for 10%

profile of v7, /device:TPU:0, one launch (start us, length us, event | category | flops | bytes accessed | tf_op | source)
XLA Modules:
  0.0 26.4 jit_solution(7697122306066355502)
XLA Ops:
  0.6 0.0 copy-start
  0.6 1.5 %far_products.1 = (f32[2,128,256]{2,1,0:T(8,128)S(1)}, f32[2,128,256]{2,1,0:T(8,128)S(1)}, bf16[128,128]{1,0:T(8,128)(2,1)S(1)}) custom-call(s32[4]{0:T(128)} %counts.3, bf16[1,128,128]{2,1,0:T(8,128)(2,1)} %cotangent.1, bf16[1,128,4096]{2,1,0:T(8,128)(2,1)} %features.3), custom_call_target="tpu_custom_call" | custom-call | flops 33554432 | bytes 786432 | tf_op jit(solution)/shard_map/far_products/pallas_call | solution.py:270
  2.1 0.5 %collective-permute-start = (f32[2,128,256]{2,1,0:T(8,128)S(1)}, f32[2,128,256]{2,1,0:T(8,128)S(1)}, u32[]{:S(2)}, u32[]{:S(2)}) collective-permute-start(f32[2,128,256]{2,1,0:T(8,128)S(1)} %get-tuple-element.30), channel_id=1, source_target_pairs={{0,1},{1,0},{2,3},{3,2},{4,5},{5,4},{6,7},{7,6},{8,9},{9,8},{10,11... | collective-permute-start | bytes 786440 | tf_op jit(solution)/shard_map/ppermute | solution.py:223
  2.6 0.0 copy-done
  2.6 0.4 %rest_products.1 = (f32[6,128,256]{2,1,0:T(8,128)S(1)}, f32[6,128,256]{2,1,0:T(8,128)S(1)}) custom-call(bf16[128,128]{1,0:T(8,128)(2,1)S(1)} %get-tuple-element.26.masked, bf16[1,128,4096]{2,1,0:T(8,128)(2,1)S(1)} %copy-done), custom_call_target="tpu_custom_call" | custom-call | tf_op jit(solution)/shard_map/rest_products/pallas_call | solution.py:285
  3.0 0.8 %collective-permute-done.refs_1_ = f32[2,128,256]{2,1,0:T(8,128)S(1)} collective-permute-done((f32[2,128,256]{2,1,0:T(8,128)S(1)}, f32[2,128,256]{2,1,0:T(8,128)S(1)}, u32[]{:S(2)}, u32[]{:S(2)}) %collective-permute-start) | collective-permute-done | bytes 262176 | tf_op jit(solution)/shard_map/ppermute | solution.py:223
  3.8 0.4 %collective-permute-start.1 = (f32[6,128,256]{2,1,0:T(8,128)S(1)}, f32[6,128,256]{2,1,0:T(8,128)S(1)}, u32[]{:S(2)}, u32[]{:S(2)}) collective-permute-start(f32[6,128,256]{2,1,0:T(8,128)S(1)} %get-tuple-element.31), channel_id=1, source_target_pairs={{0,1},{1,0},{2,3},{3,2},{4,5},{5,4},{6,7},{7,6},{8,9},{9,8},{10,11... | collective-permute-start | bytes 2359304 | tf_op jit(solution)/shard_map/ppermute | solution.py:223
  4.3 2.7 %collective-permute-start.3 = (f32[1,128,256]{2,1,0:T(8,128)S(1)}, f32[1,128,256]{2,1,0:T(8,128)S(1)}, u32[]{:S(2)}, u32[]{:S(2)}) collective-permute-start(f32[1,128,256]{2,1,0:T(8,128)S(1)} %add_a1.1.after), channel_id=1, source_target_pairs={{0,2},{1,3},{2,0},{3,1},{4,6},{5,7},{6,4},{7,5},{8,10},{9,11},{10,... | collective-permute-start | bytes 393224 | tf_op jit(solution)/shard_map/ppermute | solution.py:223
  7.6 1.0 %drift.1 = (f32[128,128]{1,0:T(8,128)S(1)}, f32[512,128]{1,0:T(8,128)S(1)}, f32[8,128]{1,0:T(8,128)S(1)}, f32[8,128]{1,0:T(8,128)S(1)}) custom-call(s32[4]{0:T(128)} %counts.3, s32[1]{0:T(128)S(6)} %copy.20.fragment, f32[1,512,128]{2,1,0:T(8,128)} %params.5, f32[128,128]{1,0:T(8,128)} %global_fragment.3, f32[1,128,256]{2,1,0:T(8,128)S(1)} %add_a1.1.after), custom_call_target="tpu_custom_call" | custom-call | tf_op jit(solution)/shard_map/drift/pallas_call | solution.py:316
  8.7 0.1 collective-permute-start.2
  8.8 2.0 %collective-permute-start.8 = (f32[128,128]{1,0:T(8,128)S(1)}, f32[128,128]{1,0:T(8,128)S(1)}, u32[]{:S(2)}, u32[]{:S(2)}) collective-permute-start(f32[128,128]{1,0:T(8,128)S(1)} %get-tuple-element.36.refs_2_), channel_id=1, source_target_pairs={{0,16},{8,24},{16,0},{24,8},{1,17},{9,25},{17,1},{25,9},{2,18},{10... | collective-permute-start | bytes 196616 | tf_op jit(solution)/shard_map/ppermute | solution.py:223
  10.7 0.0 collective-permute-done.1.refs_1_.come
  10.8 1.6 %collective-permute-start.7 = (f32[1,128,256]{2,1,0:T(8,128)S(1)}, f32[1,128,256]{2,1,0:T(8,128)S(1)}, u32[]{:S(2)}, u32[]{:S(2)}) collective-permute-start(f32[1,128,256]{2,1,0:T(8,128)S(1)} %add_n1.1), channel_id=1, source_target_pairs={{0,2},{1,3},{2,0},{3,1},{4,6},{5,7},{6,4},{7,5},{8,10},{9,11},{10,... | collective-permute-start | bytes 393224 | tf_op jit(solution)/shard_map/ppermute | solution.py:223
  12.4 0.0 collective-permute-done.3.refs_2_
  12.4 2.7 %collective-permute-start.6 = (f32[1,128,256]{2,1,0:T(8,128)S(1)}, f32[1,128,256]{2,1,0:T(8,128)S(1)}, u32[]{:S(2)}, u32[]{:S(2)}) collective-permute-start(f32[1,128,256]{2,1,0:T(8,128)S(1)} %add_c1.1.refs_3_.refs_2_), channel_id=1, source_target_pairs={{0,4},{1,5},{2,6},{3,7},{4,0},{5,1},{6,2},{7,3},{8,12},{9,13},{10,... | collective-permute-start | bytes 393224 | tf_op jit(solution)/shard_map/ppermute | solution.py:223
  15.1 1.0 %collective-permute-start.5 = (f32[1,128,256]{2,1,0:T(8,128)S(1)}, f32[1,128,256]{2,1,0:T(8,128)S(1)}, u32[]{:S(2)}, u32[]{:S(2)}) collective-permute-start(f32[1,128,256]{2,1,0:T(8,128)S(1)} %add_n2.1), channel_id=1, source_target_pairs={{0,2},{1,3},{2,0},{3,1},{4,6},{5,7},{6,4},{7,5},{8,10},{9,11},{10,... | collective-permute-start | bytes 393224 | tf_op jit(solution)/shard_map/ppermute | solution.py:223
  16.1 0.0 collective-permute-done.2.refs_2_
  16.1 0.0 copy-start.4
  16.1 0.0 copy-start.5
  16.1 1.7 %collective-permute-start.4 = (f32[1,128,256]{2,1,0:T(8,128)S(1)}, f32[1,128,256]{2,1,0:T(8,128)S(1)}, u32[]{:S(2)}, u32[]{:S(2)}) collective-permute-start(f32[1,128,256]{2,1,0:T(8,128)S(1)} %add_c2.1), channel_id=1, source_target_pairs={{0,4},{1,5},{2,6},{3,7},{4,0},{5,1},{6,2},{7,3},{8,12},{9,13},{10,... | collective-permute-start | bytes 393224 | tf_op jit(solution)/shard_map/ppermute | solution.py:223
  17.8 0.0 collective-permute-done.8
  17.8 1.6 %collective-permute-start.9 = (f32[128,128]{1,0:T(8,128)S(1)}, f32[128,128]{1,0:T(8,128)S(1)}, u32[]{:S(2)}, u32[]{:S(2)}) collective-permute-start(f32[128,128]{1,0:T(8,128)S(1)} %add.3.drift), channel_id=1, source_target_pairs={{0,8},{8,0},{16,24},{24,16},{1,9},{9,1},{17,25},{25,17},{2,10},{10... | collective-permute-start | bytes 196616 | tf_op jit(solution)/shard_map/ppermute | solution.py:223
  19.4 2.8 %collective-permute-done.9.other_drift = f32[128,128]{1,0:T(8,128)S(1)} collective-permute-done((f32[128,128]{1,0:T(8,128)S(1)}, f32[128,128]{1,0:T(8,128)S(1)}, u32[]{:S(2)}, u32[]{:S(2)}) %collective-permute-start.9) | collective-permute-done | bytes 65568 | tf_op jit(solution)/shard_map/ppermute | solution.py:223
  22.2 0.0 collective-permute-done.7.near
  22.2 0.0 collective-permute-done.6.far
  22.2 0.0 copy-done.1
  22.2 0.0 copy-done.2
  22.2 0.0 copy-done.3
  22.2 1.1 %left_step.1 = (f32[256,128]{1,0:T(8,128)S(1)}, f32[1,512,128]{2,1,0:T(8,128)}, f32[1,512,128]{2,1,0:T(8,128)}, f32[1,512,128]{2,1,0:T(8,128)}, f32[128,128]{1,0:T(8,128)}, /*index=5*/f32[128,128]{1,0:T(8,128)}) custom-call(f32[1,512,128]{2,1,0:T(8,128)S(1)} %copy-done.1, f32[1,512,128]{2,1,0:T(8,128)S(1)} %copy-done.2, f32[1,512,128]{2,1,0:T(8,128)S(1)} %copy-done.3, ...), custom_call_target="tpu_custom_call" | custom-call | flops 983040 | bytes 1310720 | tf_op jit(solution)/shard_map/left_step/pallas_call | solution.py:352
  23.3 2.2 %collective-permute-done.5.near = f32[1,128,256]{2,1,0:T(8,128)S(1)} collective-permute-done((f32[1,128,256]{2,1,0:T(8,128)S(1)}, f32[1,128,256]{2,1,0:T(8,128)S(1)}, u32[]{:S(2)}, u32[]{:S(2)}) %collective-permute-start.5) | collective-permute-done | bytes 131104 | tf_op jit(solution)/shard_map/ppermute | solution.py:223
  25.5 0.0 collective-permute-done.4.far
  25.5 1.0 %right_step.1 = (f32[1,512,128]{2,1,0:T(8,128)}, f32[1,512,128]{2,1,0:T(8,128)}, f32[1,512,128]{2,1,0:T(8,128)}) custom-call(f32[1,512,128]{2,1,0:T(8,128)S(1)} %copy-done.1, f32[1,512,128]{2,1,0:T(8,128)S(1)} %copy-done.2, f32[1,512,128]{2,1,0:T(8,128)S(1)} %copy-done.3, ...), custom_call_target="tpu_custom_call", output_to_operand_aliasing={{0}: (10, {}), {1}: (11, {}), {2}: (12, {})} | custom-call | tf_op jit(solution)/shard_map/right_step/pallas_call | solution.py:380
  (12 shorter events, 0.1 us)
Async XLA Ops:
  0.6 2.0 %copy-start = (bf16[1,128,4096]{2,1,0:T(8,128)(2,1)S(1)}, bf16[1,128,4096]{2,1,0:T(8,128)(2,1)}, u32[]{:S(2)}) copy-start(bf16[1,128,4096]{2,1,0:T(8,128)(2,1)} %features.3) | copy-start | bytes 3145732
  2.1 1.7 %collective-permute-start = (f32[2,128,256]{2,1,0:T(8,128)S(1)}, f32[2,128,256]{2,1,0:T(8,128)S(1)}, u32[]{:S(2)}, u32[]{:S(2)}) collective-permute-start(f32[2,128,256]{2,1,0:T(8,128)S(1)} %get-tuple-element.30), channel_id=1, source_target_pairs={{0,1},{1,0},{2,3},{3,2},{4,5},{5,4},{6,7},{7,6},{8,9},{9,8},{10,11... | collective-permute-start | bytes 786440 | tf_op jit(solution)/shard_map/ppermute | solution.py:223
  3.8 6.9 %collective-permute-start.1 = (f32[6,128,256]{2,1,0:T(8,128)S(1)}, f32[6,128,256]{2,1,0:T(8,128)S(1)}, u32[]{:S(2)}, u32[]{:S(2)}) collective-permute-start(f32[6,128,256]{2,1,0:T(8,128)S(1)} %get-tuple-element.31), channel_id=1, source_target_pairs={{0,1},{1,0},{2,3},{3,2},{4,5},{5,4},{6,7},{7,6},{8,9},{9,8},{10,11... | collective-permute-start | bytes 2359304 | tf_op jit(solution)/shard_map/ppermute | solution.py:223
  4.3 8.1 %collective-permute-start.3 = (f32[1,128,256]{2,1,0:T(8,128)S(1)}, f32[1,128,256]{2,1,0:T(8,128)S(1)}, u32[]{:S(2)}, u32[]{:S(2)}) collective-permute-start(f32[1,128,256]{2,1,0:T(8,128)S(1)} %add_a1.1.after), channel_id=1, source_target_pairs={{0,2},{1,3},{2,0},{3,1},{4,6},{5,7},{6,4},{7,5},{8,10},{9,11},{10,... | collective-permute-start | bytes 393224 | tf_op jit(solution)/shard_map/ppermute | solution.py:223
  8.7 7.4 %collective-permute-start.2 = (f32[1,128,256]{2,1,0:T(8,128)S(1)}, f32[1,128,256]{2,1,0:T(8,128)S(1)}, u32[]{:S(2)}, u32[]{:S(2)}) collective-permute-start(f32[1,128,256]{2,1,0:T(8,128)S(1)} %add_a2.1.refs_2_), channel_id=1, source_target_pairs={{0,2},{1,3},{2,0},{3,1},{4,6},{5,7},{6,4},{7,5},{8,10},{9,11},{10,... | collective-permute-start | bytes 393224 | tf_op jit(solution)/shard_map/ppermute | solution.py:223
  8.8 9.1 %collective-permute-start.8 = (f32[128,128]{1,0:T(8,128)S(1)}, f32[128,128]{1,0:T(8,128)S(1)}, u32[]{:S(2)}, u32[]{:S(2)}) collective-permute-start(f32[128,128]{1,0:T(8,128)S(1)} %get-tuple-element.36.refs_2_), channel_id=1, source_target_pairs={{0,16},{8,24},{16,0},{24,8},{1,17},{9,25},{17,1},{25,9},{2,18},{10... | collective-permute-start | bytes 196616 | tf_op jit(solution)/shard_map/ppermute | solution.py:223
  10.8 11.4 %collective-permute-start.7 = (f32[1,128,256]{2,1,0:T(8,128)S(1)}, f32[1,128,256]{2,1,0:T(8,128)S(1)}, u32[]{:S(2)}, u32[]{:S(2)}) collective-permute-start(f32[1,128,256]{2,1,0:T(8,128)S(1)} %add_n1.1), channel_id=1, source_target_pairs={{0,2},{1,3},{2,0},{3,1},{4,6},{5,7},{6,4},{7,5},{8,10},{9,11},{10,... | collective-permute-start | bytes 393224 | tf_op jit(solution)/shard_map/ppermute | solution.py:223
  12.4 9.8 %collective-permute-start.6 = (f32[1,128,256]{2,1,0:T(8,128)S(1)}, f32[1,128,256]{2,1,0:T(8,128)S(1)}, u32[]{:S(2)}, u32[]{:S(2)}) collective-permute-start(f32[1,128,256]{2,1,0:T(8,128)S(1)} %add_c1.1.refs_3_.refs_2_), channel_id=1, source_target_pairs={{0,4},{1,5},{2,6},{3,7},{4,0},{5,1},{6,2},{7,3},{8,12},{9,13},{10,... | collective-permute-start | bytes 393224 | tf_op jit(solution)/shard_map/ppermute | solution.py:223
  15.1 10.4 %collective-permute-start.5 = (f32[1,128,256]{2,1,0:T(8,128)S(1)}, f32[1,128,256]{2,1,0:T(8,128)S(1)}, u32[]{:S(2)}, u32[]{:S(2)}) collective-permute-start(f32[1,128,256]{2,1,0:T(8,128)S(1)} %add_n2.1), channel_id=1, source_target_pairs={{0,2},{1,3},{2,0},{3,1},{4,6},{5,7},{6,4},{7,5},{8,10},{9,11},{10,... | collective-permute-start | bytes 393224 | tf_op jit(solution)/shard_map/ppermute | solution.py:223
  16.1 6.1 %copy-start.1 = (f32[1,512,128]{2,1,0:T(8,128)S(1)}, f32[1,512,128]{2,1,0:T(8,128)}, u32[]{:S(2)}) copy-start(f32[1,512,128]{2,1,0:T(8,128)} %params.5) | copy-start | bytes 786436
  16.1 6.1 %copy-start.2 = (f32[1,512,128]{2,1,0:T(8,128)S(1)}, f32[1,512,128]{2,1,0:T(8,128)}, u32[]{:S(2)}) copy-start(f32[1,512,128]{2,1,0:T(8,128)} %first.3) | copy-start | bytes 786436
  16.1 6.1 %copy-start.3 = (f32[1,512,128]{2,1,0:T(8,128)S(1)}, f32[1,512,128]{2,1,0:T(8,128)}, u32[]{:S(2)}) copy-start(f32[1,512,128]{2,1,0:T(8,128)} %second.3) | copy-start | bytes 786436
  16.1 6.1 %copy-start.4 = (f32[128,128]{1,0:T(8,128)S(1)}, f32[128,128]{1,0:T(8,128)}, u32[]{:S(2)}) copy-start(f32[128,128]{1,0:T(8,128)} %global_fragment.3) | copy-start | bytes 196612
  16.1 6.1 %copy-start.5 = (f32[128,128]{1,0:T(8,128)S(1)}, f32[128,128]{1,0:T(8,128)}, u32[]{:S(2)}) copy-start(f32[128,128]{1,0:T(8,128)} %outer_momentum.1) | copy-start | bytes 196612
  16.1 9.4 %collective-permute-start.4 = (f32[1,128,256]{2,1,0:T(8,128)S(1)}, f32[1,128,256]{2,1,0:T(8,128)S(1)}, u32[]{:S(2)}, u32[]{:S(2)}) collective-permute-start(f32[1,128,256]{2,1,0:T(8,128)S(1)} %add_c2.1), channel_id=1, source_target_pairs={{0,4},{1,5},{2,6},{3,7},{4,0},{5,1},{6,2},{7,3},{8,12},{9,13},{10,... | collective-permute-start | bytes 393224 | tf_op jit(solution)/shard_map/ppermute | solution.py:223
  17.8 4.3 %collective-permute-start.9 = (f32[128,128]{1,0:T(8,128)S(1)}, f32[128,128]{1,0:T(8,128)S(1)}, u32[]{:S(2)}, u32[]{:S(2)}) collective-permute-start(f32[128,128]{1,0:T(8,128)S(1)} %add.3.drift), channel_id=1, source_target_pairs={{0,8},{8,0},{16,24},{24,16},{1,9},{9,1},{17,25},{25,17},{2,10},{10... | collective-permute-start | bytes 196616 | tf_op jit(solution)/shard_map/ppermute | solution.py:223

commit v8 on v7

--- a/solution.py
+++ b/solution.py
@@ -51,7 +51,9 @@
     return copies
 
 
-def first_kernel(order, counts, cotangent, features, away, kept, masked, counts_held, cot_held, held, sems):
+def first_kernel(
+    workers, order, counts, cotangent, features, away, kept, masked, info, counts_held, cot_held, held, sems
+):
     half = away.shape[2]
     small = fetch((counts, cotangent), (counts_held, cot_held), sems)
     columns = [columns_of(q, 2 * half, 0, 2 * half) for q in order]
@@ -61,6 +63,12 @@
     tokens = cot_held.shape[1]
     live = counts_held[lax.axis_index("worker")] - lax.axis_index("fsdp") * tokens
     masked[...] = masked_rows(live, cot_held[0])
+    count, total = counts_held[lax.axis_index("worker")], counts_held[0]
+    for other in range(1, workers):
+        total = total + counts_held[other]
+    info[0:1, :] = jnp.full((1, info.shape[1]), count.astype(jnp.float32))
+    info[1:2, :] = 1.0 / info[0:1, :]
+    info[2:3, :] = 1.0 / jnp.full((1, info.shape[1]), total.astype(jnp.float32))
     for slot, into in enumerate((away, kept)):
         blocks[slot].wait()
         for side in (0, 1):
@@ -76,25 +84,12 @@
             targets[into + 1 - core][at] = product(masked[...], features[0, :, columns])
 
 
-def drift_kernel(
-    workers, counts, fragment, params, global_fragment, after, drift, scale, inverse, share, *held_and_sems
-):
+def drift_kernel(info, fragment, params, global_fragment, after, drift, scale):
     del after
-    held, sems = held_and_sems[:-1], held_and_sems[-1]
-    copies = fetch((counts, fragment, params, global_fragment), held, sems)
+    mine = pl.ds(fragment[0], drift.shape[0], stride=FRAGS)
+    drift[...] = info[0:1, :] * (global_fragment[...] - params[0, mine, :])
     scale[...] = jnp.ones_like(scale)
-    for copy in copies:
-        copy.wait()
-    counts_held, fragment_held, params_held, global_held = held
-    mine = pl.ds(fragment_held[0], drift.shape[0], stride=FRAGS)
-    count = counts_held[lax.axis_index("worker")].astype(jnp.float32)
-    drift[...] = count * (global_held[...] - params_held[0, mine, :])
     scale[mine, :] = jnp.full_like(drift, 1.0 - MIXING)
-    total = counts_held[0]
-    for other in range(1, workers):
-        total = total + counts_held[other]
-    inverse[...] = jnp.ones_like(inverse) / count
-    share[...] = jnp.ones_like(share) / total.astype(jnp.float32)
 
 
 def add_kernel(picks, *refs):
@@ -117,7 +112,7 @@
     return global_fragment - OUTER_RATE * (pseudo_grad + NESTEROV * momentum), momentum
 
 
-def half_step(half, states, sums, inverse, held):
+def half_step(half, states, sums, info, held):
     params, first, second = states
     kept, come, far, near = sums
     held_first, held_second = held
@@ -126,7 +121,7 @@
         lanes, there = pl.ds(lane, LANES), pl.ds(half * rows + lane, LANES)
         summed = kept[half, :, lanes] + come[half, :, lanes] + near[0, :, lanes] + far[0, :, lanes]
         inner, held_first[lanes, :], held_second[lanes, :] = adam(
-            params[0, there, :], first[0, there, :], second[0, there, :], summed.T * inverse[0:1, :]
+            params[0, there, :], first[0, there, :], second[0, there, :], summed.T * info[1:2, :]
         )
         yield lanes, there, inner
 
@@ -144,9 +139,8 @@
     come,
     far,
     near,
-    inverse,
+    info,
     scale,
-    share,
     global_fragment,
     outer_momentum,
     drift,
@@ -166,7 +160,7 @@
     sems,
 ):
     copies = []
-    fresh, momentum = outer((drift[...] + other_drift[...]) * share[0:1, :], global_fragment[...], outer_momentum[...])
+    fresh, momentum = outer((drift[...] + other_drift[...]) * info[2:3, :], global_fragment[...], outer_momentum[...])
     held_global[...] = fresh
     held_momentum[...] = momentum
     send(copies, sems, held_global, new_global)
@@ -174,7 +168,7 @@
     for at in range(FRAGS):
         spread[pl.ds(at, fresh.shape[0], stride=FRAGS), :] = fresh
     for lanes, there, value in half_step(
-        0, (params, first, second), (kept, come, far, near), inverse, (held_first, held_second)
+        0, (params, first, second), (kept, come, far, near), info, (held_first, held_second)
     ):
         held_params[lanes, :] = scale[there, :] * value + (1.0 - scale[there, :]) * spread[there, :]
         for source, target in ((held_first, new_first), (held_second, new_second), (held_params, new_params)):
@@ -193,7 +187,7 @@
     come,
     far,
     near,
-    inverse,
+    info,
     scale,
     mix,
     left_params,
@@ -210,7 +204,7 @@
     del left_params, left_first, left_second
     copies = []
     for lanes, there, value in half_step(
-        1, (params, first, second), (kept, come, far, near), inverse, (held_first, held_second)
+        1, (params, first, second), (kept, come, far, near), info, (held_first, held_second)
     ):
         held_params[lanes, :] = scale[there, :] * value + mix[lanes, :]
         for source, target in ((held_first, new_first), (held_second, new_second), (held_params, new_params)):
@@ -250,28 +244,18 @@
 
         room = pltpu.CompilerParams(vmem_limit_bytes=ROOM)
         free = pl.CostEstimate(flops=0, bytes_accessed=0, transcendentals=0)
-        far_fragment = fragment_index
-        far_counts, far_features, far_cotangent, far_params, far_global, far_momentum = (
-            pltpu.with_memory_space_constraint(array, pltpu.HBM)
-            for array in (
-                token_counts,
-                features,
-                cotangent,
-                params,
-                global_fragment,
-                outer_momentum,
-            )
+        far_counts, far_features, far_cotangent = (
+            pltpu.with_memory_space_constraint(array, pltpu.HBM) for array in (token_counts, features, cotangent)
         )
         held_counts = pltpu.SMEM(token_counts.shape, token_counts.dtype)
-        held_fragment = pltpu.SMEM(fragment_index.shape, fragment_index.dtype)
         held_piece = pltpu.VMEM(global_fragment.shape, global_fragment.dtype)
 
         half = rows // 2
-        away_far, kept_far, masked = pl.pallas_call(
-            functools.partial(first_kernel, (7, 6)),
-            out_shape=[block((2, width, half))] * 2 + [jax.ShapeDtypeStruct((tokens, width), jnp.bfloat16)],
+        away_far, kept_far, masked, info = pl.pallas_call(
+            functools.partial(first_kernel, workers, (7, 6)),
+            out_shape=[block((2, width, half))] * 2 + [jax.ShapeDtypeStruct((tokens, width), jnp.bfloat16), block((8, width))],
             in_specs=[HBM] * 3,
-            out_specs=[VMEM] * 3,
+            out_specs=[VMEM] * 4,
             scratch_shapes=[
                 held_counts,
                 pltpu.VMEM(cotangent.shape, cotangent.dtype),
@@ -313,22 +297,15 @@
         far_left = hop(sent, "fsdp", devices, 2)
         away, _ = lax.optimization_barrier((away, sent))
         come = hop(away, "fsdp", devices, 1)
-        drift, scale, inverse, share = pl.pallas_call(
-            functools.partial(drift_kernel, workers),
-            out_shape=[piece, block((rows, width)), block((8, width)), block((8, width))],
-            in_specs=[HBM] * 4 + [ANY],
-            out_specs=[VMEM] * 4,
-            scratch_shapes=[
-                held_counts,
-                held_fragment,
-                pltpu.VMEM(params.shape, params.dtype),
-                held_piece,
-                pltpu.SemaphoreType.DMA((4,)),
-            ],
+        drift, scale = pl.pallas_call(
+            drift_kernel,
+            out_shape=[piece, block((rows, width))],
+            in_specs=[VMEM, SMEM, VMEM, VMEM, ANY],
+            out_specs=[VMEM] * 2,
             compiler_params=room,
             cost_estimate=free,
             name="drift",
-        )(far_counts, far_fragment, far_params, far_global, sent)
+        )(info, fragment_index, params, global_fragment, sent)
         sent = add((kept_far, part(1)), (come_far, part(1)), (drift, None), name="add_a2")
         far_right = hop(sent, "fsdp", devices, 2)
         passed = add((kept, part(4)), (come, part(4)), (far_left, part(0)), name="add_c1")
@@ -352,7 +329,7 @@
         mix, *results, new_global, new_momentum = pl.pallas_call(
             left_kernel,
             out_shape=[block((half, width)), state, state, state, piece, piece],
-            in_specs=[VMEM] * 14,
+            in_specs=[VMEM] * 13,
             out_specs=[VMEM] + [HBM] * 5,
             scratch_shapes=[held_half] * 3
             + [held_piece] * 2
@@ -370,9 +347,8 @@
             come,
             far_left,
             near_left,
-            inverse,
+            info,
             scale,
-            share,
             global_fragment,
             outer_momentum,
             *drifts,
@@ -387,7 +363,7 @@
             compiler_params=room,
             cost_estimate=free,
             name="right_step",
-        )(params, first, second, kept, come, far_right, near_right, inverse, scale, mix, *results)
+        )(params, first, second, kept, come, far_right, near_right, info, scale, mix, *results)
         return new_params, new_first, new_second, new_global, new_momentum
 
     return body

time: 26.6 us -> 26.2 us (0.985)
  Pallas kernels: 5.07 us -> 4.05 us
  starting transfers between devices: 14.2 us -> 14.6 us
    pallas_call x2, Pallas kernels: 2.5 us -> 1.5 us  [the longest x1 1.47 us: body(): pl.pallas_call(functools.partial(first_kernel, workers, (7, 6)), out_shap...]
    ppermute x10, starting transfers between devices: 14.2 us -> 14.6 us  [hop(): return lax.ppermute(value, axis, [(d, d ^ bit) for d in range(devices)])]
  transfers between devices with their start and end apart: 10 -> 10, of which waited for: 3 -> 3; matrix products, arithmetic and copies ran while one was open for 0% -> 0% of each run, Pallas kernels for 10% -> 6%
where the time goes in v8:
time: 26.2 us; the launch traced here: 26 us
  starting transfers between devices  14.6 us (56%)
  waiting for transfers between devices  5.9 us (23%)
  Pallas kernels  4.05 us (15%)
  between operations  1.39 us (5%)
    ppermute x10, starting transfers between devices, hop(): return lax.ppermute(value, axis, [(d, d ^ bit) for d in range(devices)])  14.6 us
    ppermute x10, waiting for transfers between devices, hop(): return lax.ppermute(value, axis, [(d, d ^ bit) for d in range(devices)])  5.9 us
    pallas_call x1, Pallas kernels, body(): pl.pallas_call(functools.partial(first_kernel, workers, (7, 6)), out_shap...  1.47 us
    pallas_call x1, Pallas kernels, body(): pl.pallas_call(left_kernel, out_shape=[block((half, width)), state, state...  1.08 us
    pallas_call x1, Pallas kernels, body(): pl.pallas_call(right_kernel, out_shape=[state] * 3, in_specs=[VMEM] * 10...  0.96 us
  transfers between devices with their start and end apart: 10, of which 3 were waited for; matrix products, arithmetic and copies ran while one was open for 0% of the time, Pallas kernels for 6%

profile of v8, /device:TPU:0, one launch (start us, length us, event | category | flops | bytes accessed | tf_op | source)
XLA Modules:
  0.0 26.0 jit_solution(17406631521523037617)
XLA Ops:
  0.6 0.0 copy-start
  0.6 1.5 %far_products.1 = (f32[2,128,256]{2,1,0:T(8,128)S(1)}, f32[2,128,256]{2,1,0:T(8,128)S(1)}, bf16[128,128]{1,0:T(8,128)(2,1)S(1)}, f32[8,128]{1,0:T(8,128)S(1)}) custom-call(s32[4]{0:T(128)} %counts.1, bf16[1,128,128]{2,1,0:T(8,128)(2,1)} %cotangent.1, bf16[1,128,4096]{2,1,0:T(8,128)(2,1)} %features.3), custom_call_target="tpu_custom_call" | custom-call | flops 33554432 | bytes 786432 | tf_op jit(solution)/shard_map/far_products/pallas_call | solution.py:254
  2.1 0.5 %collective-permute-start = (f32[2,128,256]{2,1,0:T(8,128)S(1)}, f32[2,128,256]{2,1,0:T(8,128)S(1)}, u32[]{:S(2)}, u32[]{:S(2)}) collective-permute-start(f32[2,128,256]{2,1,0:T(8,128)S(1)} %get-tuple-element.29), channel_id=1, source_target_pairs={{0,1},{1,0},{2,3},{3,2},{4,5},{5,4},{6,7},{7,6},{8,9},{9,8},{10,11... | collective-permute-start | bytes 786440 | tf_op jit(solution)/shard_map/ppermute | solution.py:217
  2.6 0.0 copy-done
  2.6 0.4 %rest_products.1 = (f32[6,128,256]{2,1,0:T(8,128)S(1)}, f32[6,128,256]{2,1,0:T(8,128)S(1)}) custom-call(bf16[128,128]{1,0:T(8,128)(2,1)S(1)} %get-tuple-element.25.masked, bf16[1,128,4096]{2,1,0:T(8,128)(2,1)S(1)} %copy-done), custom_call_target="tpu_custom_call" | custom-call | tf_op jit(solution)/shard_map/rest_products/pallas_call | solution.py:269
  3.0 0.8 %collective-permute-done.refs_1_ = f32[2,128,256]{2,1,0:T(8,128)S(1)} collective-permute-done((f32[2,128,256]{2,1,0:T(8,128)S(1)}, f32[2,128,256]{2,1,0:T(8,128)S(1)}, u32[]{:S(2)}, u32[]{:S(2)}) %collective-permute-start) | collective-permute-done | bytes 262176 | tf_op jit(solution)/shard_map/ppermute | solution.py:217
  3.8 0.4 %collective-permute-start.1 = (f32[6,128,256]{2,1,0:T(8,128)S(1)}, f32[6,128,256]{2,1,0:T(8,128)S(1)}, u32[]{:S(2)}, u32[]{:S(2)}) collective-permute-start(f32[6,128,256]{2,1,0:T(8,128)S(1)} %get-tuple-element.30), channel_id=1, source_target_pairs={{0,1},{1,0},{2,3},{3,2},{4,5},{5,4},{6,7},{7,6},{8,9},{9,8},{10,11... | collective-permute-start | bytes 2359304 | tf_op jit(solution)/shard_map/ppermute | solution.py:217
  4.3 2.7 %collective-permute-start.3 = (f32[1,128,256]{2,1,0:T(8,128)S(1)}, f32[1,128,256]{2,1,0:T(8,128)S(1)}, u32[]{:S(2)}, u32[]{:S(2)}) collective-permute-start(f32[1,128,256]{2,1,0:T(8,128)S(1)} %add_a1.1.after), channel_id=1, source_target_pairs={{0,2},{1,3},{2,0},{3,1},{4,6},{5,7},{6,4},{7,5},{8,10},{9,11},{10,... | collective-permute-start | bytes 393224 | tf_op jit(solution)/shard_map/ppermute | solution.py:217
  7.6 0.0 copy-done.1
  7.6 0.0 copy-done.4
  7.7 0.1 collective-permute-start.2
  7.8 1.9 %collective-permute-start.8 = (f32[128,128]{1,0:T(8,128)S(1)}, f32[128,128]{1,0:T(8,128)S(1)}, u32[]{:S(2)}, u32[]{:S(2)}) collective-permute-start(f32[128,128]{1,0:T(8,128)S(1)} %get-tuple-element.34.refs_2_), channel_id=1, source_target_pairs={{0,16},{8,24},{16,0},{24,8},{1,17},{9,25},{17,1},{25,9},{2,18},{10... | collective-permute-start | bytes 196616 | tf_op jit(solution)/shard_map/ppermute | solution.py:217
  9.8 0.0 collective-permute-done.1.refs_1_.come
  9.8 1.6 %collective-permute-start.7 = (f32[1,128,256]{2,1,0:T(8,128)S(1)}, f32[1,128,256]{2,1,0:T(8,128)S(1)}, u32[]{:S(2)}, u32[]{:S(2)}) collective-permute-start(f32[1,128,256]{2,1,0:T(8,128)S(1)} %add_n1.1), channel_id=1, source_target_pairs={{0,2},{1,3},{2,0},{3,1},{4,6},{5,7},{6,4},{7,5},{8,10},{9,11},{10,... | collective-permute-start | bytes 393224 | tf_op jit(solution)/shard_map/ppermute | solution.py:217
  11.4 0.0 collective-permute-done.3.refs_2_
  11.4 3.0 %collective-permute-start.6 = (f32[1,128,256]{2,1,0:T(8,128)S(1)}, f32[1,128,256]{2,1,0:T(8,128)S(1)}, u32[]{:S(2)}, u32[]{:S(2)}) collective-permute-start(f32[1,128,256]{2,1,0:T(8,128)S(1)} %add_c1.1.refs_3_.refs_2_), channel_id=1, source_target_pairs={{0,4},{1,5},{2,6},{3,7},{4,0},{5,1},{6,2},{7,3},{8,12},{9,13},{10,... | collective-permute-start | bytes 393224 | tf_op jit(solution)/shard_map/ppermute | solution.py:217
  14.4 1.6 %collective-permute-start.5 = (f32[1,128,256]{2,1,0:T(8,128)S(1)}, f32[1,128,256]{2,1,0:T(8,128)S(1)}, u32[]{:S(2)}, u32[]{:S(2)}) collective-permute-start(f32[1,128,256]{2,1,0:T(8,128)S(1)} %add_n2.1), channel_id=1, source_target_pairs={{0,2},{1,3},{2,0},{3,1},{4,6},{5,7},{6,4},{7,5},{8,10},{9,11},{10,... | collective-permute-start | bytes 393224 | tf_op jit(solution)/shard_map/ppermute | solution.py:217
  16.1 0.0 collective-permute-done.2.refs_2_
  16.1 0.0 copy-start.5
  16.1 1.1 %collective-permute-start.4 = (f32[1,128,256]{2,1,0:T(8,128)S(1)}, f32[1,128,256]{2,1,0:T(8,128)S(1)}, u32[]{:S(2)}, u32[]{:S(2)}) collective-permute-start(f32[1,128,256]{2,1,0:T(8,128)S(1)} %add_c2.1), channel_id=1, source_target_pairs={{0,4},{1,5},{2,6},{3,7},{4,0},{5,1},{6,2},{7,3},{8,12},{9,13},{10,... | collective-permute-start | bytes 393224 | tf_op jit(solution)/shard_map/ppermute | solution.py:217
  17.2 0.0 collective-permute-done.8
  17.2 1.6 %collective-permute-start.9 = (f32[128,128]{1,0:T(8,128)S(1)}, f32[128,128]{1,0:T(8,128)S(1)}, u32[]{:S(2)}, u32[]{:S(2)}) collective-permute-start(f32[128,128]{1,0:T(8,128)S(1)} %add.3.drift), channel_id=1, source_target_pairs={{0,8},{8,0},{16,24},{24,16},{1,9},{9,1},{17,25},{25,17},{2,10},{10... | collective-permute-start | bytes 196616 | tf_op jit(solution)/shard_map/ppermute | solution.py:217
  18.8 2.8 %collective-permute-done.9.other_drift = f32[128,128]{1,0:T(8,128)S(1)} collective-permute-done((f32[128,128]{1,0:T(8,128)S(1)}, f32[128,128]{1,0:T(8,128)S(1)}, u32[]{:S(2)}, u32[]{:S(2)}) %collective-permute-start.9) | collective-permute-done | bytes 65568 | tf_op jit(solution)/shard_map/ppermute | solution.py:217
  21.6 0.0 collective-permute-done.7.near
  21.6 0.0 collective-permute-done.6.far
  21.6 0.0 copy-done.2
  21.6 0.0 copy-done.3
  21.6 0.0 copy-done.5
  21.6 1.1 %left_step.1 = (f32[256,128]{1,0:T(8,128)S(1)}, f32[1,512,128]{2,1,0:T(8,128)}, f32[1,512,128]{2,1,0:T(8,128)}, f32[1,512,128]{2,1,0:T(8,128)}, f32[128,128]{1,0:T(8,128)}, /*index=5*/f32[128,128]{1,0:T(8,128)}) custom-call(f32[1,512,128]{2,1,0:T(8,128)S(1)} %copy-done.1, f32[1,512,128]{2,1,0:T(8,128)S(1)} %copy-done.2, f32[1,512,128]{2,1,0:T(8,128)S(1)} %copy-done.3, ...), custom_call_target="tpu_custom_call" | custom-call | flops 983040 | bytes 1310720 | tf_op jit(solution)/shard_map/left_step/pallas_call | solution.py:329
  22.7 2.4 %collective-permute-done.5.near = f32[1,128,256]{2,1,0:T(8,128)S(1)} collective-permute-done((f32[1,128,256]{2,1,0:T(8,128)S(1)}, f32[1,128,256]{2,1,0:T(8,128)S(1)}, u32[]{:S(2)}, u32[]{:S(2)}) %collective-permute-start.5) | collective-permute-done | bytes 131104 | tf_op jit(solution)/shard_map/ppermute | solution.py:217
  25.0 0.0 collective-permute-done.4.far
  25.0 1.0 %right_step.1 = (f32[1,512,128]{2,1,0:T(8,128)}, f32[1,512,128]{2,1,0:T(8,128)}, f32[1,512,128]{2,1,0:T(8,128)}) custom-call(f32[1,512,128]{2,1,0:T(8,128)S(1)} %copy-done.1, f32[1,512,128]{2,1,0:T(8,128)S(1)} %copy-done.2, f32[1,512,128]{2,1,0:T(8,128)S(1)} %copy-done.3, ...), custom_call_target="tpu_custom_call", output_to_operand_aliasing={{0}: (10, {}), {1}: (11, {}), {2}: (12, {})} | custom-call | tf_op jit(solution)/shard_map/right_step/pallas_call | solution.py:356
  (12 shorter events, 0.2 us)
Async XLA Ops:
  0.6 2.0 %copy-start = (bf16[1,128,4096]{2,1,0:T(8,128)(2,1)S(1)}, bf16[1,128,4096]{2,1,0:T(8,128)(2,1)}, u32[]{:S(2)}) copy-start(bf16[1,128,4096]{2,1,0:T(8,128)(2,1)} %features.3) | copy-start | bytes 3145732
  2.1 1.7 %collective-permute-start = (f32[2,128,256]{2,1,0:T(8,128)S(1)}, f32[2,128,256]{2,1,0:T(8,128)S(1)}, u32[]{:S(2)}, u32[]{:S(2)}) collective-permute-start(f32[2,128,256]{2,1,0:T(8,128)S(1)} %get-tuple-element.29), channel_id=1, source_target_pairs={{0,1},{1,0},{2,3},{3,2},{4,5},{5,4},{6,7},{7,6},{8,9},{9,8},{10,11... | collective-permute-start | bytes 786440 | tf_op jit(solution)/shard_map/ppermute | solution.py:217
  3.8 3.8 %copy-start.1 = (f32[1,512,128]{2,1,0:T(8,128)S(1)}, f32[1,512,128]{2,1,0:T(8,128)}, u32[]{:S(2)}) copy-start(f32[1,512,128]{2,1,0:T(8,128)} %params.5) | copy-start | bytes 786436
  3.8 3.8 %copy-start.4 = (f32[128,128]{1,0:T(8,128)S(1)}, f32[128,128]{1,0:T(8,128)}, u32[]{:S(2)}) copy-start(f32[128,128]{1,0:T(8,128)} %global_fragment.3) | copy-start | bytes 196612
  3.8 5.9 %collective-permute-start.1 = (f32[6,128,256]{2,1,0:T(8,128)S(1)}, f32[6,128,256]{2,1,0:T(8,128)S(1)}, u32[]{:S(2)}, u32[]{:S(2)}) collective-permute-start(f32[6,128,256]{2,1,0:T(8,128)S(1)} %get-tuple-element.30), channel_id=1, source_target_pairs={{0,1},{1,0},{2,3},{3,2},{4,5},{5,4},{6,7},{7,6},{8,9},{9,8},{10,11... | collective-permute-start | bytes 2359304 | tf_op jit(solution)/shard_map/ppermute | solution.py:217
  4.3 7.2 %collective-permute-start.3 = (f32[1,128,256]{2,1,0:T(8,128)S(1)}, f32[1,128,256]{2,1,0:T(8,128)S(1)}, u32[]{:S(2)}, u32[]{:S(2)}) collective-permute-start(f32[1,128,256]{2,1,0:T(8,128)S(1)} %add_a1.1.after), channel_id=1, source_target_pairs={{0,2},{1,3},{2,0},{3,1},{4,6},{5,7},{6,4},{7,5},{8,10},{9,11},{10,... | collective-permute-start | bytes 393224 | tf_op jit(solution)/shard_map/ppermute | solution.py:217
  7.7 8.4 %collective-permute-start.2 = (f32[1,128,256]{2,1,0:T(8,128)S(1)}, f32[1,128,256]{2,1,0:T(8,128)S(1)}, u32[]{:S(2)}, u32[]{:S(2)}) collective-permute-start(f32[1,128,256]{2,1,0:T(8,128)S(1)} %add_a2.1.refs_2_), channel_id=1, source_target_pairs={{0,2},{1,3},{2,0},{3,1},{4,6},{5,7},{6,4},{7,5},{8,10},{9,11},{10,... | collective-permute-start | bytes 393224 | tf_op jit(solution)/shard_map/ppermute | solution.py:217
  7.8 9.4 %collective-permute-start.8 = (f32[128,128]{1,0:T(8,128)S(1)}, f32[128,128]{1,0:T(8,128)S(1)}, u32[]{:S(2)}, u32[]{:S(2)}) collective-permute-start(f32[128,128]{1,0:T(8,128)S(1)} %get-tuple-element.34.refs_2_), channel_id=1, source_target_pairs={{0,16},{8,24},{16,0},{24,8},{1,17},{9,25},{17,1},{25,9},{2,18},{10... | collective-permute-start | bytes 196616 | tf_op jit(solution)/shard_map/ppermute | solution.py:217
  9.8 11.8 %collective-permute-start.7 = (f32[1,128,256]{2,1,0:T(8,128)S(1)}, f32[1,128,256]{2,1,0:T(8,128)S(1)}, u32[]{:S(2)}, u32[]{:S(2)}) collective-permute-start(f32[1,128,256]{2,1,0:T(8,128)S(1)} %add_n1.1), channel_id=1, source_target_pairs={{0,2},{1,3},{2,0},{3,1},{4,6},{5,7},{6,4},{7,5},{8,10},{9,11},{10,... | collective-permute-start | bytes 393224 | tf_op jit(solution)/shard_map/ppermute | solution.py:217
  11.4 10.1 %collective-permute-start.6 = (f32[1,128,256]{2,1,0:T(8,128)S(1)}, f32[1,128,256]{2,1,0:T(8,128)S(1)}, u32[]{:S(2)}, u32[]{:S(2)}) collective-permute-start(f32[1,128,256]{2,1,0:T(8,128)S(1)} %add_c1.1.refs_3_.refs_2_), channel_id=1, source_target_pairs={{0,4},{1,5},{2,6},{3,7},{4,0},{5,1},{6,2},{7,3},{8,12},{9,13},{10,... | collective-permute-start | bytes 393224 | tf_op jit(solution)/shard_map/ppermute | solution.py:217
  14.4 10.6 %collective-permute-start.5 = (f32[1,128,256]{2,1,0:T(8,128)S(1)}, f32[1,128,256]{2,1,0:T(8,128)S(1)}, u32[]{:S(2)}, u32[]{:S(2)}) collective-permute-start(f32[1,128,256]{2,1,0:T(8,128)S(1)} %add_n2.1), channel_id=1, source_target_pairs={{0,2},{1,3},{2,0},{3,1},{4,6},{5,7},{6,4},{7,5},{8,10},{9,11},{10,... | collective-permute-start | bytes 393224 | tf_op jit(solution)/shard_map/ppermute | solution.py:217
  16.1 5.5 %copy-start.2 = (f32[1,512,128]{2,1,0:T(8,128)S(1)}, f32[1,512,128]{2,1,0:T(8,128)}, u32[]{:S(2)}) copy-start(f32[1,512,128]{2,1,0:T(8,128)} %first.3) | copy-start | bytes 786436
  16.1 5.5 %copy-start.3 = (f32[1,512,128]{2,1,0:T(8,128)S(1)}, f32[1,512,128]{2,1,0:T(8,128)}, u32[]{:S(2)}) copy-start(f32[1,512,128]{2,1,0:T(8,128)} %second.3) | copy-start | bytes 786436
  16.1 5.5 %copy-start.5 = (f32[128,128]{1,0:T(8,128)S(1)}, f32[128,128]{1,0:T(8,128)}, u32[]{:S(2)}) copy-start(f32[128,128]{1,0:T(8,128)} %outer_momentum.1) | copy-start | bytes 196612
  16.1 8.9 %collective-permute-start.4 = (f32[1,128,256]{2,1,0:T(8,128)S(1)}, f32[1,128,256]{2,1,0:T(8,128)S(1)}, u32[]{:S(2)}, u32[]{:S(2)}) collective-permute-start(f32[1,128,256]{2,1,0:T(8,128)S(1)} %add_c2.1), channel_id=1, source_target_pairs={{0,4},{1,5},{2,6},{3,7},{4,0},{5,1},{6,2},{7,3},{8,12},{9,13},{10,... | collective-permute-start | bytes 393224 | tf_op jit(solution)/shard_map/ppermute | solution.py:217
  17.2 4.3 %collective-permute-start.9 = (f32[128,128]{1,0:T(8,128)S(1)}, f32[128,128]{1,0:T(8,128)S(1)}, u32[]{:S(2)}, u32[]{:S(2)}) collective-permute-start(f32[128,128]{1,0:T(8,128)S(1)} %add.3.drift), channel_id=1, source_target_pairs={{0,8},{8,0},{16,24},{24,16},{1,9},{9,1},{17,25},{25,17},{2,10},{10... | collective-permute-start | bytes 196616 | tf_op jit(solution)/shard_map/ppermute | solution.py:217

commit v9 on v7

--- a/solution.py
+++ b/solution.py
@@ -67,13 +67,16 @@
             into[side] = product(masked[...], held[slot, :, side * half : (side + 1) * half])
 
 
-def rest_kernel(masked, features, *targets):
-    half = targets[0].shape[2]
-    places = [(4, 0, 0, 4), (4, 1, 0, 5), (2, 0, 0, 2), (2, 1, 0, 3), (0, 0, 0, 0), (0, 1, 0, 1)]
-    for q, side, into, at in places:
-        for core in (1, 0):
-            columns = columns_of(q + core, 2 * half, side * half, half)
-            targets[into + 1 - core][at] = product(masked[...], features[0, :, columns])
+def rest_kernel(masked, features, away, kept, held, sems):
+    half = away.shape[2]
+    order = [(q + core, at) for q, at in ((4, 4), (2, 2), (0, 0)) for core in (1, 0)]
+    sources = [features.at[0, :, columns_of(q, 2 * half, 0, 2 * half)] for q, _ in order]
+    blocks = fetch(sources, [held.at[slot] for slot in range(len(order))], sems)
+    for slot, (q, at) in enumerate(order):
+        blocks[slot].wait()
+        for side in (0, 1):
+            value = product(masked[...], held[slot, :, side * half : (side + 1) * half])
+            (away if q & 1 else kept)[at + side] = value
 
 
 def drift_kernel(
@@ -285,12 +288,13 @@
         away, kept = pl.pallas_call(
             rest_kernel,
             out_shape=[block((6, width, half))] * 2,
-            in_specs=[VMEM] * 2,
+            in_specs=[VMEM, HBM],
             out_specs=[VMEM] * 2,
+            scratch_shapes=[pltpu.VMEM((6, tokens, rows), features.dtype), pltpu.SemaphoreType.DMA((6,))],
             compiler_params=room,
             cost_estimate=free,
             name="rest_products",
-        )(masked, features)
+        )(masked, far_features)
 
         def add(*terms, name, count=1):
             picks = [pick for _, pick in terms]
@@ -334,8 +338,8 @@
         passed = add((kept, part(4)), (come, part(4)), (far_left, part(0)), name="add_c1")
         far_left = hop(passed, "fsdp", devices, 4)
         near_left = add((kept, part(2)), (come, part(2)), (sent, None), name="add_n1")
-        far_right = add((kept, part(5)), (come, part(5)), (far_right, part(0)), (passed, None), name="add_c2")
-        near_right = add((kept, part(3)), (come, part(3)), (passed, None), name="add_n2")
+        far_right = add((kept, part(5)), (come, part(5)), (far_right, part(0)), (near_left, None), name="add_c2")
+        near_right = add((kept, part(3)), (come, part(3)), (far_right, None), name="add_n2")
         drift, _ = lax.optimization_barrier((drift, sent))
         bit = workers // 2
         drifts = (drift, hop(drift, "worker", workers, bit))

time: 26.6 us -> 27.4 us (1.030)
  waiting for transfers between devices: 5.71 us -> 3.96 us
  Pallas kernels: 5.07 us -> 6.8 us
  starting transfers between devices: 14.2 us -> 15 us
    pallas_call x1, Pallas kernels: 0.4 us -> 2.22 us  [body(): pl.pallas_call(rest_kernel, out_shape=[block((6, width, half))] * 2, in_s...]
    ppermute x10, waiting for transfers between devices: 5.71 us -> 3.96 us  [hop(): return lax.ppermute(value, axis, [(d, d ^ bit) for d in range(devices)])]
    ppermute x10, starting transfers between devices: 14.2 us -> 15 us  [hop(): return lax.ppermute(value, axis, [(d, d ^ bit) for d in range(devices)])]
  transfers between devices with their start and end apart: 10 -> 10, of which waited for: 3 -> 4; matrix products, arithmetic and copies ran while one was open for 0% -> 0% of each run, Pallas kernels for 10% -> 16%
where the time goes in v9:
time: 27.4 us; the launch traced here: 27.2 us
  starting transfers between devices  15 us (55%)
  Pallas kernels  6.8 us (25%)
  waiting for transfers between devices  3.96 us (14%)
  between operations  1.43 us (5%)
    ppermute x10, starting transfers between devices, hop(): return lax.ppermute(value, axis, [(d, d ^ bit) for d in range(devices)])  15 us
    ppermute x10, waiting for transfers between devices, hop(): return lax.ppermute(value, axis, [(d, d ^ bit) for d in range(devices)])  3.96 us
    pallas_call x1, Pallas kernels, body(): pl.pallas_call(rest_kernel, out_shape=[block((6, width, half))] * 2, in_s...  2.22 us
    pallas_call x1, Pallas kernels, body(): pl.pallas_call(functools.partial(first_kernel, (7, 6)), out_shape=[block(...  1.38 us
    pallas_call x1, Pallas kernels, body(): pl.pallas_call(left_kernel, out_shape=[block((half, width)), state, state...  1.08 us
    pallas_call x1, Pallas kernels, body(): pl.pallas_call(functools.partial(drift_kernel, workers), out_shape=[piece...  1.03 us
    pallas_call x1, Pallas kernels, body(): pl.pallas_call(right_kernel, out_shape=[state] * 3, in_specs=[VMEM] * 10...  0.96 us
  transfers between devices with their start and end apart: 10, of which 4 were waited for; matrix products, arithmetic and copies ran while one was open for 0% of the time, Pallas kernels for 16%

profile of v9, /device:TPU:0, one launch (start us, length us, event | category | flops | bytes accessed | tf_op | source)
XLA Modules:
  0.0 27.2 jit_solution(15844396266519946980)
XLA Ops:
  0.6 1.4 %far_products.1 = (f32[2,128,256]{2,1,0:T(8,128)S(1)}, f32[2,128,256]{2,1,0:T(8,128)S(1)}, bf16[128,128]{1,0:T(8,128)(2,1)S(1)}) custom-call(s32[4]{0:T(128)} %counts.3, bf16[1,128,128]{2,1,0:T(8,128)(2,1)} %cotangent.1, bf16[1,128,4096]{2,1,0:T(8,128)(2,1)} %features.3), custom_call_target="tpu_custom_call" | custom-call | flops 33554432 | bytes 786432 | tf_op jit(solution)/shard_map/far_products/pallas_call | solution.py:273
  2.0 0.5 %collective-permute-start = (f32[2,128,256]{2,1,0:T(8,128)S(1)}, f32[2,128,256]{2,1,0:T(8,128)S(1)}, u32[]{:S(2)}, u32[]{:S(2)}) collective-permute-start(f32[2,128,256]{2,1,0:T(8,128)S(1)} %get-tuple-element.30), channel_id=1, source_target_pairs={{0,1},{1,0},{2,3},{3,2},{4,5},{5,4},{6,7},{7,6},{8,9},{9,8},{10,11... | collective-permute-start | bytes 786440 | tf_op jit(solution)/shard_map/ppermute | solution.py:226
  2.5 2.2 %rest_products.1 = (f32[6,128,256]{2,1,0:T(8,128)S(1)}, f32[6,128,256]{2,1,0:T(8,128)S(1)}) custom-call(bf16[128,128]{1,0:T(8,128)(2,1)S(1)} %get-tuple-element.26.masked, bf16[1,128,4096]{2,1,0:T(8,128)(2,1)} %features.3), custom_call_target="tpu_custom_call" | custom-call | tf_op jit(solution)/shard_map/rest_products/pallas_call | solution.py:288
  4.8 0.0 collective-permute-done.refs_1_
  4.8 0.1 collective-permute-start.1
  4.9 3.0 %collective-permute-start.5 = (f32[1,128,256]{2,1,0:T(8,128)S(1)}, f32[1,128,256]{2,1,0:T(8,128)S(1)}, u32[]{:S(2)}, u32[]{:S(2)}) collective-permute-start(f32[1,128,256]{2,1,0:T(8,128)S(1)} %add_a1.1.after), channel_id=1, source_target_pairs={{0,2},{1,3},{2,0},{3,1},{4,6},{5,7},{6,4},{7,5},{8,10},{9,11},{10,... | collective-permute-start | bytes 393224 | tf_op jit(solution)/shard_map/ppermute | solution.py:226
  8.6 1.0 %drift.1 = (f32[128,128]{1,0:T(8,128)S(1)}, f32[512,128]{1,0:T(8,128)S(1)}, f32[8,128]{1,0:T(8,128)S(1)}, f32[8,128]{1,0:T(8,128)S(1)}) custom-call(s32[4]{0:T(128)} %counts.3, s32[1]{0:T(128)S(6)} %copy.20.fragment, f32[1,512,128]{2,1,0:T(8,128)} %params.5, f32[128,128]{1,0:T(8,128)} %global_fragment.3, f32[1,128,256]{2,1,0:T(8,128)S(1)} %add_a1.1.after), custom_call_target="tpu_custom_call" | custom-call | tf_op jit(solution)/shard_map/drift/pallas_call | solution.py:320
  9.7 0.1 collective-permute-start.2
  9.7 2.0 %collective-permute-start.8 = (f32[128,128]{1,0:T(8,128)S(1)}, f32[128,128]{1,0:T(8,128)S(1)}, u32[]{:S(2)}, u32[]{:S(2)}) collective-permute-start(f32[128,128]{1,0:T(8,128)S(1)} %get-tuple-element.36.refs_2_), channel_id=1, source_target_pairs={{0,16},{8,24},{16,0},{24,8},{1,17},{9,25},{17,1},{25,9},{2,18},{10... | collective-permute-start | bytes 196616 | tf_op jit(solution)/shard_map/ppermute | solution.py:226
  11.7 0.1 collective-permute-done.5.refs_2_
  11.8 0.0 collective-permute-done.1.refs_1_.come
  11.9 2.7 %collective-permute-start.6 = (f32[1,128,256]{2,1,0:T(8,128)S(1)}, f32[1,128,256]{2,1,0:T(8,128)S(1)}, u32[]{:S(2)}, u32[]{:S(2)}) collective-permute-start(f32[1,128,256]{2,1,0:T(8,128)S(1)} %add_c1.1), channel_id=1, source_target_pairs={{0,4},{1,5},{2,6},{3,7},{4,0},{5,1},{6,2},{7,3},{8,12},{9,13},{10,... | collective-permute-start | bytes 393224 | tf_op jit(solution)/shard_map/ppermute | solution.py:226
  14.6 2.5 %collective-permute-start.7 = (f32[1,128,256]{2,1,0:T(8,128)S(1)}, f32[1,128,256]{2,1,0:T(8,128)S(1)}, u32[]{:S(2)}, u32[]{:S(2)}) collective-permute-start(f32[1,128,256]{2,1,0:T(8,128)S(1)} %add_n1.1.refs_3_), channel_id=1, source_target_pairs={{0,2},{1,3},{2,0},{3,1},{4,6},{5,7},{6,4},{7,5},{8,10},{9,11},{10,... | collective-permute-start | bytes 393224 | tf_op jit(solution)/shard_map/ppermute | solution.py:226
  17.1 0.0 collective-permute-done.2.refs_2_
  17.1 0.0 copy-start
  17.1 0.0 copy-start.1
  17.1 0.0 copy-start.2
  17.1 0.0 copy-start.3
  17.2 0.0 copy-start.4
  17.2 0.1 collective-permute-start.4
  17.3 2.5 %collective-permute-start.3 = (f32[1,128,256]{2,1,0:T(8,128)S(1)}, f32[1,128,256]{2,1,0:T(8,128)S(1)}, u32[]{:S(2)}, u32[]{:S(2)}) collective-permute-start(f32[1,128,256]{2,1,0:T(8,128)S(1)} %add_c2.1.refs_2_), channel_id=1, source_target_pairs={{0,4},{1,5},{2,6},{3,7},{4,0},{5,1},{6,2},{7,3},{8,12},{9,13},{10,... | collective-permute-start | bytes 393224 | tf_op jit(solution)/shard_map/ppermute | solution.py:226
  19.8 0.0 collective-permute-done.8
  19.8 1.6 %collective-permute-start.9 = (f32[128,128]{1,0:T(8,128)S(1)}, f32[128,128]{1,0:T(8,128)S(1)}, u32[]{:S(2)}, u32[]{:S(2)}) collective-permute-start(f32[128,128]{1,0:T(8,128)S(1)} %add.3.drift), channel_id=1, source_target_pairs={{0,8},{8,0},{16,24},{24,16},{1,9},{9,1},{17,25},{25,17},{2,10},{10... | collective-permute-start | bytes 196616 | tf_op jit(solution)/shard_map/ppermute | solution.py:226
  21.3 2.8 %collective-permute-done.9.other_drift = f32[128,128]{1,0:T(8,128)S(1)} collective-permute-done((f32[128,128]{1,0:T(8,128)S(1)}, f32[128,128]{1,0:T(8,128)S(1)}, u32[]{:S(2)}, u32[]{:S(2)}) %collective-permute-start.9) | collective-permute-done | bytes 65568 | tf_op jit(solution)/shard_map/ppermute | solution.py:226
  24.1 0.0 collective-permute-done.6.far
  24.1 0.7 %collective-permute-done.7.near = f32[1,128,256]{2,1,0:T(8,128)S(1)} collective-permute-done((f32[1,128,256]{2,1,0:T(8,128)S(1)}, f32[1,128,256]{2,1,0:T(8,128)S(1)}, u32[]{:S(2)}, u32[]{:S(2)}) %collective-permute-start.7) | collective-permute-done | bytes 131104 | tf_op jit(solution)/shard_map/ppermute | solution.py:226
  24.9 0.0 copy-done.2
  24.9 0.0 copy-done.3
  24.9 1.1 %left_step.1 = (f32[256,128]{1,0:T(8,128)S(1)}, f32[1,512,128]{2,1,0:T(8,128)}, f32[1,512,128]{2,1,0:T(8,128)}, f32[1,512,128]{2,1,0:T(8,128)}, f32[128,128]{1,0:T(8,128)}, /*index=5*/f32[128,128]{1,0:T(8,128)}) custom-call(f32[1,512,128]{2,1,0:T(8,128)S(1)} %copy-done, f32[1,512,128]{2,1,0:T(8,128)S(1)} %copy-done.1, f32[1,512,128]{2,1,0:T(8,128)S(1)} %copy-done.2, ...), custom_call_target="tpu_custom_call" | custom-call | flops 983040 | bytes 1310720 | tf_op jit(solution)/shard_map/left_step/pallas_call | solution.py:356
  26.0 0.3 %collective-permute-done.4.near = f32[1,128,256]{2,1,0:T(8,128)S(1)} collective-permute-done((f32[1,128,256]{2,1,0:T(8,128)S(1)}, f32[1,128,256]{2,1,0:T(8,128)S(1)}, u32[]{:S(2)}, u32[]{:S(2)}) %collective-permute-start.4) | collective-permute-done | bytes 131104 | tf_op jit(solution)/shard_map/ppermute | solution.py:226
  26.3 0.0 collective-permute-done.3.far
  26.3 1.0 %right_step.1 = (f32[1,512,128]{2,1,0:T(8,128)}, f32[1,512,128]{2,1,0:T(8,128)}, f32[1,512,128]{2,1,0:T(8,128)}) custom-call(f32[1,512,128]{2,1,0:T(8,128)S(1)} %copy-done, f32[1,512,128]{2,1,0:T(8,128)S(1)} %copy-done.1, f32[1,512,128]{2,1,0:T(8,128)S(1)} %copy-done.2, ...), custom_call_target="tpu_custom_call", output_to_operand_aliasing={{0}: (10, {}), {1}: (11, {}), {2}: (12, {})} | custom-call | tf_op jit(solution)/shard_map/right_step/pallas_call | solution.py:384
  (10 shorter events, 0.1 us)
Async XLA Ops:
  2.0 2.8 %collective-permute-start = (f32[2,128,256]{2,1,0:T(8,128)S(1)}, f32[2,128,256]{2,1,0:T(8,128)S(1)}, u32[]{:S(2)}, u32[]{:S(2)}) collective-permute-start(f32[2,128,256]{2,1,0:T(8,128)S(1)} %get-tuple-element.30), channel_id=1, source_target_pairs={{0,1},{1,0},{2,3},{3,2},{4,5},{5,4},{6,7},{7,6},{8,9},{9,8},{10,11... | collective-permute-start | bytes 786440 | tf_op jit(solution)/shard_map/ppermute | solution.py:226
  4.8 7.0 %collective-permute-start.1 = (f32[6,128,256]{2,1,0:T(8,128)S(1)}, f32[6,128,256]{2,1,0:T(8,128)S(1)}, u32[]{:S(2)}, u32[]{:S(2)}) collective-permute-start(f32[6,128,256]{2,1,0:T(8,128)S(1)} %get-tuple-element.31), channel_id=1, source_target_pairs={{0,1},{1,0},{2,3},{3,2},{4,5},{5,4},{6,7},{7,6},{8,9},{9,8},{10,11... | collective-permute-start | bytes 2359304 | tf_op jit(solution)/shard_map/ppermute | solution.py:226
  4.9 6.9 %collective-permute-start.5 = (f32[1,128,256]{2,1,0:T(8,128)S(1)}, f32[1,128,256]{2,1,0:T(8,128)S(1)}, u32[]{:S(2)}, u32[]{:S(2)}) collective-permute-start(f32[1,128,256]{2,1,0:T(8,128)S(1)} %add_a1.1.after), channel_id=1, source_target_pairs={{0,2},{1,3},{2,0},{3,1},{4,6},{5,7},{6,4},{7,5},{8,10},{9,11},{10,... | collective-permute-start | bytes 393224 | tf_op jit(solution)/shard_map/ppermute | solution.py:226
  9.7 7.4 %collective-permute-start.2 = (f32[1,128,256]{2,1,0:T(8,128)S(1)}, f32[1,128,256]{2,1,0:T(8,128)S(1)}, u32[]{:S(2)}, u32[]{:S(2)}) collective-permute-start(f32[1,128,256]{2,1,0:T(8,128)S(1)} %add_a2.1.refs_2_), channel_id=1, source_target_pairs={{0,2},{1,3},{2,0},{3,1},{4,6},{5,7},{6,4},{7,5},{8,10},{9,11},{10,... | collective-permute-start | bytes 393224 | tf_op jit(solution)/shard_map/ppermute | solution.py:226
  9.7 10.0 %collective-permute-start.8 = (f32[128,128]{1,0:T(8,128)S(1)}, f32[128,128]{1,0:T(8,128)S(1)}, u32[]{:S(2)}, u32[]{:S(2)}) collective-permute-start(f32[128,128]{1,0:T(8,128)S(1)} %get-tuple-element.36.refs_2_), channel_id=1, source_target_pairs={{0,16},{8,24},{16,0},{24,8},{1,17},{9,25},{17,1},{25,9},{2,18},{10... | collective-permute-start | bytes 196616 | tf_op jit(solution)/shard_map/ppermute | solution.py:226
  11.9 12.3 %collective-permute-start.6 = (f32[1,128,256]{2,1,0:T(8,128)S(1)}, f32[1,128,256]{2,1,0:T(8,128)S(1)}, u32[]{:S(2)}, u32[]{:S(2)}) collective-permute-start(f32[1,128,256]{2,1,0:T(8,128)S(1)} %add_c1.1), channel_id=1, source_target_pairs={{0,4},{1,5},{2,6},{3,7},{4,0},{5,1},{6,2},{7,3},{8,12},{9,13},{10,... | collective-permute-start | bytes 393224 | tf_op jit(solution)/shard_map/ppermute | solution.py:226
  14.6 10.3 %collective-permute-start.7 = (f32[1,128,256]{2,1,0:T(8,128)S(1)}, f32[1,128,256]{2,1,0:T(8,128)S(1)}, u32[]{:S(2)}, u32[]{:S(2)}) collective-permute-start(f32[1,128,256]{2,1,0:T(8,128)S(1)} %add_n1.1.refs_3_), channel_id=1, source_target_pairs={{0,2},{1,3},{2,0},{3,1},{4,6},{5,7},{6,4},{7,5},{8,10},{9,11},{10,... | collective-permute-start | bytes 393224 | tf_op jit(solution)/shard_map/ppermute | solution.py:226
  17.1 7.8 %copy-start = (f32[1,512,128]{2,1,0:T(8,128)S(1)}, f32[1,512,128]{2,1,0:T(8,128)}, u32[]{:S(2)}) copy-start(f32[1,512,128]{2,1,0:T(8,128)} %params.5) | copy-start | bytes 786436
  17.1 7.8 %copy-start.1 = (f32[1,512,128]{2,1,0:T(8,128)S(1)}, f32[1,512,128]{2,1,0:T(8,128)}, u32[]{:S(2)}) copy-start(f32[1,512,128]{2,1,0:T(8,128)} %first.3) | copy-start | bytes 786436
  17.1 7.8 %copy-start.2 = (f32[1,512,128]{2,1,0:T(8,128)S(1)}, f32[1,512,128]{2,1,0:T(8,128)}, u32[]{:S(2)}) copy-start(f32[1,512,128]{2,1,0:T(8,128)} %second.3) | copy-start | bytes 786436
  17.1 7.7 %copy-start.3 = (f32[128,128]{1,0:T(8,128)S(1)}, f32[128,128]{1,0:T(8,128)}, u32[]{:S(2)}) copy-start(f32[128,128]{1,0:T(8,128)} %global_fragment.3) | copy-start | bytes 196612
  17.2 7.7 %copy-start.4 = (f32[128,128]{1,0:T(8,128)S(1)}, f32[128,128]{1,0:T(8,128)}, u32[]{:S(2)}) copy-start(f32[128,128]{1,0:T(8,128)} %outer_momentum.1) | copy-start | bytes 196612
  17.2 9.1 %collective-permute-start.4 = (f32[1,128,256]{2,1,0:T(8,128)S(1)}, f32[1,128,256]{2,1,0:T(8,128)S(1)}, u32[]{:S(2)}, u32[]{:S(2)}) collective-permute-start(f32[1,128,256]{2,1,0:T(8,128)S(1)} %add_n2.1), channel_id=1, source_target_pairs={{0,2},{1,3},{2,0},{3,1},{4,6},{5,7},{6,4},{7,5},{8,10},{9,11},{10,... | collective-permute-start | bytes 393224 | tf_op jit(solution)/shard_map/ppermute | solution.py:226
  17.3 9.0 %collective-permute-start.3 = (f32[1,128,256]{2,1,0:T(8,128)S(1)}, f32[1,128,256]{2,1,0:T(8,128)S(1)}, u32[]{:S(2)}, u32[]{:S(2)}) collective-permute-start(f32[1,128,256]{2,1,0:T(8,128)S(1)} %add_c2.1.refs_2_), channel_id=1, source_target_pairs={{0,4},{1,5},{2,6},{3,7},{4,0},{5,1},{6,2},{7,3},{8,12},{9,13},{10,... | collective-permute-start | bytes 393224 | tf_op jit(solution)/shard_map/ppermute | solution.py:226
  19.8 4.3 %collective-permute-start.9 = (f32[128,128]{1,0:T(8,128)S(1)}, f32[128,128]{1,0:T(8,128)S(1)}, u32[]{:S(2)}, u32[]{:S(2)}) collective-permute-start(f32[128,128]{1,0:T(8,128)S(1)} %add.3.drift), channel_id=1, source_target_pairs={{0,8},{8,0},{16,24},{24,16},{1,9},{9,1},{17,25},{25,17},{2,10},{10... | collective-permute-start | bytes 196616 | tf_op jit(solution)/shard_map/ppermute | solution.py:226

commit v10 on v8

--- a/solution.py
+++ b/solution.py
@@ -9,6 +9,7 @@
 
 FRAGS = 4
 LANES = 128
+SPARE = 8
 
 BETA_ONE = 0.9
 BETA_TWO = 0.95
@@ -112,6 +113,16 @@
     return global_fragment - OUTER_RATE * (pseudo_grad + NESTEROV * momentum), momentum
 
 
+def near_kernel(first, kept, come, *refs):
+    out = refs[-1]
+    rows = kept.shape[1]
+    if first:
+        out[0, :rows] = kept[2] + come[2]
+        out[0, rows:] = kept[3, :SPARE] + come[3, :SPARE]
+    else:
+        out[0] = kept[3, SPARE:] + come[3, SPARE:]
+
+
 def half_step(half, states, sums, info, held):
     params, first, second = states
     kept, come, far, near = sums
@@ -119,7 +130,7 @@
     rows = kept.shape[2]
     for lane in range(0, rows, LANES):
         lanes, there = pl.ds(lane, LANES), pl.ds(half * rows + lane, LANES)
-        summed = kept[half, :, lanes] + come[half, :, lanes] + near[0, :, lanes] + far[0, :, lanes]
+        summed = kept[half, :, lanes] + come[half, :, lanes] + near(lanes) + far[0, :, lanes]
         inner, held_first[lanes, :], held_second[lanes, :] = adam(
             params[0, there, :], first[0, there, :], second[0, there, :], summed.T * info[1:2, :]
         )
@@ -168,7 +179,7 @@
     for at in range(FRAGS):
         spread[pl.ds(at, fresh.shape[0], stride=FRAGS), :] = fresh
     for lanes, there, value in half_step(
-        0, (params, first, second), (kept, come, far, near), info, (held_first, held_second)
+        0, (params, first, second), (kept, come, far, lambda lanes: near[0, : kept.shape[1], lanes]), info, (held_first, held_second)
     ):
         held_params[lanes, :] = scale[there, :] * value + (1.0 - scale[there, :]) * spread[there, :]
         for source, target in ((held_first, new_first), (held_second, new_second), (held_params, new_params)):
@@ -187,6 +198,7 @@
     come,
     far,
     near,
+    other_near,
     info,
     scale,
     mix,
@@ -203,8 +215,12 @@
 ):
     del left_params, left_first, left_second
     copies = []
+
+    def joined(lanes):
+        return jnp.concatenate([near[0, kept.shape[1] :, lanes], other_near[0, :, lanes]])
+
     for lanes, there, value in half_step(
-        1, (params, first, second), (kept, come, far, near), info, (held_first, held_second)
+        1, (params, first, second), (kept, come, far, joined), info, (held_first, held_second)
     ):
         held_params[lanes, :] = scale[there, :] * value + mix[lanes, :]
         for source, target in ((held_first, new_first), (held_second, new_second), (held_params, new_params)):
@@ -291,9 +307,20 @@
         def part(number, count=1):
             return slice(number, number + count)
 
+        def near_sum(first, after):
+            return pl.pallas_call(
+                functools.partial(near_kernel, first),
+                out_shape=block((1, width + SPARE if first else width - SPARE, half)),
+                in_specs=[VMEM, VMEM, ANY],
+                out_specs=VMEM,
+                compiler_params=room,
+                cost_estimate=free,
+                name="add_n1" if first else "add_n2",
+            )(kept, come, after)
+
         state, piece = block(params.shape), block(global_fragment.shape)
         come_far = hop(away_far, "fsdp", devices, 1)
-        sent = add((kept_far, part(0)), (come_far, part(0)), name="add_a1")
+        sent = add((kept_far, part(0)), (come_far, part(0)), (fragment_index, None), name="add_a1")
         far_left = hop(sent, "fsdp", devices, 2)
         away, _ = lax.optimization_barrier((away, sent))
         come = hop(away, "fsdp", devices, 1)
@@ -306,13 +333,13 @@
             cost_estimate=free,
             name="drift",
         )(info, fragment_index, params, global_fragment, sent)
-        sent = add((kept_far, part(1)), (come_far, part(1)), (drift, None), name="add_a2")
+        sent = add((kept_far, part(1)), (come_far, part(1)), name="add_a2")
         far_right = hop(sent, "fsdp", devices, 2)
         passed = add((kept, part(4)), (come, part(4)), (far_left, part(0)), name="add_c1")
         far_left = hop(passed, "fsdp", devices, 4)
-        near_left = add((kept, part(2)), (come, part(2)), (sent, None), name="add_n1")
+        near_left = near_sum(True, sent)
         far_right = add((kept, part(5)), (come, part(5)), (far_right, part(0)), (passed, None), name="add_c2")
-        near_right = add((kept, part(3)), (come, part(3)), (passed, None), name="add_n2")
+        near_right = near_sum(False, far_right)
         drift, _ = lax.optimization_barrier((drift, sent))
         bit = workers // 2
         drifts = (drift, hop(drift, "worker", workers, bit))
@@ -356,14 +383,14 @@
         new_params, new_first, new_second = pl.pallas_call(
             right_kernel,
             out_shape=[state] * 3,
-            in_specs=[VMEM] * 10 + [HBM] * 3,
+            in_specs=[VMEM] * 11 + [HBM] * 3,
             out_specs=[HBM] * 3,
-            input_output_aliases={10: 0, 11: 1, 12: 2},
+            input_output_aliases={11: 0, 12: 1, 13: 2},
             scratch_shapes=[held_half] * 3 + [pltpu.SemaphoreType.DMA((3 * groups,))],
             compiler_params=room,
             cost_estimate=free,
             name="right_step",
-        )(params, first, second, kept, come, far_right, near_right, info, scale, mix, *results)
+        )(params, first, second, kept, come, far_right, near_left, near_right, info, scale, mix, *results)
         return new_params, new_first, new_second, new_global, new_momentum
 
     return body

time: 26.2 us -> 26.9 us (1.027)
  starting transfers between devices: 14.6 us -> 17.8 us
  waiting for transfers between devices: 5.9 us -> 3.38 us
    ppermute x10, starting transfers between devices: 14.6 us -> 17.8 us  [hop(): return lax.ppermute(value, axis, [(d, d ^ bit) for d in range(devices)])]
    ppermute x10, waiting for transfers between devices: 5.9 us -> 3.38 us  [hop(): return lax.ppermute(value, axis, [(d, d ^ bit) for d in range(devices)])]
    pallas_call x1 -> x3, Pallas kernels: 0.96 us -> 1.02 us  [the longest x1 0.99 us: body(): pl.pallas_call(right_kernel, out_shape=[state] * 3, in_specs=[VMEM] * 11...]
where the time goes in v10:
time: 26.9 us; the launch traced here: 26.8 us
  starting transfers between devices  17.8 us (66%)
  Pallas kernels  4.09 us (15%)
  waiting for transfers between devices  3.38 us (13%)
  between operations  1.43 us (5%)
    ppermute x10, starting transfers between devices, hop(): return lax.ppermute(value, axis, [(d, d ^ bit) for d in range(devices)])  17.8 us
    ppermute x10, waiting for transfers between devices, hop(): return lax.ppermute(value, axis, [(d, d ^ bit) for d in range(devices)])  3.38 us
    pallas_call x1, Pallas kernels, body(): pl.pallas_call(functools.partial(first_kernel, workers, (7, 6)), out_shap...  1.47 us
    pallas_call x1, Pallas kernels, body(): pl.pallas_call(left_kernel, out_shape=[block((half, width)), state, state...  1.09 us
    pallas_call x1, Pallas kernels, body(): pl.pallas_call(right_kernel, out_shape=[state] * 3, in_specs=[VMEM] * 11...  0.99 us
  transfers between devices with their start and end apart: 10, of which 3 were waited for; matrix products, arithmetic and copies ran while one was open for 0% of the time, Pallas kernels for 6%

profile of v10, /device:TPU:0, one launch (start us, length us, event | category | flops | bytes accessed | tf_op | source)
XLA Modules:
  0.0 26.8 jit_solution(396321033561947515)
XLA Ops:
  0.6 0.0 copy-start
  0.6 1.5 %far_products.1 = (f32[2,128,256]{2,1,0:T(8,128)S(1)}, f32[2,128,256]{2,1,0:T(8,128)S(1)}, bf16[128,128]{1,0:T(8,128)(2,1)S(1)}, f32[8,128]{1,0:T(8,128)S(1)}) custom-call(s32[4]{0:T(128)} %counts.1, bf16[1,128,128]{2,1,0:T(8,128)(2,1)} %cotangent.1, bf16[1,128,4096]{2,1,0:T(8,128)(2,1)} %features.3), custom_call_target="tpu_custom_call" | custom-call | flops 33554432 | bytes 786432 | tf_op jit(solution)/shard_map/far_products/pallas_call | solution.py:270
  2.1 0.5 %collective-permute-start = (f32[2,128,256]{2,1,0:T(8,128)S(1)}, f32[2,128,256]{2,1,0:T(8,128)S(1)}, u32[]{:S(2)}, u32[]{:S(2)}) collective-permute-start(f32[2,128,256]{2,1,0:T(8,128)S(1)} %get-tuple-element.29), channel_id=1, source_target_pairs={{0,1},{1,0},{2,3},{3,2},{4,5},{5,4},{6,7},{7,6},{8,9},{9,8},{10,11... | collective-permute-start | bytes 786440 | tf_op jit(solution)/shard_map/ppermute | solution.py:233
  3.3 0.0 copy-done
  3.3 0.4 %rest_products.1 = (f32[6,128,256]{2,1,0:T(8,128)S(1)}, f32[6,128,256]{2,1,0:T(8,128)S(1)}) custom-call(bf16[128,128]{1,0:T(8,128)(2,1)S(1)} %get-tuple-element.25.masked, bf16[1,128,4096]{2,1,0:T(8,128)(2,1)S(1)} %copy-done), custom_call_target="tpu_custom_call" | custom-call | tf_op jit(solution)/shard_map/rest_products/pallas_call | solution.py:285
  3.7 0.1 collective-permute-done.refs_1_
  3.8 0.4 %collective-permute-start.1 = (f32[6,128,256]{2,1,0:T(8,128)S(1)}, f32[6,128,256]{2,1,0:T(8,128)S(1)}, u32[]{:S(2)}, u32[]{:S(2)}) collective-permute-start(f32[6,128,256]{2,1,0:T(8,128)S(1)} %get-tuple-element.30), channel_id=1, source_target_pairs={{0,1},{1,0},{2,3},{3,2},{4,5},{5,4},{6,7},{7,6},{8,9},{9,8},{10,11... | collective-permute-start | bytes 2359304 | tf_op jit(solution)/shard_map/ppermute | solution.py:233
  4.3 2.7 %collective-permute-start.3 = (f32[1,128,256]{2,1,0:T(8,128)S(1)}, f32[1,128,256]{2,1,0:T(8,128)S(1)}, u32[]{:S(2)}, u32[]{:S(2)}) collective-permute-start(f32[1,128,256]{2,1,0:T(8,128)S(1)} %add_a1.1.after), channel_id=1, source_target_pairs={{0,2},{1,3},{2,0},{3,1},{4,6},{5,7},{6,4},{7,5},{8,10},{9,11},{10,... | collective-permute-start | bytes 393224 | tf_op jit(solution)/shard_map/ppermute | solution.py:233
  7.0 0.1 collective-permute-start.2
  7.1 0.0 collective-permute-done.1.refs_1_.come
  7.1 0.0 copy-start.1
  7.1 0.0 copy-start.4
  7.1 2.1 %collective-permute-start.5 = (f32[1,136,256]{2,1,0:T(8,128)S(1)}, f32[1,136,256]{2,1,0:T(8,128)S(1)}, u32[]{:S(2)}, u32[]{:S(2)}) collective-permute-start(f32[1,136,256]{2,1,0:T(8,128)S(1)} %add_n1.1), channel_id=1, source_target_pairs={{0,2},{1,3},{2,0},{3,1},{4,6},{5,7},{6,4},{7,5},{8,10},{9,11},{10,... | collective-permute-start | bytes 417800 | tf_op jit(solution)/shard_map/ppermute | solution.py:233
  9.2 0.0 copy-done.1
  9.2 1.6 %collective-permute-start.8 = (f32[128,128]{1,0:T(8,128)S(1)}, f32[128,128]{1,0:T(8,128)S(1)}, u32[]{:S(2)}, u32[]{:S(2)}) collective-permute-start(f32[128,128]{1,0:T(8,128)S(1)} %get-tuple-element.34), channel_id=1, source_target_pairs={{0,16},{8,24},{16,0},{24,8},{1,17},{9,25},{17,1},{25,9},{2,18},{10... | collective-permute-start | bytes 196616 | tf_op jit(solution)/shard_map/ppermute | solution.py:233
  10.8 0.5 %collective-permute-done.3.refs_2_ = f32[1,128,256]{2,1,0:T(8,128)S(1)} collective-permute-done((f32[1,128,256]{2,1,0:T(8,128)S(1)}, f32[1,128,256]{2,1,0:T(8,128)S(1)}, u32[]{:S(2)}, u32[]{:S(2)}) %collective-permute-start.3) | collective-permute-done | bytes 131104 | tf_op jit(solution)/shard_map/ppermute | solution.py:233
  11.3 3.1 %collective-permute-start.7 = (f32[1,128,256]{2,1,0:T(8,128)S(1)}, f32[1,128,256]{2,1,0:T(8,128)S(1)}, u32[]{:S(2)}, u32[]{:S(2)}) collective-permute-start(f32[1,128,256]{2,1,0:T(8,128)S(1)} %add_c1.1.refs_3_), channel_id=1, source_target_pairs={{0,4},{1,5},{2,6},{3,7},{4,0},{5,1},{6,2},{7,3},{8,12},{9,13},{10,... | collective-permute-start | bytes 393224 | tf_op jit(solution)/shard_map/ppermute | solution.py:233
  14.4 0.0 collective-permute-done.2.refs_2_
  14.4 2.8 %collective-permute-start.4 = (f32[1,128,256]{2,1,0:T(8,128)S(1)}, f32[1,128,256]{2,1,0:T(8,128)S(1)}, u32[]{:S(2)}, u32[]{:S(2)}) collective-permute-start(f32[1,128,256]{2,1,0:T(8,128)S(1)} %add_c2.1.refs_0_), channel_id=1, source_target_pairs={{0,4},{1,5},{2,6},{3,7},{4,0},{5,1},{6,2},{7,3},{8,12},{9,13},{10,... | collective-permute-start | bytes 393224 | tf_op jit(solution)/shard_map/ppermute | solution.py:233
  17.2 0.0 copy-start.5
  17.2 3.0 %collective-permute-start.6 = (f32[1,120,256]{2,1,0:T(8,128)S(1)}, f32[1,120,256]{2,1,0:T(8,128)S(1)}, u32[]{:S(2)}, u32[]{:S(2)}) collective-permute-start(f32[1,120,256]{2,1,0:T(8,128)S(1)} %add_n2.1), channel_id=1, source_target_pairs={{0,2},{1,3},{2,0},{3,1},{4,6},{5,7},{6,4},{7,5},{8,10},{9,11},{10,... | collective-permute-start | bytes 368648 | tf_op jit(solution)/shard_map/ppermute | solution.py:233
  20.3 0.0 collective-permute-done.8
  20.3 1.6 %collective-permute-start.9 = (f32[128,128]{1,0:T(8,128)S(1)}, f32[128,128]{1,0:T(8,128)S(1)}, u32[]{:S(2)}, u32[]{:S(2)}) collective-permute-start(f32[128,128]{1,0:T(8,128)S(1)} %add.3.drift), channel_id=1, source_target_pairs={{0,8},{8,0},{16,24},{24,16},{1,9},{9,1},{17,25},{25,17},{2,10},{10... | collective-permute-start | bytes 196616 | tf_op jit(solution)/shard_map/ppermute | solution.py:233
  21.9 2.8 %collective-permute-done.9.other_drift = f32[128,128]{1,0:T(8,128)S(1)} collective-permute-done((f32[128,128]{1,0:T(8,128)S(1)}, f32[128,128]{1,0:T(8,128)S(1)}, u32[]{:S(2)}, u32[]{:S(2)}) %collective-permute-start.9) | collective-permute-done | bytes 65568 | tf_op jit(solution)/shard_map/ppermute | solution.py:233
  24.6 0.0 collective-permute-done.7.far
  24.6 0.0 collective-permute-done.5.near
  24.6 0.0 copy-done.3
  24.7 0.0 copy-done.5
  24.7 1.1 %left_step.1 = (f32[256,128]{1,0:T(8,128)S(1)}, f32[1,512,128]{2,1,0:T(8,128)}, f32[1,512,128]{2,1,0:T(8,128)}, f32[1,512,128]{2,1,0:T(8,128)}, f32[128,128]{1,0:T(8,128)}, /*index=5*/f32[128,128]{1,0:T(8,128)}) custom-call(f32[1,512,128]{2,1,0:T(8,128)S(1)} %copy-done.1, f32[1,512,128]{2,1,0:T(8,128)S(1)} %copy-done.2, f32[1,512,128]{2,1,0:T(8,128)S(1)} %copy-done.3, ...), custom_call_target="tpu_custom_call" | custom-call | flops 983040 | bytes 1310720 | tf_op jit(solution)/shard_map/left_step/pallas_call | solution.py:356
  25.8 0.0 collective-permute-done.6.other_near
  25.8 0.0 collective-permute-done.4.far
  25.8 1.0 %right_step.1 = (f32[1,512,128]{2,1,0:T(8,128)}, f32[1,512,128]{2,1,0:T(8,128)}, f32[1,512,128]{2,1,0:T(8,128)}) custom-call(f32[1,512,128]{2,1,0:T(8,128)S(1)} %copy-done.1, f32[1,512,128]{2,1,0:T(8,128)S(1)} %copy-done.2, f32[1,512,128]{2,1,0:T(8,128)S(1)} %copy-done.3, ...), custom_call_target="tpu_custom_call", output_to_operand_aliasing={{0}: (11, {}), {1}: (12, {}), {2}: (13, {})} | custom-call | tf_op jit(solution)/shard_map/right_step/pallas_call | solution.py:383
  (12 shorter events, 0.2 us)
Async XLA Ops:
  0.6 2.7 %copy-start = (bf16[1,128,4096]{2,1,0:T(8,128)(2,1)S(1)}, bf16[1,128,4096]{2,1,0:T(8,128)(2,1)}, u32[]{:S(2)}) copy-start(bf16[1,128,4096]{2,1,0:T(8,128)(2,1)} %features.3) | copy-start | bytes 3145732
  2.1 1.7 %collective-permute-start = (f32[2,128,256]{2,1,0:T(8,128)S(1)}, f32[2,128,256]{2,1,0:T(8,128)S(1)}, u32[]{:S(2)}, u32[]{:S(2)}) collective-permute-start(f32[2,128,256]{2,1,0:T(8,128)S(1)} %get-tuple-element.29), channel_id=1, source_target_pairs={{0,1},{1,0},{2,3},{3,2},{4,5},{5,4},{6,7},{7,6},{8,9},{9,8},{10,11... | collective-permute-start | bytes 786440 | tf_op jit(solution)/shard_map/ppermute | solution.py:233
  3.8 3.3 %collective-permute-start.1 = (f32[6,128,256]{2,1,0:T(8,128)S(1)}, f32[6,128,256]{2,1,0:T(8,128)S(1)}, u32[]{:S(2)}, u32[]{:S(2)}) collective-permute-start(f32[6,128,256]{2,1,0:T(8,128)S(1)} %get-tuple-element.30), channel_id=1, source_target_pairs={{0,1},{1,0},{2,3},{3,2},{4,5},{5,4},{6,7},{7,6},{8,9},{9,8},{10,11... | collective-permute-start | bytes 2359304 | tf_op jit(solution)/shard_map/ppermute | solution.py:233
  4.3 7.0 %collective-permute-start.3 = (f32[1,128,256]{2,1,0:T(8,128)S(1)}, f32[1,128,256]{2,1,0:T(8,128)S(1)}, u32[]{:S(2)}, u32[]{:S(2)}) collective-permute-start(f32[1,128,256]{2,1,0:T(8,128)S(1)} %add_a1.1.after), channel_id=1, source_target_pairs={{0,2},{1,3},{2,0},{3,1},{4,6},{5,7},{6,4},{7,5},{8,10},{9,11},{10,... | collective-permute-start | bytes 393224 | tf_op jit(solution)/shard_map/ppermute | solution.py:233
  7.0 7.4 %collective-permute-start.2 = (f32[1,128,256]{2,1,0:T(8,128)S(1)}, f32[1,128,256]{2,1,0:T(8,128)S(1)}, u32[]{:S(2)}, u32[]{:S(2)}) collective-permute-start(f32[1,128,256]{2,1,0:T(8,128)S(1)} %add_a2.1.refs_0_), channel_id=1, source_target_pairs={{0,2},{1,3},{2,0},{3,1},{4,6},{5,7},{6,4},{7,5},{8,10},{9,11},{10,... | collective-permute-start | bytes 393224 | tf_op jit(solution)/shard_map/ppermute | solution.py:233
  7.1 2.1 %copy-start.1 = (f32[1,512,128]{2,1,0:T(8,128)S(1)}, f32[1,512,128]{2,1,0:T(8,128)}, u32[]{:S(2)}) copy-start(f32[1,512,128]{2,1,0:T(8,128)} %params.5) | copy-start | bytes 786436
  7.1 2.1 %copy-start.4 = (f32[128,128]{1,0:T(8,128)S(1)}, f32[128,128]{1,0:T(8,128)}, u32[]{:S(2)}) copy-start(f32[128,128]{1,0:T(8,128)} %global_fragment.3) | copy-start | bytes 196612
  7.1 17.5 %collective-permute-start.5 = (f32[1,136,256]{2,1,0:T(8,128)S(1)}, f32[1,136,256]{2,1,0:T(8,128)S(1)}, u32[]{:S(2)}, u32[]{:S(2)}) collective-permute-start(f32[1,136,256]{2,1,0:T(8,128)S(1)} %add_n1.1), channel_id=1, source_target_pairs={{0,2},{1,3},{2,0},{3,1},{4,6},{5,7},{6,4},{7,5},{8,10},{9,11},{10,... | collective-permute-start | bytes 417800 | tf_op jit(solution)/shard_map/ppermute | solution.py:233
  9.2 11.1 %collective-permute-start.8 = (f32[128,128]{1,0:T(8,128)S(1)}, f32[128,128]{1,0:T(8,128)S(1)}, u32[]{:S(2)}, u32[]{:S(2)}) collective-permute-start(f32[128,128]{1,0:T(8,128)S(1)} %get-tuple-element.34), channel_id=1, source_target_pairs={{0,16},{8,24},{16,0},{24,8},{1,17},{9,25},{17,1},{25,9},{2,18},{10... | collective-permute-start | bytes 196616 | tf_op jit(solution)/shard_map/ppermute | solution.py:233
  11.3 13.3 %collective-permute-start.7 = (f32[1,128,256]{2,1,0:T(8,128)S(1)}, f32[1,128,256]{2,1,0:T(8,128)S(1)}, u32[]{:S(2)}, u32[]{:S(2)}) collective-permute-start(f32[1,128,256]{2,1,0:T(8,128)S(1)} %add_c1.1.refs_3_), channel_id=1, source_target_pairs={{0,4},{1,5},{2,6},{3,7},{4,0},{5,1},{6,2},{7,3},{8,12},{9,13},{10,... | collective-permute-start | bytes 393224 | tf_op jit(solution)/shard_map/ppermute | solution.py:233
  14.4 11.4 %collective-permute-start.4 = (f32[1,128,256]{2,1,0:T(8,128)S(1)}, f32[1,128,256]{2,1,0:T(8,128)S(1)}, u32[]{:S(2)}, u32[]{:S(2)}) collective-permute-start(f32[1,128,256]{2,1,0:T(8,128)S(1)} %add_c2.1.refs_0_), channel_id=1, source_target_pairs={{0,4},{1,5},{2,6},{3,7},{4,0},{5,1},{6,2},{7,3},{8,12},{9,13},{10,... | collective-permute-start | bytes 393224 | tf_op jit(solution)/shard_map/ppermute | solution.py:233
  17.2 7.4 %copy-start.2 = (f32[1,512,128]{2,1,0:T(8,128)S(1)}, f32[1,512,128]{2,1,0:T(8,128)}, u32[]{:S(2)}) copy-start(f32[1,512,128]{2,1,0:T(8,128)} %first.3) | copy-start | bytes 786436
  17.2 7.4 %copy-start.3 = (f32[1,512,128]{2,1,0:T(8,128)S(1)}, f32[1,512,128]{2,1,0:T(8,128)}, u32[]{:S(2)}) copy-start(f32[1,512,128]{2,1,0:T(8,128)} %second.3) | copy-start | bytes 786436
  17.2 7.4 %copy-start.5 = (f32[128,128]{1,0:T(8,128)S(1)}, f32[128,128]{1,0:T(8,128)}, u32[]{:S(2)}) copy-start(f32[128,128]{1,0:T(8,128)} %outer_momentum.1) | copy-start | bytes 196612
  17.2 8.5 %collective-permute-start.6 = (f32[1,120,256]{2,1,0:T(8,128)S(1)}, f32[1,120,256]{2,1,0:T(8,128)S(1)}, u32[]{:S(2)}, u32[]{:S(2)}) collective-permute-start(f32[1,120,256]{2,1,0:T(8,128)S(1)} %add_n2.1), channel_id=1, source_target_pairs={{0,2},{1,3},{2,0},{3,1},{4,6},{5,7},{6,4},{7,5},{8,10},{9,11},{10,... | collective-permute-start | bytes 368648 | tf_op jit(solution)/shard_map/ppermute | solution.py:233
  20.3 4.3 %collective-permute-start.9 = (f32[128,128]{1,0:T(8,128)S(1)}, f32[128,128]{1,0:T(8,128)S(1)}, u32[]{:S(2)}, u32[]{:S(2)}) collective-permute-start(f32[128,128]{1,0:T(8,128)S(1)} %add.3.drift), channel_id=1, source_target_pairs={{0,8},{8,0},{16,24},{24,16},{1,9},{9,1},{17,25},{25,17},{2,10},{10... | collective-permute-start | bytes 196616 | tf_op jit(solution)/shard_map/ppermute | solution.py:233

commit v11 on v10

--- a/solution.py
+++ b/solution.py
@@ -143,6 +143,24 @@
 
 
 def left_kernel(
+    params, first, second, kept, come, far, near, info, inner, new_first, new_second, held_first, held_second, sems
+):
+    copies = []
+    for lanes, there, value in half_step(
+        0,
+        (params, first, second),
+        (kept, come, far, lambda lanes: near[0, : kept.shape[1], lanes]),
+        info,
+        (held_first, held_second),
+    ):
+        inner[lanes, :] = value
+        for source, target in ((held_first, new_first), (held_second, new_second)):
+            send(copies, sems, source.at[lanes], target.at[0, there])
+    for copy in copies:
+        copy.wait()
+
+
+def right_kernel(
     params,
     first,
     second,
@@ -150,13 +168,16 @@
     come,
     far,
     near,
+    other_near,
     info,
     scale,
+    inner,
     global_fragment,
     outer_momentum,
     drift,
     other_drift,
-    mix,
+    left_first,
+    left_second,
     new_params,
     new_first,
     new_second,
@@ -170,51 +191,20 @@
     spread,
     sems,
 ):
+    del left_first, left_second
     copies = []
     fresh, momentum = outer((drift[...] + other_drift[...]) * info[2:3, :], global_fragment[...], outer_momentum[...])
     held_global[...] = fresh
     held_momentum[...] = momentum
-    send(copies, sems, held_global, new_global)
-    send(copies, sems, held_momentum, new_momentum)
     for at in range(FRAGS):
         spread[pl.ds(at, fresh.shape[0], stride=FRAGS), :] = fresh
-    for lanes, there, value in half_step(
-        0, (params, first, second), (kept, come, far, lambda lanes: near[0, : kept.shape[1], lanes]), info, (held_first, held_second)
-    ):
-        held_params[lanes, :] = scale[there, :] * value + (1.0 - scale[there, :]) * spread[there, :]
-        for source, target in ((held_first, new_first), (held_second, new_second), (held_params, new_params)):
-            send(copies, sems, source.at[lanes], target.at[0, there])
-    right = pl.ds(mix.shape[0], mix.shape[0])
-    mix[...] = (1.0 - scale[right, :]) * spread[right, :]
-    for copy in copies:
-        copy.wait()
-
-
-def right_kernel(
-    params,
-    first,
-    second,
-    kept,
-    come,
-    far,
-    near,
-    other_near,
-    info,
-    scale,
-    mix,
-    left_params,
-    left_first,
-    left_second,
-    new_params,
-    new_first,
-    new_second,
-    held_params,
-    held_first,
-    held_second,
-    sems,
-):
-    del left_params, left_first, left_second
-    copies = []
+
+    def mixed(there, value):
+        held_params[there, :] = scale[there, :] * value + (1.0 - scale[there, :]) * spread[there, :]
+
+    left = pl.ds(0, inner.shape[0])
+    mixed(left, inner[...])
+    send(copies, sems, held_params.at[left], new_params.at[0, left])
 
     def joined(lanes):
         return jnp.concatenate([near[0, kept.shape[1] :, lanes], other_near[0, :, lanes]])
@@ -222,9 +212,15 @@
     for lanes, there, value in half_step(
         1, (params, first, second), (kept, come, far, joined), info, (held_first, held_second)
     ):
-        held_params[lanes, :] = scale[there, :] * value + mix[lanes, :]
-        for source, target in ((held_first, new_first), (held_second, new_second), (held_params, new_params)):
-            send(copies, sems, source.at[lanes], target.at[0, there])
+        mixed(there, value)
+        for source, target in (
+            (held_first.at[lanes], new_first),
+            (held_second.at[lanes], new_second),
+            (held_params.at[there], new_params),
+        ):
+            send(copies, sems, source, target.at[0, there])
+    send(copies, sems, held_global, new_global)
+    send(copies, sems, held_momentum, new_momentum)
     for copy in copies:
         copy.wait()
 
@@ -320,7 +316,7 @@
 
         state, piece = block(params.shape), block(global_fragment.shape)
         come_far = hop(away_far, "fsdp", devices, 1)
-        sent = add((kept_far, part(0)), (come_far, part(0)), (fragment_index, None), name="add_a1")
+        sent = add((kept_far, part(0)), (come_far, part(0)), name="add_a1")
         far_left = hop(sent, "fsdp", devices, 2)
         away, _ = lax.optimization_barrier((away, sent))
         come = hop(away, "fsdp", devices, 1)
@@ -333,7 +329,7 @@
             cost_estimate=free,
             name="drift",
         )(info, fragment_index, params, global_fragment, sent)
-        sent = add((kept_far, part(1)), (come_far, part(1)), name="add_a2")
+        sent = add((kept_far, part(1)), (come_far, part(1)), (drift, None), name="add_a2")
         far_right = hop(sent, "fsdp", devices, 2)
         passed = add((kept, part(4)), (come, part(4)), (far_left, part(0)), name="add_c1")
         far_left = hop(passed, "fsdp", devices, 4)
@@ -353,44 +349,49 @@
         near_right = hop(near_right, "fsdp", devices, 2)
         groups = half // LANES
         held_half = pltpu.VMEM((half, width), jnp.float32)
-        mix, *results, new_global, new_momentum = pl.pallas_call(
+        inner, new_first, new_second = pl.pallas_call(
             left_kernel,
-            out_shape=[block((half, width)), state, state, state, piece, piece],
-            in_specs=[VMEM] * 13,
-            out_specs=[VMEM] + [HBM] * 5,
-            scratch_shapes=[held_half] * 3
-            + [held_piece] * 2
-            + [pltpu.VMEM((rows, width), jnp.float32), pltpu.SemaphoreType.DMA((2 + 3 * groups,))],
+            out_shape=[block((half, width)), state, state],
+            in_specs=[VMEM] * 8,
+            out_specs=[VMEM] + [HBM] * 2,
+            scratch_shapes=[held_half] * 2 + [pltpu.SemaphoreType.DMA((2 * groups,))],
             compiler_params=room,
             cost_estimate=pl.CostEstimate(
                 flops=30 * half * width, bytes_accessed=40 * half * width, transcendentals=2 * half * width
             ),
             name="left_step",
+        )(params, first, second, kept, come, far_left, near_left, info)
+        new_params, new_first, new_second, new_global, new_momentum = pl.pallas_call(
+            right_kernel,
+            out_shape=[state] * 3 + [piece] * 2,
+            in_specs=[VMEM] * 15 + [HBM] * 2,
+            out_specs=[HBM] * 5,
+            input_output_aliases={15: 1, 16: 2},
+            scratch_shapes=[pltpu.VMEM((rows, width), jnp.float32)]
+            + [held_half] * 2
+            + [held_piece] * 2
+            + [pltpu.VMEM((rows, width), jnp.float32), pltpu.SemaphoreType.DMA((3 + 3 * groups,))],
+            compiler_params=room,
+            cost_estimate=free,
+            name="right_step",
         )(
             params,
             first,
             second,
             kept,
             come,
-            far_left,
+            far_right,
             near_left,
+            near_right,
             info,
             scale,
+            inner,
             global_fragment,
             outer_momentum,
             *drifts,
+            new_first,
+            new_second,
         )
-        new_params, new_first, new_second = pl.pallas_call(
-            right_kernel,
-            out_shape=[state] * 3,
-            in_specs=[VMEM] * 11 + [HBM] * 3,
-            out_specs=[HBM] * 3,
-            input_output_aliases={11: 0, 12: 1, 13: 2},
-            scratch_shapes=[held_half] * 3 + [pltpu.SemaphoreType.DMA((3 * groups,))],
-            compiler_params=room,
-            cost_estimate=free,
-            name="right_step",
-        )(params, first, second, kept, come, far_right, near_left, near_right, info, scale, mix, *results)
         return new_params, new_first, new_second, new_global, new_momentum
 
     return body

time: 26.9 us -> 27.7 us (1.030)
  waiting for transfers between devices: 3.38 us -> 5.76 us
  starting transfers between devices: 17.8 us -> 16.3 us
    ppermute x10, waiting for transfers between devices: 3.38 us -> 5.76 us  [hop(): return lax.ppermute(value, axis, [(d, d ^ bit) for d in range(devices)])]
    ppermute x10, starting transfers between devices: 17.8 us -> 16.3 us  [hop(): return lax.ppermute(value, axis, [(d, d ^ bit) for d in range(devices)])]
  transfers between devices with their start and end apart: 10 -> 10, of which waited for: 3 -> 4; matrix products, arithmetic and copies ran while one was open for 0% -> 0% of each run, Pallas kernels for 6% -> 5%
where the time goes in v11:
time: 27.7 us; the launch traced here: 27.5 us
  starting transfers between devices  16.3 us (59%)
  waiting for transfers between devices  5.76 us (21%)
  Pallas kernels  4.06 us (15%)
  between operations  1.39 us (5%)
    ppermute x10, starting transfers between devices, hop(): return lax.ppermute(value, axis, [(d, d ^ bit) for d in range(devices)])  16.3 us
    ppermute x10, waiting for transfers between devices, hop(): return lax.ppermute(value, axis, [(d, d ^ bit) for d in range(devices)])  5.76 us
    pallas_call x1, Pallas kernels, body(): pl.pallas_call(functools.partial(first_kernel, workers, (7, 6)), out_shap...  1.47 us
    pallas_call x1, Pallas kernels, body(): pl.pallas_call(right_kernel, out_shape=[state] * 3 + [piece] * 2, in_spec...  1.14 us
    pallas_call x1, Pallas kernels, body(): pl.pallas_call(left_kernel, out_shape=[block((half, width)), state, state...  0.91 us
  transfers between devices with their start and end apart: 10, of which 4 were waited for; matrix products, arithmetic and copies ran while one was open for 0% of the time, Pallas kernels for 5%

profile of v11, /device:TPU:0, one launch (start us, length us, event | category | flops | bytes accessed | tf_op | source)
XLA Modules:
  0.0 27.5 jit_solution(14338151502052446194)
XLA Ops:
  0.6 0.0 copy-start
  0.6 1.5 %far_products.1 = (f32[2,128,256]{2,1,0:T(8,128)S(1)}, f32[2,128,256]{2,1,0:T(8,128)S(1)}, bf16[128,128]{1,0:T(8,128)(2,1)S(1)}, f32[8,128]{1,0:T(8,128)S(1)}) custom-call(s32[4]{0:T(128)} %counts.1, bf16[1,128,128]{2,1,0:T(8,128)(2,1)} %cotangent.1, bf16[1,128,4096]{2,1,0:T(8,128)(2,1)} %features.3), custom_call_target="tpu_custom_call" | custom-call | flops 33554432 | bytes 786432 | tf_op jit(solution)/shard_map/far_products/pallas_call | solution.py:266
  2.1 0.5 %collective-permute-start = (f32[2,128,256]{2,1,0:T(8,128)S(1)}, f32[2,128,256]{2,1,0:T(8,128)S(1)}, u32[]{:S(2)}, u32[]{:S(2)}) collective-permute-start(f32[2,128,256]{2,1,0:T(8,128)S(1)} %get-tuple-element.23), channel_id=1, source_target_pairs={{0,1},{1,0},{2,3},{3,2},{4,5},{5,4},{6,7},{7,6},{8,9},{9,8},{10,11... | collective-permute-start | bytes 786440 | tf_op jit(solution)/shard_map/ppermute | solution.py:229
  2.6 0.0 copy-done
  2.6 0.4 %rest_products.1 = (f32[6,128,256]{2,1,0:T(8,128)S(1)}, f32[6,128,256]{2,1,0:T(8,128)S(1)}) custom-call(bf16[128,128]{1,0:T(8,128)(2,1)S(1)} %get-tuple-element.19.masked, bf16[1,128,4096]{2,1,0:T(8,128)(2,1)S(1)} %copy-done), custom_call_target="tpu_custom_call" | custom-call | tf_op jit(solution)/shard_map/rest_products/pallas_call | solution.py:281
  3.0 0.8 %collective-permute-done.refs_1_ = f32[2,128,256]{2,1,0:T(8,128)S(1)} collective-permute-done((f32[2,128,256]{2,1,0:T(8,128)S(1)}, f32[2,128,256]{2,1,0:T(8,128)S(1)}, u32[]{:S(2)}, u32[]{:S(2)}) %collective-permute-start) | collective-permute-done | bytes 262176 | tf_op jit(solution)/shard_map/ppermute | solution.py:229
  3.8 0.4 %collective-permute-start.1 = (f32[6,128,256]{2,1,0:T(8,128)S(1)}, f32[6,128,256]{2,1,0:T(8,128)S(1)}, u32[]{:S(2)}, u32[]{:S(2)}) collective-permute-start(f32[6,128,256]{2,1,0:T(8,128)S(1)} %get-tuple-element.24), channel_id=1, source_target_pairs={{0,1},{1,0},{2,3},{3,2},{4,5},{5,4},{6,7},{7,6},{8,9},{9,8},{10,11... | collective-permute-start | bytes 2359304 | tf_op jit(solution)/shard_map/ppermute | solution.py:229
  4.3 2.7 %collective-permute-start.3 = (f32[1,128,256]{2,1,0:T(8,128)S(1)}, f32[1,128,256]{2,1,0:T(8,128)S(1)}, u32[]{:S(2)}, u32[]{:S(2)}) collective-permute-start(f32[1,128,256]{2,1,0:T(8,128)S(1)} %add_a1.1.after), channel_id=1, source_target_pairs={{0,2},{1,3},{2,0},{3,1},{4,6},{5,7},{6,4},{7,5},{8,10},{9,11},{10,... | collective-permute-start | bytes 393224 | tf_op jit(solution)/shard_map/ppermute | solution.py:229
  7.6 0.0 copy-done.1
  7.6 0.0 copy-done.4
  7.7 0.1 collective-permute-start.2
  7.8 0.0 collective-permute-done.1.refs_1_.come
  7.8 2.1 %collective-permute-start.5 = (f32[1,136,256]{2,1,0:T(8,128)S(1)}, f32[1,136,256]{2,1,0:T(8,128)S(1)}, u32[]{:S(2)}, u32[]{:S(2)}) collective-permute-start(f32[1,136,256]{2,1,0:T(8,128)S(1)} %add_n1.1), channel_id=1, source_target_pairs={{0,2},{1,3},{2,0},{3,1},{4,6},{5,7},{6,4},{7,5},{8,10},{9,11},{10,... | collective-permute-start | bytes 417800 | tf_op jit(solution)/shard_map/ppermute | solution.py:229
  9.9 1.4 %collective-permute-done.3.refs_2_ = f32[1,128,256]{2,1,0:T(8,128)S(1)} collective-permute-done((f32[1,128,256]{2,1,0:T(8,128)S(1)}, f32[1,128,256]{2,1,0:T(8,128)S(1)}, u32[]{:S(2)}, u32[]{:S(2)}) %collective-permute-start.3) | collective-permute-done | bytes 131104 | tf_op jit(solution)/shard_map/ppermute | solution.py:229
  11.3 3.1 %collective-permute-start.7 = (f32[1,128,256]{2,1,0:T(8,128)S(1)}, f32[1,128,256]{2,1,0:T(8,128)S(1)}, u32[]{:S(2)}, u32[]{:S(2)}) collective-permute-start(f32[1,128,256]{2,1,0:T(8,128)S(1)} %add_c1.1.refs_3_), channel_id=1, source_target_pairs={{0,4},{1,5},{2,6},{3,7},{4,0},{5,1},{6,2},{7,3},{8,12},{9,13},{10,... | collective-permute-start | bytes 393224 | tf_op jit(solution)/shard_map/ppermute | solution.py:229
  14.4 1.5 %collective-permute-start.8 = (f32[128,128]{1,0:T(8,128)S(1)}, f32[128,128]{1,0:T(8,128)S(1)}, u32[]{:S(2)}, u32[]{:S(2)}) collective-permute-start(f32[128,128]{1,0:T(8,128)S(1)} %get-tuple-element.29.refs_2_), channel_id=1, source_target_pairs={{0,16},{8,24},{16,0},{24,8},{1,17},{9,25},{17,1},{25,9},{2,18},{10... | collective-permute-start | bytes 196616 | tf_op jit(solution)/shard_map/ppermute | solution.py:229
  15.9 0.0 collective-permute-done.2.refs_2_
  16.0 1.3 %collective-permute-start.4 = (f32[1,128,256]{2,1,0:T(8,128)S(1)}, f32[1,128,256]{2,1,0:T(8,128)S(1)}, u32[]{:S(2)}, u32[]{:S(2)}) collective-permute-start(f32[1,128,256]{2,1,0:T(8,128)S(1)} %add_c2.1.refs_0_), channel_id=1, source_target_pairs={{0,4},{1,5},{2,6},{3,7},{4,0},{5,1},{6,2},{7,3},{8,12},{9,13},{10,... | collective-permute-start | bytes 393224 | tf_op jit(solution)/shard_map/ppermute | solution.py:229
  17.2 3.0 %collective-permute-start.6 = (f32[1,120,256]{2,1,0:T(8,128)S(1)}, f32[1,120,256]{2,1,0:T(8,128)S(1)}, u32[]{:S(2)}, u32[]{:S(2)}) collective-permute-start(f32[1,120,256]{2,1,0:T(8,128)S(1)} %add_n2.1), channel_id=1, source_target_pairs={{0,2},{1,3},{2,0},{3,1},{4,6},{5,7},{6,4},{7,5},{8,10},{9,11},{10,... | collective-permute-start | bytes 368648 | tf_op jit(solution)/shard_map/ppermute | solution.py:229
  20.3 0.0 collective-permute-done.8
  20.3 0.0 copy-start.5
  20.3 1.6 %collective-permute-start.9 = (f32[128,128]{1,0:T(8,128)S(1)}, f32[128,128]{1,0:T(8,128)S(1)}, u32[]{:S(2)}, u32[]{:S(2)}) collective-permute-start(f32[128,128]{1,0:T(8,128)S(1)} %add.3.drift), channel_id=1, source_target_pairs={{0,8},{8,0},{16,24},{24,16},{1,9},{9,1},{17,25},{25,17},{2,10},{10... | collective-permute-start | bytes 196616 | tf_op jit(solution)/shard_map/ppermute | solution.py:229
  21.9 0.0 collective-permute-done.7.far
  21.9 0.0 collective-permute-done.5.near
  21.9 0.0 copy-done.2
  21.9 0.0 copy-done.3
  21.9 0.9 %left_step.1 = (f32[256,128]{1,0:T(8,128)S(1)}, f32[1,512,128]{2,1,0:T(8,128)}, f32[1,512,128]{2,1,0:T(8,128)}) custom-call(f32[1,512,128]{2,1,0:T(8,128)S(1)} %copy-done.1, f32[1,512,128]{2,1,0:T(8,128)S(1)} %copy-done.2, f32[1,512,128]{2,1,0:T(8,128)S(1)} %copy-done.3, f32[6,128,256]{2,1,0:T(8,128)S(1)} %get-tuple-element.20.refs_0_.kept, ...), custom_call_target="tpu_custom_call" | custom-call | flops 983040 | bytes 1310720 | tf_op jit(solution)/shard_map/left_step/pallas_call | solution.py:352
  22.8 1.8 %collective-permute-done.9.other_drift = f32[128,128]{1,0:T(8,128)S(1)} collective-permute-done((f32[128,128]{1,0:T(8,128)S(1)}, f32[128,128]{1,0:T(8,128)S(1)}, u32[]{:S(2)}, u32[]{:S(2)}) %collective-permute-start.9) | collective-permute-done | bytes 65568 | tf_op jit(solution)/shard_map/ppermute | solution.py:229
  24.6 0.0 collective-permute-done.6.other_near
  24.6 1.7 %collective-permute-done.4.far = f32[1,128,256]{2,1,0:T(8,128)S(1)} collective-permute-done((f32[1,128,256]{2,1,0:T(8,128)S(1)}, f32[1,128,256]{2,1,0:T(8,128)S(1)}, u32[]{:S(2)}, u32[]{:S(2)}) %collective-permute-start.4) | collective-permute-done | bytes 131104 | tf_op jit(solution)/shard_map/ppermute | solution.py:229
  26.4 0.0 copy-done.5
  26.4 1.1 %right_step.1 = (f32[1,512,128]{2,1,0:T(8,128)}, f32[1,512,128]{2,1,0:T(8,128)}, f32[1,512,128]{2,1,0:T(8,128)}, f32[128,128]{1,0:T(8,128)}, f32[128,128]{1,0:T(8,128)}) custom-call(f32[1,512,128]{2,1,0:T(8,128)S(1)} %copy-done.1, f32[1,512,128]{2,1,0:T(8,128)S(1)} %copy-done.2, ...), custom_call_target="tpu_custom_call", output_to_operand_aliasing={{1}: (15, {}), {2}: (16, {})} | custom-call | tf_op jit(solution)/shard_map/right_step/pallas_call | solution.py:364
  (12 shorter events, 0.2 us)
Async XLA Ops:
  0.6 2.0 %copy-start = (bf16[1,128,4096]{2,1,0:T(8,128)(2,1)S(1)}, bf16[1,128,4096]{2,1,0:T(8,128)(2,1)}, u32[]{:S(2)}) copy-start(bf16[1,128,4096]{2,1,0:T(8,128)(2,1)} %features.3) | copy-start | bytes 3145732
  2.1 1.7 %collective-permute-start = (f32[2,128,256]{2,1,0:T(8,128)S(1)}, f32[2,128,256]{2,1,0:T(8,128)S(1)}, u32[]{:S(2)}, u32[]{:S(2)}) collective-permute-start(f32[2,128,256]{2,1,0:T(8,128)S(1)} %get-tuple-element.23), channel_id=1, source_target_pairs={{0,1},{1,0},{2,3},{3,2},{4,5},{5,4},{6,7},{7,6},{8,9},{9,8},{10,11... | collective-permute-start | bytes 786440 | tf_op jit(solution)/shard_map/ppermute | solution.py:229
  3.8 3.8 %copy-start.1 = (f32[1,512,128]{2,1,0:T(8,128)S(1)}, f32[1,512,128]{2,1,0:T(8,128)}, u32[]{:S(2)}) copy-start(f32[1,512,128]{2,1,0:T(8,128)} %params.5) | copy-start | bytes 786436
  3.8 3.8 %copy-start.4 = (f32[128,128]{1,0:T(8,128)S(1)}, f32[128,128]{1,0:T(8,128)}, u32[]{:S(2)}) copy-start(f32[128,128]{1,0:T(8,128)} %global_fragment.3) | copy-start | bytes 196612
  3.8 4.0 %collective-permute-start.1 = (f32[6,128,256]{2,1,0:T(8,128)S(1)}, f32[6,128,256]{2,1,0:T(8,128)S(1)}, u32[]{:S(2)}, u32[]{:S(2)}) collective-permute-start(f32[6,128,256]{2,1,0:T(8,128)S(1)} %get-tuple-element.24), channel_id=1, source_target_pairs={{0,1},{1,0},{2,3},{3,2},{4,5},{5,4},{6,7},{7,6},{8,9},{9,8},{10,11... | collective-permute-start | bytes 2359304 | tf_op jit(solution)/shard_map/ppermute | solution.py:229
  4.3 7.1 %collective-permute-start.3 = (f32[1,128,256]{2,1,0:T(8,128)S(1)}, f32[1,128,256]{2,1,0:T(8,128)S(1)}, u32[]{:S(2)}, u32[]{:S(2)}) collective-permute-start(f32[1,128,256]{2,1,0:T(8,128)S(1)} %add_a1.1.after), channel_id=1, source_target_pairs={{0,2},{1,3},{2,0},{3,1},{4,6},{5,7},{6,4},{7,5},{8,10},{9,11},{10,... | collective-permute-start | bytes 393224 | tf_op jit(solution)/shard_map/ppermute | solution.py:229
  7.7 8.2 %collective-permute-start.2 = (f32[1,128,256]{2,1,0:T(8,128)S(1)}, f32[1,128,256]{2,1,0:T(8,128)S(1)}, u32[]{:S(2)}, u32[]{:S(2)}) collective-permute-start(f32[1,128,256]{2,1,0:T(8,128)S(1)} %add_a2.1.refs_0_), channel_id=1, source_target_pairs={{0,2},{1,3},{2,0},{3,1},{4,6},{5,7},{6,4},{7,5},{8,10},{9,11},{10,... | collective-permute-start | bytes 393224 | tf_op jit(solution)/shard_map/ppermute | solution.py:229
  7.8 14.0 %collective-permute-start.5 = (f32[1,136,256]{2,1,0:T(8,128)S(1)}, f32[1,136,256]{2,1,0:T(8,128)S(1)}, u32[]{:S(2)}, u32[]{:S(2)}) collective-permute-start(f32[1,136,256]{2,1,0:T(8,128)S(1)} %add_n1.1), channel_id=1, source_target_pairs={{0,2},{1,3},{2,0},{3,1},{4,6},{5,7},{6,4},{7,5},{8,10},{9,11},{10,... | collective-permute-start | bytes 417800 | tf_op jit(solution)/shard_map/ppermute | solution.py:229
  11.3 10.5 %collective-permute-start.7 = (f32[1,128,256]{2,1,0:T(8,128)S(1)}, f32[1,128,256]{2,1,0:T(8,128)S(1)}, u32[]{:S(2)}, u32[]{:S(2)}) collective-permute-start(f32[1,128,256]{2,1,0:T(8,128)S(1)} %add_c1.1.refs_3_), channel_id=1, source_target_pairs={{0,4},{1,5},{2,6},{3,7},{4,0},{5,1},{6,2},{7,3},{8,12},{9,13},{10,... | collective-permute-start | bytes 393224 | tf_op jit(solution)/shard_map/ppermute | solution.py:229
  14.4 5.9 %collective-permute-start.8 = (f32[128,128]{1,0:T(8,128)S(1)}, f32[128,128]{1,0:T(8,128)S(1)}, u32[]{:S(2)}, u32[]{:S(2)}) collective-permute-start(f32[128,128]{1,0:T(8,128)S(1)} %get-tuple-element.29.refs_2_), channel_id=1, source_target_pairs={{0,16},{8,24},{16,0},{24,8},{1,17},{9,25},{17,1},{25,9},{2,18},{10... | collective-permute-start | bytes 196616 | tf_op jit(solution)/shard_map/ppermute | solution.py:229
  16.0 10.4 %collective-permute-start.4 = (f32[1,128,256]{2,1,0:T(8,128)S(1)}, f32[1,128,256]{2,1,0:T(8,128)S(1)}, u32[]{:S(2)}, u32[]{:S(2)}) collective-permute-start(f32[1,128,256]{2,1,0:T(8,128)S(1)} %add_c2.1.refs_0_), channel_id=1, source_target_pairs={{0,4},{1,5},{2,6},{3,7},{4,0},{5,1},{6,2},{7,3},{8,12},{9,13},{10,... | collective-permute-start | bytes 393224 | tf_op jit(solution)/shard_map/ppermute | solution.py:229
  17.2 4.7 %copy-start.2 = (f32[1,512,128]{2,1,0:T(8,128)S(1)}, f32[1,512,128]{2,1,0:T(8,128)}, u32[]{:S(2)}) copy-start(f32[1,512,128]{2,1,0:T(8,128)} %first.3) | copy-start | bytes 786436
  17.2 4.7 %copy-start.3 = (f32[1,512,128]{2,1,0:T(8,128)S(1)}, f32[1,512,128]{2,1,0:T(8,128)}, u32[]{:S(2)}) copy-start(f32[1,512,128]{2,1,0:T(8,128)} %second.3) | copy-start | bytes 786436
  17.2 7.4 %collective-permute-start.6 = (f32[1,120,256]{2,1,0:T(8,128)S(1)}, f32[1,120,256]{2,1,0:T(8,128)S(1)}, u32[]{:S(2)}, u32[]{:S(2)}) collective-permute-start(f32[1,120,256]{2,1,0:T(8,128)S(1)} %add_n2.1), channel_id=1, source_target_pairs={{0,2},{1,3},{2,0},{3,1},{4,6},{5,7},{6,4},{7,5},{8,10},{9,11},{10,... | collective-permute-start | bytes 368648 | tf_op jit(solution)/shard_map/ppermute | solution.py:229
  20.3 6.1 %copy-start.5 = (f32[128,128]{1,0:T(8,128)S(1)}, f32[128,128]{1,0:T(8,128)}, u32[]{:S(2)}) copy-start(f32[128,128]{1,0:T(8,128)} %outer_momentum.1) | copy-start | bytes 196612
  20.3 4.3 %collective-permute-start.9 = (f32[128,128]{1,0:T(8,128)S(1)}, f32[128,128]{1,0:T(8,128)S(1)}, u32[]{:S(2)}, u32[]{:S(2)}) collective-permute-start(f32[128,128]{1,0:T(8,128)S(1)} %add.3.drift), channel_id=1, source_target_pairs={{0,8},{8,0},{16,24},{24,16},{1,9},{9,1},{17,25},{25,17},{2,10},{10... | collective-permute-start | bytes 196616 | tf_op jit(solution)/shard_map/ppermute | solution.py:229

commit v12 on v8

--- a/solution.py
+++ b/solution.py
@@ -9,6 +9,7 @@
 
 FRAGS = 4
 LANES = 128
+SPARE = 8
 
 BETA_ONE = 0.9
 BETA_TWO = 0.95
@@ -72,12 +73,13 @@
     for slot, into in enumerate((away, kept)):
         blocks[slot].wait()
         for side in (0, 1):
-            into[side] = product(masked[...], held[slot, :, side * half : (side + 1) * half])
+            into[side, : masked.shape[1]] = product(masked[...], held[slot, :, side * half : (side + 1) * half])
+    away[:, masked.shape[1] :] = jnp.zeros((2, SPARE, half), jnp.float32)
 
 
 def rest_kernel(masked, features, *targets):
     half = targets[0].shape[2]
-    places = [(4, 0, 0, 4), (4, 1, 0, 5), (2, 0, 0, 2), (2, 1, 0, 3), (0, 0, 0, 0), (0, 1, 0, 1)]
+    places = [(4, 0, 0, 0), (4, 1, 0, 1), (0, 1, 0, 2), (2, 0, 2, 1), (2, 1, 2, 2), (0, 0, 2, 0)]
     for q, side, into, at in places:
         for core in (1, 0):
             columns = columns_of(q + core, 2 * half, side * half, half)
@@ -119,7 +121,7 @@
     rows = kept.shape[2]
     for lane in range(0, rows, LANES):
         lanes, there = pl.ds(lane, LANES), pl.ds(half * rows + lane, LANES)
-        summed = kept[half, :, lanes] + come[half, :, lanes] + near[0, :, lanes] + far[0, :, lanes]
+        summed = kept[2 * half, :, lanes] + come[2 * half, :, lanes] + near[0, :, lanes] + far[0, :, lanes]
         inner, held_first[lanes, :], held_second[lanes, :] = adam(
             params[0, there, :], first[0, there, :], second[0, there, :], summed.T * info[1:2, :]
         )
@@ -253,7 +255,12 @@
         half = rows // 2
         away_far, kept_far, masked, info = pl.pallas_call(
             functools.partial(first_kernel, workers, (7, 6)),
-            out_shape=[block((2, width, half))] * 2 + [jax.ShapeDtypeStruct((tokens, width), jnp.bfloat16), block((8, width))],
+            out_shape=[
+                block((2, width + SPARE, half)),
+                block((2, width, half)),
+                jax.ShapeDtypeStruct((tokens, width), jnp.bfloat16),
+                block((8, width)),
+            ],
             in_specs=[HBM] * 3,
             out_specs=[VMEM] * 4,
             scratch_shapes=[
@@ -266,11 +273,11 @@
             cost_estimate=cost(2),
             name="far_products",
         )(far_counts, far_cotangent, far_features)
-        away, kept = pl.pallas_call(
+        away_pass, kept_pass, away, kept = pl.pallas_call(
             rest_kernel,
-            out_shape=[block((6, width, half))] * 2,
+            out_shape=[block((3, width, half))] * 4,
             in_specs=[VMEM] * 2,
-            out_specs=[VMEM] * 2,
+            out_specs=[VMEM] * 4,
             compiler_params=room,
             cost_estimate=free,
             name="rest_products",
@@ -293,9 +300,9 @@
 
         state, piece = block(params.shape), block(global_fragment.shape)
         come_far = hop(away_far, "fsdp", devices, 1)
-        sent = add((kept_far, part(0)), (come_far, part(0)), name="add_a1")
+        sent = add((kept_far, part(0)), (come_far, (part(0), part(0, width))), name="add_a1")
         far_left = hop(sent, "fsdp", devices, 2)
-        away, _ = lax.optimization_barrier((away, sent))
+        come_pass = hop(away_pass, "fsdp", devices, 1)
         come = hop(away, "fsdp", devices, 1)
         drift, scale = pl.pallas_call(
             drift_kernel,
@@ -306,13 +313,13 @@
             cost_estimate=free,
             name="drift",
         )(info, fragment_index, params, global_fragment, sent)
-        sent = add((kept_far, part(1)), (come_far, part(1)), (drift, None), name="add_a2")
+        sent = add((kept_far, part(1)), (come_far, (part(1), part(0, width))), (drift, None), name="add_a2")
         far_right = hop(sent, "fsdp", devices, 2)
-        passed = add((kept, part(4)), (come, part(4)), (far_left, part(0)), name="add_c1")
+        passed = add((kept_pass, part(0)), (come_pass, part(0)), (far_left, part(0)), name="add_c1")
         far_left = hop(passed, "fsdp", devices, 4)
-        near_left = add((kept, part(2)), (come, part(2)), (sent, None), name="add_n1")
-        far_right = add((kept, part(5)), (come, part(5)), (far_right, part(0)), (passed, None), name="add_c2")
-        near_right = add((kept, part(3)), (come, part(3)), (passed, None), name="add_n2")
+        near_left = add((kept, part(1)), (come, part(1)), (passed, None), name="add_n1")
+        far_right = add((kept_pass, part(1)), (come_pass, part(1)), (far_right, part(0)), (passed, None), name="add_c2")
+        near_right = add((kept, part(2)), (come, part(2)), (far_right, None), name="add_n2")
         drift, _ = lax.optimization_barrier((drift, sent))
         bit = workers // 2
         drifts = (drift, hop(drift, "worker", workers, bit))
@@ -363,7 +370,7 @@
             compiler_params=room,
             cost_estimate=free,
             name="right_step",
-        )(params, first, second, kept, come, far_right, near_right, info, scale, mix, *results)
+        )(params, first, second, kept_pass, come_pass, far_right, near_right, info, scale, mix, *results)
         return new_params, new_first, new_second, new_global, new_momentum
 
     return body

time: 26.2 us -> 26.6 us (1.015)
  starting transfers between devices: 14.6 us -> 15.1 us
    ppermute x10 -> x11, starting transfers between devices: 14.6 us -> 15.1 us  [hop(): return lax.ppermute(value, axis, [(d, d ^ bit) for d in range(devices)])]
    ppermute x10 -> x11, waiting for transfers between devices: 5.9 us -> 5.87 us  [hop(): return lax.ppermute(value, axis, [(d, d ^ bit) for d in range(devices)])]
  transfers between devices with their start and end apart: 10 -> 11, of which waited for: 3 -> 6; matrix products, arithmetic and copies ran while one was open for 0% -> 0% of each run, Pallas kernels for 6% -> 6%
where the time goes in v12:
time: 26.6 us; the launch traced here: 26.4 us
  starting transfers between devices  15.1 us (57%)
  waiting for transfers between devices  5.87 us (22%)
  Pallas kernels  4.07 us (15%)
  between operations  1.38 us (5%)
    ppermute x11, starting transfers between devices, hop(): return lax.ppermute(value, axis, [(d, d ^ bit) for d in range(devices)])  15.1 us
    ppermute x11, waiting for transfers between devices, hop(): return lax.ppermute(value, axis, [(d, d ^ bit) for d in range(devices)])  5.87 us
    pallas_call x1, Pallas kernels, body(): pl.pallas_call(functools.partial(first_kernel, workers, (7, 6)), out_shap...  1.47 us
    pallas_call x1, Pallas kernels, body(): pl.pallas_call(left_kernel, out_shape=[block((half, width)), state, state...  1.09 us
    pallas_call x1, Pallas kernels, body(): pl.pallas_call(right_kernel, out_shape=[state] * 3, in_specs=[VMEM] * 10...  0.97 us
  transfers between devices with their start and end apart: 11, of which 6 were waited for; matrix products, arithmetic and copies ran while one was open for 0% of the time, Pallas kernels for 6%

profile of v12, /device:TPU:0, one launch (start us, length us, event | category | flops | bytes accessed | tf_op | source)
XLA Modules:
  0.0 26.4 jit_solution(4357545067979534482)
XLA Ops:
  0.6 0.0 copy-start
  0.6 1.5 %far_products.1 = (f32[2,136,256]{2,1,0:T(8,128)S(1)}, f32[2,128,256]{2,1,0:T(8,128)S(1)}, bf16[128,128]{1,0:T(8,128)(2,1)S(1)}, f32[8,128]{1,0:T(8,128)S(1)}) custom-call(s32[4]{0:T(128)} %counts.1, bf16[1,128,128]{2,1,0:T(8,128)(2,1)} %cotangent.1, bf16[1,128,4096]{2,1,0:T(8,128)(2,1)} %features.3), custom_call_target="tpu_custom_call" | custom-call | flops 33554432 | bytes 786432 | tf_op jit(solution)/shard_map/far_products/pallas_call | solution.py:256
  2.1 0.5 %collective-permute-start.1 = (f32[2,136,256]{2,1,0:T(8,128)S(1)}, f32[2,136,256]{2,1,0:T(8,128)S(1)}, u32[]{:S(2)}, u32[]{:S(2)}) collective-permute-start(f32[2,136,256]{2,1,0:T(8,128)S(1)} %get-tuple-element.30), channel_id=1, source_target_pairs={{0,1},{1,0},{2,3},{3,2},{4,5},{5,4},{6,7},{7,6},{8,9},{9,8},{10,11... | collective-permute-start | bytes 835592 | tf_op jit(solution)/shard_map/ppermute | solution.py:219
  2.6 0.0 copy-done
  2.6 0.4 %rest_products.1 = (f32[3,128,256]{2,1,0:T(8,128)S(1)}, f32[3,128,256]{2,1,0:T(8,128)S(1)}, f32[3,128,256]{2,1,0:T(8,128)S(1)}, f32[3,128,256]{2,1,0:T(8,128)S(1)}) custom-call(bf16[128,128]{1,0:T(8,128)(2,1)S(1)} %get-tuple-element.26.masked, bf16[1,128,4096]{2,1,0:T(8,128)(2,1)S(1)} %copy-done), custom_call_target="tpu_custom_call" | custom-call | tf_op jit(solution)/shard_map/rest_products/pallas_call | solution.py:276
  3.0 0.1 collective-permute-start
  3.2 0.5 %collective-permute-start.5 = (f32[3,128,256]{2,1,0:T(8,128)S(1)}, f32[3,128,256]{2,1,0:T(8,128)S(1)}, u32[]{:S(2)}, u32[]{:S(2)}) collective-permute-start(f32[3,128,256]{2,1,0:T(8,128)S(1)} %get-tuple-element.34), channel_id=1, source_target_pairs={{0,1},{1,0},{2,3},{3,2},{4,5},{5,4},{6,7},{7,6},{8,9},{9,8},{10,11... | collective-permute-start | bytes 1179656 | tf_op jit(solution)/shard_map/ppermute | solution.py:219
  3.6 0.2 collective-permute-done.1.refs_1_
  3.8 3.0 %collective-permute-start.3 = (f32[1,128,256]{2,1,0:T(8,128)S(1)}, f32[1,128,256]{2,1,0:T(8,128)S(1)}, u32[]{:S(2)}, u32[]{:S(2)}) collective-permute-start(f32[1,128,256]{2,1,0:T(8,128)S(1)} %add_a1.1.after), channel_id=1, source_target_pairs={{0,2},{1,3},{2,0},{3,1},{4,6},{5,7},{6,4},{7,5},{8,10},{9,11},{10,... | collective-permute-start | bytes 393224 | tf_op jit(solution)/shard_map/ppermute | solution.py:219
  7.5 0.0 copy-done.1
  7.5 0.0 copy-done.4
  7.6 0.3 collective-permute-start.2
  7.8 1.8 %collective-permute-start.9 = (f32[128,128]{1,0:T(8,128)S(1)}, f32[128,128]{1,0:T(8,128)S(1)}, u32[]{:S(2)}, u32[]{:S(2)}) collective-permute-start(f32[128,128]{1,0:T(8,128)S(1)} %get-tuple-element.36.refs_2_), channel_id=1, source_target_pairs={{0,16},{8,24},{16,0},{24,8},{1,17},{9,25},{17,1},{25,9},{2,18},{10... | collective-permute-start | bytes 196616 | tf_op jit(solution)/shard_map/ppermute | solution.py:219
  9.6 0.0 collective-permute-done.refs_1_.come
  9.6 1.5 %collective-permute-done.3.refs_2_ = f32[1,128,256]{2,1,0:T(8,128)S(1)} collective-permute-done((f32[1,128,256]{2,1,0:T(8,128)S(1)}, f32[1,128,256]{2,1,0:T(8,128)S(1)}, u32[]{:S(2)}, u32[]{:S(2)}) %collective-permute-start.3) | collective-permute-done | bytes 131104 | tf_op jit(solution)/shard_map/ppermute | solution.py:219
  11.2 3.0 %collective-permute-start.7 = (f32[1,128,256]{2,1,0:T(8,128)S(1)}, f32[1,128,256]{2,1,0:T(8,128)S(1)}, u32[]{:S(2)}, u32[]{:S(2)}) collective-permute-start(f32[1,128,256]{2,1,0:T(8,128)S(1)} %add_c1.1.refs_3_.refs_2_), channel_id=1, source_target_pairs={{0,4},{1,5},{2,6},{3,7},{4,0},{5,1},{6,2},{7,3},{8,12},{9,13},{10,... | collective-permute-start | bytes 393224 | tf_op jit(solution)/shard_map/ppermute | solution.py:219
  14.2 0.0 collective-permute-done.5.refs_1_.come
  14.2 1.8 %collective-permute-start.8 = (f32[1,128,256]{2,1,0:T(8,128)S(1)}, f32[1,128,256]{2,1,0:T(8,128)S(1)}, u32[]{:S(2)}, u32[]{:S(2)}) collective-permute-start(f32[1,128,256]{2,1,0:T(8,128)S(1)} %add_n1.1), channel_id=1, source_target_pairs={{0,2},{1,3},{2,0},{3,1},{4,6},{5,7},{6,4},{7,5},{8,10},{9,11},{10,... | collective-permute-start | bytes 393224 | tf_op jit(solution)/shard_map/ppermute | solution.py:219
  16.0 0.0 collective-permute-done.2.refs_2_
  16.0 1.0 %collective-permute-start.4 = (f32[1,128,256]{2,1,0:T(8,128)S(1)}, f32[1,128,256]{2,1,0:T(8,128)S(1)}, u32[]{:S(2)}, u32[]{:S(2)}) collective-permute-start(f32[1,128,256]{2,1,0:T(8,128)S(1)} %add_c2.1.refs_2_), channel_id=1, source_target_pairs={{0,4},{1,5},{2,6},{3,7},{4,0},{5,1},{6,2},{7,3},{8,12},{9,13},{10,... | collective-permute-start | bytes 393224 | tf_op jit(solution)/shard_map/ppermute | solution.py:219
  17.0 0.0 copy-start.5
  17.0 1.6 %collective-permute-start.6 = (f32[1,128,256]{2,1,0:T(8,128)S(1)}, f32[1,128,256]{2,1,0:T(8,128)S(1)}, u32[]{:S(2)}, u32[]{:S(2)}) collective-permute-start(f32[1,128,256]{2,1,0:T(8,128)S(1)} %add_n2.1), channel_id=1, source_target_pairs={{0,2},{1,3},{2,0},{3,1},{4,6},{5,7},{6,4},{7,5},{8,10},{9,11},{10,... | collective-permute-start | bytes 393224 | tf_op jit(solution)/shard_map/ppermute | solution.py:219
  18.6 0.0 collective-permute-done.9
  18.7 1.5 %collective-permute-start.10 = (f32[128,128]{1,0:T(8,128)S(1)}, f32[128,128]{1,0:T(8,128)S(1)}, u32[]{:S(2)}, u32[]{:S(2)}) collective-permute-start(f32[128,128]{1,0:T(8,128)S(1)} %add.3.drift), channel_id=1, source_target_pairs={{0,8},{8,0},{16,24},{24,16},{1,9},{9,1},{17,25},{25,17},{2,10},{10... | collective-permute-start | bytes 196616 | tf_op jit(solution)/shard_map/ppermute | solution.py:219
  20.2 2.8 %collective-permute-done.10.other_drift = f32[128,128]{1,0:T(8,128)S(1)} collective-permute-done((f32[128,128]{1,0:T(8,128)S(1)}, f32[128,128]{1,0:T(8,128)S(1)}, u32[]{:S(2)}, u32[]{:S(2)}) %collective-permute-start.10) | collective-permute-done | bytes 65568 | tf_op jit(solution)/shard_map/ppermute | solution.py:219
  23.0 0.0 collective-permute-done.7.far
  23.0 0.1 collective-permute-done.8.near
  23.1 0.0 copy-done.2
  23.1 1.1 %left_step.1 = (f32[256,128]{1,0:T(8,128)S(1)}, f32[1,512,128]{2,1,0:T(8,128)}, f32[1,512,128]{2,1,0:T(8,128)}, f32[1,512,128]{2,1,0:T(8,128)}, f32[128,128]{1,0:T(8,128)}, /*index=5*/f32[128,128]{1,0:T(8,128)}) custom-call(f32[1,512,128]{2,1,0:T(8,128)S(1)} %copy-done.1, f32[1,512,128]{2,1,0:T(8,128)S(1)} %copy-done.2, f32[1,512,128]{2,1,0:T(8,128)S(1)} %copy-done.3, ...), custom_call_target="tpu_custom_call" | custom-call | flops 983040 | bytes 1310720 | tf_op jit(solution)/shard_map/left_step/pallas_call | solution.py:336
  24.2 0.4 %collective-permute-done.4.far = f32[1,128,256]{2,1,0:T(8,128)S(1)} collective-permute-done((f32[1,128,256]{2,1,0:T(8,128)S(1)}, f32[1,128,256]{2,1,0:T(8,128)S(1)}, u32[]{:S(2)}, u32[]{:S(2)}) %collective-permute-start.4) | collective-permute-done | bytes 131104 | tf_op jit(solution)/shard_map/ppermute | solution.py:219
  24.7 0.8 %collective-permute-done.6.near = f32[1,128,256]{2,1,0:T(8,128)S(1)} collective-permute-done((f32[1,128,256]{2,1,0:T(8,128)S(1)}, f32[1,128,256]{2,1,0:T(8,128)S(1)}, u32[]{:S(2)}, u32[]{:S(2)}) %collective-permute-start.6) | collective-permute-done | bytes 131104 | tf_op jit(solution)/shard_map/ppermute | solution.py:219
  25.5 1.0 %right_step.1 = (f32[1,512,128]{2,1,0:T(8,128)}, f32[1,512,128]{2,1,0:T(8,128)}, f32[1,512,128]{2,1,0:T(8,128)}) custom-call(f32[1,512,128]{2,1,0:T(8,128)S(1)} %copy-done.1, f32[1,512,128]{2,1,0:T(8,128)S(1)} %copy-done.2, f32[1,512,128]{2,1,0:T(8,128)S(1)} %copy-done.3, ...), custom_call_target="tpu_custom_call", output_to_operand_aliasing={{0}: (10, {}), {1}: (11, {}), {2}: (12, {})} | custom-call | tf_op jit(solution)/shard_map/right_step/pallas_call | solution.py:363
  (14 shorter events, 0.2 us)
Async XLA Ops:
  0.6 2.0 %copy-start = (bf16[1,128,4096]{2,1,0:T(8,128)(2,1)S(1)}, bf16[1,128,4096]{2,1,0:T(8,128)(2,1)}, u32[]{:S(2)}) copy-start(bf16[1,128,4096]{2,1,0:T(8,128)(2,1)} %features.3) | copy-start | bytes 3145732
  2.1 1.7 %collective-permute-start.1 = (f32[2,136,256]{2,1,0:T(8,128)S(1)}, f32[2,136,256]{2,1,0:T(8,128)S(1)}, u32[]{:S(2)}, u32[]{:S(2)}) collective-permute-start(f32[2,136,256]{2,1,0:T(8,128)S(1)} %get-tuple-element.30), channel_id=1, source_target_pairs={{0,1},{1,0},{2,3},{3,2},{4,5},{5,4},{6,7},{7,6},{8,9},{9,8},{10,11... | collective-permute-start | bytes 835592 | tf_op jit(solution)/shard_map/ppermute | solution.py:219
  3.0 6.6 %collective-permute-start = (f32[3,128,256]{2,1,0:T(8,128)S(1)}, f32[3,128,256]{2,1,0:T(8,128)S(1)}, u32[]{:S(2)}, u32[]{:S(2)}) collective-permute-start(f32[3,128,256]{2,1,0:T(8,128)S(1)} %get-tuple-element.28), channel_id=1, source_target_pairs={{0,1},{1,0},{2,3},{3,2},{4,5},{5,4},{6,7},{7,6},{8,9},{9,8},{10,11... | collective-permute-start | bytes 1179656 | tf_op jit(solution)/shard_map/ppermute | solution.py:219
  3.2 11.0 %collective-permute-start.5 = (f32[3,128,256]{2,1,0:T(8,128)S(1)}, f32[3,128,256]{2,1,0:T(8,128)S(1)}, u32[]{:S(2)}, u32[]{:S(2)}) collective-permute-start(f32[3,128,256]{2,1,0:T(8,128)S(1)} %get-tuple-element.34), channel_id=1, source_target_pairs={{0,1},{1,0},{2,3},{3,2},{4,5},{5,4},{6,7},{7,6},{8,9},{9,8},{10,11... | collective-permute-start | bytes 1179656 | tf_op jit(solution)/shard_map/ppermute | solution.py:219
  3.8 3.7 %copy-start.1 = (f32[1,512,128]{2,1,0:T(8,128)S(1)}, f32[1,512,128]{2,1,0:T(8,128)}, u32[]{:S(2)}) copy-start(f32[1,512,128]{2,1,0:T(8,128)} %params.5) | copy-start | bytes 786436
  3.8 3.7 %copy-start.4 = (f32[128,128]{1,0:T(8,128)S(1)}, f32[128,128]{1,0:T(8,128)}, u32[]{:S(2)}) copy-start(f32[128,128]{1,0:T(8,128)} %global_fragment.3) | copy-start | bytes 196612
  3.8 7.3 %collective-permute-start.3 = (f32[1,128,256]{2,1,0:T(8,128)S(1)}, f32[1,128,256]{2,1,0:T(8,128)S(1)}, u32[]{:S(2)}, u32[]{:S(2)}) collective-permute-start(f32[1,128,256]{2,1,0:T(8,128)S(1)} %add_a1.1.after), channel_id=1, source_target_pairs={{0,2},{1,3},{2,0},{3,1},{4,6},{5,7},{6,4},{7,5},{8,10},{9,11},{10,... | collective-permute-start | bytes 393224 | tf_op jit(solution)/shard_map/ppermute | solution.py:219
  7.6 8.4 %collective-permute-start.2 = (f32[1,128,256]{2,1,0:T(8,128)S(1)}, f32[1,128,256]{2,1,0:T(8,128)S(1)}, u32[]{:S(2)}, u32[]{:S(2)}) collective-permute-start(f32[1,128,256]{2,1,0:T(8,128)S(1)} %add_a2.1), channel_id=1, source_target_pairs={{0,2},{1,3},{2,0},{3,1},{4,6},{5,7},{6,4},{7,5},{8,10},{9,11},{10,... | collective-permute-start | bytes 393224 | tf_op jit(solution)/shard_map/ppermute | solution.py:219
  7.8 10.8 %collective-permute-start.9 = (f32[128,128]{1,0:T(8,128)S(1)}, f32[128,128]{1,0:T(8,128)S(1)}, u32[]{:S(2)}, u32[]{:S(2)}) collective-permute-start(f32[128,128]{1,0:T(8,128)S(1)} %get-tuple-element.36.refs_2_), channel_id=1, source_target_pairs={{0,16},{8,24},{16,0},{24,8},{1,17},{9,25},{17,1},{25,9},{2,18},{10... | collective-permute-start | bytes 196616 | tf_op jit(solution)/shard_map/ppermute | solution.py:219
  11.2 11.8 %collective-permute-start.7 = (f32[1,128,256]{2,1,0:T(8,128)S(1)}, f32[1,128,256]{2,1,0:T(8,128)S(1)}, u32[]{:S(2)}, u32[]{:S(2)}) collective-permute-start(f32[1,128,256]{2,1,0:T(8,128)S(1)} %add_c1.1.refs_3_.refs_2_), channel_id=1, source_target_pairs={{0,4},{1,5},{2,6},{3,7},{4,0},{5,1},{6,2},{7,3},{8,12},{9,13},{10,... | collective-permute-start | bytes 393224 | tf_op jit(solution)/shard_map/ppermute | solution.py:219
  14.2 8.9 %collective-permute-start.8 = (f32[1,128,256]{2,1,0:T(8,128)S(1)}, f32[1,128,256]{2,1,0:T(8,128)S(1)}, u32[]{:S(2)}, u32[]{:S(2)}) collective-permute-start(f32[1,128,256]{2,1,0:T(8,128)S(1)} %add_n1.1), channel_id=1, source_target_pairs={{0,2},{1,3},{2,0},{3,1},{4,6},{5,7},{6,4},{7,5},{8,10},{9,11},{10,... | collective-permute-start | bytes 393224 | tf_op jit(solution)/shard_map/ppermute | solution.py:219
  16.0 8.7 %collective-permute-start.4 = (f32[1,128,256]{2,1,0:T(8,128)S(1)}, f32[1,128,256]{2,1,0:T(8,128)S(1)}, u32[]{:S(2)}, u32[]{:S(2)}) collective-permute-start(f32[1,128,256]{2,1,0:T(8,128)S(1)} %add_c2.1.refs_2_), channel_id=1, source_target_pairs={{0,4},{1,5},{2,6},{3,7},{4,0},{5,1},{6,2},{7,3},{8,12},{9,13},{10,... | collective-permute-start | bytes 393224 | tf_op jit(solution)/shard_map/ppermute | solution.py:219
  17.0 6.1 %copy-start.2 = (f32[1,512,128]{2,1,0:T(8,128)S(1)}, f32[1,512,128]{2,1,0:T(8,128)}, u32[]{:S(2)}) copy-start(f32[1,512,128]{2,1,0:T(8,128)} %first.3) | copy-start | bytes 786436
  17.0 6.1 %copy-start.3 = (f32[1,512,128]{2,1,0:T(8,128)S(1)}, f32[1,512,128]{2,1,0:T(8,128)}, u32[]{:S(2)}) copy-start(f32[1,512,128]{2,1,0:T(8,128)} %second.3) | copy-start | bytes 786436
  17.0 6.1 %copy-start.5 = (f32[128,128]{1,0:T(8,128)S(1)}, f32[128,128]{1,0:T(8,128)}, u32[]{:S(2)}) copy-start(f32[128,128]{1,0:T(8,128)} %outer_momentum.1) | copy-start | bytes 196612
  17.0 8.4 %collective-permute-start.6 = (f32[1,128,256]{2,1,0:T(8,128)S(1)}, f32[1,128,256]{2,1,0:T(8,128)S(1)}, u32[]{:S(2)}, u32[]{:S(2)}) collective-permute-start(f32[1,128,256]{2,1,0:T(8,128)S(1)} %add_n2.1), channel_id=1, source_target_pairs={{0,2},{1,3},{2,0},{3,1},{4,6},{5,7},{6,4},{7,5},{8,10},{9,11},{10,... | collective-permute-start | bytes 393224 | tf_op jit(solution)/shard_map/ppermute | solution.py:219
  18.7 4.3 %collective-permute-start.10 = (f32[128,128]{1,0:T(8,128)S(1)}, f32[128,128]{1,0:T(8,128)S(1)}, u32[]{:S(2)}, u32[]{:S(2)}) collective-permute-start(f32[128,128]{1,0:T(8,128)S(1)} %add.3.drift), channel_id=1, source_target_pairs={{0,8},{8,0},{16,24},{24,16},{1,9},{9,1},{17,25},{25,17},{2,10},{10... | collective-permute-start | bytes 196616 | tf_op jit(solution)/shard_map/ppermute | solution.py:219

commit v13 on v12

--- a/solution.py
+++ b/solution.py
@@ -317,7 +317,7 @@
         far_right = hop(sent, "fsdp", devices, 2)
         passed = add((kept_pass, part(0)), (come_pass, part(0)), (far_left, part(0)), name="add_c1")
         far_left = hop(passed, "fsdp", devices, 4)
-        near_left = add((kept, part(1)), (come, part(1)), (passed, None), name="add_n1")
+        near_left = add((kept, part(1)), (come, part(1)), (sent, None), name="add_n1")
         far_right = add((kept_pass, part(1)), (come_pass, part(1)), (far_right, part(0)), (passed, None), name="add_c2")
         near_right = add((kept, part(2)), (come, part(2)), (far_right, None), name="add_n2")
         drift, _ = lax.optimization_barrier((drift, sent))

time: 26.6 us -> 27 us (1.015)
  starting transfers between devices: 15.1 us -> 16.5 us
  waiting for transfers between devices: 5.87 us -> 4.82 us
    ppermute x11, starting transfers between devices: 15.1 us -> 16.5 us  [hop(): return lax.ppermute(value, axis, [(d, d ^ bit) for d in range(devices)])]
    ppermute x11, waiting for transfers between devices: 5.87 us -> 4.82 us  [hop(): return lax.ppermute(value, axis, [(d, d ^ bit) for d in range(devices)])]
  transfers between devices with their start and end apart: 11 -> 11, of which waited for: 6 -> 3; matrix products, arithmetic and copies ran while one was open for 0% -> 0% of each run, Pallas kernels for 6% -> 6%
where the time goes in v13:
time: 27 us; the launch traced here: 26.8 us
  starting transfers between devices  16.5 us (61%)
  waiting for transfers between devices  4.82 us (18%)
  Pallas kernels  4.07 us (15%)
  between operations  1.4 us (5%)
    ppermute x11, starting transfers between devices, hop(): return lax.ppermute(value, axis, [(d, d ^ bit) for d in range(devices)])  16.5 us
    ppermute x11, waiting for transfers between devices, hop(): return lax.ppermute(value, axis, [(d, d ^ bit) for d in range(devices)])  4.82 us
    pallas_call x1, Pallas kernels, body(): pl.pallas_call(functools.partial(first_kernel, workers, (7, 6)), out_shap...  1.47 us
    pallas_call x1, Pallas kernels, body(): pl.pallas_call(left_kernel, out_shape=[block((half, width)), state, state...  1.08 us
    pallas_call x1, Pallas kernels, body(): pl.pallas_call(right_kernel, out_shape=[state] * 3, in_specs=[VMEM] * 10...  0.97 us
  transfers between devices with their start and end apart: 11, of which 3 were waited for; matrix products, arithmetic and copies ran while one was open for 0% of the time, Pallas kernels for 6%

profile of v13, /device:TPU:0, one launch (start us, length us, event | category | flops | bytes accessed | tf_op | source)
XLA Modules:
  0.0 26.8 jit_solution(10138573053703890363)
XLA Ops:
  0.6 0.0 copy-start
  0.6 1.5 %far_products.1 = (f32[2,136,256]{2,1,0:T(8,128)S(1)}, f32[2,128,256]{2,1,0:T(8,128)S(1)}, bf16[128,128]{1,0:T(8,128)(2,1)S(1)}, f32[8,128]{1,0:T(8,128)S(1)}) custom-call(s32[4]{0:T(128)} %counts.1, bf16[1,128,128]{2,1,0:T(8,128)(2,1)} %cotangent.1, bf16[1,128,4096]{2,1,0:T(8,128)(2,1)} %features.3), custom_call_target="tpu_custom_call" | custom-call | flops 33554432 | bytes 786432 | tf_op jit(solution)/shard_map/far_products/pallas_call | solution.py:256
  2.1 0.5 %collective-permute-start.1 = (f32[2,136,256]{2,1,0:T(8,128)S(1)}, f32[2,136,256]{2,1,0:T(8,128)S(1)}, u32[]{:S(2)}, u32[]{:S(2)}) collective-permute-start(f32[2,136,256]{2,1,0:T(8,128)S(1)} %get-tuple-element.30), channel_id=1, source_target_pairs={{0,1},{1,0},{2,3},{3,2},{4,5},{5,4},{6,7},{7,6},{8,9},{9,8},{10,11... | collective-permute-start | bytes 835592 | tf_op jit(solution)/shard_map/ppermute | solution.py:219
  2.6 0.0 copy-done
  2.6 0.4 %rest_products.1 = (f32[3,128,256]{2,1,0:T(8,128)S(1)}, f32[3,128,256]{2,1,0:T(8,128)S(1)}, f32[3,128,256]{2,1,0:T(8,128)S(1)}, f32[3,128,256]{2,1,0:T(8,128)S(1)}) custom-call(bf16[128,128]{1,0:T(8,128)(2,1)S(1)} %get-tuple-element.26.masked, bf16[1,128,4096]{2,1,0:T(8,128)(2,1)S(1)} %copy-done), custom_call_target="tpu_custom_call" | custom-call | tf_op jit(solution)/shard_map/rest_products/pallas_call | solution.py:276
  3.0 0.1 collective-permute-start.5
  3.2 0.5 %collective-permute-start = (f32[3,128,256]{2,1,0:T(8,128)S(1)}, f32[3,128,256]{2,1,0:T(8,128)S(1)}, u32[]{:S(2)}, u32[]{:S(2)}) collective-permute-start(f32[3,128,256]{2,1,0:T(8,128)S(1)} %get-tuple-element.28), channel_id=1, source_target_pairs={{0,1},{1,0},{2,3},{3,2},{4,5},{5,4},{6,7},{7,6},{8,9},{9,8},{10,11... | collective-permute-start | bytes 1179656 | tf_op jit(solution)/shard_map/ppermute | solution.py:219
  4.3 0.0 collective-permute-done.1.refs_1_
  4.3 0.0 copy-start.1
  4.3 0.0 copy-start.4
  4.3 2.7 %collective-permute-start.3 = (f32[1,128,256]{2,1,0:T(8,128)S(1)}, f32[1,128,256]{2,1,0:T(8,128)S(1)}, u32[]{:S(2)}, u32[]{:S(2)}) collective-permute-start(f32[1,128,256]{2,1,0:T(8,128)S(1)} %add_a1.1.after), channel_id=1, source_target_pairs={{0,2},{1,3},{2,0},{3,1},{4,6},{5,7},{6,4},{7,5},{8,10},{9,11},{10,... | collective-permute-start | bytes 393224 | tf_op jit(solution)/shard_map/ppermute | solution.py:219
  7.1 0.9 %collective-permute-start.2 = (f32[1,128,256]{2,1,0:T(8,128)S(1)}, f32[1,128,256]{2,1,0:T(8,128)S(1)}, u32[]{:S(2)}, u32[]{:S(2)}) collective-permute-start(f32[1,128,256]{2,1,0:T(8,128)S(1)} %add_a2.1.refs_2_), channel_id=1, source_target_pairs={{0,2},{1,3},{2,0},{3,1},{4,6},{5,7},{6,4},{7,5},{8,10},{9,11},{10,... | collective-permute-start | bytes 393224 | tf_op jit(solution)/shard_map/ppermute | solution.py:219
  8.0 1.5 %collective-permute-start.9 = (f32[128,128]{1,0:T(8,128)S(1)}, f32[128,128]{1,0:T(8,128)S(1)}, u32[]{:S(2)}, u32[]{:S(2)}) collective-permute-start(f32[128,128]{1,0:T(8,128)S(1)} %get-tuple-element.36.refs_2_), channel_id=1, source_target_pairs={{0,16},{8,24},{16,0},{24,8},{1,17},{9,25},{17,1},{25,9},{2,18},{10... | collective-permute-start | bytes 196616 | tf_op jit(solution)/shard_map/ppermute | solution.py:219
  9.5 0.0 collective-permute-done.5.refs_1_.come
  9.5 1.3 %collective-permute-start.8 = (f32[1,128,256]{2,1,0:T(8,128)S(1)}, f32[1,128,256]{2,1,0:T(8,128)S(1)}, u32[]{:S(2)}, u32[]{:S(2)}) collective-permute-start(f32[1,128,256]{2,1,0:T(8,128)S(1)} %add_n1.1), channel_id=1, source_target_pairs={{0,2},{1,3},{2,0},{3,1},{4,6},{5,7},{6,4},{7,5},{8,10},{9,11},{10,... | collective-permute-start | bytes 393224 | tf_op jit(solution)/shard_map/ppermute | solution.py:219
  10.8 0.0 collective-permute-done.refs_1_.come
  10.8 0.6 %collective-permute-done.3.refs_2_ = f32[1,128,256]{2,1,0:T(8,128)S(1)} collective-permute-done((f32[1,128,256]{2,1,0:T(8,128)S(1)}, f32[1,128,256]{2,1,0:T(8,128)S(1)}, u32[]{:S(2)}, u32[]{:S(2)}) %collective-permute-start.3) | collective-permute-done | bytes 131104 | tf_op jit(solution)/shard_map/ppermute | solution.py:219
  11.4 3.0 %collective-permute-start.7 = (f32[1,128,256]{2,1,0:T(8,128)S(1)}, f32[1,128,256]{2,1,0:T(8,128)S(1)}, u32[]{:S(2)}, u32[]{:S(2)}) collective-permute-start(f32[1,128,256]{2,1,0:T(8,128)S(1)} %add_c1.1.refs_3_), channel_id=1, source_target_pairs={{0,4},{1,5},{2,6},{3,7},{4,0},{5,1},{6,2},{7,3},{8,12},{9,13},{10,... | collective-permute-start | bytes 393224 | tf_op jit(solution)/shard_map/ppermute | solution.py:219
  14.4 0.0 collective-permute-done.2.refs_2_
  14.5 2.8 %collective-permute-start.4 = (f32[1,128,256]{2,1,0:T(8,128)S(1)}, f32[1,128,256]{2,1,0:T(8,128)S(1)}, u32[]{:S(2)}, u32[]{:S(2)}) collective-permute-start(f32[1,128,256]{2,1,0:T(8,128)S(1)} %add_c2.1.refs_2_), channel_id=1, source_target_pairs={{0,4},{1,5},{2,6},{3,7},{4,0},{5,1},{6,2},{7,3},{8,12},{9,13},{10,... | collective-permute-start | bytes 393224 | tf_op jit(solution)/shard_map/ppermute | solution.py:219
  17.3 0.0 copy-start.5
  17.3 1.7 %collective-permute-start.6 = (f32[1,128,256]{2,1,0:T(8,128)S(1)}, f32[1,128,256]{2,1,0:T(8,128)S(1)}, u32[]{:S(2)}, u32[]{:S(2)}) collective-permute-start(f32[1,128,256]{2,1,0:T(8,128)S(1)} %add_n2.1), channel_id=1, source_target_pairs={{0,2},{1,3},{2,0},{3,1},{4,6},{5,7},{6,4},{7,5},{8,10},{9,11},{10,... | collective-permute-start | bytes 393224 | tf_op jit(solution)/shard_map/ppermute | solution.py:219
  18.9 0.0 collective-permute-done.9
  19.0 1.6 %collective-permute-start.10 = (f32[128,128]{1,0:T(8,128)S(1)}, f32[128,128]{1,0:T(8,128)S(1)}, u32[]{:S(2)}, u32[]{:S(2)}) collective-permute-start(f32[128,128]{1,0:T(8,128)S(1)} %add.3.drift), channel_id=1, source_target_pairs={{0,8},{8,0},{16,24},{24,16},{1,9},{9,1},{17,25},{25,17},{2,10},{10... | collective-permute-start | bytes 196616 | tf_op jit(solution)/shard_map/ppermute | solution.py:219
  20.5 2.8 %collective-permute-done.10.other_drift = f32[128,128]{1,0:T(8,128)S(1)} collective-permute-done((f32[128,128]{1,0:T(8,128)S(1)}, f32[128,128]{1,0:T(8,128)S(1)}, u32[]{:S(2)}, u32[]{:S(2)}) %collective-permute-start.10) | collective-permute-done | bytes 65568 | tf_op jit(solution)/shard_map/ppermute | solution.py:219
  23.3 0.0 collective-permute-done.8.near
  23.3 0.0 collective-permute-done.7.far
  23.3 0.0 copy-done.2
  23.3 1.1 %left_step.1 = (f32[256,128]{1,0:T(8,128)S(1)}, f32[1,512,128]{2,1,0:T(8,128)}, f32[1,512,128]{2,1,0:T(8,128)}, f32[1,512,128]{2,1,0:T(8,128)}, f32[128,128]{1,0:T(8,128)}, /*index=5*/f32[128,128]{1,0:T(8,128)}) custom-call(f32[1,512,128]{2,1,0:T(8,128)S(1)} %copy-done.1, f32[1,512,128]{2,1,0:T(8,128)S(1)} %copy-done.2, f32[1,512,128]{2,1,0:T(8,128)S(1)} %copy-done.3, ...), custom_call_target="tpu_custom_call" | custom-call | flops 983040 | bytes 1310720 | tf_op jit(solution)/shard_map/left_step/pallas_call | solution.py:336
  24.4 1.4 %collective-permute-done.4.far = f32[1,128,256]{2,1,0:T(8,128)S(1)} collective-permute-done((f32[1,128,256]{2,1,0:T(8,128)S(1)}, f32[1,128,256]{2,1,0:T(8,128)S(1)}, u32[]{:S(2)}, u32[]{:S(2)}) %collective-permute-start.4) | collective-permute-done | bytes 131104 | tf_op jit(solution)/shard_map/ppermute | solution.py:219
  25.9 0.0 collective-permute-done.6.near
  25.9 1.0 %right_step.1 = (f32[1,512,128]{2,1,0:T(8,128)}, f32[1,512,128]{2,1,0:T(8,128)}, f32[1,512,128]{2,1,0:T(8,128)}) custom-call(f32[1,512,128]{2,1,0:T(8,128)S(1)} %copy-done.1, f32[1,512,128]{2,1,0:T(8,128)S(1)} %copy-done.2, f32[1,512,128]{2,1,0:T(8,128)S(1)} %copy-done.3, ...), custom_call_target="tpu_custom_call", output_to_operand_aliasing={{0}: (10, {}), {1}: (11, {}), {2}: (12, {})} | custom-call | tf_op jit(solution)/shard_map/right_step/pallas_call | solution.py:363
  (14 shorter events, 0.2 us)
Async XLA Ops:
  0.6 2.0 %copy-start = (bf16[1,128,4096]{2,1,0:T(8,128)(2,1)S(1)}, bf16[1,128,4096]{2,1,0:T(8,128)(2,1)}, u32[]{:S(2)}) copy-start(bf16[1,128,4096]{2,1,0:T(8,128)(2,1)} %features.3) | copy-start | bytes 3145732
  2.1 2.2 %collective-permute-start.1 = (f32[2,136,256]{2,1,0:T(8,128)S(1)}, f32[2,136,256]{2,1,0:T(8,128)S(1)}, u32[]{:S(2)}, u32[]{:S(2)}) collective-permute-start(f32[2,136,256]{2,1,0:T(8,128)S(1)} %get-tuple-element.30), channel_id=1, source_target_pairs={{0,1},{1,0},{2,3},{3,2},{4,5},{5,4},{6,7},{7,6},{8,9},{9,8},{10,11... | collective-permute-start | bytes 835592 | tf_op jit(solution)/shard_map/ppermute | solution.py:219
  3.0 6.5 %collective-permute-start.5 = (f32[3,128,256]{2,1,0:T(8,128)S(1)}, f32[3,128,256]{2,1,0:T(8,128)S(1)}, u32[]{:S(2)}, u32[]{:S(2)}) collective-permute-start(f32[3,128,256]{2,1,0:T(8,128)S(1)} %get-tuple-element.34), channel_id=1, source_target_pairs={{0,1},{1,0},{2,3},{3,2},{4,5},{5,4},{6,7},{7,6},{8,9},{9,8},{10,11... | collective-permute-start | bytes 1179656 | tf_op jit(solution)/shard_map/ppermute | solution.py:219
  3.2 7.6 %collective-permute-start = (f32[3,128,256]{2,1,0:T(8,128)S(1)}, f32[3,128,256]{2,1,0:T(8,128)S(1)}, u32[]{:S(2)}, u32[]{:S(2)}) collective-permute-start(f32[3,128,256]{2,1,0:T(8,128)S(1)} %get-tuple-element.28), channel_id=1, source_target_pairs={{0,1},{1,0},{2,3},{3,2},{4,5},{5,4},{6,7},{7,6},{8,9},{9,8},{10,11... | collective-permute-start | bytes 1179656 | tf_op jit(solution)/shard_map/ppermute | solution.py:219
  4.3 2.8 %copy-start.1 = (f32[1,512,128]{2,1,0:T(8,128)S(1)}, f32[1,512,128]{2,1,0:T(8,128)}, u32[]{:S(2)}) copy-start(f32[1,512,128]{2,1,0:T(8,128)} %params.5) | copy-start | bytes 786436
  4.3 2.8 %copy-start.4 = (f32[128,128]{1,0:T(8,128)S(1)}, f32[128,128]{1,0:T(8,128)}, u32[]{:S(2)}) copy-start(f32[128,128]{1,0:T(8,128)} %global_fragment.3) | copy-start | bytes 196612
  4.3 7.1 %collective-permute-start.3 = (f32[1,128,256]{2,1,0:T(8,128)S(1)}, f32[1,128,256]{2,1,0:T(8,128)S(1)}, u32[]{:S(2)}, u32[]{:S(2)}) collective-permute-start(f32[1,128,256]{2,1,0:T(8,128)S(1)} %add_a1.1.after), channel_id=1, source_target_pairs={{0,2},{1,3},{2,0},{3,1},{4,6},{5,7},{6,4},{7,5},{8,10},{9,11},{10,... | collective-permute-start | bytes 393224 | tf_op jit(solution)/shard_map/ppermute | solution.py:219
  7.1 7.3 %collective-permute-start.2 = (f32[1,128,256]{2,1,0:T(8,128)S(1)}, f32[1,128,256]{2,1,0:T(8,128)S(1)}, u32[]{:S(2)}, u32[]{:S(2)}) collective-permute-start(f32[1,128,256]{2,1,0:T(8,128)S(1)} %add_a2.1.refs_2_), channel_id=1, source_target_pairs={{0,2},{1,3},{2,0},{3,1},{4,6},{5,7},{6,4},{7,5},{8,10},{9,11},{10,... | collective-permute-start | bytes 393224 | tf_op jit(solution)/shard_map/ppermute | solution.py:219
  8.0 10.9 %collective-permute-start.9 = (f32[128,128]{1,0:T(8,128)S(1)}, f32[128,128]{1,0:T(8,128)S(1)}, u32[]{:S(2)}, u32[]{:S(2)}) collective-permute-start(f32[128,128]{1,0:T(8,128)S(1)} %get-tuple-element.36.refs_2_), channel_id=1, source_target_pairs={{0,16},{8,24},{16,0},{24,8},{1,17},{9,25},{17,1},{25,9},{2,18},{10... | collective-permute-start | bytes 196616 | tf_op jit(solution)/shard_map/ppermute | solution.py:219
  9.5 13.7 %collective-permute-start.8 = (f32[1,128,256]{2,1,0:T(8,128)S(1)}, f32[1,128,256]{2,1,0:T(8,128)S(1)}, u32[]{:S(2)}, u32[]{:S(2)}) collective-permute-start(f32[1,128,256]{2,1,0:T(8,128)S(1)} %add_n1.1), channel_id=1, source_target_pairs={{0,2},{1,3},{2,0},{3,1},{4,6},{5,7},{6,4},{7,5},{8,10},{9,11},{10,... | collective-permute-start | bytes 393224 | tf_op jit(solution)/shard_map/ppermute | solution.py:219
  11.4 11.9 %collective-permute-start.7 = (f32[1,128,256]{2,1,0:T(8,128)S(1)}, f32[1,128,256]{2,1,0:T(8,128)S(1)}, u32[]{:S(2)}, u32[]{:S(2)}) collective-permute-start(f32[1,128,256]{2,1,0:T(8,128)S(1)} %add_c1.1.refs_3_), channel_id=1, source_target_pairs={{0,4},{1,5},{2,6},{3,7},{4,0},{5,1},{6,2},{7,3},{8,12},{9,13},{10,... | collective-permute-start | bytes 393224 | tf_op jit(solution)/shard_map/ppermute | solution.py:219
  14.5 11.4 %collective-permute-start.4 = (f32[1,128,256]{2,1,0:T(8,128)S(1)}, f32[1,128,256]{2,1,0:T(8,128)S(1)}, u32[]{:S(2)}, u32[]{:S(2)}) collective-permute-start(f32[1,128,256]{2,1,0:T(8,128)S(1)} %add_c2.1.refs_2_), channel_id=1, source_target_pairs={{0,4},{1,5},{2,6},{3,7},{4,0},{5,1},{6,2},{7,3},{8,12},{9,13},{10,... | collective-permute-start | bytes 393224 | tf_op jit(solution)/shard_map/ppermute | solution.py:219
  17.3 6.0 %copy-start.2 = (f32[1,512,128]{2,1,0:T(8,128)S(1)}, f32[1,512,128]{2,1,0:T(8,128)}, u32[]{:S(2)}) copy-start(f32[1,512,128]{2,1,0:T(8,128)} %first.3) | copy-start | bytes 786436
  17.3 6.0 %copy-start.3 = (f32[1,512,128]{2,1,0:T(8,128)S(1)}, f32[1,512,128]{2,1,0:T(8,128)}, u32[]{:S(2)}) copy-start(f32[1,512,128]{2,1,0:T(8,128)} %second.3) | copy-start | bytes 786436
  17.3 6.0 %copy-start.5 = (f32[128,128]{1,0:T(8,128)S(1)}, f32[128,128]{1,0:T(8,128)}, u32[]{:S(2)}) copy-start(f32[128,128]{1,0:T(8,128)} %outer_momentum.1) | copy-start | bytes 196612
  17.3 8.6 %collective-permute-start.6 = (f32[1,128,256]{2,1,0:T(8,128)S(1)}, f32[1,128,256]{2,1,0:T(8,128)S(1)}, u32[]{:S(2)}, u32[]{:S(2)}) collective-permute-start(f32[1,128,256]{2,1,0:T(8,128)S(1)} %add_n2.1), channel_id=1, source_target_pairs={{0,2},{1,3},{2,0},{3,1},{4,6},{5,7},{6,4},{7,5},{8,10},{9,11},{10,... | collective-permute-start | bytes 393224 | tf_op jit(solution)/shard_map/ppermute | solution.py:219
  19.0 4.3 %collective-permute-start.10 = (f32[128,128]{1,0:T(8,128)S(1)}, f32[128,128]{1,0:T(8,128)S(1)}, u32[]{:S(2)}, u32[]{:S(2)}) collective-permute-start(f32[128,128]{1,0:T(8,128)S(1)} %add.3.drift), channel_id=1, source_target_pairs={{0,8},{8,0},{16,24},{24,16},{1,9},{9,1},{17,25},{25,17},{2,10},{10... | collective-permute-start | bytes 196616 | tf_op jit(solution)/shard_map/ppermute | solution.py:219

commit v14 on v12

--- a/solution.py
+++ b/solution.py
@@ -86,12 +86,15 @@
             targets[into + 1 - core][at] = product(masked[...], features[0, :, columns])
 
 
-def drift_kernel(info, fragment, params, global_fragment, after, drift, scale):
+def drift_kernel(info, fragment, params, global_fragment, after, drift, scale, params_held, global_held, sems):
     del after
+    copies = fetch((params, global_fragment), (params_held, global_held), sems)
     mine = pl.ds(fragment[0], drift.shape[0], stride=FRAGS)
-    drift[...] = info[0:1, :] * (global_fragment[...] - params[0, mine, :])
     scale[...] = jnp.ones_like(scale)
     scale[mine, :] = jnp.full_like(drift, 1.0 - MIXING)
+    for copy in copies:
+        copy.wait()
+    drift[...] = info[0:1, :] * (global_held[...] - params_held[0, mine, :])
 
 
 def add_kernel(picks, *refs):
@@ -246,8 +249,9 @@
 
         room = pltpu.CompilerParams(vmem_limit_bytes=ROOM)
         free = pl.CostEstimate(flops=0, bytes_accessed=0, transcendentals=0)
-        far_counts, far_features, far_cotangent = (
-            pltpu.with_memory_space_constraint(array, pltpu.HBM) for array in (token_counts, features, cotangent)
+        far_counts, far_features, far_cotangent, far_params, far_global = (
+            pltpu.with_memory_space_constraint(array, pltpu.HBM)
+            for array in (token_counts, features, cotangent, params, global_fragment)
         )
         held_counts = pltpu.SMEM(token_counts.shape, token_counts.dtype)
         held_piece = pltpu.VMEM(global_fragment.shape, global_fragment.dtype)
@@ -307,12 +311,13 @@
         drift, scale = pl.pallas_call(
             drift_kernel,
             out_shape=[piece, block((rows, width))],
-            in_specs=[VMEM, SMEM, VMEM, VMEM, ANY],
+            in_specs=[VMEM, SMEM, HBM, HBM, ANY],
             out_specs=[VMEM] * 2,
+            scratch_shapes=[pltpu.VMEM(params.shape, params.dtype), held_piece, pltpu.SemaphoreType.DMA((2,))],
             compiler_params=room,
             cost_estimate=free,
             name="drift",
-        )(info, fragment_index, params, global_fragment, sent)
+        )(info, fragment_index, far_params, far_global, sent)
         sent = add((kept_far, part(1)), (come_far, (part(1), part(0, width))), (drift, None), name="add_a2")
         far_right = hop(sent, "fsdp", devices, 2)
         passed = add((kept_pass, part(0)), (come_pass, part(0)), (far_left, part(0)), name="add_c1")

time: 26.6 us -> 26.5 us (level)
  waiting for transfers between devices: 5.87 us -> 4.34 us
  Pallas kernels: 4.07 us -> 5.03 us
  starting transfers between devices: 15.1 us -> 15.5 us
    ppermute x11, waiting for transfers between devices: 5.87 us -> 4.34 us  [hop(): return lax.ppermute(value, axis, [(d, d ^ bit) for d in range(devices)])]
    pallas_call x1, Pallas kernels: 0.03 us -> 0.99 us  [body(): pl.pallas_call(drift_kernel, out_shape=[piece, block((rows, width))], in_...]
    ppermute x11, starting transfers between devices: 15.1 us -> 15.5 us  [hop(): return lax.ppermute(value, axis, [(d, d ^ bit) for d in range(devices)])]
  transfers between devices with their start and end apart: 11 -> 11, of which waited for: 6 -> 6; matrix products, arithmetic and copies ran while one was open for 0% -> 0% of each run, Pallas kernels for 6% -> 10%
where the time goes in v14:
time: 26.5 us; the launch traced here: 26.3 us
  starting transfers between devices  15.5 us (58%)
  Pallas kernels  5.03 us (19%)
  waiting for transfers between devices  4.34 us (16%)
  between operations  1.39 us (5%)
    ppermute x11, starting transfers between devices, hop(): return lax.ppermute(value, axis, [(d, d ^ bit) for d in range(devices)])  15.5 us
    ppermute x11, waiting for transfers between devices, hop(): return lax.ppermute(value, axis, [(d, d ^ bit) for d in range(devices)])  4.34 us
    pallas_call x1, Pallas kernels, body(): pl.pallas_call(functools.partial(first_kernel, workers, (7, 6)), out_shap...  1.47 us
    pallas_call x1, Pallas kernels, body(): pl.pallas_call(left_kernel, out_shape=[block((half, width)), state, state...  1.08 us
    pallas_call x1, Pallas kernels, body(): pl.pallas_call(drift_kernel, out_shape=[piece, block((rows, width))], in_...  0.99 us
    pallas_call x1, Pallas kernels, body(): pl.pallas_call(right_kernel, out_shape=[state] * 3, in_specs=[VMEM] * 10...  0.97 us
  transfers between devices with their start and end apart: 11, of which 6 were waited for; matrix products, arithmetic and copies ran while one was open for 0% of the time, Pallas kernels for 10%

profile of v14, /device:TPU:0, one launch (start us, length us, event | category | flops | bytes accessed | tf_op | source)
XLA Modules:
  0.0 26.3 jit_solution(11224845150269616970)
XLA Ops:
  0.6 0.0 copy-start
  0.6 1.5 %far_products.1 = (f32[2,136,256]{2,1,0:T(8,128)S(1)}, f32[2,128,256]{2,1,0:T(8,128)S(1)}, bf16[128,128]{1,0:T(8,128)(2,1)S(1)}, f32[8,128]{1,0:T(8,128)S(1)}) custom-call(s32[4]{0:T(128)} %counts.1, bf16[1,128,128]{2,1,0:T(8,128)(2,1)} %cotangent.1, bf16[1,128,4096]{2,1,0:T(8,128)(2,1)} %features.3), custom_call_target="tpu_custom_call" | custom-call | flops 33554432 | bytes 786432 | tf_op jit(solution)/shard_map/far_products/pallas_call | solution.py:260
  2.1 0.5 %collective-permute-start.1 = (f32[2,136,256]{2,1,0:T(8,128)S(1)}, f32[2,136,256]{2,1,0:T(8,128)S(1)}, u32[]{:S(2)}, u32[]{:S(2)}) collective-permute-start(f32[2,136,256]{2,1,0:T(8,128)S(1)} %get-tuple-element.30), channel_id=1, source_target_pairs={{0,1},{1,0},{2,3},{3,2},{4,5},{5,4},{6,7},{7,6},{8,9},{9,8},{10,11... | collective-permute-start | bytes 835592 | tf_op jit(solution)/shard_map/ppermute | solution.py:222
  2.6 0.4 %rest_products.1 = (f32[3,128,256]{2,1,0:T(8,128)S(1)}, f32[3,128,256]{2,1,0:T(8,128)S(1)}, f32[3,128,256]{2,1,0:T(8,128)S(1)}, f32[3,128,256]{2,1,0:T(8,128)S(1)}) custom-call(bf16[128,128]{1,0:T(8,128)(2,1)S(1)} %get-tuple-element.26.masked, bf16[1,128,4096]{2,1,0:T(8,128)(2,1)S(1)} %copy-done), custom_call_target="tpu_custom_call" | custom-call | tf_op jit(solution)/shard_map/rest_products/pallas_call | solution.py:280
  3.0 0.1 collective-permute-start
  3.2 0.5 %collective-permute-start.5 = (f32[3,128,256]{2,1,0:T(8,128)S(1)}, f32[3,128,256]{2,1,0:T(8,128)S(1)}, u32[]{:S(2)}, u32[]{:S(2)}) collective-permute-start(f32[3,128,256]{2,1,0:T(8,128)S(1)} %get-tuple-element.34), channel_id=1, source_target_pairs={{0,1},{1,0},{2,3},{3,2},{4,5},{5,4},{6,7},{7,6},{8,9},{9,8},{10,11... | collective-permute-start | bytes 1179656 | tf_op jit(solution)/shard_map/ppermute | solution.py:222
  3.6 0.2 collective-permute-done.1.refs_1_
  3.8 3.0 %collective-permute-start.3 = (f32[1,128,256]{2,1,0:T(8,128)S(1)}, f32[1,128,256]{2,1,0:T(8,128)S(1)}, u32[]{:S(2)}, u32[]{:S(2)}) collective-permute-start(f32[1,128,256]{2,1,0:T(8,128)S(1)} %add_a1.1.after), channel_id=1, source_target_pairs={{0,2},{1,3},{2,0},{3,1},{4,6},{5,7},{6,4},{7,5},{8,10},{9,11},{10,... | collective-permute-start | bytes 393224 | tf_op jit(solution)/shard_map/ppermute | solution.py:222
  7.5 1.0 %drift.1 = (f32[128,128]{1,0:T(8,128)S(1)}, f32[512,128]{1,0:T(8,128)S(1)}) custom-call(f32[8,128]{1,0:T(8,128)S(1)} %get-tuple-element.31.info, s32[1]{0:T(128)S(6)} %copy.20.fragment, f32[1,512,128]{2,1,0:T(8,128)} %params.5, f32[128,128]{1,0:T(8,128)} %global_fragment.3, f32[1,128,256]{2,1,0:T(8,128)S(1)} %add_a1.1.after), custom_call_target="tpu_custom_call" | custom-call | tf_op jit(solution)/shard_map/drift/pallas_call | solution.py:311
  8.5 0.1 collective-permute-start.2
  8.6 2.0 %collective-permute-start.9 = (f32[128,128]{1,0:T(8,128)S(1)}, f32[128,128]{1,0:T(8,128)S(1)}, u32[]{:S(2)}, u32[]{:S(2)}) collective-permute-start(f32[128,128]{1,0:T(8,128)S(1)} %get-tuple-element.36.refs_2_), channel_id=1, source_target_pairs={{0,16},{8,24},{16,0},{24,8},{1,17},{9,25},{17,1},{25,9},{2,18},{10... | collective-permute-start | bytes 196616 | tf_op jit(solution)/shard_map/ppermute | solution.py:222
  10.6 0.0 collective-permute-done.refs_1_.come
  10.6 0.1 collective-permute-done.3.refs_2_
  10.7 2.8 %collective-permute-start.7 = (f32[1,128,256]{2,1,0:T(8,128)S(1)}, f32[1,128,256]{2,1,0:T(8,128)S(1)}, u32[]{:S(2)}, u32[]{:S(2)}) collective-permute-start(f32[1,128,256]{2,1,0:T(8,128)S(1)} %add_c1.1.refs_3_.refs_2_), channel_id=1, source_target_pairs={{0,4},{1,5},{2,6},{3,7},{4,0},{5,1},{6,2},{7,3},{8,12},{9,13},{10,... | collective-permute-start | bytes 393224 | tf_op jit(solution)/shard_map/ppermute | solution.py:222
  13.5 0.0 collective-permute-done.5.refs_1_.come
  13.5 2.4 %collective-permute-start.8 = (f32[1,128,256]{2,1,0:T(8,128)S(1)}, f32[1,128,256]{2,1,0:T(8,128)S(1)}, u32[]{:S(2)}, u32[]{:S(2)}) collective-permute-start(f32[1,128,256]{2,1,0:T(8,128)S(1)} %add_n1.1), channel_id=1, source_target_pairs={{0,2},{1,3},{2,0},{3,1},{4,6},{5,7},{6,4},{7,5},{8,10},{9,11},{10,... | collective-permute-start | bytes 393224 | tf_op jit(solution)/shard_map/ppermute | solution.py:222
  16.0 0.0 collective-permute-done.2.refs_2_
  16.0 1.7 %collective-permute-start.4 = (f32[1,128,256]{2,1,0:T(8,128)S(1)}, f32[1,128,256]{2,1,0:T(8,128)S(1)}, u32[]{:S(2)}, u32[]{:S(2)}) collective-permute-start(f32[1,128,256]{2,1,0:T(8,128)S(1)} %add_c2.1.refs_2_), channel_id=1, source_target_pairs={{0,4},{1,5},{2,6},{3,7},{4,0},{5,1},{6,2},{7,3},{8,12},{9,13},{10,... | collective-permute-start | bytes 393224 | tf_op jit(solution)/shard_map/ppermute | solution.py:222
  17.7 0.0 copy-start.4
  17.7 0.0 copy-start.5
  17.7 1.0 %collective-permute-start.6 = (f32[1,128,256]{2,1,0:T(8,128)S(1)}, f32[1,128,256]{2,1,0:T(8,128)S(1)}, u32[]{:S(2)}, u32[]{:S(2)}) collective-permute-start(f32[1,128,256]{2,1,0:T(8,128)S(1)} %add_n2.1), channel_id=1, source_target_pairs={{0,2},{1,3},{2,0},{3,1},{4,6},{5,7},{6,4},{7,5},{8,10},{9,11},{10,... | collective-permute-start | bytes 393224 | tf_op jit(solution)/shard_map/ppermute | solution.py:222
  18.7 0.0 collective-permute-done.9
  18.7 1.5 %collective-permute-start.10 = (f32[128,128]{1,0:T(8,128)S(1)}, f32[128,128]{1,0:T(8,128)S(1)}, u32[]{:S(2)}, u32[]{:S(2)}) collective-permute-start(f32[128,128]{1,0:T(8,128)S(1)} %add.3.drift), channel_id=1, source_target_pairs={{0,8},{8,0},{16,24},{24,16},{1,9},{9,1},{17,25},{25,17},{2,10},{10... | collective-permute-start | bytes 196616 | tf_op jit(solution)/shard_map/ppermute | solution.py:222
  20.2 2.8 %collective-permute-done.10.other_drift = f32[128,128]{1,0:T(8,128)S(1)} collective-permute-done((f32[128,128]{1,0:T(8,128)S(1)}, f32[128,128]{1,0:T(8,128)S(1)}, u32[]{:S(2)}, u32[]{:S(2)}) %collective-permute-start.10) | collective-permute-done | bytes 65568 | tf_op jit(solution)/shard_map/ppermute | solution.py:222
  23.0 0.0 collective-permute-done.7.far
  23.0 0.1 collective-permute-done.8.near
  23.1 0.0 copy-done.1
  23.1 0.0 copy-done.3
  23.1 1.1 %left_step.1 = (f32[256,128]{1,0:T(8,128)S(1)}, f32[1,512,128]{2,1,0:T(8,128)}, f32[1,512,128]{2,1,0:T(8,128)}, f32[1,512,128]{2,1,0:T(8,128)}, f32[128,128]{1,0:T(8,128)}, /*index=5*/f32[128,128]{1,0:T(8,128)}) custom-call(f32[1,512,128]{2,1,0:T(8,128)S(1)} %copy-done.1, f32[1,512,128]{2,1,0:T(8,128)S(1)} %copy-done.2, f32[1,512,128]{2,1,0:T(8,128)S(1)} %copy-done.3, ...), custom_call_target="tpu_custom_call" | custom-call | flops 983040 | bytes 1310720 | tf_op jit(solution)/shard_map/left_step/pallas_call | solution.py:341
  24.2 0.3 %collective-permute-done.4.far = f32[1,128,256]{2,1,0:T(8,128)S(1)} collective-permute-done((f32[1,128,256]{2,1,0:T(8,128)S(1)}, f32[1,128,256]{2,1,0:T(8,128)S(1)}, u32[]{:S(2)}, u32[]{:S(2)}) %collective-permute-start.4) | collective-permute-done | bytes 131104 | tf_op jit(solution)/shard_map/ppermute | solution.py:222
  24.5 0.8 %collective-permute-done.6.near = f32[1,128,256]{2,1,0:T(8,128)S(1)} collective-permute-done((f32[1,128,256]{2,1,0:T(8,128)S(1)}, f32[1,128,256]{2,1,0:T(8,128)S(1)}, u32[]{:S(2)}, u32[]{:S(2)}) %collective-permute-start.6) | collective-permute-done | bytes 131104 | tf_op jit(solution)/shard_map/ppermute | solution.py:222
  25.3 1.0 %right_step.1 = (f32[1,512,128]{2,1,0:T(8,128)}, f32[1,512,128]{2,1,0:T(8,128)}, f32[1,512,128]{2,1,0:T(8,128)}) custom-call(f32[1,512,128]{2,1,0:T(8,128)S(1)} %copy-done.1, f32[1,512,128]{2,1,0:T(8,128)S(1)} %copy-done.2, f32[1,512,128]{2,1,0:T(8,128)S(1)} %copy-done.3, ...), custom_call_target="tpu_custom_call", output_to_operand_aliasing={{0}: (10, {}), {1}: (11, {}), {2}: (12, {})} | custom-call | tf_op jit(solution)/shard_map/right_step/pallas_call | solution.py:368
  (14 shorter events, 0.1 us)
Async XLA Ops:
  0.6 2.0 %copy-start = (bf16[1,128,4096]{2,1,0:T(8,128)(2,1)S(1)}, bf16[1,128,4096]{2,1,0:T(8,128)(2,1)}, u32[]{:S(2)}) copy-start(bf16[1,128,4096]{2,1,0:T(8,128)(2,1)} %features.3) | copy-start | bytes 3145732
  2.1 1.7 %collective-permute-start.1 = (f32[2,136,256]{2,1,0:T(8,128)S(1)}, f32[2,136,256]{2,1,0:T(8,128)S(1)}, u32[]{:S(2)}, u32[]{:S(2)}) collective-permute-start(f32[2,136,256]{2,1,0:T(8,128)S(1)} %get-tuple-element.30), channel_id=1, source_target_pairs={{0,1},{1,0},{2,3},{3,2},{4,5},{5,4},{6,7},{7,6},{8,9},{9,8},{10,11... | collective-permute-start | bytes 835592 | tf_op jit(solution)/shard_map/ppermute | solution.py:222
  3.0 7.5 %collective-permute-start = (f32[3,128,256]{2,1,0:T(8,128)S(1)}, f32[3,128,256]{2,1,0:T(8,128)S(1)}, u32[]{:S(2)}, u32[]{:S(2)}) collective-permute-start(f32[3,128,256]{2,1,0:T(8,128)S(1)} %get-tuple-element.28), channel_id=1, source_target_pairs={{0,1},{1,0},{2,3},{3,2},{4,5},{5,4},{6,7},{7,6},{8,9},{9,8},{10,11... | collective-permute-start | bytes 1179656 | tf_op jit(solution)/shard_map/ppermute | solution.py:222
  3.2 10.3 %collective-permute-start.5 = (f32[3,128,256]{2,1,0:T(8,128)S(1)}, f32[3,128,256]{2,1,0:T(8,128)S(1)}, u32[]{:S(2)}, u32[]{:S(2)}) collective-permute-start(f32[3,128,256]{2,1,0:T(8,128)S(1)} %get-tuple-element.34), channel_id=1, source_target_pairs={{0,1},{1,0},{2,3},{3,2},{4,5},{5,4},{6,7},{7,6},{8,9},{9,8},{10,11... | collective-permute-start | bytes 1179656 | tf_op jit(solution)/shard_map/ppermute | solution.py:222
  3.8 6.9 %collective-permute-start.3 = (f32[1,128,256]{2,1,0:T(8,128)S(1)}, f32[1,128,256]{2,1,0:T(8,128)S(1)}, u32[]{:S(2)}, u32[]{:S(2)}) collective-permute-start(f32[1,128,256]{2,1,0:T(8,128)S(1)} %add_a1.1.after), channel_id=1, source_target_pairs={{0,2},{1,3},{2,0},{3,1},{4,6},{5,7},{6,4},{7,5},{8,10},{9,11},{10,... | collective-permute-start | bytes 393224 | tf_op jit(solution)/shard_map/ppermute | solution.py:222
  8.5 7.4 %collective-permute-start.2 = (f32[1,128,256]{2,1,0:T(8,128)S(1)}, f32[1,128,256]{2,1,0:T(8,128)S(1)}, u32[]{:S(2)}, u32[]{:S(2)}) collective-permute-start(f32[1,128,256]{2,1,0:T(8,128)S(1)} %add_a2.1), channel_id=1, source_target_pairs={{0,2},{1,3},{2,0},{3,1},{4,6},{5,7},{6,4},{7,5},{8,10},{9,11},{10,... | collective-permute-start | bytes 393224 | tf_op jit(solution)/shard_map/ppermute | solution.py:222
  8.6 10.1 %collective-permute-start.9 = (f32[128,128]{1,0:T(8,128)S(1)}, f32[128,128]{1,0:T(8,128)S(1)}, u32[]{:S(2)}, u32[]{:S(2)}) collective-permute-start(f32[128,128]{1,0:T(8,128)S(1)} %get-tuple-element.36.refs_2_), channel_id=1, source_target_pairs={{0,16},{8,24},{16,0},{24,8},{1,17},{9,25},{17,1},{25,9},{2,18},{10... | collective-permute-start | bytes 196616 | tf_op jit(solution)/shard_map/ppermute | solution.py:222
  10.7 12.3 %collective-permute-start.7 = (f32[1,128,256]{2,1,0:T(8,128)S(1)}, f32[1,128,256]{2,1,0:T(8,128)S(1)}, u32[]{:S(2)}, u32[]{:S(2)}) collective-permute-start(f32[1,128,256]{2,1,0:T(8,128)S(1)} %add_c1.1.refs_3_.refs_2_), channel_id=1, source_target_pairs={{0,4},{1,5},{2,6},{3,7},{4,0},{5,1},{6,2},{7,3},{8,12},{9,13},{10,... | collective-permute-start | bytes 393224 | tf_op jit(solution)/shard_map/ppermute | solution.py:222
  13.5 9.6 %collective-permute-start.8 = (f32[1,128,256]{2,1,0:T(8,128)S(1)}, f32[1,128,256]{2,1,0:T(8,128)S(1)}, u32[]{:S(2)}, u32[]{:S(2)}) collective-permute-start(f32[1,128,256]{2,1,0:T(8,128)S(1)} %add_n1.1), channel_id=1, source_target_pairs={{0,2},{1,3},{2,0},{3,1},{4,6},{5,7},{6,4},{7,5},{8,10},{9,11},{10,... | collective-permute-start | bytes 393224 | tf_op jit(solution)/shard_map/ppermute | solution.py:222
  16.0 8.5 %collective-permute-start.4 = (f32[1,128,256]{2,1,0:T(8,128)S(1)}, f32[1,128,256]{2,1,0:T(8,128)S(1)}, u32[]{:S(2)}, u32[]{:S(2)}) collective-permute-start(f32[1,128,256]{2,1,0:T(8,128)S(1)} %add_c2.1.refs_2_), channel_id=1, source_target_pairs={{0,4},{1,5},{2,6},{3,7},{4,0},{5,1},{6,2},{7,3},{8,12},{9,13},{10,... | collective-permute-start | bytes 393224 | tf_op jit(solution)/shard_map/ppermute | solution.py:222
  17.7 5.4 %copy-start.1 = (f32[1,512,128]{2,1,0:T(8,128)S(1)}, f32[1,512,128]{2,1,0:T(8,128)}, u32[]{:S(2)}) copy-start(f32[1,512,128]{2,1,0:T(8,128)} %params.5) | copy-start | bytes 786436
  17.7 5.4 %copy-start.2 = (f32[1,512,128]{2,1,0:T(8,128)S(1)}, f32[1,512,128]{2,1,0:T(8,128)}, u32[]{:S(2)}) copy-start(f32[1,512,128]{2,1,0:T(8,128)} %first.3) | copy-start | bytes 786436
  17.7 5.4 %copy-start.3 = (f32[1,512,128]{2,1,0:T(8,128)S(1)}, f32[1,512,128]{2,1,0:T(8,128)}, u32[]{:S(2)}) copy-start(f32[1,512,128]{2,1,0:T(8,128)} %second.3) | copy-start | bytes 786436
  17.7 5.4 %copy-start.4 = (f32[128,128]{1,0:T(8,128)S(1)}, f32[128,128]{1,0:T(8,128)}, u32[]{:S(2)}) copy-start(f32[128,128]{1,0:T(8,128)} %global_fragment.3) | copy-start | bytes 196612
  17.7 5.4 %copy-start.5 = (f32[128,128]{1,0:T(8,128)S(1)}, f32[128,128]{1,0:T(8,128)}, u32[]{:S(2)}) copy-start(f32[128,128]{1,0:T(8,128)} %outer_momentum.1) | copy-start | bytes 196612
  17.7 7.6 %collective-permute-start.6 = (f32[1,128,256]{2,1,0:T(8,128)S(1)}, f32[1,128,256]{2,1,0:T(8,128)S(1)}, u32[]{:S(2)}, u32[]{:S(2)}) collective-permute-start(f32[1,128,256]{2,1,0:T(8,128)S(1)} %add_n2.1), channel_id=1, source_target_pairs={{0,2},{1,3},{2,0},{3,1},{4,6},{5,7},{6,4},{7,5},{8,10},{9,11},{10,... | collective-permute-start | bytes 393224 | tf_op jit(solution)/shard_map/ppermute | solution.py:222
  18.7 4.3 %collective-permute-start.10 = (f32[128,128]{1,0:T(8,128)S(1)}, f32[128,128]{1,0:T(8,128)S(1)}, u32[]{:S(2)}, u32[]{:S(2)}) collective-permute-start(f32[128,128]{1,0:T(8,128)S(1)} %add.3.drift), channel_id=1, source_target_pairs={{0,8},{8,0},{16,24},{24,16},{1,9},{9,1},{17,25},{25,17},{2,10},{10... | collective-permute-start | bytes 196616 | tf_op jit(solution)/shard_map/ppermute | solution.py:222

commit v15 on v12

--- a/solution.py
+++ b/solution.py
@@ -313,7 +313,7 @@
             cost_estimate=free,
             name="drift",
         )(info, fragment_index, params, global_fragment, sent)
-        sent = add((kept_far, part(1)), (come_far, (part(1), part(0, width))), (drift, None), name="add_a2")
+        sent = add((kept_far, part(1)), (come_far, (part(1), part(0, width))), name="add_a2")
         far_right = hop(sent, "fsdp", devices, 2)
         passed = add((kept_pass, part(0)), (come_pass, part(0)), (far_left, part(0)), name="add_c1")
         far_left = hop(passed, "fsdp", devices, 4)

time: 26.6 us -> 26.7 us (level)
  no operation moved by 1% of the time
where the time goes in v15:
time: 26.7 us; the launch traced here: 26.5 us
  starting transfers between devices  15.2 us (57%)
  waiting for transfers between devices  5.83 us (22%)
  Pallas kernels  4.07 us (15%)
  between operations  1.39 us (5%)
    ppermute x11, starting transfers between devices, hop(): return lax.ppermute(value, axis, [(d, d ^ bit) for d in range(devices)])  15.2 us
    ppermute x11, waiting for transfers between devices, hop(): return lax.ppermute(value, axis, [(d, d ^ bit) for d in range(devices)])  5.83 us
    pallas_call x1, Pallas kernels, body(): pl.pallas_call(functools.partial(first_kernel, workers, (7, 6)), out_shap...  1.47 us
    pallas_call x1, Pallas kernels, body(): pl.pallas_call(left_kernel, out_shape=[block((half, width)), state, state...  1.09 us
    pallas_call x1, Pallas kernels, body(): pl.pallas_call(right_kernel, out_shape=[state] * 3, in_specs=[VMEM] * 10...  0.97 us
  transfers between devices with their start and end apart: 11, of which 6 were waited for; matrix products, arithmetic and copies ran while one was open for 0% of the time, Pallas kernels for 6%

profile of v15, /device:TPU:0, one launch (start us, length us, event | category | flops | bytes accessed | tf_op | source)
XLA Modules:
  0.0 26.5 jit_solution(746366585698807859)
XLA Ops:
  0.6 0.0 copy-start
  0.6 1.5 %far_products.1 = (f32[2,136,256]{2,1,0:T(8,128)S(1)}, f32[2,128,256]{2,1,0:T(8,128)S(1)}, bf16[128,128]{1,0:T(8,128)(2,1)S(1)}, f32[8,128]{1,0:T(8,128)S(1)}) custom-call(s32[4]{0:T(128)} %counts.1, bf16[1,128,128]{2,1,0:T(8,128)(2,1)} %cotangent.1, bf16[1,128,4096]{2,1,0:T(8,128)(2,1)} %features.3), custom_call_target="tpu_custom_call" | custom-call | flops 33554432 | bytes 786432 | tf_op jit(solution)/shard_map/far_products/pallas_call | solution.py:256
  2.1 0.5 %collective-permute-start.1 = (f32[2,136,256]{2,1,0:T(8,128)S(1)}, f32[2,136,256]{2,1,0:T(8,128)S(1)}, u32[]{:S(2)}, u32[]{:S(2)}) collective-permute-start(f32[2,136,256]{2,1,0:T(8,128)S(1)} %get-tuple-element.30), channel_id=1, source_target_pairs={{0,1},{1,0},{2,3},{3,2},{4,5},{5,4},{6,7},{7,6},{8,9},{9,8},{10,11... | collective-permute-start | bytes 835592 | tf_op jit(solution)/shard_map/ppermute | solution.py:219
  2.6 0.0 copy-done
  2.6 0.4 %rest_products.1 = (f32[3,128,256]{2,1,0:T(8,128)S(1)}, f32[3,128,256]{2,1,0:T(8,128)S(1)}, f32[3,128,256]{2,1,0:T(8,128)S(1)}, f32[3,128,256]{2,1,0:T(8,128)S(1)}) custom-call(bf16[128,128]{1,0:T(8,128)(2,1)S(1)} %get-tuple-element.26.masked, bf16[1,128,4096]{2,1,0:T(8,128)(2,1)S(1)} %copy-done), custom_call_target="tpu_custom_call" | custom-call | tf_op jit(solution)/shard_map/rest_products/pallas_call | solution.py:276
  3.0 0.1 collective-permute-start
  3.2 0.5 %collective-permute-start.5 = (f32[3,128,256]{2,1,0:T(8,128)S(1)}, f32[3,128,256]{2,1,0:T(8,128)S(1)}, u32[]{:S(2)}, u32[]{:S(2)}) collective-permute-start(f32[3,128,256]{2,1,0:T(8,128)S(1)} %get-tuple-element.32), channel_id=1, source_target_pairs={{0,1},{1,0},{2,3},{3,2},{4,5},{5,4},{6,7},{7,6},{8,9},{9,8},{10,11... | collective-permute-start | bytes 1179656 | tf_op jit(solution)/shard_map/ppermute | solution.py:219
  3.6 0.2 collective-permute-done.1.refs_1_
  3.8 0.0 copy-start.1
  3.9 0.0 copy-start.4
  3.9 3.0 %collective-permute-start.3 = (f32[1,128,256]{2,1,0:T(8,128)S(1)}, f32[1,128,256]{2,1,0:T(8,128)S(1)}, u32[]{:S(2)}, u32[]{:S(2)}) collective-permute-start(f32[1,128,256]{2,1,0:T(8,128)S(1)} %add_a1.1.after), channel_id=1, source_target_pairs={{0,2},{1,3},{2,0},{3,1},{4,6},{5,7},{6,4},{7,5},{8,10},{9,11},{10,... | collective-permute-start | bytes 393224 | tf_op jit(solution)/shard_map/ppermute | solution.py:219
  6.9 0.1 collective-permute-start.2
  7.7 2.0 %collective-permute-start.9 = (f32[128,128]{1,0:T(8,128)S(1)}, f32[128,128]{1,0:T(8,128)S(1)}, u32[]{:S(2)}, u32[]{:S(2)}) collective-permute-start(f32[128,128]{1,0:T(8,128)S(1)} %get-tuple-element.36), channel_id=1, source_target_pairs={{0,16},{8,24},{16,0},{24,8},{1,17},{9,25},{17,1},{25,9},{2,18},{10... | collective-permute-start | bytes 196616 | tf_op jit(solution)/shard_map/ppermute | solution.py:219
  9.7 0.0 collective-permute-done.refs_1_.come
  9.7 1.5 %collective-permute-done.3.refs_2_ = f32[1,128,256]{2,1,0:T(8,128)S(1)} collective-permute-done((f32[1,128,256]{2,1,0:T(8,128)S(1)}, f32[1,128,256]{2,1,0:T(8,128)S(1)}, u32[]{:S(2)}, u32[]{:S(2)}) %collective-permute-start.3) | collective-permute-done | bytes 131104 | tf_op jit(solution)/shard_map/ppermute | solution.py:219
  11.2 3.1 %collective-permute-start.7 = (f32[1,128,256]{2,1,0:T(8,128)S(1)}, f32[1,128,256]{2,1,0:T(8,128)S(1)}, u32[]{:S(2)}, u32[]{:S(2)}) collective-permute-start(f32[1,128,256]{2,1,0:T(8,128)S(1)} %add_c1.1.refs_3_.refs_2_), channel_id=1, source_target_pairs={{0,4},{1,5},{2,6},{3,7},{4,0},{5,1},{6,2},{7,3},{8,12},{9,13},{10,... | collective-permute-start | bytes 393224 | tf_op jit(solution)/shard_map/ppermute | solution.py:219
  14.3 0.0 collective-permute-done.5.refs_1_.come
  14.3 1.7 %collective-permute-start.8 = (f32[1,128,256]{2,1,0:T(8,128)S(1)}, f32[1,128,256]{2,1,0:T(8,128)S(1)}, u32[]{:S(2)}, u32[]{:S(2)}) collective-permute-start(f32[1,128,256]{2,1,0:T(8,128)S(1)} %add_n1.1), channel_id=1, source_target_pairs={{0,2},{1,3},{2,0},{3,1},{4,6},{5,7},{6,4},{7,5},{8,10},{9,11},{10,... | collective-permute-start | bytes 393224 | tf_op jit(solution)/shard_map/ppermute | solution.py:219
  16.0 0.0 collective-permute-done.2.refs_2_
  16.1 1.1 %collective-permute-start.4 = (f32[1,128,256]{2,1,0:T(8,128)S(1)}, f32[1,128,256]{2,1,0:T(8,128)S(1)}, u32[]{:S(2)}, u32[]{:S(2)}) collective-permute-start(f32[1,128,256]{2,1,0:T(8,128)S(1)} %add_c2.1.refs_2_), channel_id=1, source_target_pairs={{0,4},{1,5},{2,6},{3,7},{4,0},{5,1},{6,2},{7,3},{8,12},{9,13},{10,... | collective-permute-start | bytes 393224 | tf_op jit(solution)/shard_map/ppermute | solution.py:219
  17.2 0.0 copy-start.5
  17.2 1.5 %collective-permute-start.6 = (f32[1,128,256]{2,1,0:T(8,128)S(1)}, f32[1,128,256]{2,1,0:T(8,128)S(1)}, u32[]{:S(2)}, u32[]{:S(2)}) collective-permute-start(f32[1,128,256]{2,1,0:T(8,128)S(1)} %add_n2.1), channel_id=1, source_target_pairs={{0,2},{1,3},{2,0},{3,1},{4,6},{5,7},{6,4},{7,5},{8,10},{9,11},{10,... | collective-permute-start | bytes 393224 | tf_op jit(solution)/shard_map/ppermute | solution.py:219
  18.7 0.0 collective-permute-done.9
  18.7 1.6 %collective-permute-start.10 = (f32[128,128]{1,0:T(8,128)S(1)}, f32[128,128]{1,0:T(8,128)S(1)}, u32[]{:S(2)}, u32[]{:S(2)}) collective-permute-start(f32[128,128]{1,0:T(8,128)S(1)} %add.3.drift), channel_id=1, source_target_pairs={{0,8},{8,0},{16,24},{24,16},{1,9},{9,1},{17,25},{25,17},{2,10},{10... | collective-permute-start | bytes 196616 | tf_op jit(solution)/shard_map/ppermute | solution.py:219
  20.3 2.7 %collective-permute-done.10.other_drift = f32[128,128]{1,0:T(8,128)S(1)} collective-permute-done((f32[128,128]{1,0:T(8,128)S(1)}, f32[128,128]{1,0:T(8,128)S(1)}, u32[]{:S(2)}, u32[]{:S(2)}) %collective-permute-start.10) | collective-permute-done | bytes 65568 | tf_op jit(solution)/shard_map/ppermute | solution.py:219
  23.0 0.0 collective-permute-done.7.far
  23.0 0.5 %collective-permute-done.8.near = f32[1,128,256]{2,1,0:T(8,128)S(1)} collective-permute-done((f32[1,128,256]{2,1,0:T(8,128)S(1)}, f32[1,128,256]{2,1,0:T(8,128)S(1)}, u32[]{:S(2)}, u32[]{:S(2)}) %collective-permute-start.8) | collective-permute-done | bytes 131104 | tf_op jit(solution)/shard_map/ppermute | solution.py:219
  23.5 0.0 copy-done.3
  23.5 1.1 %left_step.1 = (f32[256,128]{1,0:T(8,128)S(1)}, f32[1,512,128]{2,1,0:T(8,128)}, f32[1,512,128]{2,1,0:T(8,128)}, f32[1,512,128]{2,1,0:T(8,128)}, f32[128,128]{1,0:T(8,128)}, /*index=5*/f32[128,128]{1,0:T(8,128)}) custom-call(f32[1,512,128]{2,1,0:T(8,128)S(1)} %copy-done.1, f32[1,512,128]{2,1,0:T(8,128)S(1)} %copy-done.2, f32[1,512,128]{2,1,0:T(8,128)S(1)} %copy-done.3, ...), custom_call_target="tpu_custom_call" | custom-call | flops 983040 | bytes 1310720 | tf_op jit(solution)/shard_map/left_step/pallas_call | solution.py:336
  24.6 0.1 collective-permute-done.4.far
  24.7 0.9 %collective-permute-done.6.near = f32[1,128,256]{2,1,0:T(8,128)S(1)} collective-permute-done((f32[1,128,256]{2,1,0:T(8,128)S(1)}, f32[1,128,256]{2,1,0:T(8,128)S(1)}, u32[]{:S(2)}, u32[]{:S(2)}) %collective-permute-start.6) | collective-permute-done | bytes 131104 | tf_op jit(solution)/shard_map/ppermute | solution.py:219
  25.5 1.0 %right_step.1 = (f32[1,512,128]{2,1,0:T(8,128)}, f32[1,512,128]{2,1,0:T(8,128)}, f32[1,512,128]{2,1,0:T(8,128)}) custom-call(f32[1,512,128]{2,1,0:T(8,128)S(1)} %copy-done.1, f32[1,512,128]{2,1,0:T(8,128)S(1)} %copy-done.2, f32[1,512,128]{2,1,0:T(8,128)S(1)} %copy-done.3, ...), custom_call_target="tpu_custom_call", output_to_operand_aliasing={{0}: (10, {}), {1}: (11, {}), {2}: (12, {})} | custom-call | tf_op jit(solution)/shard_map/right_step/pallas_call | solution.py:363
  (14 shorter events, 0.2 us)
Async XLA Ops:
  0.6 2.0 %copy-start = (bf16[1,128,4096]{2,1,0:T(8,128)(2,1)S(1)}, bf16[1,128,4096]{2,1,0:T(8,128)(2,1)}, u32[]{:S(2)}) copy-start(bf16[1,128,4096]{2,1,0:T(8,128)(2,1)} %features.3) | copy-start | bytes 3145732
  2.1 1.7 %collective-permute-start.1 = (f32[2,136,256]{2,1,0:T(8,128)S(1)}, f32[2,136,256]{2,1,0:T(8,128)S(1)}, u32[]{:S(2)}, u32[]{:S(2)}) collective-permute-start(f32[2,136,256]{2,1,0:T(8,128)S(1)} %get-tuple-element.30), channel_id=1, source_target_pairs={{0,1},{1,0},{2,3},{3,2},{4,5},{5,4},{6,7},{7,6},{8,9},{9,8},{10,11... | collective-permute-start | bytes 835592 | tf_op jit(solution)/shard_map/ppermute | solution.py:219
  3.0 6.7 %collective-permute-start = (f32[3,128,256]{2,1,0:T(8,128)S(1)}, f32[3,128,256]{2,1,0:T(8,128)S(1)}, u32[]{:S(2)}, u32[]{:S(2)}) collective-permute-start(f32[3,128,256]{2,1,0:T(8,128)S(1)} %get-tuple-element.28), channel_id=1, source_target_pairs={{0,1},{1,0},{2,3},{3,2},{4,5},{5,4},{6,7},{7,6},{8,9},{9,8},{10,11... | collective-permute-start | bytes 1179656 | tf_op jit(solution)/shard_map/ppermute | solution.py:219
  3.2 11.2 %collective-permute-start.5 = (f32[3,128,256]{2,1,0:T(8,128)S(1)}, f32[3,128,256]{2,1,0:T(8,128)S(1)}, u32[]{:S(2)}, u32[]{:S(2)}) collective-permute-start(f32[3,128,256]{2,1,0:T(8,128)S(1)} %get-tuple-element.32), channel_id=1, source_target_pairs={{0,1},{1,0},{2,3},{3,2},{4,5},{5,4},{6,7},{7,6},{8,9},{9,8},{10,11... | collective-permute-start | bytes 1179656 | tf_op jit(solution)/shard_map/ppermute | solution.py:219
  3.8 3.8 %copy-start.1 = (f32[1,512,128]{2,1,0:T(8,128)S(1)}, f32[1,512,128]{2,1,0:T(8,128)}, u32[]{:S(2)}) copy-start(f32[1,512,128]{2,1,0:T(8,128)} %params.5) | copy-start | bytes 786436
  3.9 3.8 %copy-start.4 = (f32[128,128]{1,0:T(8,128)S(1)}, f32[128,128]{1,0:T(8,128)}, u32[]{:S(2)}) copy-start(f32[128,128]{1,0:T(8,128)} %global_fragment.3) | copy-start | bytes 196612
  3.9 7.3 %collective-permute-start.3 = (f32[1,128,256]{2,1,0:T(8,128)S(1)}, f32[1,128,256]{2,1,0:T(8,128)S(1)}, u32[]{:S(2)}, u32[]{:S(2)}) collective-permute-start(f32[1,128,256]{2,1,0:T(8,128)S(1)} %add_a1.1.after), channel_id=1, source_target_pairs={{0,2},{1,3},{2,0},{3,1},{4,6},{5,7},{6,4},{7,5},{8,10},{9,11},{10,... | collective-permute-start | bytes 393224 | tf_op jit(solution)/shard_map/ppermute | solution.py:219
  6.9 9.1 %collective-permute-start.2 = (f32[1,128,256]{2,1,0:T(8,128)S(1)}, f32[1,128,256]{2,1,0:T(8,128)S(1)}, u32[]{:S(2)}, u32[]{:S(2)}) collective-permute-start(f32[1,128,256]{2,1,0:T(8,128)S(1)} %add_a2.1), channel_id=1, source_target_pairs={{0,2},{1,3},{2,0},{3,1},{4,6},{5,7},{6,4},{7,5},{8,10},{9,11},{10,... | collective-permute-start | bytes 393224 | tf_op jit(solution)/shard_map/ppermute | solution.py:219
  7.7 11.0 %collective-permute-start.9 = (f32[128,128]{1,0:T(8,128)S(1)}, f32[128,128]{1,0:T(8,128)S(1)}, u32[]{:S(2)}, u32[]{:S(2)}) collective-permute-start(f32[128,128]{1,0:T(8,128)S(1)} %get-tuple-element.36), channel_id=1, source_target_pairs={{0,16},{8,24},{16,0},{24,8},{1,17},{9,25},{17,1},{25,9},{2,18},{10... | collective-permute-start | bytes 196616 | tf_op jit(solution)/shard_map/ppermute | solution.py:219
  11.2 11.8 %collective-permute-start.7 = (f32[1,128,256]{2,1,0:T(8,128)S(1)}, f32[1,128,256]{2,1,0:T(8,128)S(1)}, u32[]{:S(2)}, u32[]{:S(2)}) collective-permute-start(f32[1,128,256]{2,1,0:T(8,128)S(1)} %add_c1.1.refs_3_.refs_2_), channel_id=1, source_target_pairs={{0,4},{1,5},{2,6},{3,7},{4,0},{5,1},{6,2},{7,3},{8,12},{9,13},{10,... | collective-permute-start | bytes 393224 | tf_op jit(solution)/shard_map/ppermute | solution.py:219
  14.3 9.2 %collective-permute-start.8 = (f32[1,128,256]{2,1,0:T(8,128)S(1)}, f32[1,128,256]{2,1,0:T(8,128)S(1)}, u32[]{:S(2)}, u32[]{:S(2)}) collective-permute-start(f32[1,128,256]{2,1,0:T(8,128)S(1)} %add_n1.1), channel_id=1, source_target_pairs={{0,2},{1,3},{2,0},{3,1},{4,6},{5,7},{6,4},{7,5},{8,10},{9,11},{10,... | collective-permute-start | bytes 393224 | tf_op jit(solution)/shard_map/ppermute | solution.py:219
  16.1 8.6 %collective-permute-start.4 = (f32[1,128,256]{2,1,0:T(8,128)S(1)}, f32[1,128,256]{2,1,0:T(8,128)S(1)}, u32[]{:S(2)}, u32[]{:S(2)}) collective-permute-start(f32[1,128,256]{2,1,0:T(8,128)S(1)} %add_c2.1.refs_2_), channel_id=1, source_target_pairs={{0,4},{1,5},{2,6},{3,7},{4,0},{5,1},{6,2},{7,3},{8,12},{9,13},{10,... | collective-permute-start | bytes 393224 | tf_op jit(solution)/shard_map/ppermute | solution.py:219
  17.1 6.4 %copy-start.2 = (f32[1,512,128]{2,1,0:T(8,128)S(1)}, f32[1,512,128]{2,1,0:T(8,128)}, u32[]{:S(2)}) copy-start(f32[1,512,128]{2,1,0:T(8,128)} %first.3) | copy-start | bytes 786436
  17.1 6.4 %copy-start.3 = (f32[1,512,128]{2,1,0:T(8,128)S(1)}, f32[1,512,128]{2,1,0:T(8,128)}, u32[]{:S(2)}) copy-start(f32[1,512,128]{2,1,0:T(8,128)} %second.3) | copy-start | bytes 786436
  17.2 6.4 %copy-start.5 = (f32[128,128]{1,0:T(8,128)S(1)}, f32[128,128]{1,0:T(8,128)}, u32[]{:S(2)}) copy-start(f32[128,128]{1,0:T(8,128)} %outer_momentum.1) | copy-start | bytes 196612
  17.2 8.4 %collective-permute-start.6 = (f32[1,128,256]{2,1,0:T(8,128)S(1)}, f32[1,128,256]{2,1,0:T(8,128)S(1)}, u32[]{:S(2)}, u32[]{:S(2)}) collective-permute-start(f32[1,128,256]{2,1,0:T(8,128)S(1)} %add_n2.1), channel_id=1, source_target_pairs={{0,2},{1,3},{2,0},{3,1},{4,6},{5,7},{6,4},{7,5},{8,10},{9,11},{10,... | collective-permute-start | bytes 393224 | tf_op jit(solution)/shard_map/ppermute | solution.py:219
  18.7 4.3 %collective-permute-start.10 = (f32[128,128]{1,0:T(8,128)S(1)}, f32[128,128]{1,0:T(8,128)S(1)}, u32[]{:S(2)}, u32[]{:S(2)}) collective-permute-start(f32[128,128]{1,0:T(8,128)S(1)} %add.3.drift), channel_id=1, source_target_pairs={{0,8},{8,0},{16,24},{24,16},{1,9},{9,1},{17,25},{25,17},{2,10},{10... | collective-permute-start | bytes 196616 | tf_op jit(solution)/shard_map/ppermute | solution.py:219

commit v16 on v8

--- a/solution.py
+++ b/solution.py
@@ -28,9 +28,10 @@
 ROOM = 8 << 20
 
 
-def masked_rows(live, cotangent):
-    rows = lax.broadcasted_iota(jnp.int32, cotangent.shape, 0)
-    return jnp.where(rows < live, cotangent.astype(jnp.float32), 0.0).astype(jnp.bfloat16)
+def masked_columns(live, cotangent):
+    turned = cotangent.astype(jnp.float32).T
+    tokens = lax.broadcasted_iota(jnp.int32, turned.shape, 1)
+    return jnp.where(tokens < live, turned, 0.0).astype(jnp.bfloat16)
 
 
 def columns_of(relative, rows, start, size):
@@ -38,7 +39,7 @@
 
 
 def product(masked, features):
-    return lax.dot_general(masked, features, (((0,), (0,)), ((), ())), preferred_element_type=jnp.float32)
+    return jnp.dot(masked, features, preferred_element_type=jnp.float32)
 
 
 def fetch(sources, targets, sems, start=0):
@@ -62,17 +63,17 @@
         copy.wait()
     tokens = cot_held.shape[1]
     live = counts_held[lax.axis_index("worker")] - lax.axis_index("fsdp") * tokens
-    masked[...] = masked_rows(live, cot_held[0])
+    masked[...] = masked_columns(live, cot_held[0])
+    for slot, into in enumerate((away, kept)):
+        blocks[slot].wait()
+        for side in (0, 1):
+            into[side] = product(masked[...], held[slot, :, side * half : (side + 1) * half])
     count, total = counts_held[lax.axis_index("worker")], counts_held[0]
     for other in range(1, workers):
         total = total + counts_held[other]
     info[0:1, :] = jnp.full((1, info.shape[1]), count.astype(jnp.float32))
     info[1:2, :] = 1.0 / info[0:1, :]
     info[2:3, :] = 1.0 / jnp.full((1, info.shape[1]), total.astype(jnp.float32))
-    for slot, into in enumerate((away, kept)):
-        blocks[slot].wait()
-        for side in (0, 1):
-            into[side] = product(masked[...], held[slot, :, side * half : (side + 1) * half])
 
 
 def rest_kernel(masked, features, *targets):
@@ -253,7 +254,7 @@
         half = rows // 2
         away_far, kept_far, masked, info = pl.pallas_call(
             functools.partial(first_kernel, workers, (7, 6)),
-            out_shape=[block((2, width, half))] * 2 + [jax.ShapeDtypeStruct((tokens, width), jnp.bfloat16), block((8, width))],
+            out_shape=[block((2, width, half))] * 2 + [jax.ShapeDtypeStruct((width, tokens), jnp.bfloat16), block((8, width))],
             in_specs=[HBM] * 3,
             out_specs=[VMEM] * 4,
             scratch_shapes=[

time: 26.2 us -> 26.1 us (level)
  no operation moved by 1% of the time
where the time goes in v16:
time: 26.1 us; the launch traced here: 25.9 us
  starting transfers between devices  14.6 us (56%)
  waiting for transfers between devices  5.94 us (23%)
  Pallas kernels  3.94 us (15%)
  between operations  1.4 us (5%)
    ppermute x10, starting transfers between devices, hop(): return lax.ppermute(value, axis, [(d, d ^ bit) for d in range(devices)])  14.6 us
    ppermute x10, waiting for transfers between devices, hop(): return lax.ppermute(value, axis, [(d, d ^ bit) for d in range(devices)])  5.94 us
    pallas_call x1, Pallas kernels, body(): pl.pallas_call(functools.partial(first_kernel, workers, (7, 6)), out_shap...  1.4 us
    pallas_call x1, Pallas kernels, body(): pl.pallas_call(left_kernel, out_shape=[block((half, width)), state, state...  1.08 us
    pallas_call x1, Pallas kernels, body(): pl.pallas_call(right_kernel, out_shape=[state] * 3, in_specs=[VMEM] * 10...  0.96 us
  transfers between devices with their start and end apart: 10, of which 3 were waited for; matrix products, arithmetic and copies ran while one was open for 0% of the time, Pallas kernels for 6%

profile of v16, /device:TPU:0, one launch (start us, length us, event | category | flops | bytes accessed | tf_op | source)
XLA Modules:
  0.0 25.9 jit_solution(12383163174961939364)
XLA Ops:
  0.6 0.0 copy-start
  0.6 1.4 %far_products.1 = (f32[2,128,256]{2,1,0:T(8,128)S(1)}, f32[2,128,256]{2,1,0:T(8,128)S(1)}, bf16[128,128]{1,0:T(8,128)(2,1)S(1)}, f32[8,128]{1,0:T(8,128)S(1)}) custom-call(s32[4]{0:T(128)} %counts.1, bf16[1,128,128]{2,1,0:T(8,128)(2,1)} %cotangent.1, bf16[1,128,4096]{2,1,0:T(8,128)(2,1)} %features.3), custom_call_target="tpu_custom_call" | custom-call | flops 33554432 | bytes 786432 | tf_op jit(solution)/shard_map/far_products/pallas_call | solution.py:255
  2.0 0.5 %collective-permute-start = (f32[2,128,256]{2,1,0:T(8,128)S(1)}, f32[2,128,256]{2,1,0:T(8,128)S(1)}, u32[]{:S(2)}, u32[]{:S(2)}) collective-permute-start(f32[2,128,256]{2,1,0:T(8,128)S(1)} %get-tuple-element.29), channel_id=1, source_target_pairs={{0,1},{1,0},{2,3},{3,2},{4,5},{5,4},{6,7},{7,6},{8,9},{9,8},{10,11... | collective-permute-start | bytes 786440 | tf_op jit(solution)/shard_map/ppermute | solution.py:218
  2.6 0.0 copy-done
  2.6 0.4 %rest_products.1 = (f32[6,128,256]{2,1,0:T(8,128)S(1)}, f32[6,128,256]{2,1,0:T(8,128)S(1)}) custom-call(bf16[128,128]{1,0:T(8,128)(2,1)S(1)} %get-tuple-element.25.masked, bf16[1,128,4096]{2,1,0:T(8,128)(2,1)S(1)} %copy-done), custom_call_target="tpu_custom_call" | custom-call | tf_op jit(solution)/shard_map/rest_products/pallas_call | solution.py:270
  2.9 0.8 %collective-permute-done.refs_1_ = f32[2,128,256]{2,1,0:T(8,128)S(1)} collective-permute-done((f32[2,128,256]{2,1,0:T(8,128)S(1)}, f32[2,128,256]{2,1,0:T(8,128)S(1)}, u32[]{:S(2)}, u32[]{:S(2)}) %collective-permute-start) | collective-permute-done | bytes 262176 | tf_op jit(solution)/shard_map/ppermute | solution.py:218
  3.8 0.4 %collective-permute-start.1 = (f32[6,128,256]{2,1,0:T(8,128)S(1)}, f32[6,128,256]{2,1,0:T(8,128)S(1)}, u32[]{:S(2)}, u32[]{:S(2)}) collective-permute-start(f32[6,128,256]{2,1,0:T(8,128)S(1)} %get-tuple-element.30), channel_id=1, source_target_pairs={{0,1},{1,0},{2,3},{3,2},{4,5},{5,4},{6,7},{7,6},{8,9},{9,8},{10,11... | collective-permute-start | bytes 2359304 | tf_op jit(solution)/shard_map/ppermute | solution.py:218
  4.2 2.7 %collective-permute-start.3 = (f32[1,128,256]{2,1,0:T(8,128)S(1)}, f32[1,128,256]{2,1,0:T(8,128)S(1)}, u32[]{:S(2)}, u32[]{:S(2)}) collective-permute-start(f32[1,128,256]{2,1,0:T(8,128)S(1)} %add_a1.1.after), channel_id=1, source_target_pairs={{0,2},{1,3},{2,0},{3,1},{4,6},{5,7},{6,4},{7,5},{8,10},{9,11},{10,... | collective-permute-start | bytes 393224 | tf_op jit(solution)/shard_map/ppermute | solution.py:218
  7.6 0.0 copy-done.1
  7.6 0.0 copy-done.4
  7.6 0.1 collective-permute-start.2
  7.7 1.9 %collective-permute-start.8 = (f32[128,128]{1,0:T(8,128)S(1)}, f32[128,128]{1,0:T(8,128)S(1)}, u32[]{:S(2)}, u32[]{:S(2)}) collective-permute-start(f32[128,128]{1,0:T(8,128)S(1)} %get-tuple-element.34.refs_2_), channel_id=1, source_target_pairs={{0,16},{8,24},{16,0},{24,8},{1,17},{9,25},{17,1},{25,9},{2,18},{10... | collective-permute-start | bytes 196616 | tf_op jit(solution)/shard_map/ppermute | solution.py:218
  9.7 0.0 collective-permute-done.1.refs_1_.come
  9.7 1.6 %collective-permute-start.7 = (f32[1,128,256]{2,1,0:T(8,128)S(1)}, f32[1,128,256]{2,1,0:T(8,128)S(1)}, u32[]{:S(2)}, u32[]{:S(2)}) collective-permute-start(f32[1,128,256]{2,1,0:T(8,128)S(1)} %add_n1.1), channel_id=1, source_target_pairs={{0,2},{1,3},{2,0},{3,1},{4,6},{5,7},{6,4},{7,5},{8,10},{9,11},{10,... | collective-permute-start | bytes 393224 | tf_op jit(solution)/shard_map/ppermute | solution.py:218
  11.3 0.0 collective-permute-done.3.refs_2_
  11.4 3.0 %collective-permute-start.6 = (f32[1,128,256]{2,1,0:T(8,128)S(1)}, f32[1,128,256]{2,1,0:T(8,128)S(1)}, u32[]{:S(2)}, u32[]{:S(2)}) collective-permute-start(f32[1,128,256]{2,1,0:T(8,128)S(1)} %add_c1.1.refs_3_.refs_2_), channel_id=1, source_target_pairs={{0,4},{1,5},{2,6},{3,7},{4,0},{5,1},{6,2},{7,3},{8,12},{9,13},{10,... | collective-permute-start | bytes 393224 | tf_op jit(solution)/shard_map/ppermute | solution.py:218
  14.3 1.6 %collective-permute-start.5 = (f32[1,128,256]{2,1,0:T(8,128)S(1)}, f32[1,128,256]{2,1,0:T(8,128)S(1)}, u32[]{:S(2)}, u32[]{:S(2)}) collective-permute-start(f32[1,128,256]{2,1,0:T(8,128)S(1)} %add_n2.1), channel_id=1, source_target_pairs={{0,2},{1,3},{2,0},{3,1},{4,6},{5,7},{6,4},{7,5},{8,10},{9,11},{10,... | collective-permute-start | bytes 393224 | tf_op jit(solution)/shard_map/ppermute | solution.py:218
  16.0 0.0 collective-permute-done.2.refs_2_
  16.0 0.0 copy-start.5
  16.0 1.1 %collective-permute-start.4 = (f32[1,128,256]{2,1,0:T(8,128)S(1)}, f32[1,128,256]{2,1,0:T(8,128)S(1)}, u32[]{:S(2)}, u32[]{:S(2)}) collective-permute-start(f32[1,128,256]{2,1,0:T(8,128)S(1)} %add_c2.1), channel_id=1, source_target_pairs={{0,4},{1,5},{2,6},{3,7},{4,0},{5,1},{6,2},{7,3},{8,12},{9,13},{10,... | collective-permute-start | bytes 393224 | tf_op jit(solution)/shard_map/ppermute | solution.py:218
  17.2 0.0 collective-permute-done.8
  17.2 1.6 %collective-permute-start.9 = (f32[128,128]{1,0:T(8,128)S(1)}, f32[128,128]{1,0:T(8,128)S(1)}, u32[]{:S(2)}, u32[]{:S(2)}) collective-permute-start(f32[128,128]{1,0:T(8,128)S(1)} %add.3.drift), channel_id=1, source_target_pairs={{0,8},{8,0},{16,24},{24,16},{1,9},{9,1},{17,25},{25,17},{2,10},{10... | collective-permute-start | bytes 196616 | tf_op jit(solution)/shard_map/ppermute | solution.py:218
  18.7 2.8 %collective-permute-done.9.other_drift = f32[128,128]{1,0:T(8,128)S(1)} collective-permute-done((f32[128,128]{1,0:T(8,128)S(1)}, f32[128,128]{1,0:T(8,128)S(1)}, u32[]{:S(2)}, u32[]{:S(2)}) %collective-permute-start.9) | collective-permute-done | bytes 65568 | tf_op jit(solution)/shard_map/ppermute | solution.py:218
  21.5 0.0 collective-permute-done.7.near
  21.5 0.0 collective-permute-done.6.far
  21.5 0.0 copy-done.2
  21.5 0.0 copy-done.3
  21.5 0.0 copy-done.5
  21.5 1.1 %left_step.1 = (f32[256,128]{1,0:T(8,128)S(1)}, f32[1,512,128]{2,1,0:T(8,128)}, f32[1,512,128]{2,1,0:T(8,128)}, f32[1,512,128]{2,1,0:T(8,128)}, f32[128,128]{1,0:T(8,128)}, /*index=5*/f32[128,128]{1,0:T(8,128)}) custom-call(f32[1,512,128]{2,1,0:T(8,128)S(1)} %copy-done.1, f32[1,512,128]{2,1,0:T(8,128)S(1)} %copy-done.2, f32[1,512,128]{2,1,0:T(8,128)S(1)} %copy-done.3, ...), custom_call_target="tpu_custom_call" | custom-call | flops 983040 | bytes 1310720 | tf_op jit(solution)/shard_map/left_step/pallas_call | solution.py:330
  22.6 2.4 %collective-permute-done.5.near = f32[1,128,256]{2,1,0:T(8,128)S(1)} collective-permute-done((f32[1,128,256]{2,1,0:T(8,128)S(1)}, f32[1,128,256]{2,1,0:T(8,128)S(1)}, u32[]{:S(2)}, u32[]{:S(2)}) %collective-permute-start.5) | collective-permute-done | bytes 131104 | tf_op jit(solution)/shard_map/ppermute | solution.py:218
  25.0 0.0 collective-permute-done.4.far
  25.0 1.0 %right_step.1 = (f32[1,512,128]{2,1,0:T(8,128)}, f32[1,512,128]{2,1,0:T(8,128)}, f32[1,512,128]{2,1,0:T(8,128)}) custom-call(f32[1,512,128]{2,1,0:T(8,128)S(1)} %copy-done.1, f32[1,512,128]{2,1,0:T(8,128)S(1)} %copy-done.2, f32[1,512,128]{2,1,0:T(8,128)S(1)} %copy-done.3, ...), custom_call_target="tpu_custom_call", output_to_operand_aliasing={{0}: (10, {}), {1}: (11, {}), {2}: (12, {})} | custom-call | tf_op jit(solution)/shard_map/right_step/pallas_call | solution.py:357
  (12 shorter events, 0.2 us)
Async XLA Ops:
  0.6 1.9 %copy-start = (bf16[1,128,4096]{2,1,0:T(8,128)(2,1)S(1)}, bf16[1,128,4096]{2,1,0:T(8,128)(2,1)}, u32[]{:S(2)}) copy-start(bf16[1,128,4096]{2,1,0:T(8,128)(2,1)} %features.3) | copy-start | bytes 3145732
  2.0 1.7 %collective-permute-start = (f32[2,128,256]{2,1,0:T(8,128)S(1)}, f32[2,128,256]{2,1,0:T(8,128)S(1)}, u32[]{:S(2)}, u32[]{:S(2)}) collective-permute-start(f32[2,128,256]{2,1,0:T(8,128)S(1)} %get-tuple-element.29), channel_id=1, source_target_pairs={{0,1},{1,0},{2,3},{3,2},{4,5},{5,4},{6,7},{7,6},{8,9},{9,8},{10,11... | collective-permute-start | bytes 786440 | tf_op jit(solution)/shard_map/ppermute | solution.py:218
  3.7 3.8 %copy-start.1 = (f32[1,512,128]{2,1,0:T(8,128)S(1)}, f32[1,512,128]{2,1,0:T(8,128)}, u32[]{:S(2)}) copy-start(f32[1,512,128]{2,1,0:T(8,128)} %params.5) | copy-start | bytes 786436
  3.7 3.8 %copy-start.4 = (f32[128,128]{1,0:T(8,128)S(1)}, f32[128,128]{1,0:T(8,128)}, u32[]{:S(2)}) copy-start(f32[128,128]{1,0:T(8,128)} %global_fragment.3) | copy-start | bytes 196612
  3.8 5.9 %collective-permute-start.1 = (f32[6,128,256]{2,1,0:T(8,128)S(1)}, f32[6,128,256]{2,1,0:T(8,128)S(1)}, u32[]{:S(2)}, u32[]{:S(2)}) collective-permute-start(f32[6,128,256]{2,1,0:T(8,128)S(1)} %get-tuple-element.30), channel_id=1, source_target_pairs={{0,1},{1,0},{2,3},{3,2},{4,5},{5,4},{6,7},{7,6},{8,9},{9,8},{10,11... | collective-permute-start | bytes 2359304 | tf_op jit(solution)/shard_map/ppermute | solution.py:218
  4.2 7.2 %collective-permute-start.3 = (f32[1,128,256]{2,1,0:T(8,128)S(1)}, f32[1,128,256]{2,1,0:T(8,128)S(1)}, u32[]{:S(2)}, u32[]{:S(2)}) collective-permute-start(f32[1,128,256]{2,1,0:T(8,128)S(1)} %add_a1.1.after), channel_id=1, source_target_pairs={{0,2},{1,3},{2,0},{3,1},{4,6},{5,7},{6,4},{7,5},{8,10},{9,11},{10,... | collective-permute-start | bytes 393224 | tf_op jit(solution)/shard_map/ppermute | solution.py:218
  7.6 8.3 %collective-permute-start.2 = (f32[1,128,256]{2,1,0:T(8,128)S(1)}, f32[1,128,256]{2,1,0:T(8,128)S(1)}, u32[]{:S(2)}, u32[]{:S(2)}) collective-permute-start(f32[1,128,256]{2,1,0:T(8,128)S(1)} %add_a2.1.refs_2_), channel_id=1, source_target_pairs={{0,2},{1,3},{2,0},{3,1},{4,6},{5,7},{6,4},{7,5},{8,10},{9,11},{10,... | collective-permute-start | bytes 393224 | tf_op jit(solution)/shard_map/ppermute | solution.py:218
  7.7 9.4 %collective-permute-start.8 = (f32[128,128]{1,0:T(8,128)S(1)}, f32[128,128]{1,0:T(8,128)S(1)}, u32[]{:S(2)}, u32[]{:S(2)}) collective-permute-start(f32[128,128]{1,0:T(8,128)S(1)} %get-tuple-element.34.refs_2_), channel_id=1, source_target_pairs={{0,16},{8,24},{16,0},{24,8},{1,17},{9,25},{17,1},{25,9},{2,18},{10... | collective-permute-start | bytes 196616 | tf_op jit(solution)/shard_map/ppermute | solution.py:218
  9.7 11.8 %collective-permute-start.7 = (f32[1,128,256]{2,1,0:T(8,128)S(1)}, f32[1,128,256]{2,1,0:T(8,128)S(1)}, u32[]{:S(2)}, u32[]{:S(2)}) collective-permute-start(f32[1,128,256]{2,1,0:T(8,128)S(1)} %add_n1.1), channel_id=1, source_target_pairs={{0,2},{1,3},{2,0},{3,1},{4,6},{5,7},{6,4},{7,5},{8,10},{9,11},{10,... | collective-permute-start | bytes 393224 | tf_op jit(solution)/shard_map/ppermute | solution.py:218
  11.4 10.1 %collective-permute-start.6 = (f32[1,128,256]{2,1,0:T(8,128)S(1)}, f32[1,128,256]{2,1,0:T(8,128)S(1)}, u32[]{:S(2)}, u32[]{:S(2)}) collective-permute-start(f32[1,128,256]{2,1,0:T(8,128)S(1)} %add_c1.1.refs_3_.refs_2_), channel_id=1, source_target_pairs={{0,4},{1,5},{2,6},{3,7},{4,0},{5,1},{6,2},{7,3},{8,12},{9,13},{10,... | collective-permute-start | bytes 393224 | tf_op jit(solution)/shard_map/ppermute | solution.py:218
  14.3 10.6 %collective-permute-start.5 = (f32[1,128,256]{2,1,0:T(8,128)S(1)}, f32[1,128,256]{2,1,0:T(8,128)S(1)}, u32[]{:S(2)}, u32[]{:S(2)}) collective-permute-start(f32[1,128,256]{2,1,0:T(8,128)S(1)} %add_n2.1), channel_id=1, source_target_pairs={{0,2},{1,3},{2,0},{3,1},{4,6},{5,7},{6,4},{7,5},{8,10},{9,11},{10,... | collective-permute-start | bytes 393224 | tf_op jit(solution)/shard_map/ppermute | solution.py:218
  16.0 5.5 %copy-start.2 = (f32[1,512,128]{2,1,0:T(8,128)S(1)}, f32[1,512,128]{2,1,0:T(8,128)}, u32[]{:S(2)}) copy-start(f32[1,512,128]{2,1,0:T(8,128)} %first.3) | copy-start | bytes 786436
  16.0 5.5 %copy-start.3 = (f32[1,512,128]{2,1,0:T(8,128)S(1)}, f32[1,512,128]{2,1,0:T(8,128)}, u32[]{:S(2)}) copy-start(f32[1,512,128]{2,1,0:T(8,128)} %second.3) | copy-start | bytes 786436
  16.0 5.5 %copy-start.5 = (f32[128,128]{1,0:T(8,128)S(1)}, f32[128,128]{1,0:T(8,128)}, u32[]{:S(2)}) copy-start(f32[128,128]{1,0:T(8,128)} %outer_momentum.1) | copy-start | bytes 196612
  16.0 8.9 %collective-permute-start.4 = (f32[1,128,256]{2,1,0:T(8,128)S(1)}, f32[1,128,256]{2,1,0:T(8,128)S(1)}, u32[]{:S(2)}, u32[]{:S(2)}) collective-permute-start(f32[1,128,256]{2,1,0:T(8,128)S(1)} %add_c2.1), channel_id=1, source_target_pairs={{0,4},{1,5},{2,6},{3,7},{4,0},{5,1},{6,2},{7,3},{8,12},{9,13},{10,... | collective-permute-start | bytes 393224 | tf_op jit(solution)/shard_map/ppermute | solution.py:218
  17.2 4.3 %collective-permute-start.9 = (f32[128,128]{1,0:T(8,128)S(1)}, f32[128,128]{1,0:T(8,128)S(1)}, u32[]{:S(2)}, u32[]{:S(2)}) collective-permute-start(f32[128,128]{1,0:T(8,128)S(1)} %add.3.drift), channel_id=1, source_target_pairs={{0,8},{8,0},{16,24},{24,16},{1,9},{9,1},{17,25},{25,17},{2,10},{10... | collective-permute-start | bytes 196616 | tf_op jit(solution)/shard_map/ppermute | solution.py:218

commit v17 on v16

--- a/solution.py
+++ b/solution.py
@@ -57,7 +57,7 @@
 ):
     half = away.shape[2]
     small = fetch((counts, cotangent), (counts_held, cot_held), sems)
-    columns = [columns_of(q, 2 * half, 0, 2 * half) for q in order]
+    columns = [columns_of(q, 2 * half, 0, half) for q in order]
     blocks = fetch([features.at[0, :, c] for c in columns], [held.at[n] for n in range(len(order))], sems, len(small))
     for copy in small:
         copy.wait()
@@ -66,8 +66,7 @@
     masked[...] = masked_columns(live, cot_held[0])
     for slot, into in enumerate((away, kept)):
         blocks[slot].wait()
-        for side in (0, 1):
-            into[side] = product(masked[...], held[slot, :, side * half : (side + 1) * half])
+        into[0] = product(masked[...], held[slot])
     count, total = counts_held[lax.axis_index("worker")], counts_held[0]
     for other in range(1, workers):
         total = total + counts_held[other]
@@ -76,13 +75,12 @@
     info[2:3, :] = 1.0 / jnp.full((1, info.shape[1]), total.astype(jnp.float32))
 
 
-def rest_kernel(masked, features, *targets):
-    half = targets[0].shape[2]
-    places = [(4, 0, 0, 4), (4, 1, 0, 5), (2, 0, 0, 2), (2, 1, 0, 3), (0, 0, 0, 0), (0, 1, 0, 1)]
-    for q, side, into, at in places:
-        for core in (1, 0):
+def rest_kernel(masked, features, away, kept):
+    half = away.shape[2]
+    for at, (q, side) in enumerate(((0, 0), (0, 1), (2, 0), (2, 1), (4, 0), (4, 1), (6, 1))):
+        for core, into in ((1, away), (0, kept)):
             columns = columns_of(q + core, 2 * half, side * half, half)
-            targets[into + 1 - core][at] = product(masked[...], features[0, :, columns])
+            into[at] = product(masked[...], features[0, :, columns])
 
 
 def drift_kernel(info, fragment, params, global_fragment, after, drift, scale):
@@ -254,13 +252,13 @@
         half = rows // 2
         away_far, kept_far, masked, info = pl.pallas_call(
             functools.partial(first_kernel, workers, (7, 6)),
-            out_shape=[block((2, width, half))] * 2 + [jax.ShapeDtypeStruct((width, tokens), jnp.bfloat16), block((8, width))],
+            out_shape=[block((1, width, half))] * 2 + [jax.ShapeDtypeStruct((width, tokens), jnp.bfloat16), block((8, width))],
             in_specs=[HBM] * 3,
             out_specs=[VMEM] * 4,
             scratch_shapes=[
                 held_counts,
                 pltpu.VMEM(cotangent.shape, cotangent.dtype),
-                pltpu.VMEM((2, tokens, rows), features.dtype),
+                pltpu.VMEM((2, tokens, half), features.dtype),
                 pltpu.SemaphoreType.DMA((4,)),
             ],
             compiler_params=room,
@@ -269,7 +267,7 @@
         )(far_counts, far_cotangent, far_features)
         away, kept = pl.pallas_call(
             rest_kernel,
-            out_shape=[block((6, width, half))] * 2,
+            out_shape=[block((7, width, half))] * 2,
             in_specs=[VMEM] * 2,
             out_specs=[VMEM] * 2,
             compiler_params=room,
@@ -294,7 +292,7 @@
 
         state, piece = block(params.shape), block(global_fragment.shape)
         come_far = hop(away_far, "fsdp", devices, 1)
-        sent = add((kept_far, part(0)), (come_far, part(0)), name="add_a1")
+        sent = add((kept_far, part(0)), (come_far, part(0)), (fragment_index, None), name="add_a1")
         far_left = hop(sent, "fsdp", devices, 2)
         away, _ = lax.optimization_barrier((away, sent))
         come = hop(away, "fsdp", devices, 1)
@@ -307,7 +305,7 @@
             cost_estimate=free,
             name="drift",
         )(info, fragment_index, params, global_fragment, sent)
-        sent = add((kept_far, part(1)), (come_far, part(1)), (drift, None), name="add_a2")
+        sent = add((kept, part(6)), (come, part(6)), (drift, None), name="add_a2")
         far_right = hop(sent, "fsdp", devices, 2)
         passed = add((kept, part(4)), (come, part(4)), (far_left, part(0)), name="add_c1")
         far_left = hop(passed, "fsdp", devices, 4)

time: 26.1 us -> 25.8 us (0.989)
  waiting for transfers between devices: 5.94 us -> 5.29 us
  starting transfers between devices: 14.6 us -> 15 us
    ppermute x10, waiting for transfers between devices: 5.94 us -> 5.29 us  [hop(): return lax.ppermute(value, axis, [(d, d ^ bit) for d in range(devices)])]
    ppermute x10, starting transfers between devices: 14.6 us -> 15 us  [hop(): return lax.ppermute(value, axis, [(d, d ^ bit) for d in range(devices)])]
where the time goes in v17:
time: 25.8 us; the launch traced here: 25.7 us
  starting transfers between devices  15 us (58%)
  waiting for transfers between devices  5.29 us (21%)
  Pallas kernels  3.89 us (15%)
  between operations  1.41 us (5%)
    ppermute x10, starting transfers between devices, hop(): return lax.ppermute(value, axis, [(d, d ^ bit) for d in range(devices)])  15 us
    ppermute x10, waiting for transfers between devices, hop(): return lax.ppermute(value, axis, [(d, d ^ bit) for d in range(devices)])  5.29 us
    pallas_call x1, Pallas kernels, body(): pl.pallas_call(functools.partial(first_kernel, workers, (7, 6)), out_shap...  1.32 us
    pallas_call x1, Pallas kernels, body(): pl.pallas_call(left_kernel, out_shape=[block((half, width)), state, state...  1.08 us
    pallas_call x1, Pallas kernels, body(): pl.pallas_call(right_kernel, out_shape=[state] * 3, in_specs=[VMEM] * 10...  0.96 us
  transfers between devices with their start and end apart: 10, of which 3 were waited for; matrix products, arithmetic and copies ran while one was open for 0% of the time, Pallas kernels for 6%

profile of v17, /device:TPU:0, one launch (start us, length us, event | category | flops | bytes accessed | tf_op | source)
XLA Modules:
  0.0 25.7 jit_solution(5394299328308542965)
XLA Ops:
  0.6 0.0 copy-start
  0.6 1.3 %far_products.1 = (f32[1,128,256]{2,1,0:T(8,128)S(1)}, f32[1,128,256]{2,1,0:T(8,128)S(1)}, bf16[128,128]{1,0:T(8,128)(2,1)S(1)}, f32[8,128]{1,0:T(8,128)S(1)}) custom-call(s32[4]{0:T(128)} %counts.1, bf16[1,128,128]{2,1,0:T(8,128)(2,1)} %cotangent.1, bf16[1,128,4096]{2,1,0:T(8,128)(2,1)} %features.3), custom_call_target="tpu_custom_call" | custom-call | flops 33554432 | bytes 786432 | tf_op jit(solution)/shard_map/far_products/pallas_call | solution.py:253
  2.0 0.5 %collective-permute-start = (f32[1,128,256]{2,1,0:T(8,128)S(1)}, f32[1,128,256]{2,1,0:T(8,128)S(1)}, u32[]{:S(2)}, u32[]{:S(2)}) collective-permute-start(f32[1,128,256]{2,1,0:T(8,128)S(1)} %get-tuple-element.29), channel_id=1, source_target_pairs={{0,1},{1,0},{2,3},{3,2},{4,5},{5,4},{6,7},{7,6},{8,9},{9,8},{10,11... | collective-permute-start | bytes 393224 | tf_op jit(solution)/shard_map/ppermute | solution.py:216
  3.1 0.0 copy-done
  3.1 0.4 %rest_products.1 = (f32[7,128,256]{2,1,0:T(8,128)S(1)}, f32[7,128,256]{2,1,0:T(8,128)S(1)}) custom-call(bf16[128,128]{1,0:T(8,128)(2,1)S(1)} %get-tuple-element.25.masked, bf16[1,128,4096]{2,1,0:T(8,128)(2,1)S(1)} %copy-done), custom_call_target="tpu_custom_call" | custom-call | tf_op jit(solution)/shard_map/rest_products/pallas_call | solution.py:268
  3.6 0.0 copy-start.1
  3.6 0.0 collective-permute-done.refs_1_
  3.6 0.0 copy-start.4
  3.6 0.3 %collective-permute-start.1 = (f32[7,128,256]{2,1,0:T(8,128)S(1)}, f32[7,128,256]{2,1,0:T(8,128)S(1)}, u32[]{:S(2)}, u32[]{:S(2)}) collective-permute-start(f32[7,128,256]{2,1,0:T(8,128)S(1)} %get-tuple-element.30), channel_id=1, source_target_pairs={{0,1},{1,0},{2,3},{3,2},{4,5},{5,4},{6,7},{7,6},{8,9},{9,8},{10,11... | collective-permute-start | bytes 2752520 | tf_op jit(solution)/shard_map/ppermute | solution.py:216
  3.9 2.8 %collective-permute-start.3 = (f32[1,128,256]{2,1,0:T(8,128)S(1)}, f32[1,128,256]{2,1,0:T(8,128)S(1)}, u32[]{:S(2)}, u32[]{:S(2)}) collective-permute-start(f32[1,128,256]{2,1,0:T(8,128)S(1)} %add_a1.1.after), channel_id=1, source_target_pairs={{0,2},{1,3},{2,0},{3,1},{4,6},{5,7},{6,4},{7,5},{8,10},{9,11},{10,... | collective-permute-start | bytes 393224 | tf_op jit(solution)/shard_map/ppermute | solution.py:216
  6.8 0.0 copy-done.1
  6.8 0.0 copy-done.4
  6.8 0.0 collective-permute-done.1.refs_1_.come
  6.8 2.2 %collective-permute-start.2 = (f32[1,128,256]{2,1,0:T(8,128)S(1)}, f32[1,128,256]{2,1,0:T(8,128)S(1)}, u32[]{:S(2)}, u32[]{:S(2)}) collective-permute-start(f32[1,128,256]{2,1,0:T(8,128)S(1)} %add_a2.1.refs_2_), channel_id=1, source_target_pairs={{0,2},{1,3},{2,0},{3,1},{4,6},{5,7},{6,4},{7,5},{8,10},{9,11},{10,... | collective-permute-start | bytes 393224 | tf_op jit(solution)/shard_map/ppermute | solution.py:216
  9.0 1.5 %collective-permute-start.8 = (f32[128,128]{1,0:T(8,128)S(1)}, f32[128,128]{1,0:T(8,128)S(1)}, u32[]{:S(2)}, u32[]{:S(2)}) collective-permute-start(f32[128,128]{1,0:T(8,128)S(1)} %get-tuple-element.34.refs_2_), channel_id=1, source_target_pairs={{0,16},{8,24},{16,0},{24,8},{1,17},{9,25},{17,1},{25,9},{2,18},{10... | collective-permute-start | bytes 196616 | tf_op jit(solution)/shard_map/ppermute | solution.py:216
  10.6 0.5 %collective-permute-start.7 = (f32[1,128,256]{2,1,0:T(8,128)S(1)}, f32[1,128,256]{2,1,0:T(8,128)S(1)}, u32[]{:S(2)}, u32[]{:S(2)}) collective-permute-start(f32[1,128,256]{2,1,0:T(8,128)S(1)} %add_n1.1), channel_id=1, source_target_pairs={{0,2},{1,3},{2,0},{3,1},{4,6},{5,7},{6,4},{7,5},{8,10},{9,11},{10,... | collective-permute-start | bytes 393224 | tf_op jit(solution)/shard_map/ppermute | solution.py:216
  11.1 0.0 collective-permute-done.3.refs_2_
  11.1 2.8 %collective-permute-start.6 = (f32[1,128,256]{2,1,0:T(8,128)S(1)}, f32[1,128,256]{2,1,0:T(8,128)S(1)}, u32[]{:S(2)}, u32[]{:S(2)}) collective-permute-start(f32[1,128,256]{2,1,0:T(8,128)S(1)} %add_c1.1.refs_3_.refs_2_), channel_id=1, source_target_pairs={{0,4},{1,5},{2,6},{3,7},{4,0},{5,1},{6,2},{7,3},{8,12},{9,13},{10,... | collective-permute-start | bytes 393224 | tf_op jit(solution)/shard_map/ppermute | solution.py:216
  13.9 1.6 %collective-permute-start.5 = (f32[1,128,256]{2,1,0:T(8,128)S(1)}, f32[1,128,256]{2,1,0:T(8,128)S(1)}, u32[]{:S(2)}, u32[]{:S(2)}) collective-permute-start(f32[1,128,256]{2,1,0:T(8,128)S(1)} %add_n2.1), channel_id=1, source_target_pairs={{0,2},{1,3},{2,0},{3,1},{4,6},{5,7},{6,4},{7,5},{8,10},{9,11},{10,... | collective-permute-start | bytes 393224 | tf_op jit(solution)/shard_map/ppermute | solution.py:216
  15.6 0.0 collective-permute-done.2.refs_2_
  15.6 0.0 copy-start.5
  15.6 1.1 %collective-permute-start.4 = (f32[1,128,256]{2,1,0:T(8,128)S(1)}, f32[1,128,256]{2,1,0:T(8,128)S(1)}, u32[]{:S(2)}, u32[]{:S(2)}) collective-permute-start(f32[1,128,256]{2,1,0:T(8,128)S(1)} %add_c2.1), channel_id=1, source_target_pairs={{0,4},{1,5},{2,6},{3,7},{4,0},{5,1},{6,2},{7,3},{8,12},{9,13},{10,... | collective-permute-start | bytes 393224 | tf_op jit(solution)/shard_map/ppermute | solution.py:216
  16.7 0.0 collective-permute-done.8
  16.8 1.6 %collective-permute-start.9 = (f32[128,128]{1,0:T(8,128)S(1)}, f32[128,128]{1,0:T(8,128)S(1)}, u32[]{:S(2)}, u32[]{:S(2)}) collective-permute-start(f32[128,128]{1,0:T(8,128)S(1)} %add.3.drift), channel_id=1, source_target_pairs={{0,8},{8,0},{16,24},{24,16},{1,9},{9,1},{17,25},{25,17},{2,10},{10... | collective-permute-start | bytes 196616 | tf_op jit(solution)/shard_map/ppermute | solution.py:216
  18.3 2.3 %collective-permute-done.7.near = f32[1,128,256]{2,1,0:T(8,128)S(1)} collective-permute-done((f32[1,128,256]{2,1,0:T(8,128)S(1)}, f32[1,128,256]{2,1,0:T(8,128)S(1)}, u32[]{:S(2)}, u32[]{:S(2)}) %collective-permute-start.7) | collective-permute-done | bytes 131104 | tf_op jit(solution)/shard_map/ppermute | solution.py:216
  20.6 0.0 collective-permute-done.6.far
  20.6 0.5 %collective-permute-done.9.other_drift = f32[128,128]{1,0:T(8,128)S(1)} collective-permute-done((f32[128,128]{1,0:T(8,128)S(1)}, f32[128,128]{1,0:T(8,128)S(1)}, u32[]{:S(2)}, u32[]{:S(2)}) %collective-permute-start.9) | collective-permute-done | bytes 65568 | tf_op jit(solution)/shard_map/ppermute | solution.py:216
  21.1 0.0 copy-done.2
  21.1 1.1 %left_step.1 = (f32[256,128]{1,0:T(8,128)S(1)}, f32[1,512,128]{2,1,0:T(8,128)}, f32[1,512,128]{2,1,0:T(8,128)}, f32[1,512,128]{2,1,0:T(8,128)}, f32[128,128]{1,0:T(8,128)}, /*index=5*/f32[128,128]{1,0:T(8,128)}) custom-call(f32[1,512,128]{2,1,0:T(8,128)S(1)} %copy-done.1, f32[1,512,128]{2,1,0:T(8,128)S(1)} %copy-done.2, f32[1,512,128]{2,1,0:T(8,128)S(1)} %copy-done.3, ...), custom_call_target="tpu_custom_call" | custom-call | flops 983040 | bytes 1310720 | tf_op jit(solution)/shard_map/left_step/pallas_call | solution.py:328
  22.2 2.5 %collective-permute-done.5.near = f32[1,128,256]{2,1,0:T(8,128)S(1)} collective-permute-done((f32[1,128,256]{2,1,0:T(8,128)S(1)}, f32[1,128,256]{2,1,0:T(8,128)S(1)}, u32[]{:S(2)}, u32[]{:S(2)}) %collective-permute-start.5) | collective-permute-done | bytes 131104 | tf_op jit(solution)/shard_map/ppermute | solution.py:216
  24.7 0.0 collective-permute-done.4.far
  24.7 1.0 %right_step.1 = (f32[1,512,128]{2,1,0:T(8,128)}, f32[1,512,128]{2,1,0:T(8,128)}, f32[1,512,128]{2,1,0:T(8,128)}) custom-call(f32[1,512,128]{2,1,0:T(8,128)S(1)} %copy-done.1, f32[1,512,128]{2,1,0:T(8,128)S(1)} %copy-done.2, f32[1,512,128]{2,1,0:T(8,128)S(1)} %copy-done.3, ...), custom_call_target="tpu_custom_call", output_to_operand_aliasing={{0}: (10, {}), {1}: (11, {}), {2}: (12, {})} | custom-call | tf_op jit(solution)/shard_map/right_step/pallas_call | solution.py:355
  (12 shorter events, 0.1 us)
Async XLA Ops:
  0.6 2.5 %copy-start = (bf16[1,128,4096]{2,1,0:T(8,128)(2,1)S(1)}, bf16[1,128,4096]{2,1,0:T(8,128)(2,1)}, u32[]{:S(2)}) copy-start(bf16[1,128,4096]{2,1,0:T(8,128)(2,1)} %features.3) | copy-start | bytes 3145732
  2.0 1.6 %collective-permute-start = (f32[1,128,256]{2,1,0:T(8,128)S(1)}, f32[1,128,256]{2,1,0:T(8,128)S(1)}, u32[]{:S(2)}, u32[]{:S(2)}) collective-permute-start(f32[1,128,256]{2,1,0:T(8,128)S(1)} %get-tuple-element.29), channel_id=1, source_target_pairs={{0,1},{1,0},{2,3},{3,2},{4,5},{5,4},{6,7},{7,6},{8,9},{9,8},{10,11... | collective-permute-start | bytes 393224 | tf_op jit(solution)/shard_map/ppermute | solution.py:216
  3.6 3.2 %copy-start.1 = (f32[1,512,128]{2,1,0:T(8,128)S(1)}, f32[1,512,128]{2,1,0:T(8,128)}, u32[]{:S(2)}) copy-start(f32[1,512,128]{2,1,0:T(8,128)} %params.5) | copy-start | bytes 786436
  3.6 3.2 %copy-start.4 = (f32[128,128]{1,0:T(8,128)S(1)}, f32[128,128]{1,0:T(8,128)}, u32[]{:S(2)}) copy-start(f32[128,128]{1,0:T(8,128)} %global_fragment.3) | copy-start | bytes 196612
  3.6 3.2 %collective-permute-start.1 = (f32[7,128,256]{2,1,0:T(8,128)S(1)}, f32[7,128,256]{2,1,0:T(8,128)S(1)}, u32[]{:S(2)}, u32[]{:S(2)}) collective-permute-start(f32[7,128,256]{2,1,0:T(8,128)S(1)} %get-tuple-element.30), channel_id=1, source_target_pairs={{0,1},{1,0},{2,3},{3,2},{4,5},{5,4},{6,7},{7,6},{8,9},{9,8},{10,11... | collective-permute-start | bytes 2752520 | tf_op jit(solution)/shard_map/ppermute | solution.py:216
  3.9 7.2 %collective-permute-start.3 = (f32[1,128,256]{2,1,0:T(8,128)S(1)}, f32[1,128,256]{2,1,0:T(8,128)S(1)}, u32[]{:S(2)}, u32[]{:S(2)}) collective-permute-start(f32[1,128,256]{2,1,0:T(8,128)S(1)} %add_a1.1.after), channel_id=1, source_target_pairs={{0,2},{1,3},{2,0},{3,1},{4,6},{5,7},{6,4},{7,5},{8,10},{9,11},{10,... | collective-permute-start | bytes 393224 | tf_op jit(solution)/shard_map/ppermute | solution.py:216
  6.8 8.8 %collective-permute-start.2 = (f32[1,128,256]{2,1,0:T(8,128)S(1)}, f32[1,128,256]{2,1,0:T(8,128)S(1)}, u32[]{:S(2)}, u32[]{:S(2)}) collective-permute-start(f32[1,128,256]{2,1,0:T(8,128)S(1)} %add_a2.1.refs_2_), channel_id=1, source_target_pairs={{0,2},{1,3},{2,0},{3,1},{4,6},{5,7},{6,4},{7,5},{8,10},{9,11},{10,... | collective-permute-start | bytes 393224 | tf_op jit(solution)/shard_map/ppermute | solution.py:216
  9.0 7.7 %collective-permute-start.8 = (f32[128,128]{1,0:T(8,128)S(1)}, f32[128,128]{1,0:T(8,128)S(1)}, u32[]{:S(2)}, u32[]{:S(2)}) collective-permute-start(f32[128,128]{1,0:T(8,128)S(1)} %get-tuple-element.34.refs_2_), channel_id=1, source_target_pairs={{0,16},{8,24},{16,0},{24,8},{1,17},{9,25},{17,1},{25,9},{2,18},{10... | collective-permute-start | bytes 196616 | tf_op jit(solution)/shard_map/ppermute | solution.py:216
  10.6 10.0 %collective-permute-start.7 = (f32[1,128,256]{2,1,0:T(8,128)S(1)}, f32[1,128,256]{2,1,0:T(8,128)S(1)}, u32[]{:S(2)}, u32[]{:S(2)}) collective-permute-start(f32[1,128,256]{2,1,0:T(8,128)S(1)} %add_n1.1), channel_id=1, source_target_pairs={{0,2},{1,3},{2,0},{3,1},{4,6},{5,7},{6,4},{7,5},{8,10},{9,11},{10,... | collective-permute-start | bytes 393224 | tf_op jit(solution)/shard_map/ppermute | solution.py:216
  11.1 9.5 %collective-permute-start.6 = (f32[1,128,256]{2,1,0:T(8,128)S(1)}, f32[1,128,256]{2,1,0:T(8,128)S(1)}, u32[]{:S(2)}, u32[]{:S(2)}) collective-permute-start(f32[1,128,256]{2,1,0:T(8,128)S(1)} %add_c1.1.refs_3_.refs_2_), channel_id=1, source_target_pairs={{0,4},{1,5},{2,6},{3,7},{4,0},{5,1},{6,2},{7,3},{8,12},{9,13},{10,... | collective-permute-start | bytes 393224 | tf_op jit(solution)/shard_map/ppermute | solution.py:216
  13.9 10.8 %collective-permute-start.5 = (f32[1,128,256]{2,1,0:T(8,128)S(1)}, f32[1,128,256]{2,1,0:T(8,128)S(1)}, u32[]{:S(2)}, u32[]{:S(2)}) collective-permute-start(f32[1,128,256]{2,1,0:T(8,128)S(1)} %add_n2.1), channel_id=1, source_target_pairs={{0,2},{1,3},{2,0},{3,1},{4,6},{5,7},{6,4},{7,5},{8,10},{9,11},{10,... | collective-permute-start | bytes 393224 | tf_op jit(solution)/shard_map/ppermute | solution.py:216
  15.6 5.5 %copy-start.2 = (f32[1,512,128]{2,1,0:T(8,128)S(1)}, f32[1,512,128]{2,1,0:T(8,128)}, u32[]{:S(2)}) copy-start(f32[1,512,128]{2,1,0:T(8,128)} %first.3) | copy-start | bytes 786436
  15.6 5.5 %copy-start.3 = (f32[1,512,128]{2,1,0:T(8,128)S(1)}, f32[1,512,128]{2,1,0:T(8,128)}, u32[]{:S(2)}) copy-start(f32[1,512,128]{2,1,0:T(8,128)} %second.3) | copy-start | bytes 786436
  15.6 5.5 %copy-start.5 = (f32[128,128]{1,0:T(8,128)S(1)}, f32[128,128]{1,0:T(8,128)}, u32[]{:S(2)}) copy-start(f32[128,128]{1,0:T(8,128)} %outer_momentum.1) | copy-start | bytes 196612
  15.6 9.1 %collective-permute-start.4 = (f32[1,128,256]{2,1,0:T(8,128)S(1)}, f32[1,128,256]{2,1,0:T(8,128)S(1)}, u32[]{:S(2)}, u32[]{:S(2)}) collective-permute-start(f32[1,128,256]{2,1,0:T(8,128)S(1)} %add_c2.1), channel_id=1, source_target_pairs={{0,4},{1,5},{2,6},{3,7},{4,0},{5,1},{6,2},{7,3},{8,12},{9,13},{10,... | collective-permute-start | bytes 393224 | tf_op jit(solution)/shard_map/ppermute | solution.py:216
  16.8 4.3 %collective-permute-start.9 = (f32[128,128]{1,0:T(8,128)S(1)}, f32[128,128]{1,0:T(8,128)S(1)}, u32[]{:S(2)}, u32[]{:S(2)}) collective-permute-start(f32[128,128]{1,0:T(8,128)S(1)} %add.3.drift), channel_id=1, source_target_pairs={{0,8},{8,0},{16,24},{24,16},{1,9},{9,1},{17,25},{25,17},{2,10},{10... | collective-permute-start | bytes 196616 | tf_op jit(solution)/shard_map/ppermute | solution.py:216

commit v18 on v17

--- a/solution.py
+++ b/solution.py
@@ -85,10 +85,14 @@
 
 def drift_kernel(info, fragment, params, global_fragment, after, drift, scale):
     del after
-    mine = pl.ds(fragment[0], drift.shape[0], stride=FRAGS)
-    drift[...] = info[0:1, :] * (global_fragment[...] - params[0, mine, :])
-    scale[...] = jnp.ones_like(scale)
-    scale[mine, :] = jnp.full_like(drift, 1.0 - MIXING)
+    index = fragment[0]
+    pieces = drift.shape[0]
+    old = params[0, pl.ds(0, pieces, stride=FRAGS), :]
+    for at in range(1, FRAGS):
+        old = jnp.where(index == at, params[0, pl.ds(at, pieces, stride=FRAGS), :], old)
+    drift[...] = info[0:1, :] * (global_fragment[...] - old)
+    rows = lax.broadcasted_iota(jnp.int32, scale.shape, 0)
+    scale[...] = jnp.where(lax.rem(rows, FRAGS) == index, 1.0 - MIXING, 1.0)
 
 
 def add_kernel(picks, *refs):

time: 25.8 us -> 25.8 us (level)
  no operation moved by 1% of the time
where the time goes in v18:
time: 25.8 us; the launch traced here: 25.7 us
  starting transfers between devices  15 us (58%)
  waiting for transfers between devices  5.29 us (21%)
  Pallas kernels  3.92 us (15%)
  between operations  1.41 us (5%)
    ppermute x10, starting transfers between devices, hop(): return lax.ppermute(value, axis, [(d, d ^ bit) for d in range(devices)])  15 us
    ppermute x10, waiting for transfers between devices, hop(): return lax.ppermute(value, axis, [(d, d ^ bit) for d in range(devices)])  5.29 us
    pallas_call x1, Pallas kernels, body(): pl.pallas_call(functools.partial(first_kernel, workers, (7, 6)), out_shap...  1.32 us
    pallas_call x1, Pallas kernels, body(): pl.pallas_call(left_kernel, out_shape=[block((half, width)), state, state...  1.08 us
    pallas_call x1, Pallas kernels, body(): pl.pallas_call(right_kernel, out_shape=[state] * 3, in_specs=[VMEM] * 10...  0.96 us
  transfers between devices with their start and end apart: 10, of which 3 were waited for; matrix products, arithmetic and copies ran while one was open for 0% of the time, Pallas kernels for 6%

profile of v18, /device:TPU:0, one launch (start us, length us, event | category | flops | bytes accessed | tf_op | source)
XLA Modules:
  0.0 25.7 jit_solution(11847535383021856895)
XLA Ops:
  0.6 0.0 copy-start
  0.6 1.3 %far_products.1 = (f32[1,128,256]{2,1,0:T(8,128)S(1)}, f32[1,128,256]{2,1,0:T(8,128)S(1)}, bf16[128,128]{1,0:T(8,128)(2,1)S(1)}, f32[8,128]{1,0:T(8,128)S(1)}) custom-call(s32[4]{0:T(128)} %counts.1, bf16[1,128,128]{2,1,0:T(8,128)(2,1)} %cotangent.1, bf16[1,128,4096]{2,1,0:T(8,128)(2,1)} %features.3), custom_call_target="tpu_custom_call" | custom-call | flops 33554432 | bytes 786432 | tf_op jit(solution)/shard_map/far_products/pallas_call | solution.py:257
  2.0 0.5 %collective-permute-start = (f32[1,128,256]{2,1,0:T(8,128)S(1)}, f32[1,128,256]{2,1,0:T(8,128)S(1)}, u32[]{:S(2)}, u32[]{:S(2)}) collective-permute-start(f32[1,128,256]{2,1,0:T(8,128)S(1)} %get-tuple-element.29), channel_id=1, source_target_pairs={{0,1},{1,0},{2,3},{3,2},{4,5},{5,4},{6,7},{7,6},{8,9},{9,8},{10,11... | collective-permute-start | bytes 393224 | tf_op jit(solution)/shard_map/ppermute | solution.py:220
  3.1 0.0 copy-done
  3.1 0.4 %rest_products.1 = (f32[7,128,256]{2,1,0:T(8,128)S(1)}, f32[7,128,256]{2,1,0:T(8,128)S(1)}) custom-call(bf16[128,128]{1,0:T(8,128)(2,1)S(1)} %get-tuple-element.25.masked, bf16[1,128,4096]{2,1,0:T(8,128)(2,1)S(1)} %copy-done), custom_call_target="tpu_custom_call" | custom-call | tf_op jit(solution)/shard_map/rest_products/pallas_call | solution.py:272
  3.6 0.0 copy-start.1
  3.6 0.0 collective-permute-done.refs_1_
  3.6 0.0 copy-start.4
  3.6 0.3 %collective-permute-start.1 = (f32[7,128,256]{2,1,0:T(8,128)S(1)}, f32[7,128,256]{2,1,0:T(8,128)S(1)}, u32[]{:S(2)}, u32[]{:S(2)}) collective-permute-start(f32[7,128,256]{2,1,0:T(8,128)S(1)} %get-tuple-element.30), channel_id=1, source_target_pairs={{0,1},{1,0},{2,3},{3,2},{4,5},{5,4},{6,7},{7,6},{8,9},{9,8},{10,11... | collective-permute-start | bytes 2752520 | tf_op jit(solution)/shard_map/ppermute | solution.py:220
  3.9 2.8 %collective-permute-start.3 = (f32[1,128,256]{2,1,0:T(8,128)S(1)}, f32[1,128,256]{2,1,0:T(8,128)S(1)}, u32[]{:S(2)}, u32[]{:S(2)}) collective-permute-start(f32[1,128,256]{2,1,0:T(8,128)S(1)} %add_a1.1.after), channel_id=1, source_target_pairs={{0,2},{1,3},{2,0},{3,1},{4,6},{5,7},{6,4},{7,5},{8,10},{9,11},{10,... | collective-permute-start | bytes 393224 | tf_op jit(solution)/shard_map/ppermute | solution.py:220
  6.8 0.0 copy-done.1
  6.8 0.0 copy-done.4
  6.8 0.1 drift.1
  6.8 0.0 collective-permute-done.1.refs_1_.come
  6.9 2.2 %collective-permute-start.2 = (f32[1,128,256]{2,1,0:T(8,128)S(1)}, f32[1,128,256]{2,1,0:T(8,128)S(1)}, u32[]{:S(2)}, u32[]{:S(2)}) collective-permute-start(f32[1,128,256]{2,1,0:T(8,128)S(1)} %add_a2.1.refs_2_), channel_id=1, source_target_pairs={{0,2},{1,3},{2,0},{3,1},{4,6},{5,7},{6,4},{7,5},{8,10},{9,11},{10,... | collective-permute-start | bytes 393224 | tf_op jit(solution)/shard_map/ppermute | solution.py:220
  9.0 1.5 %collective-permute-start.8 = (f32[128,128]{1,0:T(8,128)S(1)}, f32[128,128]{1,0:T(8,128)S(1)}, u32[]{:S(2)}, u32[]{:S(2)}) collective-permute-start(f32[128,128]{1,0:T(8,128)S(1)} %get-tuple-element.34.refs_2_), channel_id=1, source_target_pairs={{0,16},{8,24},{16,0},{24,8},{1,17},{9,25},{17,1},{25,9},{2,18},{10... | collective-permute-start | bytes 196616 | tf_op jit(solution)/shard_map/ppermute | solution.py:220
  10.6 0.5 %collective-permute-start.7 = (f32[1,128,256]{2,1,0:T(8,128)S(1)}, f32[1,128,256]{2,1,0:T(8,128)S(1)}, u32[]{:S(2)}, u32[]{:S(2)}) collective-permute-start(f32[1,128,256]{2,1,0:T(8,128)S(1)} %add_n1.1), channel_id=1, source_target_pairs={{0,2},{1,3},{2,0},{3,1},{4,6},{5,7},{6,4},{7,5},{8,10},{9,11},{10,... | collective-permute-start | bytes 393224 | tf_op jit(solution)/shard_map/ppermute | solution.py:220
  11.1 0.0 collective-permute-done.3.refs_2_
  11.1 2.8 %collective-permute-start.6 = (f32[1,128,256]{2,1,0:T(8,128)S(1)}, f32[1,128,256]{2,1,0:T(8,128)S(1)}, u32[]{:S(2)}, u32[]{:S(2)}) collective-permute-start(f32[1,128,256]{2,1,0:T(8,128)S(1)} %add_c1.1.refs_3_.refs_2_), channel_id=1, source_target_pairs={{0,4},{1,5},{2,6},{3,7},{4,0},{5,1},{6,2},{7,3},{8,12},{9,13},{10,... | collective-permute-start | bytes 393224 | tf_op jit(solution)/shard_map/ppermute | solution.py:220
  13.9 1.6 %collective-permute-start.5 = (f32[1,128,256]{2,1,0:T(8,128)S(1)}, f32[1,128,256]{2,1,0:T(8,128)S(1)}, u32[]{:S(2)}, u32[]{:S(2)}) collective-permute-start(f32[1,128,256]{2,1,0:T(8,128)S(1)} %add_n2.1), channel_id=1, source_target_pairs={{0,2},{1,3},{2,0},{3,1},{4,6},{5,7},{6,4},{7,5},{8,10},{9,11},{10,... | collective-permute-start | bytes 393224 | tf_op jit(solution)/shard_map/ppermute | solution.py:220
  15.6 0.0 collective-permute-done.2.refs_2_
  15.6 0.0 copy-start.5
  15.6 1.1 %collective-permute-start.4 = (f32[1,128,256]{2,1,0:T(8,128)S(1)}, f32[1,128,256]{2,1,0:T(8,128)S(1)}, u32[]{:S(2)}, u32[]{:S(2)}) collective-permute-start(f32[1,128,256]{2,1,0:T(8,128)S(1)} %add_c2.1), channel_id=1, source_target_pairs={{0,4},{1,5},{2,6},{3,7},{4,0},{5,1},{6,2},{7,3},{8,12},{9,13},{10,... | collective-permute-start | bytes 393224 | tf_op jit(solution)/shard_map/ppermute | solution.py:220
  16.7 0.0 collective-permute-done.8
  16.8 1.6 %collective-permute-start.9 = (f32[128,128]{1,0:T(8,128)S(1)}, f32[128,128]{1,0:T(8,128)S(1)}, u32[]{:S(2)}, u32[]{:S(2)}) collective-permute-start(f32[128,128]{1,0:T(8,128)S(1)} %add.3.drift), channel_id=1, source_target_pairs={{0,8},{8,0},{16,24},{24,16},{1,9},{9,1},{17,25},{25,17},{2,10},{10... | collective-permute-start | bytes 196616 | tf_op jit(solution)/shard_map/ppermute | solution.py:220
  18.3 2.3 %collective-permute-done.7.near = f32[1,128,256]{2,1,0:T(8,128)S(1)} collective-permute-done((f32[1,128,256]{2,1,0:T(8,128)S(1)}, f32[1,128,256]{2,1,0:T(8,128)S(1)}, u32[]{:S(2)}, u32[]{:S(2)}) %collective-permute-start.7) | collective-permute-done | bytes 131104 | tf_op jit(solution)/shard_map/ppermute | solution.py:220
  20.6 0.0 collective-permute-done.6.far
  20.6 0.5 %collective-permute-done.9.other_drift = f32[128,128]{1,0:T(8,128)S(1)} collective-permute-done((f32[128,128]{1,0:T(8,128)S(1)}, f32[128,128]{1,0:T(8,128)S(1)}, u32[]{:S(2)}, u32[]{:S(2)}) %collective-permute-start.9) | collective-permute-done | bytes 65568 | tf_op jit(solution)/shard_map/ppermute | solution.py:220
  21.1 1.1 %left_step.1 = (f32[256,128]{1,0:T(8,128)S(1)}, f32[1,512,128]{2,1,0:T(8,128)}, f32[1,512,128]{2,1,0:T(8,128)}, f32[1,512,128]{2,1,0:T(8,128)}, f32[128,128]{1,0:T(8,128)}, /*index=5*/f32[128,128]{1,0:T(8,128)}) custom-call(f32[1,512,128]{2,1,0:T(8,128)S(1)} %copy-done.1, f32[1,512,128]{2,1,0:T(8,128)S(1)} %copy-done.2, f32[1,512,128]{2,1,0:T(8,128)S(1)} %copy-done.3, ...), custom_call_target="tpu_custom_call" | custom-call | flops 983040 | bytes 1310720 | tf_op jit(solution)/shard_map/left_step/pallas_call | solution.py:332
  22.2 2.5 %collective-permute-done.5.near = f32[1,128,256]{2,1,0:T(8,128)S(1)} collective-permute-done((f32[1,128,256]{2,1,0:T(8,128)S(1)}, f32[1,128,256]{2,1,0:T(8,128)S(1)}, u32[]{:S(2)}, u32[]{:S(2)}) %collective-permute-start.5) | collective-permute-done | bytes 131104 | tf_op jit(solution)/shard_map/ppermute | solution.py:220
  24.7 0.0 collective-permute-done.4.far
  24.7 1.0 %right_step.1 = (f32[1,512,128]{2,1,0:T(8,128)}, f32[1,512,128]{2,1,0:T(8,128)}, f32[1,512,128]{2,1,0:T(8,128)}) custom-call(f32[1,512,128]{2,1,0:T(8,128)S(1)} %copy-done.1, f32[1,512,128]{2,1,0:T(8,128)S(1)} %copy-done.2, f32[1,512,128]{2,1,0:T(8,128)S(1)} %copy-done.3, ...), custom_call_target="tpu_custom_call", output_to_operand_aliasing={{0}: (10, {}), {1}: (11, {}), {2}: (12, {})} | custom-call | tf_op jit(solution)/shard_map/right_step/pallas_call | solution.py:359
  (12 shorter events, 0.1 us)
Async XLA Ops:
  0.6 2.5 %copy-start = (bf16[1,128,4096]{2,1,0:T(8,128)(2,1)S(1)}, bf16[1,128,4096]{2,1,0:T(8,128)(2,1)}, u32[]{:S(2)}) copy-start(bf16[1,128,4096]{2,1,0:T(8,128)(2,1)} %features.3) | copy-start | bytes 3145732
  2.0 1.6 %collective-permute-start = (f32[1,128,256]{2,1,0:T(8,128)S(1)}, f32[1,128,256]{2,1,0:T(8,128)S(1)}, u32[]{:S(2)}, u32[]{:S(2)}) collective-permute-start(f32[1,128,256]{2,1,0:T(8,128)S(1)} %get-tuple-element.29), channel_id=1, source_target_pairs={{0,1},{1,0},{2,3},{3,2},{4,5},{5,4},{6,7},{7,6},{8,9},{9,8},{10,11... | collective-permute-start | bytes 393224 | tf_op jit(solution)/shard_map/ppermute | solution.py:220
  3.6 3.2 %copy-start.1 = (f32[1,512,128]{2,1,0:T(8,128)S(1)}, f32[1,512,128]{2,1,0:T(8,128)}, u32[]{:S(2)}) copy-start(f32[1,512,128]{2,1,0:T(8,128)} %params.5) | copy-start | bytes 786436
  3.6 3.2 %copy-start.4 = (f32[128,128]{1,0:T(8,128)S(1)}, f32[128,128]{1,0:T(8,128)}, u32[]{:S(2)}) copy-start(f32[128,128]{1,0:T(8,128)} %global_fragment.3) | copy-start | bytes 196612
  3.6 3.2 %collective-permute-start.1 = (f32[7,128,256]{2,1,0:T(8,128)S(1)}, f32[7,128,256]{2,1,0:T(8,128)S(1)}, u32[]{:S(2)}, u32[]{:S(2)}) collective-permute-start(f32[7,128,256]{2,1,0:T(8,128)S(1)} %get-tuple-element.30), channel_id=1, source_target_pairs={{0,1},{1,0},{2,3},{3,2},{4,5},{5,4},{6,7},{7,6},{8,9},{9,8},{10,11... | collective-permute-start | bytes 2752520 | tf_op jit(solution)/shard_map/ppermute | solution.py:220
  3.9 7.2 %collective-permute-start.3 = (f32[1,128,256]{2,1,0:T(8,128)S(1)}, f32[1,128,256]{2,1,0:T(8,128)S(1)}, u32[]{:S(2)}, u32[]{:S(2)}) collective-permute-start(f32[1,128,256]{2,1,0:T(8,128)S(1)} %add_a1.1.after), channel_id=1, source_target_pairs={{0,2},{1,3},{2,0},{3,1},{4,6},{5,7},{6,4},{7,5},{8,10},{9,11},{10,... | collective-permute-start | bytes 393224 | tf_op jit(solution)/shard_map/ppermute | solution.py:220
  6.9 8.7 %collective-permute-start.2 = (f32[1,128,256]{2,1,0:T(8,128)S(1)}, f32[1,128,256]{2,1,0:T(8,128)S(1)}, u32[]{:S(2)}, u32[]{:S(2)}) collective-permute-start(f32[1,128,256]{2,1,0:T(8,128)S(1)} %add_a2.1.refs_2_), channel_id=1, source_target_pairs={{0,2},{1,3},{2,0},{3,1},{4,6},{5,7},{6,4},{7,5},{8,10},{9,11},{10,... | collective-permute-start | bytes 393224 | tf_op jit(solution)/shard_map/ppermute | solution.py:220
  9.0 7.7 %collective-permute-start.8 = (f32[128,128]{1,0:T(8,128)S(1)}, f32[128,128]{1,0:T(8,128)S(1)}, u32[]{:S(2)}, u32[]{:S(2)}) collective-permute-start(f32[128,128]{1,0:T(8,128)S(1)} %get-tuple-element.34.refs_2_), channel_id=1, source_target_pairs={{0,16},{8,24},{16,0},{24,8},{1,17},{9,25},{17,1},{25,9},{2,18},{10... | collective-permute-start | bytes 196616 | tf_op jit(solution)/shard_map/ppermute | solution.py:220
  10.6 10.0 %collective-permute-start.7 = (f32[1,128,256]{2,1,0:T(8,128)S(1)}, f32[1,128,256]{2,1,0:T(8,128)S(1)}, u32[]{:S(2)}, u32[]{:S(2)}) collective-permute-start(f32[1,128,256]{2,1,0:T(8,128)S(1)} %add_n1.1), channel_id=1, source_target_pairs={{0,2},{1,3},{2,0},{3,1},{4,6},{5,7},{6,4},{7,5},{8,10},{9,11},{10,... | collective-permute-start | bytes 393224 | tf_op jit(solution)/shard_map/ppermute | solution.py:220
  11.1 9.5 %collective-permute-start.6 = (f32[1,128,256]{2,1,0:T(8,128)S(1)}, f32[1,128,256]{2,1,0:T(8,128)S(1)}, u32[]{:S(2)}, u32[]{:S(2)}) collective-permute-start(f32[1,128,256]{2,1,0:T(8,128)S(1)} %add_c1.1.refs_3_.refs_2_), channel_id=1, source_target_pairs={{0,4},{1,5},{2,6},{3,7},{4,0},{5,1},{6,2},{7,3},{8,12},{9,13},{10,... | collective-permute-start | bytes 393224 | tf_op jit(solution)/shard_map/ppermute | solution.py:220
  13.9 10.8 %collective-permute-start.5 = (f32[1,128,256]{2,1,0:T(8,128)S(1)}, f32[1,128,256]{2,1,0:T(8,128)S(1)}, u32[]{:S(2)}, u32[]{:S(2)}) collective-permute-start(f32[1,128,256]{2,1,0:T(8,128)S(1)} %add_n2.1), channel_id=1, source_target_pairs={{0,2},{1,3},{2,0},{3,1},{4,6},{5,7},{6,4},{7,5},{8,10},{9,11},{10,... | collective-permute-start | bytes 393224 | tf_op jit(solution)/shard_map/ppermute | solution.py:220
  15.6 5.5 %copy-start.2 = (f32[1,512,128]{2,1,0:T(8,128)S(1)}, f32[1,512,128]{2,1,0:T(8,128)}, u32[]{:S(2)}) copy-start(f32[1,512,128]{2,1,0:T(8,128)} %first.3) | copy-start | bytes 786436
  15.6 5.5 %copy-start.3 = (f32[1,512,128]{2,1,0:T(8,128)S(1)}, f32[1,512,128]{2,1,0:T(8,128)}, u32[]{:S(2)}) copy-start(f32[1,512,128]{2,1,0:T(8,128)} %second.3) | copy-start | bytes 786436
  15.6 5.5 %copy-start.5 = (f32[128,128]{1,0:T(8,128)S(1)}, f32[128,128]{1,0:T(8,128)}, u32[]{:S(2)}) copy-start(f32[128,128]{1,0:T(8,128)} %outer_momentum.1) | copy-start | bytes 196612
  15.6 9.1 %collective-permute-start.4 = (f32[1,128,256]{2,1,0:T(8,128)S(1)}, f32[1,128,256]{2,1,0:T(8,128)S(1)}, u32[]{:S(2)}, u32[]{:S(2)}) collective-permute-start(f32[1,128,256]{2,1,0:T(8,128)S(1)} %add_c2.1), channel_id=1, source_target_pairs={{0,4},{1,5},{2,6},{3,7},{4,0},{5,1},{6,2},{7,3},{8,12},{9,13},{10,... | collective-permute-start | bytes 393224 | tf_op jit(solution)/shard_map/ppermute | solution.py:220
  16.8 4.3 %collective-permute-start.9 = (f32[128,128]{1,0:T(8,128)S(1)}, f32[128,128]{1,0:T(8,128)S(1)}, u32[]{:S(2)}, u32[]{:S(2)}) collective-permute-start(f32[128,128]{1,0:T(8,128)S(1)} %add.3.drift), channel_id=1, source_target_pairs={{0,8},{8,0},{16,24},{24,16},{1,9},{9,1},{17,25},{25,17},{2,10},{10... | collective-permute-start | bytes 196616 | tf_op jit(solution)/shard_map/ppermute | solution.py:220

commit v19 on v18

--- a/solution.py
+++ b/solution.py
@@ -148,7 +148,11 @@
     outer_momentum,
     drift,
     other_drift,
-    mix,
+    own,
+    first_base,
+    second_base,
+    base,
+    step,
     new_params,
     new_first,
     new_second,
@@ -176,23 +180,29 @@
         held_params[lanes, :] = scale[there, :] * value + (1.0 - scale[there, :]) * spread[there, :]
         for source, target in ((held_first, new_first), (held_second, new_second), (held_params, new_params)):
             send(copies, sems, source.at[lanes], target.at[0, there])
-    right = pl.ds(mix.shape[0], mix.shape[0])
-    mix[...] = (1.0 - scale[right, :]) * spread[right, :]
+    rows = own.shape[0]
+    for lane in range(0, rows, LANES):
+        lanes, there = pl.ds(lane, LANES), pl.ds(rows + lane, LANES)
+        own[lanes, :] = (kept[1, :, lanes] + come[1, :, lanes]).T * info[1:2, :]
+        first_base[lanes, :] = BETA_ONE * first[0, there, :]
+        second_base[lanes, :] = BETA_TWO * second[0, there, :]
+        base[lanes, :] = scale[there, :] * ((1.0 - LEARN_RATE * DECAY_RATE) * params[0, there, :]) + (
+            1.0 - scale[there, :]
+        ) * spread[there, :]
+        step[lanes, :] = (LEARN_RATE / CORRECT_ONE) * scale[there, :]
     for copy in copies:
         copy.wait()
 
 
 def right_kernel(
-    params,
-    first,
-    second,
-    kept,
-    come,
     far,
     near,
     info,
-    scale,
-    mix,
+    own,
+    first_base,
+    second_base,
+    base,
+    step,
     left_params,
     left_first,
     left_second,
@@ -206,10 +216,17 @@
 ):
     del left_params, left_first, left_second
     copies = []
-    for lanes, there, value in half_step(
-        1, (params, first, second), (kept, come, far, near), info, (held_first, held_second)
-    ):
-        held_params[lanes, :] = scale[there, :] * value + mix[lanes, :]
+    rows = own.shape[0]
+    for lane in range(0, rows, LANES):
+        lanes, there = pl.ds(lane, LANES), pl.ds(rows + lane, LANES)
+        gradient = own[lanes, :] + (near[0, :, lanes] + far[0, :, lanes]).T * info[1:2, :]
+        first_new = first_base[lanes, :] + (1.0 - BETA_ONE) * gradient
+        second_new = second_base[lanes, :] + (1.0 - BETA_TWO) * gradient * gradient
+        held_first[lanes, :] = first_new
+        held_second[lanes, :] = second_new
+        held_params[lanes, :] = base[lanes, :] - step[lanes, :] * first_new / (
+            jnp.sqrt(second_new * (1.0 / CORRECT_TWO)) + ADAM_EPS
+        )
         for source, target in ((held_first, new_first), (held_second, new_second), (held_params, new_params)):
             send(copies, sems, source.at[lanes], target.at[0, there])
     for copy in copies:
@@ -329,11 +346,11 @@
         near_right = hop(near_right, "fsdp", devices, 2)
         groups = half // LANES
         held_half = pltpu.VMEM((half, width), jnp.float32)
-        mix, *results, new_global, new_momentum = pl.pallas_call(
+        own, first_base, second_base, base, step, *results, new_global, new_momentum = pl.pallas_call(
             left_kernel,
-            out_shape=[block((half, width)), state, state, state, piece, piece],
+            out_shape=[block((half, width))] * 5 + [state] * 3 + [piece] * 2,
             in_specs=[VMEM] * 13,
-            out_specs=[VMEM] + [HBM] * 5,
+            out_specs=[VMEM] * 5 + [HBM] * 5,
             scratch_shapes=[held_half] * 3
             + [held_piece] * 2
             + [pltpu.VMEM((rows, width), jnp.float32), pltpu.SemaphoreType.DMA((2 + 3 * groups,))],
@@ -359,14 +376,14 @@
         new_params, new_first, new_second = pl.pallas_call(
             right_kernel,
             out_shape=[state] * 3,
-            in_specs=[VMEM] * 10 + [HBM] * 3,
+            in_specs=[VMEM] * 8 + [HBM] * 3,
             out_specs=[HBM] * 3,
-            input_output_aliases={10: 0, 11: 1, 12: 2},
+            input_output_aliases={8: 0, 9: 1, 10: 2},
             scratch_shapes=[held_half] * 3 + [pltpu.SemaphoreType.DMA((3 * groups,))],
             compiler_params=room,
             cost_estimate=free,
             name="right_step",
-        )(params, first, second, kept, come, far_right, near_right, info, scale, mix, *results)
+        )(far_right, near_right, info, own, first_base, second_base, base, step, *results)
         return new_params, new_first, new_second, new_global, new_momentum
 
     return body

time: 25.8 us -> 25.8 us (level)
  no operation moved by 1% of the time
where the time goes in v19:
time: 25.8 us; the launch traced here: 25.6 us
  starting transfers between devices  15 us (58%)
  waiting for transfers between devices  5.28 us (20%)
  Pallas kernels  3.9 us (15%)
  between operations  1.41 us (5%)
    ppermute x10, starting transfers between devices, hop(): return lax.ppermute(value, axis, [(d, d ^ bit) for d in range(devices)])  15 us
    ppermute x10, waiting for transfers between devices, hop(): return lax.ppermute(value, axis, [(d, d ^ bit) for d in range(devices)])  5.28 us
    pallas_call x1, Pallas kernels, body(): pl.pallas_call(functools.partial(first_kernel, workers, (7, 6)), out_shap...  1.32 us
    pallas_call x1, Pallas kernels, body(): pl.pallas_call(left_kernel, out_shape=[block((half, width))] * 5 + [state...  1.09 us
    pallas_call x1, Pallas kernels, body(): pl.pallas_call(right_kernel, out_shape=[state] * 3, in_specs=[VMEM] * 8 +...  0.94 us
  transfers between devices with their start and end apart: 10, of which 3 were waited for; matrix products, arithmetic and copies ran while one was open for 0% of the time, Pallas kernels for 6%

profile of v19, /device:TPU:0, one launch (start us, length us, event | category | flops | bytes accessed | tf_op | source)
XLA Modules:
  0.0 25.6 jit_solution(14624509332675666837)
XLA Ops:
  0.6 0.0 copy-start
  0.6 1.3 %far_products.1 = (f32[1,128,256]{2,1,0:T(8,128)S(1)}, f32[1,128,256]{2,1,0:T(8,128)S(1)}, bf16[128,128]{1,0:T(8,128)(2,1)S(1)}, f32[8,128]{1,0:T(8,128)S(1)}) custom-call(s32[4]{0:T(128)} %counts.1, bf16[1,128,128]{2,1,0:T(8,128)(2,1)} %cotangent.1, bf16[1,128,4096]{2,1,0:T(8,128)(2,1)} %features.3), custom_call_target="tpu_custom_call" | custom-call | flops 33554432 | bytes 786432 | tf_op jit(solution)/shard_map/far_products/pallas_call | solution.py:274
  2.0 0.5 %collective-permute-start = (f32[1,128,256]{2,1,0:T(8,128)S(1)}, f32[1,128,256]{2,1,0:T(8,128)S(1)}, u32[]{:S(2)}, u32[]{:S(2)}) collective-permute-start(f32[1,128,256]{2,1,0:T(8,128)S(1)} %get-tuple-element.33), channel_id=1, source_target_pairs={{0,1},{1,0},{2,3},{3,2},{4,5},{5,4},{6,7},{7,6},{8,9},{9,8},{10,11... | collective-permute-start | bytes 393224 | tf_op jit(solution)/shard_map/ppermute | solution.py:237
  3.1 0.0 copy-done
  3.1 0.4 %rest_products.1 = (f32[7,128,256]{2,1,0:T(8,128)S(1)}, f32[7,128,256]{2,1,0:T(8,128)S(1)}) custom-call(bf16[128,128]{1,0:T(8,128)(2,1)S(1)} %get-tuple-element.29.masked, bf16[1,128,4096]{2,1,0:T(8,128)(2,1)S(1)} %copy-done), custom_call_target="tpu_custom_call" | custom-call | tf_op jit(solution)/shard_map/rest_products/pallas_call | solution.py:289
  3.6 0.0 copy-start.1
  3.6 0.0 collective-permute-done.refs_1_
  3.6 0.0 copy-start.4
  3.6 0.3 %collective-permute-start.1 = (f32[7,128,256]{2,1,0:T(8,128)S(1)}, f32[7,128,256]{2,1,0:T(8,128)S(1)}, u32[]{:S(2)}, u32[]{:S(2)}) collective-permute-start(f32[7,128,256]{2,1,0:T(8,128)S(1)} %get-tuple-element.34), channel_id=1, source_target_pairs={{0,1},{1,0},{2,3},{3,2},{4,5},{5,4},{6,7},{7,6},{8,9},{9,8},{10,11... | collective-permute-start | bytes 2752520 | tf_op jit(solution)/shard_map/ppermute | solution.py:237
  3.9 2.8 %collective-permute-start.3 = (f32[1,128,256]{2,1,0:T(8,128)S(1)}, f32[1,128,256]{2,1,0:T(8,128)S(1)}, u32[]{:S(2)}, u32[]{:S(2)}) collective-permute-start(f32[1,128,256]{2,1,0:T(8,128)S(1)} %add_a1.1.after), channel_id=1, source_target_pairs={{0,2},{1,3},{2,0},{3,1},{4,6},{5,7},{6,4},{7,5},{8,10},{9,11},{10,... | collective-permute-start | bytes 393224 | tf_op jit(solution)/shard_map/ppermute | solution.py:237
  6.8 0.0 copy-done.1
  6.8 0.0 copy-done.4
  6.8 0.1 drift.1
  6.8 0.0 collective-permute-done.1.refs_1_.come
  6.9 2.2 %collective-permute-start.2 = (f32[1,128,256]{2,1,0:T(8,128)S(1)}, f32[1,128,256]{2,1,0:T(8,128)S(1)}, u32[]{:S(2)}, u32[]{:S(2)}) collective-permute-start(f32[1,128,256]{2,1,0:T(8,128)S(1)} %add_a2.1.refs_2_), channel_id=1, source_target_pairs={{0,2},{1,3},{2,0},{3,1},{4,6},{5,7},{6,4},{7,5},{8,10},{9,11},{10,... | collective-permute-start | bytes 393224 | tf_op jit(solution)/shard_map/ppermute | solution.py:237
  9.0 1.5 %collective-permute-start.8 = (f32[128,128]{1,0:T(8,128)S(1)}, f32[128,128]{1,0:T(8,128)S(1)}, u32[]{:S(2)}, u32[]{:S(2)}) collective-permute-start(f32[128,128]{1,0:T(8,128)S(1)} %get-tuple-element.38.refs_2_), channel_id=1, source_target_pairs={{0,16},{8,24},{16,0},{24,8},{1,17},{9,25},{17,1},{25,9},{2,18},{10... | collective-permute-start | bytes 196616 | tf_op jit(solution)/shard_map/ppermute | solution.py:237
  10.6 0.5 %collective-permute-start.7 = (f32[1,128,256]{2,1,0:T(8,128)S(1)}, f32[1,128,256]{2,1,0:T(8,128)S(1)}, u32[]{:S(2)}, u32[]{:S(2)}) collective-permute-start(f32[1,128,256]{2,1,0:T(8,128)S(1)} %add_n1.1), channel_id=1, source_target_pairs={{0,2},{1,3},{2,0},{3,1},{4,6},{5,7},{6,4},{7,5},{8,10},{9,11},{10,... | collective-permute-start | bytes 393224 | tf_op jit(solution)/shard_map/ppermute | solution.py:237
  11.1 0.0 collective-permute-done.3.refs_2_
  11.1 2.8 %collective-permute-start.6 = (f32[1,128,256]{2,1,0:T(8,128)S(1)}, f32[1,128,256]{2,1,0:T(8,128)S(1)}, u32[]{:S(2)}, u32[]{:S(2)}) collective-permute-start(f32[1,128,256]{2,1,0:T(8,128)S(1)} %add_c1.1.refs_3_.refs_2_), channel_id=1, source_target_pairs={{0,4},{1,5},{2,6},{3,7},{4,0},{5,1},{6,2},{7,3},{8,12},{9,13},{10,... | collective-permute-start | bytes 393224 | tf_op jit(solution)/shard_map/ppermute | solution.py:237
  13.9 1.6 %collective-permute-start.5 = (f32[1,128,256]{2,1,0:T(8,128)S(1)}, f32[1,128,256]{2,1,0:T(8,128)S(1)}, u32[]{:S(2)}, u32[]{:S(2)}) collective-permute-start(f32[1,128,256]{2,1,0:T(8,128)S(1)} %add_n2.1), channel_id=1, source_target_pairs={{0,2},{1,3},{2,0},{3,1},{4,6},{5,7},{6,4},{7,5},{8,10},{9,11},{10,... | collective-permute-start | bytes 393224 | tf_op jit(solution)/shard_map/ppermute | solution.py:237
  15.6 0.0 collective-permute-done.2.refs_2_
  15.6 0.0 copy-start.5
  15.6 1.1 %collective-permute-start.4 = (f32[1,128,256]{2,1,0:T(8,128)S(1)}, f32[1,128,256]{2,1,0:T(8,128)S(1)}, u32[]{:S(2)}, u32[]{:S(2)}) collective-permute-start(f32[1,128,256]{2,1,0:T(8,128)S(1)} %add_c2.1), channel_id=1, source_target_pairs={{0,4},{1,5},{2,6},{3,7},{4,0},{5,1},{6,2},{7,3},{8,12},{9,13},{10,... | collective-permute-start | bytes 393224 | tf_op jit(solution)/shard_map/ppermute | solution.py:237
  16.7 0.0 collective-permute-done.8
  16.8 1.6 %collective-permute-start.9 = (f32[128,128]{1,0:T(8,128)S(1)}, f32[128,128]{1,0:T(8,128)S(1)}, u32[]{:S(2)}, u32[]{:S(2)}) collective-permute-start(f32[128,128]{1,0:T(8,128)S(1)} %add.3.drift), channel_id=1, source_target_pairs={{0,8},{8,0},{16,24},{24,16},{1,9},{9,1},{17,25},{25,17},{2,10},{10... | collective-permute-start | bytes 196616 | tf_op jit(solution)/shard_map/ppermute | solution.py:237
  18.3 2.3 %collective-permute-done.7.near = f32[1,128,256]{2,1,0:T(8,128)S(1)} collective-permute-done((f32[1,128,256]{2,1,0:T(8,128)S(1)}, f32[1,128,256]{2,1,0:T(8,128)S(1)}, u32[]{:S(2)}, u32[]{:S(2)}) %collective-permute-start.7) | collective-permute-done | bytes 131104 | tf_op jit(solution)/shard_map/ppermute | solution.py:237
  20.6 0.0 collective-permute-done.6.far
  20.6 0.5 %collective-permute-done.9.other_drift = f32[128,128]{1,0:T(8,128)S(1)} collective-permute-done((f32[128,128]{1,0:T(8,128)S(1)}, f32[128,128]{1,0:T(8,128)S(1)}, u32[]{:S(2)}, u32[]{:S(2)}) %collective-permute-start.9) | collective-permute-done | bytes 65568 | tf_op jit(solution)/shard_map/ppermute | solution.py:237
  21.1 1.1 %left_step.1 = (f32[256,128]{1,0:T(8,128)S(1)}, f32[256,128]{1,0:T(8,128)S(1)}, f32[256,128]{1,0:T(8,128)S(1)}, f32[256,128]{1,0:T(8,128)S(1)}, f32[256,128]{1,0...) custom-call(f32[1,512,128]{2,1,0:T(8,128)S(1)} %copy-done.1, ...), custom_call_target="tpu_custom_call" | custom-call | flops 983040 | bytes 1310720 | tf_op jit(solution)/shard_map/left_step/pallas_call | solution.py:349
  22.2 2.5 %collective-permute-done.5.near = f32[1,128,256]{2,1,0:T(8,128)S(1)} collective-permute-done((f32[1,128,256]{2,1,0:T(8,128)S(1)}, f32[1,128,256]{2,1,0:T(8,128)S(1)}, u32[]{:S(2)}, u32[]{:S(2)}) %collective-permute-start.5) | collective-permute-done | bytes 131104 | tf_op jit(solution)/shard_map/ppermute | solution.py:237
  24.7 0.0 collective-permute-done.4.far
  24.7 0.9 %right_step.1 = (f32[1,512,128]{2,1,0:T(8,128)}, f32[1,512,128]{2,1,0:T(8,128)}, f32[1,512,128]{2,1,0:T(8,128)}) custom-call(f32[1,128,256]{2,1,0:T(8,128)S(1)} %collective-permute-done.4.far, f32[1,128,256]{2,1,0:T(8,128)S(1)} %collective-permute-done.5.near, ...), custom_call_target="tpu_custom_call", output_to_operand_aliasing={{0}: (8, {}), {1}: (9, {}), {2}: (10, {})} | custom-call | tf_op jit(solution)/shard_map/right_step/pallas_call | solution.py:376
  (12 shorter events, 0.1 us)
Async XLA Ops:
  0.6 2.5 %copy-start = (bf16[1,128,4096]{2,1,0:T(8,128)(2,1)S(1)}, bf16[1,128,4096]{2,1,0:T(8,128)(2,1)}, u32[]{:S(2)}) copy-start(bf16[1,128,4096]{2,1,0:T(8,128)(2,1)} %features.3) | copy-start | bytes 3145732
  2.0 1.6 %collective-permute-start = (f32[1,128,256]{2,1,0:T(8,128)S(1)}, f32[1,128,256]{2,1,0:T(8,128)S(1)}, u32[]{:S(2)}, u32[]{:S(2)}) collective-permute-start(f32[1,128,256]{2,1,0:T(8,128)S(1)} %get-tuple-element.33), channel_id=1, source_target_pairs={{0,1},{1,0},{2,3},{3,2},{4,5},{5,4},{6,7},{7,6},{8,9},{9,8},{10,11... | collective-permute-start | bytes 393224 | tf_op jit(solution)/shard_map/ppermute | solution.py:237
  3.6 3.2 %copy-start.1 = (f32[1,512,128]{2,1,0:T(8,128)S(1)}, f32[1,512,128]{2,1,0:T(8,128)}, u32[]{:S(2)}) copy-start(f32[1,512,128]{2,1,0:T(8,128)} %params.3) | copy-start | bytes 786436
  3.6 3.2 %copy-start.4 = (f32[128,128]{1,0:T(8,128)S(1)}, f32[128,128]{1,0:T(8,128)}, u32[]{:S(2)}) copy-start(f32[128,128]{1,0:T(8,128)} %global_fragment.3) | copy-start | bytes 196612
  3.6 3.2 %collective-permute-start.1 = (f32[7,128,256]{2,1,0:T(8,128)S(1)}, f32[7,128,256]{2,1,0:T(8,128)S(1)}, u32[]{:S(2)}, u32[]{:S(2)}) collective-permute-start(f32[7,128,256]{2,1,0:T(8,128)S(1)} %get-tuple-element.34), channel_id=1, source_target_pairs={{0,1},{1,0},{2,3},{3,2},{4,5},{5,4},{6,7},{7,6},{8,9},{9,8},{10,11... | collective-permute-start | bytes 2752520 | tf_op jit(solution)/shard_map/ppermute | solution.py:237
  3.9 7.2 %collective-permute-start.3 = (f32[1,128,256]{2,1,0:T(8,128)S(1)}, f32[1,128,256]{2,1,0:T(8,128)S(1)}, u32[]{:S(2)}, u32[]{:S(2)}) collective-permute-start(f32[1,128,256]{2,1,0:T(8,128)S(1)} %add_a1.1.after), channel_id=1, source_target_pairs={{0,2},{1,3},{2,0},{3,1},{4,6},{5,7},{6,4},{7,5},{8,10},{9,11},{10,... | collective-permute-start | bytes 393224 | tf_op jit(solution)/shard_map/ppermute | solution.py:237
  6.9 8.7 %collective-permute-start.2 = (f32[1,128,256]{2,1,0:T(8,128)S(1)}, f32[1,128,256]{2,1,0:T(8,128)S(1)}, u32[]{:S(2)}, u32[]{:S(2)}) collective-permute-start(f32[1,128,256]{2,1,0:T(8,128)S(1)} %add_a2.1.refs_2_), channel_id=1, source_target_pairs={{0,2},{1,3},{2,0},{3,1},{4,6},{5,7},{6,4},{7,5},{8,10},{9,11},{10,... | collective-permute-start | bytes 393224 | tf_op jit(solution)/shard_map/ppermute | solution.py:237
  9.0 7.7 %collective-permute-start.8 = (f32[128,128]{1,0:T(8,128)S(1)}, f32[128,128]{1,0:T(8,128)S(1)}, u32[]{:S(2)}, u32[]{:S(2)}) collective-permute-start(f32[128,128]{1,0:T(8,128)S(1)} %get-tuple-element.38.refs_2_), channel_id=1, source_target_pairs={{0,16},{8,24},{16,0},{24,8},{1,17},{9,25},{17,1},{25,9},{2,18},{10... | collective-permute-start | bytes 196616 | tf_op jit(solution)/shard_map/ppermute | solution.py:237
  10.6 10.0 %collective-permute-start.7 = (f32[1,128,256]{2,1,0:T(8,128)S(1)}, f32[1,128,256]{2,1,0:T(8,128)S(1)}, u32[]{:S(2)}, u32[]{:S(2)}) collective-permute-start(f32[1,128,256]{2,1,0:T(8,128)S(1)} %add_n1.1), channel_id=1, source_target_pairs={{0,2},{1,3},{2,0},{3,1},{4,6},{5,7},{6,4},{7,5},{8,10},{9,11},{10,... | collective-permute-start | bytes 393224 | tf_op jit(solution)/shard_map/ppermute | solution.py:237
  11.1 9.5 %collective-permute-start.6 = (f32[1,128,256]{2,1,0:T(8,128)S(1)}, f32[1,128,256]{2,1,0:T(8,128)S(1)}, u32[]{:S(2)}, u32[]{:S(2)}) collective-permute-start(f32[1,128,256]{2,1,0:T(8,128)S(1)} %add_c1.1.refs_3_.refs_2_), channel_id=1, source_target_pairs={{0,4},{1,5},{2,6},{3,7},{4,0},{5,1},{6,2},{7,3},{8,12},{9,13},{10,... | collective-permute-start | bytes 393224 | tf_op jit(solution)/shard_map/ppermute | solution.py:237
  13.9 10.8 %collective-permute-start.5 = (f32[1,128,256]{2,1,0:T(8,128)S(1)}, f32[1,128,256]{2,1,0:T(8,128)S(1)}, u32[]{:S(2)}, u32[]{:S(2)}) collective-permute-start(f32[1,128,256]{2,1,0:T(8,128)S(1)} %add_n2.1), channel_id=1, source_target_pairs={{0,2},{1,3},{2,0},{3,1},{4,6},{5,7},{6,4},{7,5},{8,10},{9,11},{10,... | collective-permute-start | bytes 393224 | tf_op jit(solution)/shard_map/ppermute | solution.py:237
  15.6 5.5 %copy-start.2 = (f32[1,512,128]{2,1,0:T(8,128)S(1)}, f32[1,512,128]{2,1,0:T(8,128)}, u32[]{:S(2)}) copy-start(f32[1,512,128]{2,1,0:T(8,128)} %first.1) | copy-start | bytes 786436
  15.6 5.5 %copy-start.3 = (f32[1,512,128]{2,1,0:T(8,128)S(1)}, f32[1,512,128]{2,1,0:T(8,128)}, u32[]{:S(2)}) copy-start(f32[1,512,128]{2,1,0:T(8,128)} %second.1) | copy-start | bytes 786436
  15.6 5.5 %copy-start.5 = (f32[128,128]{1,0:T(8,128)S(1)}, f32[128,128]{1,0:T(8,128)}, u32[]{:S(2)}) copy-start(f32[128,128]{1,0:T(8,128)} %outer_momentum.1) | copy-start | bytes 196612
  15.6 9.1 %collective-permute-start.4 = (f32[1,128,256]{2,1,0:T(8,128)S(1)}, f32[1,128,256]{2,1,0:T(8,128)S(1)}, u32[]{:S(2)}, u32[]{:S(2)}) collective-permute-start(f32[1,128,256]{2,1,0:T(8,128)S(1)} %add_c2.1), channel_id=1, source_target_pairs={{0,4},{1,5},{2,6},{3,7},{4,0},{5,1},{6,2},{7,3},{8,12},{9,13},{10,... | collective-permute-start | bytes 393224 | tf_op jit(solution)/shard_map/ppermute | solution.py:237
  16.8 4.3 %collective-permute-start.9 = (f32[128,128]{1,0:T(8,128)S(1)}, f32[128,128]{1,0:T(8,128)S(1)}, u32[]{:S(2)}, u32[]{:S(2)}) collective-permute-start(f32[128,128]{1,0:T(8,128)S(1)} %add.3.drift), channel_id=1, source_target_pairs={{0,8},{8,0},{16,24},{24,16},{1,9},{9,1},{17,25},{25,17},{2,10},{10... | collective-permute-start | bytes 196616 | tf_op jit(solution)/shard_map/ppermute | solution.py:237

commit v20 on v19

--- a/solution.py
+++ b/solution.py
@@ -218,17 +218,20 @@
     copies = []
     rows = own.shape[0]
     for lane in range(0, rows, LANES):
-        lanes, there = pl.ds(lane, LANES), pl.ds(rows + lane, LANES)
-        gradient = own[lanes, :] + (near[0, :, lanes] + far[0, :, lanes]).T * info[1:2, :]
-        first_new = first_base[lanes, :] + (1.0 - BETA_ONE) * gradient
-        second_new = second_base[lanes, :] + (1.0 - BETA_TWO) * gradient * gradient
-        held_first[lanes, :] = first_new
-        held_second[lanes, :] = second_new
-        held_params[lanes, :] = base[lanes, :] - step[lanes, :] * first_new / (
-            jnp.sqrt(second_new * (1.0 / CORRECT_TWO)) + ADAM_EPS
-        )
-        for source, target in ((held_first, new_first), (held_second, new_second), (held_params, new_params)):
-            send(copies, sems, source.at[lanes], target.at[0, there])
+        lanes = pl.ds(lane, LANES)
+        arrived = (near[0, :, lanes] + far[0, :, lanes]).T * info[1:2, :]
+        for at in range(0, LANES, LANES // 2):
+            here, there = pl.ds(lane + at, LANES // 2), pl.ds(rows + lane + at, LANES // 2)
+            gradient = own[here, :] + arrived[at : at + LANES // 2]
+            first_new = first_base[here, :] + (1.0 - BETA_ONE) * gradient
+            second_new = second_base[here, :] + (1.0 - BETA_TWO) * gradient * gradient
+            held_first[here, :] = first_new
+            held_second[here, :] = second_new
+            held_params[here, :] = base[here, :] - step[here, :] * first_new / (
+                jnp.sqrt(second_new * (1.0 / CORRECT_TWO)) + ADAM_EPS
+            )
+            for source, target in ((held_first, new_first), (held_second, new_second), (held_params, new_params)):
+                send(copies, sems, source.at[here], target.at[0, there])
     for copy in copies:
         copy.wait()
 
@@ -379,7 +382,7 @@
             in_specs=[VMEM] * 8 + [HBM] * 3,
             out_specs=[HBM] * 3,
             input_output_aliases={8: 0, 9: 1, 10: 2},
-            scratch_shapes=[held_half] * 3 + [pltpu.SemaphoreType.DMA((3 * groups,))],
+            scratch_shapes=[held_half] * 3 + [pltpu.SemaphoreType.DMA((6 * groups,))],
             compiler_params=room,
             cost_estimate=free,
             name="right_step",

time: 25.8 us -> 25.8 us (level)
  no operation moved by 1% of the time
where the time goes in v20:
time: 25.8 us; the launch traced here: 25.7 us
  starting transfers between devices  15 us (58%)
  waiting for transfers between devices  5.28 us (20%)
  Pallas kernels  3.92 us (15%)
  between operations  1.41 us (5%)
    ppermute x10, starting transfers between devices, hop(): return lax.ppermute(value, axis, [(d, d ^ bit) for d in range(devices)])  15 us
    ppermute x10, waiting for transfers between devices, hop(): return lax.ppermute(value, axis, [(d, d ^ bit) for d in range(devices)])  5.28 us
    pallas_call x1, Pallas kernels, body(): pl.pallas_call(functools.partial(first_kernel, workers, (7, 6)), out_shap...  1.32 us
    pallas_call x1, Pallas kernels, body(): pl.pallas_call(left_kernel, out_shape=[block((half, width))] * 5 + [state...  1.09 us
    pallas_call x1, Pallas kernels, body(): pl.pallas_call(right_kernel, out_shape=[state] * 3, in_specs=[VMEM] * 8 +...  0.96 us
  transfers between devices with their start and end apart: 10, of which 3 were waited for; matrix products, arithmetic and copies ran while one was open for 0% of the time, Pallas kernels for 6%

profile of v20, /device:TPU:0, one launch (start us, length us, event | category | flops | bytes accessed | tf_op | source)
XLA Modules:
  0.0 25.7 jit_solution(5065172732713334336)
XLA Ops:
  0.6 0.0 copy-start
  0.6 1.3 %far_products.1 = (f32[1,128,256]{2,1,0:T(8,128)S(1)}, f32[1,128,256]{2,1,0:T(8,128)S(1)}, bf16[128,128]{1,0:T(8,128)(2,1)S(1)}, f32[8,128]{1,0:T(8,128)S(1)}) custom-call(s32[4]{0:T(128)} %counts.1, bf16[1,128,128]{2,1,0:T(8,128)(2,1)} %cotangent.1, bf16[1,128,4096]{2,1,0:T(8,128)(2,1)} %features.3), custom_call_target="tpu_custom_call" | custom-call | flops 33554432 | bytes 786432 | tf_op jit(solution)/shard_map/far_products/pallas_call | solution.py:277
  2.0 0.5 %collective-permute-start = (f32[1,128,256]{2,1,0:T(8,128)S(1)}, f32[1,128,256]{2,1,0:T(8,128)S(1)}, u32[]{:S(2)}, u32[]{:S(2)}) collective-permute-start(f32[1,128,256]{2,1,0:T(8,128)S(1)} %get-tuple-element.33), channel_id=1, source_target_pairs={{0,1},{1,0},{2,3},{3,2},{4,5},{5,4},{6,7},{7,6},{8,9},{9,8},{10,11... | collective-permute-start | bytes 393224 | tf_op jit(solution)/shard_map/ppermute | solution.py:240
  3.1 0.0 copy-done
  3.1 0.4 %rest_products.1 = (f32[7,128,256]{2,1,0:T(8,128)S(1)}, f32[7,128,256]{2,1,0:T(8,128)S(1)}) custom-call(bf16[128,128]{1,0:T(8,128)(2,1)S(1)} %get-tuple-element.29.masked, bf16[1,128,4096]{2,1,0:T(8,128)(2,1)S(1)} %copy-done), custom_call_target="tpu_custom_call" | custom-call | tf_op jit(solution)/shard_map/rest_products/pallas_call | solution.py:292
  3.6 0.0 copy-start.1
  3.6 0.0 collective-permute-done.refs_1_
  3.6 0.0 copy-start.4
  3.6 0.3 %collective-permute-start.1 = (f32[7,128,256]{2,1,0:T(8,128)S(1)}, f32[7,128,256]{2,1,0:T(8,128)S(1)}, u32[]{:S(2)}, u32[]{:S(2)}) collective-permute-start(f32[7,128,256]{2,1,0:T(8,128)S(1)} %get-tuple-element.34), channel_id=1, source_target_pairs={{0,1},{1,0},{2,3},{3,2},{4,5},{5,4},{6,7},{7,6},{8,9},{9,8},{10,11... | collective-permute-start | bytes 2752520 | tf_op jit(solution)/shard_map/ppermute | solution.py:240
  3.9 2.8 %collective-permute-start.3 = (f32[1,128,256]{2,1,0:T(8,128)S(1)}, f32[1,128,256]{2,1,0:T(8,128)S(1)}, u32[]{:S(2)}, u32[]{:S(2)}) collective-permute-start(f32[1,128,256]{2,1,0:T(8,128)S(1)} %add_a1.1.after), channel_id=1, source_target_pairs={{0,2},{1,3},{2,0},{3,1},{4,6},{5,7},{6,4},{7,5},{8,10},{9,11},{10,... | collective-permute-start | bytes 393224 | tf_op jit(solution)/shard_map/ppermute | solution.py:240
  6.8 0.0 copy-done.1
  6.8 0.0 copy-done.4
  6.8 0.1 drift.1
  6.8 0.0 collective-permute-done.1.refs_1_.come
  6.9 2.2 %collective-permute-start.2 = (f32[1,128,256]{2,1,0:T(8,128)S(1)}, f32[1,128,256]{2,1,0:T(8,128)S(1)}, u32[]{:S(2)}, u32[]{:S(2)}) collective-permute-start(f32[1,128,256]{2,1,0:T(8,128)S(1)} %add_a2.1.refs_2_), channel_id=1, source_target_pairs={{0,2},{1,3},{2,0},{3,1},{4,6},{5,7},{6,4},{7,5},{8,10},{9,11},{10,... | collective-permute-start | bytes 393224 | tf_op jit(solution)/shard_map/ppermute | solution.py:240
  9.0 1.5 %collective-permute-start.8 = (f32[128,128]{1,0:T(8,128)S(1)}, f32[128,128]{1,0:T(8,128)S(1)}, u32[]{:S(2)}, u32[]{:S(2)}) collective-permute-start(f32[128,128]{1,0:T(8,128)S(1)} %get-tuple-element.38.refs_2_), channel_id=1, source_target_pairs={{0,16},{8,24},{16,0},{24,8},{1,17},{9,25},{17,1},{25,9},{2,18},{10... | collective-permute-start | bytes 196616 | tf_op jit(solution)/shard_map/ppermute | solution.py:240
  10.6 0.5 %collective-permute-start.7 = (f32[1,128,256]{2,1,0:T(8,128)S(1)}, f32[1,128,256]{2,1,0:T(8,128)S(1)}, u32[]{:S(2)}, u32[]{:S(2)}) collective-permute-start(f32[1,128,256]{2,1,0:T(8,128)S(1)} %add_n1.1), channel_id=1, source_target_pairs={{0,2},{1,3},{2,0},{3,1},{4,6},{5,7},{6,4},{7,5},{8,10},{9,11},{10,... | collective-permute-start | bytes 393224 | tf_op jit(solution)/shard_map/ppermute | solution.py:240
  11.1 0.0 collective-permute-done.3.refs_2_
  11.1 2.8 %collective-permute-start.6 = (f32[1,128,256]{2,1,0:T(8,128)S(1)}, f32[1,128,256]{2,1,0:T(8,128)S(1)}, u32[]{:S(2)}, u32[]{:S(2)}) collective-permute-start(f32[1,128,256]{2,1,0:T(8,128)S(1)} %add_c1.1.refs_3_.refs_2_), channel_id=1, source_target_pairs={{0,4},{1,5},{2,6},{3,7},{4,0},{5,1},{6,2},{7,3},{8,12},{9,13},{10,... | collective-permute-start | bytes 393224 | tf_op jit(solution)/shard_map/ppermute | solution.py:240
  13.9 1.6 %collective-permute-start.5 = (f32[1,128,256]{2,1,0:T(8,128)S(1)}, f32[1,128,256]{2,1,0:T(8,128)S(1)}, u32[]{:S(2)}, u32[]{:S(2)}) collective-permute-start(f32[1,128,256]{2,1,0:T(8,128)S(1)} %add_n2.1), channel_id=1, source_target_pairs={{0,2},{1,3},{2,0},{3,1},{4,6},{5,7},{6,4},{7,5},{8,10},{9,11},{10,... | collective-permute-start | bytes 393224 | tf_op jit(solution)/shard_map/ppermute | solution.py:240
  15.6 0.0 collective-permute-done.2.refs_2_
  15.6 0.0 copy-start.5
  15.6 1.1 %collective-permute-start.4 = (f32[1,128,256]{2,1,0:T(8,128)S(1)}, f32[1,128,256]{2,1,0:T(8,128)S(1)}, u32[]{:S(2)}, u32[]{:S(2)}) collective-permute-start(f32[1,128,256]{2,1,0:T(8,128)S(1)} %add_c2.1), channel_id=1, source_target_pairs={{0,4},{1,5},{2,6},{3,7},{4,0},{5,1},{6,2},{7,3},{8,12},{9,13},{10,... | collective-permute-start | bytes 393224 | tf_op jit(solution)/shard_map/ppermute | solution.py:240
  16.7 0.0 collective-permute-done.8
  16.8 1.6 %collective-permute-start.9 = (f32[128,128]{1,0:T(8,128)S(1)}, f32[128,128]{1,0:T(8,128)S(1)}, u32[]{:S(2)}, u32[]{:S(2)}) collective-permute-start(f32[128,128]{1,0:T(8,128)S(1)} %add.3.drift), channel_id=1, source_target_pairs={{0,8},{8,0},{16,24},{24,16},{1,9},{9,1},{17,25},{25,17},{2,10},{10... | collective-permute-start | bytes 196616 | tf_op jit(solution)/shard_map/ppermute | solution.py:240
  18.3 2.3 %collective-permute-done.7.near = f32[1,128,256]{2,1,0:T(8,128)S(1)} collective-permute-done((f32[1,128,256]{2,1,0:T(8,128)S(1)}, f32[1,128,256]{2,1,0:T(8,128)S(1)}, u32[]{:S(2)}, u32[]{:S(2)}) %collective-permute-start.7) | collective-permute-done | bytes 131104 | tf_op jit(solution)/shard_map/ppermute | solution.py:240
  20.6 0.0 collective-permute-done.6.far
  20.6 0.5 %collective-permute-done.9.other_drift = f32[128,128]{1,0:T(8,128)S(1)} collective-permute-done((f32[128,128]{1,0:T(8,128)S(1)}, f32[128,128]{1,0:T(8,128)S(1)}, u32[]{:S(2)}, u32[]{:S(2)}) %collective-permute-start.9) | collective-permute-done | bytes 65568 | tf_op jit(solution)/shard_map/ppermute | solution.py:240
  21.1 1.1 %left_step.1 = (f32[256,128]{1,0:T(8,128)S(1)}, f32[256,128]{1,0:T(8,128)S(1)}, f32[256,128]{1,0:T(8,128)S(1)}, f32[256,128]{1,0:T(8,128)S(1)}, f32[256,128]{1,0...) custom-call(f32[1,512,128]{2,1,0:T(8,128)S(1)} %copy-done.1, ...), custom_call_target="tpu_custom_call" | custom-call | flops 983040 | bytes 1310720 | tf_op jit(solution)/shard_map/left_step/pallas_call | solution.py:352
  22.2 2.5 %collective-permute-done.5.near = f32[1,128,256]{2,1,0:T(8,128)S(1)} collective-permute-done((f32[1,128,256]{2,1,0:T(8,128)S(1)}, f32[1,128,256]{2,1,0:T(8,128)S(1)}, u32[]{:S(2)}, u32[]{:S(2)}) %collective-permute-start.5) | collective-permute-done | bytes 131104 | tf_op jit(solution)/shard_map/ppermute | solution.py:240
  24.7 0.0 collective-permute-done.4.far
  24.7 1.0 %right_step.1 = (f32[1,512,128]{2,1,0:T(8,128)}, f32[1,512,128]{2,1,0:T(8,128)}, f32[1,512,128]{2,1,0:T(8,128)}) custom-call(f32[1,128,256]{2,1,0:T(8,128)S(1)} %collective-permute-done.4.far, f32[1,128,256]{2,1,0:T(8,128)S(1)} %collective-permute-done.5.near, ...), custom_call_target="tpu_custom_call", output_to_operand_aliasing={{0}: (8, {}), {1}: (9, {}), {2}: (10, {})} | custom-call | tf_op jit(solution)/shard_map/right_step/pallas_call | solution.py:379
  (12 shorter events, 0.1 us)
Async XLA Ops:
  0.6 2.5 %copy-start = (bf16[1,128,4096]{2,1,0:T(8,128)(2,1)S(1)}, bf16[1,128,4096]{2,1,0:T(8,128)(2,1)}, u32[]{:S(2)}) copy-start(bf16[1,128,4096]{2,1,0:T(8,128)(2,1)} %features.3) | copy-start | bytes 3145732
  2.0 1.6 %collective-permute-start = (f32[1,128,256]{2,1,0:T(8,128)S(1)}, f32[1,128,256]{2,1,0:T(8,128)S(1)}, u32[]{:S(2)}, u32[]{:S(2)}) collective-permute-start(f32[1,128,256]{2,1,0:T(8,128)S(1)} %get-tuple-element.33), channel_id=1, source_target_pairs={{0,1},{1,0},{2,3},{3,2},{4,5},{5,4},{6,7},{7,6},{8,9},{9,8},{10,11... | collective-permute-start | bytes 393224 | tf_op jit(solution)/shard_map/ppermute | solution.py:240
  3.6 3.2 %copy-start.1 = (f32[1,512,128]{2,1,0:T(8,128)S(1)}, f32[1,512,128]{2,1,0:T(8,128)}, u32[]{:S(2)}) copy-start(f32[1,512,128]{2,1,0:T(8,128)} %params.3) | copy-start | bytes 786436
  3.6 3.2 %copy-start.4 = (f32[128,128]{1,0:T(8,128)S(1)}, f32[128,128]{1,0:T(8,128)}, u32[]{:S(2)}) copy-start(f32[128,128]{1,0:T(8,128)} %global_fragment.3) | copy-start | bytes 196612
  3.6 3.2 %collective-permute-start.1 = (f32[7,128,256]{2,1,0:T(8,128)S(1)}, f32[7,128,256]{2,1,0:T(8,128)S(1)}, u32[]{:S(2)}, u32[]{:S(2)}) collective-permute-start(f32[7,128,256]{2,1,0:T(8,128)S(1)} %get-tuple-element.34), channel_id=1, source_target_pairs={{0,1},{1,0},{2,3},{3,2},{4,5},{5,4},{6,7},{7,6},{8,9},{9,8},{10,11... | collective-permute-start | bytes 2752520 | tf_op jit(solution)/shard_map/ppermute | solution.py:240
  3.9 7.2 %collective-permute-start.3 = (f32[1,128,256]{2,1,0:T(8,128)S(1)}, f32[1,128,256]{2,1,0:T(8,128)S(1)}, u32[]{:S(2)}, u32[]{:S(2)}) collective-permute-start(f32[1,128,256]{2,1,0:T(8,128)S(1)} %add_a1.1.after), channel_id=1, source_target_pairs={{0,2},{1,3},{2,0},{3,1},{4,6},{5,7},{6,4},{7,5},{8,10},{9,11},{10,... | collective-permute-start | bytes 393224 | tf_op jit(solution)/shard_map/ppermute | solution.py:240
  6.9 8.7 %collective-permute-start.2 = (f32[1,128,256]{2,1,0:T(8,128)S(1)}, f32[1,128,256]{2,1,0:T(8,128)S(1)}, u32[]{:S(2)}, u32[]{:S(2)}) collective-permute-start(f32[1,128,256]{2,1,0:T(8,128)S(1)} %add_a2.1.refs_2_), channel_id=1, source_target_pairs={{0,2},{1,3},{2,0},{3,1},{4,6},{5,7},{6,4},{7,5},{8,10},{9,11},{10,... | collective-permute-start | bytes 393224 | tf_op jit(solution)/shard_map/ppermute | solution.py:240
  9.0 7.7 %collective-permute-start.8 = (f32[128,128]{1,0:T(8,128)S(1)}, f32[128,128]{1,0:T(8,128)S(1)}, u32[]{:S(2)}, u32[]{:S(2)}) collective-permute-start(f32[128,128]{1,0:T(8,128)S(1)} %get-tuple-element.38.refs_2_), channel_id=1, source_target_pairs={{0,16},{8,24},{16,0},{24,8},{1,17},{9,25},{17,1},{25,9},{2,18},{10... | collective-permute-start | bytes 196616 | tf_op jit(solution)/shard_map/ppermute | solution.py:240
  10.6 10.0 %collective-permute-start.7 = (f32[1,128,256]{2,1,0:T(8,128)S(1)}, f32[1,128,256]{2,1,0:T(8,128)S(1)}, u32[]{:S(2)}, u32[]{:S(2)}) collective-permute-start(f32[1,128,256]{2,1,0:T(8,128)S(1)} %add_n1.1), channel_id=1, source_target_pairs={{0,2},{1,3},{2,0},{3,1},{4,6},{5,7},{6,4},{7,5},{8,10},{9,11},{10,... | collective-permute-start | bytes 393224 | tf_op jit(solution)/shard_map/ppermute | solution.py:240
  11.1 9.5 %collective-permute-start.6 = (f32[1,128,256]{2,1,0:T(8,128)S(1)}, f32[1,128,256]{2,1,0:T(8,128)S(1)}, u32[]{:S(2)}, u32[]{:S(2)}) collective-permute-start(f32[1,128,256]{2,1,0:T(8,128)S(1)} %add_c1.1.refs_3_.refs_2_), channel_id=1, source_target_pairs={{0,4},{1,5},{2,6},{3,7},{4,0},{5,1},{6,2},{7,3},{8,12},{9,13},{10,... | collective-permute-start | bytes 393224 | tf_op jit(solution)/shard_map/ppermute | solution.py:240
  13.9 10.8 %collective-permute-start.5 = (f32[1,128,256]{2,1,0:T(8,128)S(1)}, f32[1,128,256]{2,1,0:T(8,128)S(1)}, u32[]{:S(2)}, u32[]{:S(2)}) collective-permute-start(f32[1,128,256]{2,1,0:T(8,128)S(1)} %add_n2.1), channel_id=1, source_target_pairs={{0,2},{1,3},{2,0},{3,1},{4,6},{5,7},{6,4},{7,5},{8,10},{9,11},{10,... | collective-permute-start | bytes 393224 | tf_op jit(solution)/shard_map/ppermute | solution.py:240
  15.6 5.5 %copy-start.2 = (f32[1,512,128]{2,1,0:T(8,128)S(1)}, f32[1,512,128]{2,1,0:T(8,128)}, u32[]{:S(2)}) copy-start(f32[1,512,128]{2,1,0:T(8,128)} %first.1) | copy-start | bytes 786436
  15.6 5.5 %copy-start.3 = (f32[1,512,128]{2,1,0:T(8,128)S(1)}, f32[1,512,128]{2,1,0:T(8,128)}, u32[]{:S(2)}) copy-start(f32[1,512,128]{2,1,0:T(8,128)} %second.1) | copy-start | bytes 786436
  15.6 5.5 %copy-start.5 = (f32[128,128]{1,0:T(8,128)S(1)}, f32[128,128]{1,0:T(8,128)}, u32[]{:S(2)}) copy-start(f32[128,128]{1,0:T(8,128)} %outer_momentum.1) | copy-start | bytes 196612
  15.6 9.1 %collective-permute-start.4 = (f32[1,128,256]{2,1,0:T(8,128)S(1)}, f32[1,128,256]{2,1,0:T(8,128)S(1)}, u32[]{:S(2)}, u32[]{:S(2)}) collective-permute-start(f32[1,128,256]{2,1,0:T(8,128)S(1)} %add_c2.1), channel_id=1, source_target_pairs={{0,4},{1,5},{2,6},{3,7},{4,0},{5,1},{6,2},{7,3},{8,12},{9,13},{10,... | collective-permute-start | bytes 393224 | tf_op jit(solution)/shard_map/ppermute | solution.py:240
  16.8 4.3 %collective-permute-start.9 = (f32[128,128]{1,0:T(8,128)S(1)}, f32[128,128]{1,0:T(8,128)S(1)}, u32[]{:S(2)}, u32[]{:S(2)}) collective-permute-start(f32[128,128]{1,0:T(8,128)S(1)} %add.3.drift), channel_id=1, source_target_pairs={{0,8},{8,0},{16,24},{24,16},{1,9},{9,1},{17,25},{25,17},{2,10},{10... | collective-permute-start | bytes 196616 | tf_op jit(solution)/shard_map/ppermute | solution.py:240

commit v21 on v19

--- a/solution.py
+++ b/solution.py
@@ -71,8 +71,7 @@
     for other in range(1, workers):
         total = total + counts_held[other]
     info[0:1, :] = jnp.full((1, info.shape[1]), count.astype(jnp.float32))
-    info[1:2, :] = 1.0 / info[0:1, :]
-    info[2:3, :] = 1.0 / jnp.full((1, info.shape[1]), total.astype(jnp.float32))
+    info[1:2, :] = jnp.full((1, info.shape[1]), total.astype(jnp.float32))
 
 
 def rest_kernel(masked, features, away, kept):
@@ -83,7 +82,7 @@
             into[at] = product(masked[...], features[0, :, columns])
 
 
-def drift_kernel(info, fragment, params, global_fragment, after, drift, scale):
+def drift_kernel(info, fragment, params, global_fragment, after, drift, scale, rates):
     del after
     index = fragment[0]
     pieces = drift.shape[0]
@@ -91,6 +90,7 @@
     for at in range(1, FRAGS):
         old = jnp.where(index == at, params[0, pl.ds(at, pieces, stride=FRAGS), :], old)
     drift[...] = info[0:1, :] * (global_fragment[...] - old)
+    rates[1:3, :] = 1.0 / info[0:2, :]
     rows = lax.broadcasted_iota(jnp.int32, scale.shape, 0)
     scale[...] = jnp.where(lax.rem(rows, FRAGS) == index, 1.0 - MIXING, 1.0)
 
@@ -317,11 +317,11 @@
         far_left = hop(sent, "fsdp", devices, 2)
         away, _ = lax.optimization_barrier((away, sent))
         come = hop(away, "fsdp", devices, 1)
-        drift, scale = pl.pallas_call(
+        drift, scale, rates = pl.pallas_call(
             drift_kernel,
-            out_shape=[piece, block((rows, width))],
+            out_shape=[piece, block((rows, width)), block((8, width))],
             in_specs=[VMEM, SMEM, VMEM, VMEM, ANY],
-            out_specs=[VMEM] * 2,
+            out_specs=[VMEM] * 3,
             compiler_params=room,
             cost_estimate=free,
             name="drift",
@@ -367,7 +367,7 @@
             come,
             far_left,
             near_left,
-            info,
+            rates,
             scale,
             global_fragment,
             outer_momentum,
@@ -383,7 +383,7 @@
             compiler_params=room,
             cost_estimate=free,
             name="right_step",
-        )(far_right, near_right, info, own, first_base, second_base, base, step, *results)
+        )(far_right, near_right, rates, own, first_base, second_base, base, step, *results)
         return new_params, new_first, new_second, new_global, new_momentum
 
     return body

time: 25.8 us -> 25.8 us (level)
  no operation moved by 1% of the time
where the time goes in v21:
time: 25.8 us; the launch traced here: 25.6 us
  starting transfers between devices  15 us (58%)
  waiting for transfers between devices  5.29 us (21%)
  Pallas kernels  3.9 us (15%)
  between operations  1.41 us (5%)
    ppermute x10, starting transfers between devices, hop(): return lax.ppermute(value, axis, [(d, d ^ bit) for d in range(devices)])  15 us
    ppermute x10, waiting for transfers between devices, hop(): return lax.ppermute(value, axis, [(d, d ^ bit) for d in range(devices)])  5.29 us
    pallas_call x1, Pallas kernels, body(): pl.pallas_call(functools.partial(first_kernel, workers, (7, 6)), out_shap...  1.31 us
    pallas_call x1, Pallas kernels, body(): pl.pallas_call(left_kernel, out_shape=[block((half, width))] * 5 + [state...  1.09 us
    pallas_call x1, Pallas kernels, body(): pl.pallas_call(right_kernel, out_shape=[state] * 3, in_specs=[VMEM] * 8 +...  0.94 us
  transfers between devices with their start and end apart: 10, of which 3 were waited for; matrix products, arithmetic and copies ran while one was open for 0% of the time, Pallas kernels for 6%

profile of v21, /device:TPU:0, one launch (start us, length us, event | category | flops | bytes accessed | tf_op | source)
XLA Modules:
  0.0 25.6 jit_solution(14238921251193610348)
XLA Ops:
  0.6 0.0 copy-start
  0.6 1.3 %far_products.1 = (f32[1,128,256]{2,1,0:T(8,128)S(1)}, f32[1,128,256]{2,1,0:T(8,128)S(1)}, bf16[128,128]{1,0:T(8,128)(2,1)S(1)}, f32[8,128]{1,0:T(8,128)S(1)}) custom-call(s32[4]{0:T(128)} %counts.1, bf16[1,128,128]{2,1,0:T(8,128)(2,1)} %cotangent.1, bf16[1,128,4096]{2,1,0:T(8,128)(2,1)} %features.3), custom_call_target="tpu_custom_call" | custom-call | flops 33554432 | bytes 786432 | tf_op jit(solution)/shard_map/far_products/pallas_call | solution.py:274
  2.0 0.5 %collective-permute-start = (f32[1,128,256]{2,1,0:T(8,128)S(1)}, f32[1,128,256]{2,1,0:T(8,128)S(1)}, u32[]{:S(2)}, u32[]{:S(2)}) collective-permute-start(f32[1,128,256]{2,1,0:T(8,128)S(1)} %get-tuple-element.34), channel_id=1, source_target_pairs={{0,1},{1,0},{2,3},{3,2},{4,5},{5,4},{6,7},{7,6},{8,9},{9,8},{10,11... | collective-permute-start | bytes 393224 | tf_op jit(solution)/shard_map/ppermute | solution.py:237
  3.1 0.0 copy-done
  3.1 0.4 %rest_products.1 = (f32[7,128,256]{2,1,0:T(8,128)S(1)}, f32[7,128,256]{2,1,0:T(8,128)S(1)}) custom-call(bf16[128,128]{1,0:T(8,128)(2,1)S(1)} %get-tuple-element.30.masked, bf16[1,128,4096]{2,1,0:T(8,128)(2,1)S(1)} %copy-done), custom_call_target="tpu_custom_call" | custom-call | tf_op jit(solution)/shard_map/rest_products/pallas_call | solution.py:289
  3.6 0.0 copy-start.1
  3.6 0.0 collective-permute-done.refs_1_
  3.6 0.0 copy-start.4
  3.6 0.3 %collective-permute-start.1 = (f32[7,128,256]{2,1,0:T(8,128)S(1)}, f32[7,128,256]{2,1,0:T(8,128)S(1)}, u32[]{:S(2)}, u32[]{:S(2)}) collective-permute-start(f32[7,128,256]{2,1,0:T(8,128)S(1)} %get-tuple-element.35), channel_id=1, source_target_pairs={{0,1},{1,0},{2,3},{3,2},{4,5},{5,4},{6,7},{7,6},{8,9},{9,8},{10,11... | collective-permute-start | bytes 2752520 | tf_op jit(solution)/shard_map/ppermute | solution.py:237
  3.9 2.8 %collective-permute-start.3 = (f32[1,128,256]{2,1,0:T(8,128)S(1)}, f32[1,128,256]{2,1,0:T(8,128)S(1)}, u32[]{:S(2)}, u32[]{:S(2)}) collective-permute-start(f32[1,128,256]{2,1,0:T(8,128)S(1)} %add_a1.1.after), channel_id=1, source_target_pairs={{0,2},{1,3},{2,0},{3,1},{4,6},{5,7},{6,4},{7,5},{8,10},{9,11},{10,... | collective-permute-start | bytes 393224 | tf_op jit(solution)/shard_map/ppermute | solution.py:237
  6.8 0.0 copy-done.1
  6.8 0.0 copy-done.4
  6.8 0.1 drift.1
  6.8 0.0 collective-permute-done.1.refs_1_.come
  6.9 2.2 %collective-permute-start.2 = (f32[1,128,256]{2,1,0:T(8,128)S(1)}, f32[1,128,256]{2,1,0:T(8,128)S(1)}, u32[]{:S(2)}, u32[]{:S(2)}) collective-permute-start(f32[1,128,256]{2,1,0:T(8,128)S(1)} %add_a2.1.refs_2_), channel_id=1, source_target_pairs={{0,2},{1,3},{2,0},{3,1},{4,6},{5,7},{6,4},{7,5},{8,10},{9,11},{10,... | collective-permute-start | bytes 393224 | tf_op jit(solution)/shard_map/ppermute | solution.py:237
  9.0 1.5 %collective-permute-start.8 = (f32[128,128]{1,0:T(8,128)S(1)}, f32[128,128]{1,0:T(8,128)S(1)}, u32[]{:S(2)}, u32[]{:S(2)}) collective-permute-start(f32[128,128]{1,0:T(8,128)S(1)} %get-tuple-element.40.refs_2_), channel_id=1, source_target_pairs={{0,16},{8,24},{16,0},{24,8},{1,17},{9,25},{17,1},{25,9},{2,18},{10... | collective-permute-start | bytes 196616 | tf_op jit(solution)/shard_map/ppermute | solution.py:237
  10.6 0.5 %collective-permute-start.7 = (f32[1,128,256]{2,1,0:T(8,128)S(1)}, f32[1,128,256]{2,1,0:T(8,128)S(1)}, u32[]{:S(2)}, u32[]{:S(2)}) collective-permute-start(f32[1,128,256]{2,1,0:T(8,128)S(1)} %add_n1.1), channel_id=1, source_target_pairs={{0,2},{1,3},{2,0},{3,1},{4,6},{5,7},{6,4},{7,5},{8,10},{9,11},{10,... | collective-permute-start | bytes 393224 | tf_op jit(solution)/shard_map/ppermute | solution.py:237
  11.1 0.0 collective-permute-done.3.refs_2_
  11.1 2.8 %collective-permute-start.6 = (f32[1,128,256]{2,1,0:T(8,128)S(1)}, f32[1,128,256]{2,1,0:T(8,128)S(1)}, u32[]{:S(2)}, u32[]{:S(2)}) collective-permute-start(f32[1,128,256]{2,1,0:T(8,128)S(1)} %add_c1.1.refs_3_.refs_2_), channel_id=1, source_target_pairs={{0,4},{1,5},{2,6},{3,7},{4,0},{5,1},{6,2},{7,3},{8,12},{9,13},{10,... | collective-permute-start | bytes 393224 | tf_op jit(solution)/shard_map/ppermute | solution.py:237
  13.9 1.6 %collective-permute-start.5 = (f32[1,128,256]{2,1,0:T(8,128)S(1)}, f32[1,128,256]{2,1,0:T(8,128)S(1)}, u32[]{:S(2)}, u32[]{:S(2)}) collective-permute-start(f32[1,128,256]{2,1,0:T(8,128)S(1)} %add_n2.1), channel_id=1, source_target_pairs={{0,2},{1,3},{2,0},{3,1},{4,6},{5,7},{6,4},{7,5},{8,10},{9,11},{10,... | collective-permute-start | bytes 393224 | tf_op jit(solution)/shard_map/ppermute | solution.py:237
  15.6 0.0 collective-permute-done.2.refs_2_
  15.6 0.0 copy-start.5
  15.6 1.1 %collective-permute-start.4 = (f32[1,128,256]{2,1,0:T(8,128)S(1)}, f32[1,128,256]{2,1,0:T(8,128)S(1)}, u32[]{:S(2)}, u32[]{:S(2)}) collective-permute-start(f32[1,128,256]{2,1,0:T(8,128)S(1)} %add_c2.1), channel_id=1, source_target_pairs={{0,4},{1,5},{2,6},{3,7},{4,0},{5,1},{6,2},{7,3},{8,12},{9,13},{10,... | collective-permute-start | bytes 393224 | tf_op jit(solution)/shard_map/ppermute | solution.py:237
  16.7 0.0 collective-permute-done.8
  16.8 1.6 %collective-permute-start.9 = (f32[128,128]{1,0:T(8,128)S(1)}, f32[128,128]{1,0:T(8,128)S(1)}, u32[]{:S(2)}, u32[]{:S(2)}) collective-permute-start(f32[128,128]{1,0:T(8,128)S(1)} %add.3.drift), channel_id=1, source_target_pairs={{0,8},{8,0},{16,24},{24,16},{1,9},{9,1},{17,25},{25,17},{2,10},{10... | collective-permute-start | bytes 196616 | tf_op jit(solution)/shard_map/ppermute | solution.py:237
  18.3 2.3 %collective-permute-done.7.near = f32[1,128,256]{2,1,0:T(8,128)S(1)} collective-permute-done((f32[1,128,256]{2,1,0:T(8,128)S(1)}, f32[1,128,256]{2,1,0:T(8,128)S(1)}, u32[]{:S(2)}, u32[]{:S(2)}) %collective-permute-start.7) | collective-permute-done | bytes 131104 | tf_op jit(solution)/shard_map/ppermute | solution.py:237
  20.6 0.0 collective-permute-done.6.far
  20.6 0.5 %collective-permute-done.9.other_drift = f32[128,128]{1,0:T(8,128)S(1)} collective-permute-done((f32[128,128]{1,0:T(8,128)S(1)}, f32[128,128]{1,0:T(8,128)S(1)}, u32[]{:S(2)}, u32[]{:S(2)}) %collective-permute-start.9) | collective-permute-done | bytes 65568 | tf_op jit(solution)/shard_map/ppermute | solution.py:237
  21.1 1.1 %left_step.1 = (f32[256,128]{1,0:T(8,128)S(1)}, f32[256,128]{1,0:T(8,128)S(1)}, f32[256,128]{1,0:T(8,128)S(1)}, f32[256,128]{1,0:T(8,128)S(1)}, f32[256,128]{1,0...) custom-call(f32[1,512,128]{2,1,0:T(8,128)S(1)} %copy-done.1, ...), custom_call_target="tpu_custom_call" | custom-call | flops 983040 | bytes 1310720 | tf_op jit(solution)/shard_map/left_step/pallas_call | solution.py:349
  22.2 2.5 %collective-permute-done.5.near = f32[1,128,256]{2,1,0:T(8,128)S(1)} collective-permute-done((f32[1,128,256]{2,1,0:T(8,128)S(1)}, f32[1,128,256]{2,1,0:T(8,128)S(1)}, u32[]{:S(2)}, u32[]{:S(2)}) %collective-permute-start.5) | collective-permute-done | bytes 131104 | tf_op jit(solution)/shard_map/ppermute | solution.py:237
  24.7 0.0 collective-permute-done.4.far
  24.7 0.9 %right_step.1 = (f32[1,512,128]{2,1,0:T(8,128)}, f32[1,512,128]{2,1,0:T(8,128)}, f32[1,512,128]{2,1,0:T(8,128)}) custom-call(f32[1,128,256]{2,1,0:T(8,128)S(1)} %collective-permute-done.4.far, f32[1,128,256]{2,1,0:T(8,128)S(1)} %collective-permute-done.5.near, ...), custom_call_target="tpu_custom_call", output_to_operand_aliasing={{0}: (8, {}), {1}: (9, {}), {2}: (10, {})} | custom-call | tf_op jit(solution)/shard_map/right_step/pallas_call | solution.py:376
  (12 shorter events, 0.1 us)
Async XLA Ops:
  0.6 2.5 %copy-start = (bf16[1,128,4096]{2,1,0:T(8,128)(2,1)S(1)}, bf16[1,128,4096]{2,1,0:T(8,128)(2,1)}, u32[]{:S(2)}) copy-start(bf16[1,128,4096]{2,1,0:T(8,128)(2,1)} %features.3) | copy-start | bytes 3145732
  2.0 1.6 %collective-permute-start = (f32[1,128,256]{2,1,0:T(8,128)S(1)}, f32[1,128,256]{2,1,0:T(8,128)S(1)}, u32[]{:S(2)}, u32[]{:S(2)}) collective-permute-start(f32[1,128,256]{2,1,0:T(8,128)S(1)} %get-tuple-element.34), channel_id=1, source_target_pairs={{0,1},{1,0},{2,3},{3,2},{4,5},{5,4},{6,7},{7,6},{8,9},{9,8},{10,11... | collective-permute-start | bytes 393224 | tf_op jit(solution)/shard_map/ppermute | solution.py:237
  3.6 3.2 %copy-start.1 = (f32[1,512,128]{2,1,0:T(8,128)S(1)}, f32[1,512,128]{2,1,0:T(8,128)}, u32[]{:S(2)}) copy-start(f32[1,512,128]{2,1,0:T(8,128)} %params.3) | copy-start | bytes 786436
  3.6 3.2 %copy-start.4 = (f32[128,128]{1,0:T(8,128)S(1)}, f32[128,128]{1,0:T(8,128)}, u32[]{:S(2)}) copy-start(f32[128,128]{1,0:T(8,128)} %global_fragment.3) | copy-start | bytes 196612
  3.6 3.2 %collective-permute-start.1 = (f32[7,128,256]{2,1,0:T(8,128)S(1)}, f32[7,128,256]{2,1,0:T(8,128)S(1)}, u32[]{:S(2)}, u32[]{:S(2)}) collective-permute-start(f32[7,128,256]{2,1,0:T(8,128)S(1)} %get-tuple-element.35), channel_id=1, source_target_pairs={{0,1},{1,0},{2,3},{3,2},{4,5},{5,4},{6,7},{7,6},{8,9},{9,8},{10,11... | collective-permute-start | bytes 2752520 | tf_op jit(solution)/shard_map/ppermute | solution.py:237
  3.9 7.2 %collective-permute-start.3 = (f32[1,128,256]{2,1,0:T(8,128)S(1)}, f32[1,128,256]{2,1,0:T(8,128)S(1)}, u32[]{:S(2)}, u32[]{:S(2)}) collective-permute-start(f32[1,128,256]{2,1,0:T(8,128)S(1)} %add_a1.1.after), channel_id=1, source_target_pairs={{0,2},{1,3},{2,0},{3,1},{4,6},{5,7},{6,4},{7,5},{8,10},{9,11},{10,... | collective-permute-start | bytes 393224 | tf_op jit(solution)/shard_map/ppermute | solution.py:237
  6.9 8.7 %collective-permute-start.2 = (f32[1,128,256]{2,1,0:T(8,128)S(1)}, f32[1,128,256]{2,1,0:T(8,128)S(1)}, u32[]{:S(2)}, u32[]{:S(2)}) collective-permute-start(f32[1,128,256]{2,1,0:T(8,128)S(1)} %add_a2.1.refs_2_), channel_id=1, source_target_pairs={{0,2},{1,3},{2,0},{3,1},{4,6},{5,7},{6,4},{7,5},{8,10},{9,11},{10,... | collective-permute-start | bytes 393224 | tf_op jit(solution)/shard_map/ppermute | solution.py:237
  9.0 7.7 %collective-permute-start.8 = (f32[128,128]{1,0:T(8,128)S(1)}, f32[128,128]{1,0:T(8,128)S(1)}, u32[]{:S(2)}, u32[]{:S(2)}) collective-permute-start(f32[128,128]{1,0:T(8,128)S(1)} %get-tuple-element.40.refs_2_), channel_id=1, source_target_pairs={{0,16},{8,24},{16,0},{24,8},{1,17},{9,25},{17,1},{25,9},{2,18},{10... | collective-permute-start | bytes 196616 | tf_op jit(solution)/shard_map/ppermute | solution.py:237
  10.6 10.0 %collective-permute-start.7 = (f32[1,128,256]{2,1,0:T(8,128)S(1)}, f32[1,128,256]{2,1,0:T(8,128)S(1)}, u32[]{:S(2)}, u32[]{:S(2)}) collective-permute-start(f32[1,128,256]{2,1,0:T(8,128)S(1)} %add_n1.1), channel_id=1, source_target_pairs={{0,2},{1,3},{2,0},{3,1},{4,6},{5,7},{6,4},{7,5},{8,10},{9,11},{10,... | collective-permute-start | bytes 393224 | tf_op jit(solution)/shard_map/ppermute | solution.py:237
  11.1 9.5 %collective-permute-start.6 = (f32[1,128,256]{2,1,0:T(8,128)S(1)}, f32[1,128,256]{2,1,0:T(8,128)S(1)}, u32[]{:S(2)}, u32[]{:S(2)}) collective-permute-start(f32[1,128,256]{2,1,0:T(8,128)S(1)} %add_c1.1.refs_3_.refs_2_), channel_id=1, source_target_pairs={{0,4},{1,5},{2,6},{3,7},{4,0},{5,1},{6,2},{7,3},{8,12},{9,13},{10,... | collective-permute-start | bytes 393224 | tf_op jit(solution)/shard_map/ppermute | solution.py:237
  13.9 10.8 %collective-permute-start.5 = (f32[1,128,256]{2,1,0:T(8,128)S(1)}, f32[1,128,256]{2,1,0:T(8,128)S(1)}, u32[]{:S(2)}, u32[]{:S(2)}) collective-permute-start(f32[1,128,256]{2,1,0:T(8,128)S(1)} %add_n2.1), channel_id=1, source_target_pairs={{0,2},{1,3},{2,0},{3,1},{4,6},{5,7},{6,4},{7,5},{8,10},{9,11},{10,... | collective-permute-start | bytes 393224 | tf_op jit(solution)/shard_map/ppermute | solution.py:237
  15.6 5.5 %copy-start.2 = (f32[1,512,128]{2,1,0:T(8,128)S(1)}, f32[1,512,128]{2,1,0:T(8,128)}, u32[]{:S(2)}) copy-start(f32[1,512,128]{2,1,0:T(8,128)} %first.1) | copy-start | bytes 786436
  15.6 5.5 %copy-start.3 = (f32[1,512,128]{2,1,0:T(8,128)S(1)}, f32[1,512,128]{2,1,0:T(8,128)}, u32[]{:S(2)}) copy-start(f32[1,512,128]{2,1,0:T(8,128)} %second.1) | copy-start | bytes 786436
  15.6 5.5 %copy-start.5 = (f32[128,128]{1,0:T(8,128)S(1)}, f32[128,128]{1,0:T(8,128)}, u32[]{:S(2)}) copy-start(f32[128,128]{1,0:T(8,128)} %outer_momentum.1) | copy-start | bytes 196612
  15.6 9.1 %collective-permute-start.4 = (f32[1,128,256]{2,1,0:T(8,128)S(1)}, f32[1,128,256]{2,1,0:T(8,128)S(1)}, u32[]{:S(2)}, u32[]{:S(2)}) collective-permute-start(f32[1,128,256]{2,1,0:T(8,128)S(1)} %add_c2.1), channel_id=1, source_target_pairs={{0,4},{1,5},{2,6},{3,7},{4,0},{5,1},{6,2},{7,3},{8,12},{9,13},{10,... | collective-permute-start | bytes 393224 | tf_op jit(solution)/shard_map/ppermute | solution.py:237
  16.8 4.3 %collective-permute-start.9 = (f32[128,128]{1,0:T(8,128)S(1)}, f32[128,128]{1,0:T(8,128)S(1)}, u32[]{:S(2)}, u32[]{:S(2)}) collective-permute-start(f32[128,128]{1,0:T(8,128)S(1)} %add.3.drift), channel_id=1, source_target_pairs={{0,8},{8,0},{16,24},{24,16},{1,9},{9,1},{17,25},{25,17},{2,10},{10... | collective-permute-start | bytes 196616 | tf_op jit(solution)/shard_map/ppermute | solution.py:237
